TPU v7x, 32 devices: a whole 2x2x4 slice. The times are simulated.
32 devices in a mesh: dp: 2 (over x), seq: 4 (over z), tp: 4 (over y, core).
Axes of the slice: x: 2, y: 2, z: 4, core: 2. Of those that a mesh axis runs over, the one named last changes fastest.
Arguments:
- tokens: float32 [4, 1024, 768], P('dp', ('seq', 'tp')), may hold values from -6 to 6
- ln1_gain: bfloat16 [768], P('dp'), may hold values from 0.5 to 1.5
- ln1_bias: bfloat16 [768], P('dp'), may hold values from -1.5 to 1.5
- qkv_weight: bfloat16 [768, 2304], P('dp'), may hold values from -0.21875 to 0.21875
- rel_h: bfloat16 [63, 64], P(None, 'dp'), may hold values from -0.75 to 0.75
- rel_w: bfloat16 [63, 64], P(None, 'dp'), may hold values from -0.75 to 0.75
- proj_weight: bfloat16 [768, 768], P('dp'), may hold values from -3 to 3
- ln2_gain: bfloat16 [768], P('dp'), may hold values from 0.5 to 1.5
- ln2_bias: bfloat16 [768], P('dp'), may hold values from -1.5 to 1.5
- fc1_weight: bfloat16 [768, 3072], P('dp', 'tp'), may hold values from -0.21875 to 0.21875
- fc2_weight: bfloat16 [3072, 768], P('tp', 'dp'), may hold values from -0.109375 to 0.109375
- cotangent: bfloat16 [4, 1024, 768], P('dp', ('seq', 'tp')), may hold values from -6 to 6
Outputs:
- output: float32 [4, 1024, 768], P('dp', ('seq', 'tp'))
- tokens_grad: float32 [4, 1024, 768], P('dp', ('seq', 'tp'))
- ln1_gain_grad: float32 [768], P('dp')
- ln1_bias_grad: float32 [768], P('dp')
- qkv_grad: float32 [768, 2304], P('dp')
- rel_h_grad: float32 [63, 64], P(None, 'dp')
- rel_w_grad: float32 [63, 64], P(None, 'dp')
- proj_grad: float32 [768, 768], P('dp')
- ln2_gain_grad: float32 [768], P('dp')
- ln2_bias_grad: float32 [768], P('dp')
- fc1_grad: float32 [768, 3072], P('dp', 'tp')
- fc2_grad: float32 [3072, 768], P('tp', 'dp')
All inputs are finite; a program needn't handle non-finite values.
Results may differ from a plain program's by a relative error of at most 0.02.
Values may be sent and summed in bfloat16 or wider, within the bound.
No kernel may reach another device: no remote copies, remote signals or barrier semaphores. Data moves between devices by JAX's collectives and lax.ppermute only.
A program may use at most 128 MiB of HBM per device.

v0:
```python
from functools import partial

import jax
import jax.numpy as jnp
from jax import lax
from jax.sharding import PartitionSpec as P

EPS = 1e-06
HIGH = lax.Precision.HIGHEST


def layer_norm(values, gain_vec, shift_vec):
    center = values - jnp.mean(values, axis=-1, keepdims=True)
    spread = jnp.mean(center * center, axis=-1, keepdims=True)
    return center * lax.rsqrt(spread + EPS) * gain_vec + shift_vec


def rel_terms(queries, table_h, table_w, group_rows):
    grid_side = (table_h.shape[0] + 1) // 2
    head_width = table_h.shape[1]
    group_count = queries.shape[0] // grid_side
    reach_idx = jnp.arange(grid_side, dtype=jnp.int32)
    query_grid = queries.reshape(group_count, grid_side, head_width)
    pick_h = group_rows[:, None] - reach_idx[None, :] + (grid_side - 1)
    pick_w = reach_idx[:, None] - reach_idx[None, :] + (grid_side - 1)
    window_h = jnp.take(table_h, pick_h, axis=0)
    window_w = jnp.take(table_w, pick_w, axis=0)
    term_h = jnp.einsum(
        "gce,gae->gca", query_grid, window_h, precision=HIGH, preferred_element_type=jnp.float32
    )
    term_w = jnp.einsum(
        "gce,cae->gca", query_grid, window_w, precision=HIGH, preferred_element_type=jnp.float32
    )
    return (term_h.reshape(-1, grid_side), term_w.reshape(-1, grid_side))


def inner_rows(left_mat, right_mat):
    return lax.dot_general(
        left_mat, right_mat, (((0,), (0,)), ((), ())), preferred_element_type=jnp.float32
    )


def inner_cols(left_mat, right_mat):
    return lax.dot_general(
        left_mat, right_mat, (((1,), (1,)), ((), ())), preferred_element_type=jnp.float32
    )


def gelu_exact(values):
    return jax.nn.gelu(values, approximate=False)


def sum_attention(gain_one, shift_one, mix_grad, table_h, table_w, out_grad, gain_two, shift_two):
    return (
        lax.psum(gain_one.astype(jnp.bfloat16), ("seq", "tp")).astype(jnp.float32),
        lax.psum(shift_one.astype(jnp.bfloat16), ("seq", "tp")).astype(jnp.float32),
        lax.psum(mix_grad.astype(jnp.bfloat16), ("seq", "tp")).astype(jnp.float32),
        lax.psum(table_h.astype(jnp.bfloat16), ("seq", "tp")).astype(jnp.float32),
        lax.psum(table_w.astype(jnp.bfloat16), ("seq", "tp")).astype(jnp.float32),
        lax.psum(out_grad.astype(jnp.bfloat16), ("seq", "tp")).astype(jnp.float32),
        lax.psum(gain_two.astype(jnp.bfloat16), ("seq", "tp")).astype(jnp.float32),
        lax.psum(shift_two.astype(jnp.bfloat16), ("seq", "tp")).astype(jnp.float32),
    )


def sum_feedforward(up_grad, down_grad):
    return (
        lax.psum(up_grad.astype(jnp.bfloat16), "seq").astype(jnp.float32),
        lax.psum(down_grad.astype(jnp.bfloat16), "seq").astype(jnp.float32),
    )


def split_data(
    gain_one,
    shift_one,
    mix_grad,
    table_h,
    table_w,
    out_grad,
    gain_two,
    shift_two,
    up_grad,
    down_grad,
):
    return (
        lax.psum_scatter(
            gain_one.astype(jnp.bfloat16), "dp", scatter_dimension=0, tiled=True
        ).astype(jnp.float32),
        lax.psum_scatter(
            shift_one.astype(jnp.bfloat16), "dp", scatter_dimension=0, tiled=True
        ).astype(jnp.float32),
        lax.psum_scatter(
            mix_grad.astype(jnp.bfloat16), "dp", scatter_dimension=0, tiled=True
        ).astype(jnp.float32),
        lax.psum_scatter(
            table_h.astype(jnp.bfloat16), "dp", scatter_dimension=1, tiled=True
        ).astype(jnp.float32),
        lax.psum_scatter(
            table_w.astype(jnp.bfloat16), "dp", scatter_dimension=1, tiled=True
        ).astype(jnp.float32),
        lax.psum_scatter(
            out_grad.astype(jnp.bfloat16), "dp", scatter_dimension=0, tiled=True
        ).astype(jnp.float32),
        lax.psum_scatter(
            gain_two.astype(jnp.bfloat16), "dp", scatter_dimension=0, tiled=True
        ).astype(jnp.float32),
        lax.psum_scatter(
            shift_two.astype(jnp.bfloat16), "dp", scatter_dimension=0, tiled=True
        ).astype(jnp.float32),
        lax.psum_scatter(
            up_grad.astype(jnp.bfloat16), "dp", scatter_dimension=0, tiled=True
        ).astype(jnp.float32),
        lax.psum_scatter(
            down_grad.astype(jnp.bfloat16), "dp", scatter_dimension=1, tiled=True
        ).astype(jnp.float32),
    )


def on_device(
    tokens,
    ln1_gain,
    ln1_bias,
    qkv_weight,
    rel_h,
    rel_w,
    proj_weight,
    ln2_gain,
    ln2_bias,
    fc1_weight,
    fc2_weight,
    cotangent,
):
    gathered = (
        lax.all_gather(ln1_gain, "dp", axis=0, tiled=True),
        lax.all_gather(ln1_bias, "dp", axis=0, tiled=True),
        lax.all_gather(qkv_weight, "dp", axis=0, tiled=True),
        lax.all_gather(rel_h, "dp", axis=1, tiled=True),
        lax.all_gather(rel_w, "dp", axis=1, tiled=True),
        lax.all_gather(proj_weight, "dp", axis=0, tiled=True),
        lax.all_gather(ln2_gain, "dp", axis=0, tiled=True),
        lax.all_gather(ln2_bias, "dp", axis=0, tiled=True),
        lax.all_gather(fc1_weight, "dp", axis=0, tiled=True),
        lax.all_gather(fc2_weight, "dp", axis=1, tiled=True),
    )
    gain_one = gathered[0].astype(jnp.float32)
    shift_one = gathered[1].astype(jnp.float32)
    mix_weight = gathered[2]
    table_h = gathered[3].astype(jnp.float32)
    table_w = gathered[4].astype(jnp.float32)
    out_weight = gathered[5]
    gain_two = gathered[6].astype(jnp.float32)
    shift_two = gathered[7].astype(jnp.float32)
    up_weight = gathered[8]
    down_weight = gathered[9]
    images, tok_count, model_width = tokens.shape
    tp_count = lax.axis_size("tp")
    tp_index = lax.axis_index("tp")
    head_width = table_h.shape[1]
    grid_side = (table_h.shape[0] + 1) // 2
    score_scale = head_width ** (-0.5)
    flat_rows = tokens.reshape(images * tok_count, model_width)
    norm_one, pull_one = jax.vjp(layer_norm, flat_rows, gain_one, shift_one)
    norm_one_low = norm_one.astype(jnp.bfloat16)
    mixed_rows = jnp.dot(norm_one_low, mix_weight, preferred_element_type=jnp.float32).astype(
        jnp.bfloat16
    )
    mixed_rows = mixed_rows.reshape(images, tok_count, 3 * model_width)
    query_heads, key_heads, value_heads = (
        lax.all_to_all(
            mixed_rows[:, :, :model_width], "seq", split_axis=2, concat_axis=1, tiled=True
        ),
        lax.all_to_all(
            mixed_rows[:, :, model_width : 2 * model_width],
            "seq",
            split_axis=2,
            concat_axis=1,
            tiled=True,
        ),
        lax.all_to_all(
            mixed_rows[:, :, 2 * model_width :], "seq", split_axis=2, concat_axis=1, tiled=True
        ),
    )
    key_all, value_all = (
        lax.all_gather(key_heads, "tp", axis=1, tiled=True),
        lax.all_gather(value_heads, "tp", axis=1, tiled=True),
    )
    query_rows = query_heads.shape[1]
    local_width = query_heads.shape[2]
    local_heads = local_width // head_width
    key_count = key_all.shape[1]
    block_rows = min(512, query_rows)
    block_count = query_rows // block_rows
    segments = query_rows // tok_count

    def natural_order(array_in):
        return (
            array_in.reshape(images, tp_count, segments, tok_count, array_in.shape[2])
            .transpose(0, 2, 1, 3, 4)
            .reshape(images, key_count, array_in.shape[2])
        )

    def gathered_order(array_in):
        return (
            array_in.reshape(images, segments, tp_count, tok_count, array_in.shape[2])
            .transpose(0, 2, 1, 3, 4)
            .reshape(images, key_count, array_in.shape[2])
        )

    key_nat = natural_order(key_all)
    value_nat = natural_order(value_all)
    places = jnp.arange(query_rows, dtype=jnp.int32)
    query_token = (places // tok_count * tp_count + tp_index) * tok_count + places % tok_count
    group_blocks = (query_token // grid_side).reshape(
        block_count, block_rows // grid_side, grid_side
    )[:, :, 0]

    def build_bias(term_h, term_w):
        return (term_h[:, :, None] + term_w[:, None, :]).reshape(term_h.shape[0], key_count)

    def attend_image(carry_zero, pieces):
        query_img, key_img, value_img = pieces
        head_outs = []
        head_sums = []
        for head_index in range(local_heads):
            lower_col = head_index * head_width
            key_head = key_img[:, lower_col : lower_col + head_width]
            value_head = value_img[:, lower_col : lower_col + head_width]
            query_blocks = query_img[:, lower_col : lower_col + head_width].reshape(
                block_count, block_rows, head_width
            )

            def attend_block(block_in):
                query_blk, groups_blk = block_in
                term_h, term_w = rel_terms(
                    query_blk.astype(jnp.float32), table_h, table_w, groups_blk
                )
                scores = inner_cols(query_blk, key_head) * score_scale + build_bias(term_h, term_w)
                row_top = jnp.max(scores, axis=1, keepdims=True)
                expo_scores = jnp.exp(scores - row_top)
                row_total = jnp.sum(expo_scores, axis=1, keepdims=True)
                probs_low = (expo_scores / row_total).astype(jnp.bfloat16)
                result = jnp.dot(probs_low, value_head, preferred_element_type=jnp.float32)
                return (result, (row_top + jnp.log(row_total))[:, 0])

            results, log_totals = lax.map(attend_block, (query_blocks, group_blocks))
            head_outs.append(results.reshape(query_rows, head_width))
            head_sums.append(log_totals.reshape(query_rows))
        return (carry_zero, (jnp.concatenate(head_outs, axis=1), jnp.stack(head_sums)))

    carry_zero, (attended, log_sums) = lax.scan(
        attend_image, jnp.float32(0), (query_heads, key_nat, value_nat)
    )
    attended_low = attended.astype(jnp.bfloat16)
    joined = lax.all_to_all(attended_low, "seq", split_axis=1, concat_axis=2, tiled=True)
    joined_flat = joined.reshape(images * tok_count, model_width)
    branch = jnp.dot(joined_flat, out_weight, preferred_element_type=jnp.float32)
    middle = flat_rows + branch
    norm_two, pull_two = jax.vjp(layer_norm, middle, gain_two, shift_two)
    norm_two_low = norm_two.astype(jnp.bfloat16).reshape(images, tok_count, model_width)
    gathered_rows, gathered_grad = (
        lax.all_gather(norm_two_low, "tp", axis=1, tiled=True),
        lax.all_gather(cotangent, "tp", axis=1, tiled=True),
    )
    rows_all = gathered_rows.reshape(-1, model_width)
    grad_all = gathered_grad.reshape(-1, model_width)
    hidden = jnp.dot(rows_all, up_weight, preferred_element_type=jnp.float32)
    active, pull_gelu = jax.vjp(gelu_exact, hidden)
    active_low = active.astype(jnp.bfloat16)
    partial_out = jnp.dot(active_low, down_weight, preferred_element_type=jnp.float32).reshape(
        images, tok_count * tp_count, model_width
    )
    mlp_out = lax.psum_scatter(
        partial_out.astype(jnp.bfloat16), "tp", scatter_dimension=1, tiled=True
    ).astype(jnp.float32)
    output = middle.reshape(images, tok_count, model_width) + mlp_out
    grad_down = inner_rows(active_low, grad_all)
    grad_active = inner_cols(grad_all, down_weight)
    grad_hidden = pull_gelu(grad_active)[0].astype(jnp.bfloat16)
    grad_up = inner_rows(rows_all, grad_hidden)
    grad_norm_part = inner_cols(grad_hidden, up_weight).reshape(
        images, tok_count * tp_count, model_width
    )
    grad_norm_two = lax.psum_scatter(grad_norm_part, "tp", scatter_dimension=1, tiled=True).reshape(
        -1, model_width
    )
    grad_middle_norm, grad_gain_two, grad_shift_two = pull_two(grad_norm_two)
    grad_middle = cotangent.reshape(-1, model_width).astype(jnp.float32) + grad_middle_norm
    grad_branch = grad_middle.astype(jnp.bfloat16)
    grad_out = inner_rows(joined_flat, grad_branch)
    grad_joined = (
        inner_cols(grad_branch, out_weight)
        .astype(jnp.bfloat16)
        .reshape(images, tok_count, model_width)
    )
    grad_heads = lax.all_to_all(grad_joined, "seq", split_axis=2, concat_axis=1, tiled=True)

    def back_image(table_sums, pieces):
        query_img, key_img, value_img, grad_img, lse_img = pieces
        sum_h, sum_w = table_sums
        query_parts = []
        key_parts = []
        value_parts = []
        for head_index in range(local_heads):
            lower_col = head_index * head_width
            key_head = key_img[:, lower_col : lower_col + head_width]
            value_head = value_img[:, lower_col : lower_col + head_width]
            query_blocks = query_img[:, lower_col : lower_col + head_width].reshape(
                block_count, block_rows, head_width
            )
            grad_blocks = grad_img[:, lower_col : lower_col + head_width].reshape(
                block_count, block_rows, head_width
            )
            lse_blocks = lse_img[head_index].reshape(block_count, block_rows)

            def back_block(carry_state, block_in):
                acc_key, acc_value, acc_h, acc_w = carry_state
                query_blk, grad_blk, lse_blk, groups_blk = block_in
                (term_h, term_w), pull_rel = jax.vjp(
                    partial(rel_terms, group_rows=groups_blk),
                    query_blk.astype(jnp.float32),
                    table_h,
                    table_w,
                )
                scores = inner_cols(query_blk, key_head) * score_scale + build_bias(term_h, term_w)
                probs_full = jnp.exp(scores - lse_blk[:, None])
                acc_value = acc_value + inner_rows(probs_full.astype(jnp.bfloat16), grad_blk)
                grad_probs = inner_cols(grad_blk, value_head)
                center = jnp.sum(probs_full * grad_probs, axis=1, keepdims=True)
                grad_scores = (probs_full * (grad_probs - center)).astype(jnp.bfloat16)
                acc_key = acc_key + inner_rows(grad_scores, query_blk) * score_scale
                grad_query = (
                    jnp.dot(grad_scores, key_head, preferred_element_type=jnp.float32) * score_scale
                )
                grad_grid = grad_scores.astype(jnp.float32).reshape(
                    block_rows, grid_side, grid_side
                )
                grad_term_h = jnp.sum(grad_grid, axis=2)
                grad_term_w = jnp.sum(grad_grid, axis=1)
                rel_query, rel_grad_h, rel_grad_w = pull_rel((grad_term_h, grad_term_w))
                return (
                    (acc_key, acc_value, acc_h + rel_grad_h, acc_w + rel_grad_w),
                    grad_query + rel_query,
                )

            key_zero = jnp.zeros((key_count, head_width), jnp.float32)
            (acc_key, acc_value, sum_h, sum_w), query_grads = lax.scan(
                back_block,
                (key_zero, key_zero, sum_h, sum_w),
                (query_blocks, grad_blocks, lse_blocks, group_blocks),
            )
            query_parts.append(query_grads.reshape(query_rows, head_width))
            key_parts.append(acc_key)
            value_parts.append(acc_value)
        return (
            (sum_h, sum_w),
            (
                jnp.concatenate(query_parts, axis=1),
                jnp.concatenate(key_parts, axis=1),
                jnp.concatenate(value_parts, axis=1),
            ),
        )

    (grad_table_h, grad_table_w), (grad_query_all, grad_key_nat, grad_value_nat) = lax.scan(
        back_image,
        (jnp.zeros_like(table_h), jnp.zeros_like(table_w)),
        (query_heads, key_nat, value_nat, grad_heads, log_sums),
    )
    grad_key_all = gathered_order(grad_key_nat)
    grad_value_all = gathered_order(grad_value_nat)
    grad_key_mine, grad_value_mine = (
        lax.psum_scatter(
            grad_key_all.astype(jnp.bfloat16), "tp", scatter_dimension=1, tiled=True
        ).astype(jnp.float32),
        lax.psum_scatter(
            grad_value_all.astype(jnp.bfloat16), "tp", scatter_dimension=1, tiled=True
        ).astype(jnp.float32),
    )
    back_query, back_key, back_value = (
        lax.all_to_all(
            grad_query_all.astype(jnp.bfloat16), "seq", split_axis=1, concat_axis=2, tiled=True
        ),
        lax.all_to_all(
            grad_key_mine.astype(jnp.bfloat16), "seq", split_axis=1, concat_axis=2, tiled=True
        ),
        lax.all_to_all(
            grad_value_mine.astype(jnp.bfloat16), "seq", split_axis=1, concat_axis=2, tiled=True
        ),
    )
    grad_mixed = jnp.concatenate([back_query, back_key, back_value], axis=2).reshape(
        images * tok_count, 3 * model_width
    )
    grad_mix = inner_rows(norm_one_low, grad_mixed)
    grad_norm_one = inner_cols(grad_mixed, mix_weight)
    grad_flat_norm, grad_gain_one, grad_shift_one = pull_one(grad_norm_one)
    tokens_grad = (grad_middle + grad_flat_norm).reshape(images, tok_count, model_width)
    attend_totals = sum_attention(
        grad_gain_one,
        grad_shift_one,
        grad_mix,
        grad_table_h,
        grad_table_w,
        grad_out,
        grad_gain_two,
        grad_shift_two,
    )
    feed_totals = sum_feedforward(grad_up, grad_down)
    finals = split_data(
        attend_totals[0],
        attend_totals[1],
        attend_totals[2],
        attend_totals[3],
        attend_totals[4],
        attend_totals[5],
        attend_totals[6],
        attend_totals[7],
        feed_totals[0],
        feed_totals[1],
    )
    return (
        output,
        tokens_grad,
        finals[0],
        finals[1],
        finals[2],
        finals[3],
        finals[4],
        finals[5],
        finals[6],
        finals[7],
        finals[8],
        finals[9],
    )


def solution(mesh):
    return jax.shard_map(
        on_device,
        mesh=mesh,
        in_specs=(
            P("dp", ("seq", "tp"), None),
            P("dp"),
            P("dp"),
            P("dp", None),
            P(None, "dp"),
            P(None, "dp"),
            P("dp", None),
            P("dp"),
            P("dp"),
            P("dp", "tp"),
            P("tp", "dp"),
            P("dp", ("seq", "tp"), None),
        ),
        out_specs=(
            P("dp", ("seq", "tp"), None),
            P("dp", ("seq", "tp"), None),
            P("dp"),
            P("dp"),
            P("dp", None),
            P(None, "dp"),
            P(None, "dp"),
            P("dp", None),
            P("dp"),
            P("dp"),
            P("dp", "tp"),
            P("tp", "dp"),
        ),
        check_vma=False,
    )
```

profile of v0, /device:TPU:0, one launch (start us, length us, event | category | flops | bytes accessed | tf_op | source)
XLA Modules:
  0.0 745.7 jit_solution(2366063499534468010)
XLA Ops:
  10.5 5.2 all-gather
  15.8 4.3 all-gather.1
  20.3 41.4 %all-gather.9.cloned.1.call-done = bf16[768,2304]{1,0:T(8,128)(2,1)} async-done(((bf16[384,2304]{1,0:T(8,128)(2,1)}), bf16[768,2304]{1,0:T(8,128)(2,1)}) %all-gather.9.cloned.1.call-update) | async-done | bytes 3538960 | tf_op jit(solution)/shard_map/all_gather | solution.py:136
  61.7 2.6 convolution_convert_fusion.1
  65.9 4.6 all-to-all-start.2
  71.1 4.3 all-gather.2
  78.0 3.9 all-to-all-start.1
  82.0 4.3 all-gather.3
  86.3 4.4 all_gather.46
  90.8 4.4 all_gather.47
  96.7 5.1 all-to-all-start
  103.6 4.5 all-to-all-done
  109.4 10.0 %all_gather.45 = bf16[2,1024,192]{2,1,0:T(8,128)(2,1)S(1)} all-gather(bf16[2,256,192]{2,1,0:T(8,128)(2,1)S(1)} %bitcast.561), channel_id=1, replica_groups=mesh['dp'=2,'seq'=4,'tp'=4] {'tp'}, dimensions={1}, use_global_device_ids=true | all-gather | bytes 983040 | tf_op jit(solution)/shard_map/all_gather | solution.py:184
  120.4 10.3 %all_gather.48 = bf16[2,1024,192]{2,1,0:T(8,128)(2,1)S(1)} all-gather(bf16[2,256,192]{2,1,0:T(8,128)(2,1)S(1)} %bitcast.560), channel_id=1, replica_groups=mesh['dp'=2,'seq'=4,'tp'=4] {'tp'}, dimensions={1}, use_global_device_ids=true | all-gather | bytes 983040 | tf_op jit(solution)/shard_map/all_gather | solution.py:185
  132.6 36.3 %while.32 = (s32[]{:T(128)}, bf16[2,256,192]{1,2,0:T(8,128)(2,1)}, f32[2,3,256]{2,1,0:T(4,128)S(1)}, bf16[2,256,192]{2,1,0:T(8,128)(2,1)}, bf16[2,1024,192]{2,1,...) while((s32[]{:T(128)}, bf16[2,256,192]{1,2,0:T(8,128)(2,1)}, ...), condition=%wide.region_9.12_spmd, body=%wide.region_2.11_spmd.sunk | while | flops 246713344 | bytes 30512372 | solution.py:250
  135.8 2.8 gather_fusion
  154.0 2.8 gather_fusion
  170.7 3.5 all-to-all-start.3
  174.3 9.8 %all_gather.55 = bf16[2,256,768]{2,1,0:T(8,128)(2,1)} all-gather(bf16[2,64,768]{2,1,0:T(8,128)(2,1)} %param.35), channel_id=1, replica_groups=mesh['dp'=2,'seq'=4,'tp'=4] {'tp'}, dimensions={1}, use_global_device_ids=true | all-gather | bytes 983040 | tf_op jit(solution)/shard_map/all_gather | solution.py:262
  186.8 9.2 %all_gather.52 = bf16[2,256,768]{2,1,0:T(8,128)(2,1)S(1)} all-gather(bf16[2,64,768]{2,1,0:T(8,128)(2,1)S(1)} %bitcast.574), channel_id=1, replica_groups=mesh['dp'=2,'seq'=4,'tp'=4] {'tp'}, dimensions={1}, use_global_device_ids=true | all-gather | bytes 983040 | tf_op jit(solution)/shard_map/all_gather | solution.py:261
  196.0 2.0 fusion.199
  198.1 6.8 add_convert_fusion
  204.9 2.0 fusion.200
  211.9 23.4 %reduce-scatter.15.cloned.1.call-done = f32[2,64,768]{2,1,0:T(8,128)} async-done(((f32[2,256,768]{2,1,0:T(8,128)}), f32[2,64,768]{2,1,0:T(8,128)}) %reduce-scatter.15.cloned.1.call-update) | async-done | bytes 393232 | tf_op jit(solution)/shard_map/reduce_scatter | solution.py:283
  241.3 4.6 all-to-all-start.4
  247.8 5.6 all-to-all-done.4
  254.8 138.4 %while.33 = (s32[]{:T(128)}, f32[63,64]{1,0:T(8,128)S(1)}, f32[63,64]{1,0:T(8,128)S(1)}, bf16[2,256,192]{1,2,0:T(8,128)(2,1)}, bf16[2,1024,192]{1,2,0:T(8,128)(2...) while((s32[]{:T(128)}, f32[63,64]{1,0:T(8,128)S(1)}, ...), condition=%wide.region_32.37_spmd, body=%wide.region_16.36_spmd.sunk | while | flops 629963136 | bytes 95003864 | solution.py:363
  260.3 2.8 gather_fusion.2
  285.5 2.3 fusion.477
  295.0 2.0 scatter_fusion
  298.7 6.1 scatter_fusion.2
  307.6 2.0 scatter_fusion.1
  311.8 6.0 scatter_custom_fusion.22
  317.9 6.1 scatter_fusion.3
  329.3 2.8 gather_fusion.2
  354.5 2.3 fusion.477
  364.1 2.0 scatter_fusion
  367.8 6.1 scatter_fusion.2
  376.7 2.0 scatter_fusion.1
  380.8 6.0 scatter_custom_fusion.22
  386.9 6.1 scatter_fusion.3
  400.4 2.3 copy.353
  405.2 3.4 all-to-all-start.5
  408.6 10.3 %reduce-scatter.19.cloned.1.call-done = bf16[2,256,192]{2,1,0:T(8,128)(2,1)} async-done(((bf16[2,1024,192]{2,1,0:T(8,128)(2,1)}), bf16[2,256,192]{2,1,0:T(8,128)(2,1)}) %reduce-scatter.19.cloned.1.call-update) | async-done | bytes 196624 | tf_op jit(solution)/shard_map/reduce_scatter | solution.py:374
  418.9 1.9 copy.345
  420.8 4.6 all-to-all-start.7
  425.4 21.5 %reduce-scatter.17.cloned.1.call-done = bf16[2,256,192]{2,1,0:T(8,128)(2,1)} async-done(((bf16[2,1024,192]{2,1,0:T(8,128)(2,1)}), bf16[2,256,192]{2,1,0:T(8,128)(2,1)}) %reduce-scatter.17.cloned.1.call-update) | async-done | bytes 196624 | tf_op jit(solution)/shard_map/reduce_scatter | solution.py:371
  447.0 1.9 copy.340
  448.9 4.6 all-to-all-start.6
  454.5 7.9 %all-to-all-done.6 = bf16[2,256,192]{2,0,1:T(2,128)(2,1)S(1)} async-done(((bf16[2,256,192]{2,0,1:T(2,128)(2,1)}), bf16[2,256,192]{2,0,1:T(2,128)(2,1)S(1)}, u32[]{:S(2)}, u32[]{:S(2)}) %all-to-all-start.6) | async-done | bytes 196640 | tf_op jit(solution)/shard_map/all_to_all | solution.py:382
  462.9 2.9 convolution_convert_fusion
  468.7 4.1 reduce-scatter.13.cloned.1.call-done
  474.6 57.6 %all-reduce.13.cloned.1.call-done = (bf16[384,768]{1,0:T(8,128)(2,1)}, bf16[768,384]{1,0:T(8,128)(2,1)}) async-done(((bf16[384,768]{1,0:T(8,128)(2,1)}, bf16[768,384]{1,0:T(8,128)(2,1)}), (bf16[384,768]{1,0:T(8,128)(2,1)}, bf16[768,384]{1,0:T(8,128)(2,1)})) %all-reduce.13.cloned.1.call-update) | async-done | bytes 1179664 | tf_op jit(solution)/shard_map/psum | solution.py:68
  532.1 2.2 convert_element_type.267
  535.4 20.7 %reduce-scatter.27.cloned.1.call-done = bf16[384,768]{1,0:T(8,128)(2,1)} async-done(((bf16[768,768]{1,0:T(8,128)(2,1)}), bf16[384,768]{1,0:T(8,128)(2,1)}) %reduce-scatter.27.cloned.1.call-update) | async-done | bytes 589840 | tf_op jit(solution)/shard_map/reduce_scatter | solution.py:101
  556.1 50.6 %reduce-scatter.21.cloned.1.call-done = bf16[384,2304]{1,0:T(8,128)(2,1)} async-done(((bf16[768,2304]{1,0:T(8,128)(2,1)}), bf16[384,2304]{1,0:T(8,128)(2,1)}) %reduce-scatter.21.cloned.1.call-update) | async-done | bytes 1769488 | tf_op jit(solution)/shard_map/reduce_scatter | solution.py:92
  606.8 3.4 multiply_reduce_fusion.3
  610.3 5.1 all-reduce.7
  615.7 3.5 reduce-scatter.23.cloned.1.call-done
  619.2 12.4 %reduce-scatter.25.cloned.1.call-done = bf16[63,32]{0,1:T(8,128)(2,1)} async-done(((bf16[63,64]{0,1:T(8,128)(2,1)}), bf16[63,32]{0,1:T(8,128)(2,1)}) %reduce-scatter.25.cloned.1.call-update) | async-done | bytes 4048 | tf_op jit(solution)/shard_map/reduce_scatter | solution.py:98
  631.6 61.3 %all-reduce.4 = (bf16[384]{0:T(512)(128)(2,1)S(1)}, bf16[384]{0:T(512)(128)(2,1)S(1)}, bf16[63,32]{0,1:T(8,128)(2,1)S(1)}, bf16[63,32]{0,1:T(8,128)(2,1)S(1)}, b...) all-reduce(bf16[384]{0:T(512)(128)(2,1)S(1)} %dynamic-slice.10, ...), channel_id=1, replica_groups=mesh['dp'=2,'seq'=4,'tp'=4] {'seq','tp'}, use_global_device_ids=true, to_apply=%region_38.43 | all-reduce | flops 5568 | bytes 22272 | tf_op jit(solution)/shard_map/psum | solution.py:55
  697.6 36.9 %all-reduce.11.cloned.1.call-done = (bf16[384,2304]{1,0:T(8,128)(2,1)}, bf16[384,768]{1,0:T(8,128)(2,1)}) async-done(((bf16[384,2304]{1,0:T(8,128)(2,1)}, bf16[384,768]{1,0:T(8,128)(2,1)}), (bf16[384,2304]{1,0:T(8,128)(2,1)}, bf16[384,768]{1,0:T(8,128)(2,1)})) %all-reduce.11.cloned.1.call-update) | async-done | bytes 2359312 | tf_op jit(solution)/shard_map/psum | solution.py:57
  734.4 2.3 convert_element_type.261
  736.7 2.0 convert_element_type.255
  (665 shorter events, 167.5 us)
Async XLA Ops:
  7.2 8.6 %copy-start.69 = (bf16[384]{0:T(512)(128)(2,1)S(1)}, bf16[384]{0:T(512)(128)(2,1)}, u32[]{:S(2)}) copy-start(bf16[384]{0:T(512)(128)(2,1)} %param.26) | copy-start | bytes 2308
  7.2 54.5 %all-gather.9.cloned.1.call-start = ((), (), s32[]{:S(2)}) async-start(), calls=%async_computation.18 | async-start | bytes 5308416 | tf_op jit(solution)/shard_map/all_gather | solution.py:136
  7.9 176.7 %all-gather.11.cloned.1.call-start = ((), (), s32[]{:S(2)}) async-start(), calls=%async_computation.19 | async-start | bytes 1769472 | tf_op jit(solution)/shard_map/all_gather | solution.py:139
  8.7 187.3 %all-gather.13.cloned.1.call-start = ((), (), s32[]{:S(2)}) async-start(), calls=%async_computation.20 | async-start | bytes 1769472 | tf_op jit(solution)/shard_map/all_gather | solution.py:142
  9.6 54.7 %copy-start.62 = (f32[128]{0:T(128)}, f32[128]{0:T(128)S(1)}, u32[]{:S(2)}) copy-start(f32[128]{0:T(128)S(1)} %div.97) | copy-start | bytes 1540
  10.5 53.9 %copy-start.64 = (f32[128]{0:T(128)}, f32[128]{0:T(128)S(1)}, u32[]{:S(2)}) copy-start(f32[128]{0:T(128)S(1)} %rsqrt.20) | copy-start | bytes 1540
  15.8 48.6 %copy-start.53 = (f32[768]{0:T(1024)}, f32[768]{0:T(1024)S(1)}, u32[]{:S(2)}) copy-start(f32[768]{0:T(1024)S(1)} %reshape.733) | copy-start | bytes 9220
  20.3 44.1 %copy-start.28 = (bf16[128,768]{1,0:T(8,128)(2,1)}, bf16[128,768]{1,0:T(8,128)(2,1)S(1)}, u32[]{:S(2)}) copy-start(bf16[128,768]{1,0:T(8,128)(2,1)S(1)} %add_convert_fusion.2) | copy-start | bytes 589828
  64.4 6.7 copy-start.70
  64.8 17.1 %copy-start.71 = (bf16[384]{0:T(512)(128)(2,1)S(1)}, bf16[384]{0:T(512)(128)(2,1)}, u32[]{:S(2)}) copy-start(bf16[384]{0:T(512)(128)(2,1)} %param.32) | copy-start | bytes 2308
  64.9 21.5 %copy-start.60 = (bf16[63,32]{0,1:T(8,128)(2,1)S(1)}, bf16[63,32]{0,1:T(8,128)(2,1)}, u32[]{:S(2)}) copy-start(bf16[63,32]{0,1:T(8,128)(2,1)} %param.28) | copy-start | bytes 12100
  64.9 25.9 %copy-start.61 = (bf16[63,32]{0,1:T(8,128)(2,1)S(1)}, bf16[63,32]{0,1:T(8,128)(2,1)}, u32[]{:S(2)}) copy-start(bf16[63,32]{0,1:T(8,128)(2,1)} %param.29) | copy-start | bytes 12100
  65.9 12.1 %all-to-all-start.2 = ((bf16[4,2,12288]{2,1,0:T(2,128)(2,1)}), bf16[4,2,12288]{2,1,0:T(2,128)(2,1)S(1)}, u32[]{:S(2)}, u32[]{:S(2)}) async-start(bf16[4,2,12288]{2,1,0:T(2,128)(2,1)} %reshape.771), calls=%async_computation.2 | async-start | bytes 393216 | tf_op jit(solution)/shard_map/all_to_all | solution.py:179
  70.5 127.6 %all-gather.15.cloned.1.call-start = ((), (), s32[]{:S(2)}) async-start(), calls=%async_computation.21 | async-start | bytes 1769472 | tf_op jit(solution)/shard_map/all_gather | solution.py:143
  78.0 18.7 %all-to-all-start.1 = ((bf16[4,2,12288]{2,1,0:T(2,128)(2,1)}), bf16[4,2,12288]{2,1,0:T(2,128)(2,1)S(1)}, u32[]{:S(2)}, u32[]{:S(2)}) async-start(bf16[4,2,12288]{2,1,0:T(2,128)(2,1)} %reshape.769), calls=%async_computation.1 | async-start | bytes 393216 | tf_op jit(solution)/shard_map/all_to_all | solution.py:172
  96.7 11.4 %all-to-all-start = ((bf16[4,2,12288]{2,1,0:T(2,128)(2,1)}), bf16[4,2,12288]{2,1,0:T(2,128)(2,1)S(1)}, u32[]{:S(2)}, u32[]{:S(2)}) async-start(bf16[4,2,12288]{2,1,0:T(2,128)(2,1)} %reshape.767), calls=%async_computation | async-start | bytes 393216 | tf_op jit(solution)/shard_map/all_to_all | solution.py:169
  170.7 13.9 %copy-start.14 = (f32[2,64,768]{2,1,0:T(8,128)S(1)}, f32[2,64,768]{2,1,0:T(8,128)}, u32[]{:S(2)}) copy-start(f32[2,64,768]{2,1,0:T(8,128)} %param.24) | copy-start | bytes 1179652
  170.7 13.4 %all-to-all-start.3 = ((bf16[2,256,192]{2,0,1:T(2,128)(2,1)}), bf16[2,256,192]{2,0,1:T(2,128)(2,1)S(1)}, u32[]{:S(2)}, u32[]{:S(2)}) async-start(bf16[2,256,192]{2,0,1:T(2,128)(2,1)} %copy.328), calls=%async_computation.3 | async-start | bytes 524288 | tf_op jit(solution)/shard_map/all_to_all | solution.py:254
  174.3 61.0 %reduce-scatter.15.cloned.1.call-start = ((), (), s32[]{:S(2)}) async-start(), calls=%async_computation.23 | async-start | bytes 1966080 | tf_op jit(solution)/shard_map/reduce_scatter | solution.py:283
  186.4 50.7 %copy-start.16 = (f32[128,768]{1,0:T(8,128)}, f32[128,768]{1,0:T(8,128)S(1)}, u32[]{:S(2)}) copy-start(f32[128,768]{1,0:T(8,128)S(1)} %get-tuple-element.504) | copy-start | bytes 1179652
  198.1 6.8 copy-start.73
  206.8 193.5 %reduce-scatter.31.cloned.1.call-start = ((), (), s32[]{:S(2)}) async-start(), calls=%async_computation.31 | async-start | bytes 1769472
  211.8 27.3 %copy-start.34 = (bf16[2,64,768]{2,1,0:T(8,128)(2,1)S(1)}, bf16[2,64,768]{2,1,0:T(8,128)(2,1)}, u32[]{:S(2)}) copy-start(bf16[2,64,768]{2,1,0:T(8,128)(2,1)} %param.35) | copy-start | bytes 589828
  211.9 27.4 %copy-start.21 = (bf16[768,768]{1,0:T(8,128)(2,1)S(1)}, bf16[768,768]{1,0:T(8,128)(2,1)}, u32[]{:S(2)}) copy-start(bf16[768,768]{1,0:T(8,128)(2,1)} %all-gather.11.cloned.1.call-done) | copy-start | bytes 3538948
  241.3 12.1 %all-to-all-start.4 = ((bf16[4,2,12288]{2,1,0:T(2,128)(2,1)}), bf16[4,2,12288]{2,1,0:T(2,128)(2,1)S(1)}, u32[]{:S(2)}, u32[]{:S(2)}) async-start(bf16[4,2,12288]{2,1,0:T(2,128)(2,1)} %reshape.773), calls=%async_computation.6 | async-start | bytes 393216 | tf_op jit(solution)/shard_map/all_to_all | solution.py:295
  245.9 156.7 %reduce-scatter.29.cloned.1.call-start = ((), (), s32[]{:S(2)}) async-start(), calls=%async_computation.30 | async-start | bytes 1769472 | tf_op jit(solution)/shard_map/reduce_scatter | solution.py:110
  247.8 171.1 %reduce-scatter.19.cloned.1.call-start = ((), (), s32[]{:S(2)}) async-start(), calls=%async_computation.25 | async-start | bytes 1310720 | tf_op jit(solution)/shard_map/reduce_scatter | solution.py:374
  258.5 6.9 copy-start.8
  280.6 7.2 copy-start.2
  282.0 6.2 copy-start.1
  309.9 8.0 %copy-start.3 = (f32[32,32,64]{2,1,0:T(8,128)S(1)}, f32[32,32,64]{2,1,0:T(8,128)}, u32[]{:S(2)}) copy-start(f32[32,32,64]{2,1,0:T(8,128)} %fusion.477) | copy-start | bytes 786436 | tf_op jit(solution)/shard_map/while
  311.1 12.8 %copy-start.43 = (bf16[2,256,192]{1,2,0:T(8,128)(2,1)}, bf16[2,256,192]{1,2,0:T(8,128)(2,1)S(1)}, u32[]{:S(2)}) copy-start(bf16[2,256,192]{1,2,0:T(8,128)(2,1)S(1)} %fusion.487) | copy-start | bytes 589828 | tf_op jit(solution)/shard_map/while
  317.8 6.1 copy-start.27
  317.9 6.1 copy-start.56
  317.9 6.1 copy-start.58
  327.6 6.9 copy-start.8
  349.7 7.2 copy-start.2
  351.1 6.2 copy-start.1
  378.9 8.0 %copy-start.3 = (f32[32,32,64]{2,1,0:T(8,128)S(1)}, f32[32,32,64]{2,1,0:T(8,128)}, u32[]{:S(2)}) copy-start(f32[32,32,64]{2,1,0:T(8,128)} %fusion.477) | copy-start | bytes 786436 | tf_op jit(solution)/shard_map/while
  380.2 12.8 %copy-start.43 = (bf16[2,256,192]{1,2,0:T(8,128)(2,1)}, bf16[2,256,192]{1,2,0:T(8,128)(2,1)S(1)}, u32[]{:S(2)}) copy-start(bf16[2,256,192]{1,2,0:T(8,128)(2,1)S(1)} %fusion.487) | copy-start | bytes 589828 | tf_op jit(solution)/shard_map/while
  386.9 6.1 copy-start.27
  386.9 6.1 copy-start.56
  395.8 51.2 %reduce-scatter.17.cloned.1.call-start = ((), (), s32[]{:S(2)}) async-start(), calls=%async_computation.24 | async-start | bytes 1310720 | tf_op jit(solution)/shard_map/reduce_scatter | solution.py:371
  397.8 75.0 %reduce-scatter.13.cloned.1.call-start = ((), (), s32[]{:S(2)}) async-start(), calls=%async_computation.22 | async-start | bytes 983040 | tf_op jit(solution)/shard_map/reduce_scatter | solution.py:272
  400.3 131.8 %all-reduce.13.cloned.1.call-start = ((), (), s32[]{:S(2)}) async-start(), calls=%async_computation.33 | async-start | bytes 2359296 | tf_op jit(solution)/shard_map/psum | solution.py:68
  402.7 153.4 %reduce-scatter.27.cloned.1.call-start = ((), (), s32[]{:S(2)}) async-start(), calls=%async_computation.29 | async-start | bytes 1769472 | tf_op jit(solution)/shard_map/reduce_scatter | solution.py:101
  405.2 15.7 %all-to-all-start.5 = ((bf16[2,256,192]{2,0,1:T(2,128)(2,1)}), bf16[2,256,192]{2,0,1:T(2,128)(2,1)S(1)}, u32[]{:S(2)}, u32[]{:S(2)}) async-start(bf16[2,256,192]{2,0,1:T(2,128)(2,1)} %copy.335), calls=%async_computation.7 | async-start | bytes 524288 | tf_op jit(solution)/shard_map/all_to_all | solution.py:379
  420.8 28.0 %all-to-all-start.7 = ((bf16[2,256,192]{2,0,1:T(2,128)(2,1)}), bf16[2,256,192]{2,0,1:T(2,128)(2,1)S(1)}, u32[]{:S(2)}, u32[]{:S(2)}) async-start(bf16[2,256,192]{2,0,1:T(2,128)(2,1)} %copy.345), calls=%async_computation.11 | async-start | bytes 524288 | tf_op jit(solution)/shard_map/all_to_all | solution.py:385
  448.9 13.5 %all-to-all-start.6 = ((bf16[2,256,192]{2,0,1:T(2,128)(2,1)}), bf16[2,256,192]{2,0,1:T(2,128)(2,1)S(1)}, u32[]{:S(2)}, u32[]{:S(2)}) async-start(bf16[2,256,192]{2,0,1:T(2,128)(2,1)} %copy.340), calls=%async_computation.9 | async-start | bytes 524288 | tf_op jit(solution)/shard_map/all_to_all | solution.py:382
  453.5 153.2 %reduce-scatter.21.cloned.1.call-start = ((), (), s32[]{:S(2)}) async-start(), calls=%async_computation.26 | async-start | bytes 5308416 | tf_op jit(solution)/shard_map/reduce_scatter | solution.py:92
  454.0 8.9 %copy-start.29 = (bf16[128,768]{1,0:T(8,128)(2,1)S(1)}, bf16[128,768]{1,0:T(8,128)(2,1)}, u32[]{:S(2)}) copy-start(bf16[128,768]{1,0:T(8,128)(2,1)} %copy-done.28) | copy-start | bytes 589828
  465.8 7.0 copy-start.17
  465.8 8.7 %copy-start.22 = (f32[2,64,768]{2,1,0:T(8,128)S(1)}, f32[2,64,768]{2,1,0:T(8,128)}, u32[]{:S(2)}) copy-start(f32[2,64,768]{2,1,0:T(8,128)} %reduce-scatter.15.cloned.1.call-done) | copy-start | bytes 1179652
  465.9 153.3 %reduce-scatter.23.cloned.1.call-start = ((), (), s32[]{:S(2)}) async-start(), calls=%async_computation.27 | async-start | bytes 24576 | tf_op jit(solution)/shard_map/reduce_scatter | solution.py:95
  466.6 164.9 %reduce-scatter.25.cloned.1.call-start = ((), (), s32[]{:S(2)}) async-start(), calls=%async_computation.28 | async-start | bytes 24576 | tf_op jit(solution)/shard_map/reduce_scatter | solution.py:98
  468.6 265.8 %all-reduce.11.cloned.1.call-start = ((), (), s32[]{:S(2)}) async-start(), calls=%async_computation.32 | async-start | bytes 4718592 | tf_op jit(solution)/shard_map/psum | solution.py:57
  535.4 71.3 %copy-start.15 = (f32[2,64,768]{2,1,0:T(8,128)S(1)}, f32[2,64,768]{2,1,0:T(8,128)}, u32[]{:S(2)}) copy-start(f32[2,64,768]{2,1,0:T(8,128)} %param.24) | copy-start | bytes 1179652
  535.4 71.3 %copy-start.54 = (f32[768]{0:T(1024)S(1)}, f32[768]{0:T(1024)}, u32[]{:S(2)}) copy-start(f32[768]{0:T(1024)} %copy-done.53) | copy-start | bytes 9220
  535.4 71.3 %copy-start.63 = (f32[128]{0:T(128)S(1)}, f32[128]{0:T(128)}, u32[]{:S(2)}) copy-start(f32[128]{0:T(128)} %copy-done.62) | copy-start | bytes 1540
  535.4 71.3 %copy-start.65 = (f32[128]{0:T(128)S(1)}, f32[128]{0:T(128)}, u32[]{:S(2)}) copy-start(f32[128]{0:T(128)} %copy-done.64) | copy-start | bytes 1540
  606.8 89.6 %copy-start.75 = (f32[128]{0:T(128)S(1)}, f32[128]{0:T(128)}, u32[]{:S(2)}) copy-start(f32[128]{0:T(128)} %copy-done.74) | copy-start | bytes 1540
  606.8 89.8 %copy-start.35 = (bf16[2,64,768]{2,1,0:T(8,128)(2,1)S(1)}, bf16[2,64,768]{2,1,0:T(8,128)(2,1)}, u32[]{:S(2)}) copy-start(bf16[2,64,768]{2,1,0:T(8,128)(2,1)} %param.35) | copy-start | bytes 589828
  606.8 89.8 %copy-start.67 = (f32[128]{0:T(128)S(1)}, f32[128]{0:T(128)}, u32[]{:S(2)}) copy-start(f32[128]{0:T(128)} %copy-done.66) | copy-start | bytes 1540
  610.3 86.4 %copy-start.24 = (f32[128,768]{1,0:T(8,128)S(1)}, f32[128,768]{1,0:T(8,128)}, u32[]{:S(2)}) copy-start(f32[128,768]{1,0:T(8,128)} %copy-done.23) | copy-start | bytes 1179652
  (72 other events, 153.1 us)
Sparse Core Ops, SparseCore 0:
  9.6 52.0 all-gather.8
  63.2 22.8 all-gather.10
  87.6 22.7 all-gather.12
  111.8 22.7 all-gather.14
  207.0 28.3 reduce-scatter.14
  238.1 21.7 reduce-scatter.30
  262.7 21.7 reduce-scatter.28
  395.9 22.9 reduce-scatter.18
  422.0 24.8 reduce-scatter.16
  449.5 23.2 reduce-scatter.12
  475.8 56.2 all-reduce.12
  534.8 21.2 reduce-scatter.26
  559.0 47.6 reduce-scatter.20
  609.3 9.8 reduce-scatter.22
  621.8 9.7 reduce-scatter.24
  635.0 99.3 all-reduce.10
where the time goes:
time: 752 us; the launch traced here: 746 us
  waiting for transfers between devices  304 us (40%)
  blocking collectives  133 us (18%)
  local copies, waits for them, and re-layouts  99.1 us (13%)
  matrix products  79.5 us (11%)
  other arithmetic  76.9 us (10%)
  starting transfers between devices  34.9 us (5%)
  between operations  15.9 us (2%)
    psum x1, blocking collectives, sum_attention(): lax.psum(gain_one.astype(jnp.bfloat16), ('seq', 'tp')).astype(jnp.float32)  61.3 us
    psum x1, waiting for transfers between devices, sum_feedforward(): lax.psum(up_grad.astype(jnp.bfloat16), 'seq').astype(jnp.float32)  57.6 us
    reduce_scatter x1, waiting for transfers between devices, split_data(): lax.psum_scatter(mix_grad.astype(jnp.bfloat16), 'dp', scatter_dimension=0...  50.6 us
    all_gather x1, waiting for transfers between devices, on_device(): lax.all_gather(qkv_weight, 'dp', axis=0, tiled=True)  41.4 us
    psum x1, waiting for transfers between devices, sum_attention(): lax.psum(mix_grad.astype(jnp.bfloat16), ('seq', 'tp')).astype(jnp.float32)  36.9 us
    scatter-add x6, other arithmetic, rel_terms(): window_w = jnp.take(table_w, pick_w, axis=0)  36.4 us
    dot_general x22, matrix products, inner_cols(): lax.dot_general(left_mat, right_mat, (((1,), (1,)), ((), ())), preferred_...  23.7 us
    reduce_scatter x1, waiting for transfers between devices, on_device(): lax.psum_scatter(grad_norm_part, 'tp', scatter_dimension=1, tiled=True)  23.4 us
  transfers between devices with their start and end apart: 24, of which 15 were waited for; matrix products, arithmetic and copies ran while one was open for 31% of the time, Pallas kernels for 0%

commit v1 on v0

v1 whole, which is shorter than its diff:
```python
import jax
import jax.numpy as jnp
from jax import lax
from jax.experimental import pallas as pl
from jax.experimental.pallas import tpu as pltpu
from jax.sharding import PartitionSpec as P

EPS = 1e-06
LOW = jnp.bfloat16
FULL = jnp.float32
LANES = 128
CORE, ROW, NEAR, FAR = 1, 2, 4, 8


def hop(value, bits):
    count = lax.axis_size("seq") * lax.axis_size("tp")
    return lax.ppermute(value, ("seq", "tp"), [(i, i ^ bits) for i in range(count)])


def gather_dp(value, axis):
    if lax.axis_size("dp") != 2:
        return lax.all_gather(value, "dp", axis=axis, tiled=True)
    other = lax.ppermute(value, "dp", [(0, 1), (1, 0)])
    first = lax.axis_index("dp") == 0
    return jnp.concatenate(
        [jnp.where(first, value, other), jnp.where(first, other, value)], axis=axis
    )


def piece(value, index, size, axis):
    return lax.dynamic_slice_in_dim(value, index * size, size, axis)


def scatter_dp(value, axis):
    if lax.axis_size("dp") != 2:
        return lax.psum_scatter(
            value.astype(LOW), "dp", scatter_dimension=axis, tiled=True
        ).astype(FULL)
    half = value.shape[axis] // 2
    me = lax.axis_index("dp")
    sent = piece(value, 1 - me, half, axis).astype(LOW)
    got = lax.ppermute(sent, "dp", [(0, 1), (1, 0)])
    return piece(value, me, half, axis).astype(FULL) + got.astype(FULL)


def sum_dp(value):
    if lax.axis_size("dp") != 2:
        return lax.psum(value, "dp")
    return value + lax.ppermute(value, "dp", [(0, 1), (1, 0)])


def canon(blocks, index, axis):
    odd = (index & 1) == 1
    upper = (index & 2) == 2
    b = [
        jnp.where(odd, blocks[k ^ 1], blocks[k])
        for k in range(4)
    ]
    return jnp.concatenate([jnp.where(upper, b[k ^ 2], b[k]) for k in range(4)], axis=axis)


def dot_nn(a, b):
    return lax.dot_general(a, b, (((1,), (0,)), ((), ())), preferred_element_type=FULL)


def dot_nt(a, b):
    return lax.dot_general(a, b, (((1,), (1,)), ((), ())), preferred_element_type=FULL)


def dot_tn(a, b):
    return lax.dot_general(a, b, (((0,), (0,)), ((), ())), preferred_element_type=FULL)


def call(kernel, outs, flops, scratch=(), smem=0, vmem=32):
    def run(*args):
        size = sum(a.size * a.dtype.itemsize for a in args)
        size += sum(a.size * a.dtype.itemsize for a in outs)
        return pl.pallas_call(
            kernel,
            out_shape=outs,
            in_specs=[pl.BlockSpec(memory_space=pltpu.SMEM)] * smem
            + [pl.BlockSpec(memory_space=pltpu.VMEM)] * (len(args) - smem),
            out_specs=[pl.BlockSpec(memory_space=pltpu.VMEM)] * len(outs),
            scratch_shapes=scratch,
            compiler_params=pltpu.CompilerParams(vmem_limit_bytes=vmem * 2**20),
            cost_estimate=pl.CostEstimate(flops=flops, bytes_accessed=size, transcendentals=0),
        )(*args)

    return run


def shape(dims, kind):
    return jax.ShapeDtypeStruct(dims, kind)


def normal(values):
    center = values - jnp.mean(values, axis=-1, keepdims=True)
    scale = lax.rsqrt(jnp.mean(center * center, axis=-1, keepdims=True) + EPS)
    return center * scale, scale


def norm_kernel(mine, other, gain, shift, out):
    half = mine.shape[0]
    for start, part in ((0, mine), (half, other)):
        hat, _ = normal(part[...])
        out[start : start + half, :] = (hat * gain[...] + shift[...]).astype(LOW)


def lane_of(rows):
    return lax.broadcasted_iota(jnp.int32, (rows, LANES), 1)


def pieces_at(lane, first, value, rest):
    high = value.astype(LOW).astype(FULL)
    left = value - high
    mid = left.astype(LOW).astype(FULL)
    tail = left - mid
    out = jnp.where(lane == first, high, rest)
    out = jnp.where(lane == first + 1, mid, out)
    return jnp.where(lane == first + 2, tail, out)


def key_tiles(h, kva, kvb, spot_one, spot_two, keys):
    half = kva.shape[0]
    lane = lane_of(half)
    for start, part in ((0, kva), (half, kvb)):
        tile = part[:, h * LANES : (h + 1) * LANES].astype(FULL)
        spots = spot_one[start : start + half, :].astype(FULL)
        keys[start : start + half, :LANES] = jnp.where(lane < 64, tile, spots).astype(LOW)
        keys[start : start + half, LANES:] = spot_two[start : start + half, :]


def attend_kernel(
    group_rows, query, kva, kvb, spot_one, spot_two, table, out, out_low, left, keys, along
):
    rows = query.shape[0]
    heads = left.shape[0]
    lane32 = lane_of(32)
    block = 128
    lane = lane_of(block)
    for h in range(heads):
        key_tiles(h, kva, kvb, spot_one, spot_two, keys)
        tile = query[:, (h // 2) * LANES : (h // 2 + 1) * LANES].astype(FULL)
        if h % 2:
            tile = pltpu.roll(tile, 64, 1)
        along[...] = dot_nn(tile.astype(LOW), table[...])
        for g in range(rows // 32):
            here = slice(g * 32, (g + 1) * 32)
            term_h = pltpu.roll(along[here, :LANES], 33 + group_rows[g], 1)
            term_w = pltpu.roll(along[here, LANES:], 65, 1, stride=1, stride_axis=0)
            one = jnp.where(
                lane32 < 64, tile[here, :] * 0.125, jnp.where(lane32 < 96, term_h, term_w)
            )
            high = one.astype(LOW)
            rest = pltpu.roll(one - high.astype(FULL), 64, 1)
            left[h, here, :LANES] = high
            left[h, here, LANES:] = rest.astype(LOW)
        for q in range(rows // block):
            here = slice(q * block, (q + 1) * block)
            scores = dot_nt(left[h, here, :], keys[...])
            top = jnp.max(scores, axis=1, keepdims=True)
            expo = jnp.exp(scores - top)
            total = jnp.sum(expo, axis=1, keepdims=True)
            low = expo.astype(LOW)
            half = kva.shape[0]
            cols = slice(h * LANES, (h + 1) * LANES)
            result = dot_nn(low[:, :half], kva[:, cols]) + dot_nn(low[:, half:], kvb[:, cols])
            result = result / total
            if h % 2 == 0:
                result = pltpu.roll(result, 64, 1)
            spot = slice((h // 2) * LANES, (h // 2 + 1) * LANES)
            if h % 2:
                result = jnp.where(lane < 64, out[here, spot], result)
            else:
                result = jnp.where(lane < 64, result, 0.0)
            out[here, spot] = result
            out_low[here, spot] = result.astype(LOW)
            rest = left[h, here, LANES:].astype(FULL)
            left[h, here, LANES:] = pieces_at(lane, 64, -(top + jnp.log(total)), rest).astype(LOW)


def back_kernel(
    group_rows,
    left,
    kva,
    kvb,
    spot_one,
    spot_two,
    table,
    grad,
    value,
    dquery,
    dkv_mine,
    dkv_other,
    dtable,
    keys,
    vals,
    gright,
    qright,
    along,
):
    heads, rows, _ = left.shape
    half = kva.shape[0]
    lane = lane_of(rows)
    lane32 = lane_of(32)
    row = lax.broadcasted_iota(jnp.int32, (rows, LANES), 0)
    chunk = 256
    dtable[...] = jnp.zeros_like(dtable)
    for h in range(heads):
        key_tiles(h, kva, kvb, spot_one, spot_two, keys)
        cols = slice(h * LANES, (h + 1) * LANES)
        spot = slice((h // 2) * LANES, (h // 2 + 1) * LANES)
        vals[:half, :LANES] = kva[:, cols]
        vals[half:, :LANES] = kvb[:, cols]
        vals[:, LANES:] = spot_two[...]
        gtile = grad[:, spot].astype(FULL)
        otile = value[:, spot]
        if h % 2 == 0:
            gtile = pltpu.roll(gtile, 64, 1)
            otile = pltpu.roll(otile, 64, 1)
        gtile = jnp.where(lane >= 64, gtile, 0.0)
        inner = jnp.sum(gtile * otile, axis=1, keepdims=True)
        gright[:, :LANES] = gtile.astype(LOW)
        gright[:, LANES:] = pieces_at(lane, 64, -inner, jnp.zeros_like(gtile)).astype(LOW)
        qright[...] = jnp.where(lane < 64, left[h, :, :LANES].astype(FULL), 0.0).astype(LOW)
        dq_t = jnp.zeros((LANES, rows), FULL)
        for k in range(2 * half // chunk):
            here = slice(k * chunk, (k + 1) * chunk)
            probs = jnp.exp(dot_nt(keys[here, :], left[h]))
            dscores = (probs * dot_nt(vals[here, :], gright[...])).astype(LOW)
            dkv = dot_nn(probs.astype(LOW), gright[:, :LANES]) + dot_nn(dscores, qright[...])
            if k * chunk < half:
                dkv_mine[here, cols] = dkv
            else:
                dkv_other[k * chunk - half : (k + 1) * chunk - half, cols] = dkv.astype(LOW)
            dq_t = dq_t + dot_tn(keys[here, :LANES], dscores)
        dq = dq_t.T
        for g in range(rows // 32):
            here = slice(g * 32, (g + 1) * 32)
            part_h = jnp.where((lane32 >= 64) & (lane32 < 96), dq[here, :], 0.0)
            along[here, :LANES] = pltpu.roll(part_h, 95 - group_rows[g], 1).astype(LOW)
        part_w = pltpu.roll(jnp.where(lane >= 96, dq, 0.0), 63, 1)
        for bit in range(5):
            moved = pltpu.roll(part_w, LANES - 2**bit, 1)
            part_w = jnp.where((row >> bit) & 1 == 1, moved, part_w)
        along[:, LANES:] = part_w.astype(LOW)
        dq = jnp.where(lane < 64, dq * 0.125 + dot_nt(along[...], table[...]), 0.0)
        if h % 2:
            dquery[:, spot] = dquery[:, spot] + pltpu.roll(dq, 64, 1).astype(LOW)
        else:
            dquery[:, spot] = dq.astype(LOW)
        dtable[...] += dot_tn(along[...], qright[...])


def mid_kernel(j0, j1, j2, j3, weight, rows, gain, shift, middle, low):
    width = j0.shape[1]
    total = rows[...]
    for k, part in enumerate((j0, j1, j2, j3)):
        total = total + dot_nn(part[...], weight[k * width : (k + 1) * width, :])
    middle[...] = total
    hat, _ = normal(total)
    low[...] = (hat * gain[...] + shift[...]).astype(LOW)


def feed_kernel(rows, grad, up, down, active, dhidden, dnorm):
    hidden = dot_nn(rows[...], up[...])
    phi = 0.5 + 0.5 * lax.erf(hidden * 0.7071067811865476)
    active[...] = (hidden * phi).astype(LOW)
    slope = phi + hidden * (jnp.exp(hidden * hidden * -0.5) * 0.3989422804014327)
    low = (dot_nt(grad[...], down[...]) * slope).astype(LOW)
    dhidden[...] = low
    dnorm[...] = dot_nt(low, up[...]).astype(LOW)


def feed(rows, grad, up, down):
    total, width = rows.shape
    hid = up.shape[1]
    block = 128
    row_spec = pl.BlockSpec((block, width), lambda i: (i, 0))
    hid_spec = pl.BlockSpec((block, hid), lambda i: (i, 0))
    up_spec = pl.BlockSpec((width, hid), lambda i: (0, 0))
    down_spec = pl.BlockSpec((hid, width), lambda i: (0, 0))
    return pl.pallas_call(
        feed_kernel,
        grid=(total // block,),
        in_specs=[row_spec, row_spec, up_spec, down_spec],
        out_specs=[hid_spec, hid_spec, row_spec],
        out_shape=[shape((total, hid), LOW), shape((total, hid), LOW), shape((total, width), LOW)],
        compiler_params=pltpu.CompilerParams(vmem_limit_bytes=32 * 2**20),
        cost_estimate=pl.CostEstimate(
            flops=6 * total * width * hid, bytes_accessed=12 * width * hid, transcendentals=0
        ),
    )(rows, grad, up, down)


def norm_back(grad, values, gain):
    hat, scale = normal(values)
    scaled = grad * gain
    back = scale * (
        scaled
        - jnp.mean(scaled, axis=-1, keepdims=True)
        - hat * jnp.mean(scaled * hat, axis=-1, keepdims=True)
    )
    return back, jnp.sum(grad * hat, axis=0, keepdims=True), jnp.sum(grad, axis=0, keepdims=True)


def mid_back_kernel(
    a0, a1, a2, middle, gain, cot, weight, gmiddle, gbranch, b0, b1, b2, b3, dgain, dshift
):
    grad = a0[...].astype(FULL) + a1[...].astype(FULL) + a2[...].astype(FULL)
    back, dgain[...], dshift[...] = norm_back(grad, middle[...], gain[...])
    total = cot[...].astype(FULL) + back
    gmiddle[...] = total
    low = total.astype(LOW)
    gbranch[...] = low
    width = b0.shape[1]
    for k, out in enumerate((b0, b1, b2, b3)):
        out[...] = dot_nt(low, weight[k * width : (k + 1) * width, :]).astype(LOW)


def first_back_kernel(a0, a1, a2, a3, rows, gain, gmiddle, out, dgain, dshift):
    grad = (a0[...].astype(FULL) + a1[...].astype(FULL)) + (
        a2[...].astype(FULL) + a3[...].astype(FULL)
    )
    back, dgain[...], dshift[...] = norm_back(grad, rows[...], gain[...])
    out[...] = gmiddle[...] + back


def on_device(
    tokens,
    ln1_gain,
    ln1_bias,
    qkv_weight,
    rel_h,
    rel_w,
    proj_weight,
    ln2_gain,
    ln2_bias,
    fc1_weight,
    fc2_weight,
    cotangent,
):
    images, tok, width = tokens.shape
    hid = fc1_weight.shape[1]
    dp_count = lax.axis_size("dp")
    head = rel_h.shape[1] * dp_count
    reach = rel_h.shape[0]
    side = (reach + 1) // 2
    s, t = lax.axis_index("seq"), lax.axis_index("tp")
    d = lax.axis_index("dp")
    y, c = t // 2, t % 2
    image = s // 2
    group = (s % 2) * 2 + y
    groups = 4
    share = width // groups
    heads = share // head
    rows_n = 2 * tok

    def of_image(array):
        mine = lax.dynamic_index_in_dim(array, image, 0, keepdims=False)
        other = lax.dynamic_index_in_dim(array, 1 - image, 0, keepdims=False)
        return mine, other

    own, away = of_image(tokens)
    own_got = hop(away, FAR)

    small = jnp.concatenate(
        [v.reshape(1, -1) for v in (ln1_gain, ln1_bias, ln2_gain, ln2_bias)], axis=0
    )
    small = gather_dp(small, 1).astype(FULL)
    gain_one, shift_one, gain_two, shift_two = (small[k : k + 1] for k in range(4))
    tables = gather_dp(jnp.stack([rel_h, rel_w]), 2)
    tables = jnp.pad(tables[:, ::-1, :], ((0, 0), (0, LANES - reach), (0, LANES - head)))
    table_t = tables.reshape(2 * LANES, LANES)
    table = table_t.T

    cols = [
        piece(qkv_weight, p * groups + group, share, 1) for p in range(3)
    ]
    order = []
    for h in range(heads):
        order += [cols[1][:, h * head : (h + 1) * head], cols[2][:, h * head : (h + 1) * head]]
    mix = gather_dp(jnp.concatenate(order + [cols[0]], axis=1), 0)
    mix = jnp.pad(mix, ((0, 0), (0, 2 * LANES - share)))
    proj = gather_dp(proj_weight, 0)
    proj = jnp.concatenate([piece(proj, group ^ k, share, 0) for k in range(4)], axis=0)
    up = gather_dp(fc1_weight, 0)
    down = gather_dp(fc2_weight, 1)

    places = []
    for k in range(4):
        for u in range(2):
            chunk = ((s ^ (k >> 1)) ^ (2 * u)) * 4 + ((y ^ (k & 1)) * 2) + c
            places += [chunk * 2, chunk * 2 + 1]
    group_rows = jnp.stack(places).astype(jnp.int32)
    key_rows = jnp.concatenate([group_rows, group_rows ^ 2])
    key_row = jnp.repeat(key_rows, side)[:, None]
    key_col = (jnp.arange(2 * groups * rows_n, dtype=jnp.int32) % side)[:, None]
    reach_idx = jnp.arange(side, dtype=jnp.int32)[None, :]
    spots = jnp.concatenate([key_row == reach_idx, key_col == reach_idx], axis=1).astype(LOW)
    blank = jnp.zeros_like(spots)
    spot_one = jnp.concatenate([blank, spots], axis=1)
    ones = jnp.concatenate([jnp.ones_like(spots[:, :3]), blank[:, 3:]], axis=1)
    spot_two = jnp.concatenate([spots, ones], axis=1)

    normed = call(norm_kernel, [shape((rows_n, width), LOW)], 0)(
        own, own_got, gain_one, shift_one
    )[0]
    normed_all = jnp.concatenate(
        [normed, hop(normed, ROW), hop(normed, NEAR), hop(normed, ROW | NEAR)], axis=0
    )
    kv_cols = 2 * share
    kv = dot_nn(normed_all, mix[:, :kv_cols]).astype(LOW)
    kv_other = hop(kv, CORE)
    query = dot_nn(normed_all, mix[:, kv_cols:]).astype(LOW)

    n = 4 * rows_n
    pad_share = 2 * LANES
    key_n = 2 * n
    attended, attended_low, left = call(
        attend_kernel,
        [
            shape((n, pad_share), FULL),
            shape((n, pad_share), LOW),
            shape((heads, n, 2 * LANES), LOW),
        ],
        heads * 4 * n * key_n * 256,
        [pltpu.VMEM((key_n, 2 * LANES), LOW), pltpu.VMEM((n, 2 * LANES), FULL)],
        smem=1,
    )(group_rows, query, kv, kv_other, spot_one, spot_two, table)

    def block(array, k):
        return array[k * rows_n : (k + 1) * rows_n]

    way = (0, ROW, NEAR, ROW | NEAR)
    attended_low = attended_low[:, :share]
    joined = [block(attended_low, 0)] + [hop(block(attended_low, k), way[k]) for k in (1, 2, 3)]
    rows = jnp.concatenate([own, own_got], axis=0)
    middle, normed_two = call(
        mid_kernel,
        [shape((rows_n, width), FULL), shape((rows_n, width), LOW)],
        2 * rows_n * width * width,
    )(*joined, proj, rows, gain_two, shift_two)

    def gather_tp(array):
        pair = jnp.concatenate([array, hop(array, ROW)], axis=0)
        return jnp.concatenate([pair, hop(pair, CORE)], axis=0)

    cot_mine, cot_away = of_image(cotangent)
    cot = jnp.concatenate([cot_mine, hop(cot_away, FAR)], axis=0)
    cot_all = gather_tp(cot)
    feed_rows = gather_tp(normed_two)
    active, dhidden, dnorm = feed(feed_rows, cot_all, up, down)

    def scatter_tp(array):
        got = hop(array[2 * rows_n :], CORE)
        sent = (block(array, 1).astype(FULL) + block(got, 1).astype(FULL)).astype(LOW)
        return block(array, 0), block(got, 0), hop(sent, ROW)

    dnorm_parts = scatter_tp(dnorm)
    (gmiddle, gbranch, b0, b1, b2, b3, dgain_two, dshift_two) = call(
        mid_back_kernel,
        [shape((rows_n, width), FULL), shape((rows_n, width), LOW)]
        + [shape((rows_n, share), LOW)] * 4
        + [shape((1, width), FULL)] * 2,
        2 * rows_n * width * width,
    )(*dnorm_parts, middle, gain_two, cot, proj)

    grad_heads = jnp.concatenate(
        [b0] + [hop(b, bits) for b, bits in ((b1, ROW), (b2, NEAR), (b3, ROW | NEAR))], axis=0
    )
    grad_heads = jnp.pad(grad_heads, ((0, 0), (0, pad_share - share)))
    dquery, dkv_mine, dkv_other, dtable = call(
        back_kernel,
        [
            shape((n, pad_share), LOW),
            shape((n, kv_cols), FULL),
            shape((n, kv_cols), LOW),
            shape((2 * LANES, LANES), FULL),
        ],
        heads * 10 * n * key_n * 256,
        [
            pltpu.VMEM((key_n, 2 * LANES), LOW),
            pltpu.VMEM((key_n, 2 * LANES), LOW),
            pltpu.VMEM((n, 2 * LANES), LOW),
            pltpu.VMEM((n, LANES), LOW),
            pltpu.VMEM((n, 2 * LANES), LOW),
        ],
        smem=1,
    )(group_rows, left, kv, kv_other, spot_one, spot_two, table, grad_heads, attended)

    dkv = (dkv_mine + hop(dkv_other, CORE).astype(FULL)).astype(LOW)
    dmixed = jnp.concatenate([dkv, dquery], axis=1)
    dnormed = dot_nt(dmixed, mix).astype(LOW)
    dnormed_parts = [block(dnormed, 0)] + [hop(block(dnormed, k), way[k]) for k in (1, 2, 3)]
    token_rows, dgain_one, dshift_one = call(
        first_back_kernel,
        [shape((rows_n, width), FULL)] + [shape((1, width), FULL)] * 2,
        0,
    )(*dnormed_parts, rows, gain_one, gmiddle)

    def to_owner(mine, other_low):
        got = hop(other_low, FAR).astype(FULL)
        return jnp.where(image == 0, jnp.stack([mine, got]), jnp.stack([got, mine]))

    tokens_grad = to_owner(token_rows[:tok], token_rows[tok:].astype(LOW))

    fed = dot_nn(active, down).astype(LOW)
    f0, f1, f2 = scatter_tp(fed)
    change = middle - rows + (f0.astype(FULL) + f1.astype(FULL) + f2.astype(FULL))
    got = hop(change[tok:].astype(LOW), FAR).astype(FULL)
    mine_out, got_out = own + change[:tok], away + got
    output = jnp.where(
        image == 0, jnp.stack([mine_out, got_out]), jnp.stack([got_out, mine_out])
    )

    def sum_seq(value, axis):
        size = value.shape[axis] // 4
        total = piece(value, s, size, axis).astype(FULL)
        for k in (1, 2, 3):
            sent = piece(value, s ^ k, size, axis).astype(LOW)
            total = total + hop(sent, k * NEAR).astype(FULL)
        low = total.astype(LOW)
        parts = [low] + [hop(low, k * NEAR) for k in (1, 2, 3)]
        return canon(parts, s, axis).astype(FULL)

    fc2_grad = sum_seq(scatter_dp(dot_tn(active, cot_all).astype(LOW), 1), 0)
    fc1_grad = sum_seq(scatter_dp(dot_tn(feed_rows, dhidden).astype(LOW), 0), 0)

    def halve(value, bits, bit, axis):
        size = value.shape[axis] // 2
        sent = piece(value, 1 - bit, size, axis).astype(LOW)
        return piece(value, bit, size, axis).astype(FULL) + hop(sent, bits).astype(FULL)

    def double(value, bits, bit, axis):
        got = hop(value, bits)
        return jnp.concatenate(
            [jnp.where(bit == 0, value, got), jnp.where(bit == 0, got, value)], axis=axis
        )

    def exchange(value, bits):
        low = value.astype(LOW)
        return low.astype(FULL) + hop(low, bits).astype(FULL)

    joined_all = canon(joined, group, 1)
    proj_grad = dot_tn(joined_all, gbranch)
    proj_grad = halve(halve(proj_grad, CORE, c, 1), ROW, y, 1)
    proj_grad = exchange(exchange(scatter_dp(proj_grad, 0), NEAR), FAR).astype(LOW)
    proj_grad = double(double(proj_grad, ROW, y, 1), CORE, c, 1).astype(FULL)

    qkv_cols = 3 * share
    qkv_part = dot_tn(normed_all, dmixed[:, :qkv_cols])
    qkv_part = exchange(scatter_dp(halve(qkv_part, CORE, c, 1), 0), FAR).astype(LOW)
    qkv_parts = [qkv_part] + [hop(qkv_part, bits) for bits in way[1:]]
    qkv_all = jnp.stack(qkv_parts)
    qkv_all = double(qkv_all, CORE, c, 2)
    qkv_all = canon([qkv_all[k : k + 1] for k in range(4)], group, 0)
    keys_values = qkv_all[:, :, :kv_cols].reshape(groups, -1, heads, 2, head)
    depth = qkv_all.shape[1]
    qkv_grad = jnp.concatenate(
        [
            qkv_all[:, :, kv_cols:].transpose(1, 0, 2).reshape(depth, width),
            keys_values[:, :, :, 0].transpose(1, 0, 2, 3).reshape(depth, width),
            keys_values[:, :, :, 1].transpose(1, 0, 2, 3).reshape(depth, width),
        ],
        axis=1,
    ).astype(FULL)

    dtable = (dtable[:, :head] * 8.0).reshape(-1)
    vector = jnp.concatenate(
        [v.reshape(-1) for v in (dgain_one, dshift_one, dgain_two, dshift_two)] + [dtable]
    ).reshape(-1, LANES)
    for bits in (CORE, ROW, NEAR, FAR):
        vector = vector + hop(vector, bits)
    vector = sum_dp(vector).reshape(-1)
    norms = vector[: 4 * width].reshape(4, width)
    norms = piece(norms, d, width // dp_count, 1)
    dtables = vector[4 * width :].reshape(2, LANES, head)[:, :reach][:, ::-1]
    dtables = piece(dtables, d, head // dp_count, 2)
    return (
        output,
        tokens_grad,
        norms[0],
        norms[1],
        qkv_grad,
        dtables[0],
        dtables[1],
        proj_grad,
        norms[2],
        norms[3],
        fc1_grad,
        fc2_grad,
    )


def solution(mesh):
    split = P("dp", ("seq", "tp"), None)
    params = (
        P("dp"),
        P("dp"),
        P("dp", None),
        P(None, "dp"),
        P(None, "dp"),
        P("dp", None),
        P("dp"),
        P("dp"),
        P("dp", "tp"),
        P("tp", "dp"),
    )
    return jax.shard_map(
        on_device,
        mesh=mesh,
        in_specs=(split, *params, split),
        out_specs=(split, split, *params),
        check_vma=False,
    )
```

time: 752 us -> 256 us (0.34)
  waiting for transfers between devices: 304 us -> 103 us
  blocking collectives: 133 us -> 0 us
  local copies, waits for them, and re-layouts: 99.1 us -> 24.9 us
  matrix products: 79.5 us -> 6.62 us
  other arithmetic: 76.9 us -> 19.9 us
  starting transfers between devices: 34.9 us -> 75.9 us
  Pallas kernels: 0 us -> 23.4 us
  between operations: 15.9 us -> 2.2 us
    reduce_scatter x9 -> x0, waiting for transfers between devices: 147 us -> none  [the longest x1 50.6 us: split_data(): lax.psum_scatter(mix_grad.astype(jnp.bfloat16), 'dp', scatter_dimension=0...]
    ppermute x0 -> x65, waiting for transfers between devices: none -> 103 us  [the longest x54 76.8 us: hop(): lax.ppermute(value, ('seq', 'tp'), [(i, i ^ bits) for i in range(count)])]
    psum x2 -> x0, waiting for transfers between devices: 94.4 us -> none  [the longest x1 57.6 us: sum_feedforward(): lax.psum(up_grad.astype(jnp.bfloat16), 'seq').astype(jnp.float32)]
    ppermute x0 -> x65, starting transfers between devices: none -> 75.9 us  [the longest x54 58.5 us: hop(): lax.ppermute(value, ('seq', 'tp'), [(i, i ^ bits) for i in range(count)])]
    dot_general x102 -> x8, matrix products: 79.5 us -> 6.62 us  [the longest x4 4.09 us: dot_tn(): lax.dot_general(a, b, (((0,), (0,)), ((), ())), preferred_element_type=FULL)]
    all_gather x10 -> x0, blocking collectives: 66.3 us -> none  [the longest x1 10.3 us: on_device(): lax.all_gather(value_heads, 'tp', axis=1, tiled=True)]
    psum x1 -> x0, blocking collectives: 61.3 us -> none  [sum_attention(): lax.psum(gain_one.astype(jnp.bfloat16), ('seq', 'tp')).astype(jnp.float32)]
    scatter-add x12 -> x0, other arithmetic: 47.1 us -> none  [the longest x6 36.4 us: rel_terms(): window_w = jnp.take(table_w, pick_w, axis=0)]
  transfers between devices with their start and end apart: 24 -> 65, of which waited for: 15 -> 32; matrix products, arithmetic and copies ran while one was open for 31% -> 14% of each run, Pallas kernels for 0% -> 7%
where the time goes in v1:
time: 256 us
  waiting for transfers between devices  103 us (40%)
  starting transfers between devices  75.9 us (30%)
  local copies, waits for them, and re-layouts  24.9 us (10%)
  Pallas kernels  23.4 us (9%)
  other arithmetic  19.9 us (8%)
  matrix products  6.62 us (3%)
    ppermute x54, waiting for transfers between devices, hop(): lax.ppermute(value, ('seq', 'tp'), [(i, i ^ bits) for i in range(count)])  76.8 us
    ppermute x54, starting transfers between devices, hop(): lax.ppermute(value, ('seq', 'tp'), [(i, i ^ bits) for i in range(count)])  58.5 us
    pallas_call x6, Pallas kernels, run(): pl.pallas_call(kernel, out_shape=outs, in_specs=[pl.BlockSpec(memory_spac...  19.2 us
    ppermute x4, waiting for transfers between devices, scatter_dp(): got = lax.ppermute(sent, 'dp', [(0, 1), (1, 0)])  16.5 us
    unnamed x88, local copies, waits for them, and re-layouts  12.9 us
    ppermute x6, starting transfers between devices, gather_dp(): other = lax.ppermute(value, 'dp', [(0, 1), (1, 0)])  8.26 us
    ppermute x6, waiting for transfers between devices, gather_dp(): other = lax.ppermute(value, 'dp', [(0, 1), (1, 0)])  7.73 us
    ppermute x4, starting transfers between devices, scatter_dp(): got = lax.ppermute(sent, 'dp', [(0, 1), (1, 0)])  5.97 us
  transfers between devices with their start and end apart: 65, of which 32 were waited for; matrix products, arithmetic and copies ran while one was open for 14% of the time, Pallas kernels for 7%

profile of v1, /device:TPU:0, one launch (start us, length us, event | category | flops | bytes accessed | tf_op | source)
XLA Modules:
  0.0 255.6 jit_solution(15206822012582848817)
XLA Ops:
  1.8 1.4 constant_dynamic-slice_fusion.8
  3.7 3.0 %collective-permute-start.5 = (bf16[384,576]{1,0:T(8,128)(2,1)S(1)}, bf16[384,576]{1,0:T(8,128)(2,1)S(1)}, u32[]{:S(2)}, u32[]{:S(2)}) collective-permute-start(bf16[384,576]{1,0:T(8,128)(2,1)S(1)} %concatenate.100), channel_id=1, source_target_pairs={{0,16},{16,0},{1,17},{17,1},{2,18},{18,2},{3,19},{19,3},{4,20},{20... | collective-permute-start | bytes 1327112 | tf_op jit(solution)/shard_map/ppermute | solution.py:23
  6.8 2.7 %collective-permute-start = (f32[64,768]{1,0:T(8,128)S(1)}, f32[64,768]{1,0:T(8,128)S(1)}, u32[]{:S(2)}, u32[]{:S(2)}) collective-permute-start(f32[64,768]{1,0:T(8,128)S(1)} %get-tuple-element.141), channel_id=1, source_target_pairs={{0,8},{1,9},{2,10},{3,11},{4,12},{5,13},{6,14},{7,15},{8,0},{9,1},... | collective-permute-start | bytes 589832 | tf_op jit(solution)/shard_map/ppermute | solution.py:17
  10.1 1.6 collective-permute-start.7
  13.6 5.2 %collective-permute-done.1 = bf16[4,384]{1,0:T(4,128)(2,1)S(1)} collective-permute-done((bf16[4,384]{1,0:T(4,128)(2,1)S(1)}, bf16[4,384]{1,0:T(4,128)(2,1)S(1)}, u32[]{:S(2)}, u32[]{:S(2)}) %collective-permute-start.1) | collective-permute-done | bytes 3104 | tf_op jit(solution)/shard_map/ppermute | solution.py:23
  18.8 2.1 collective-permute-start.11
  21.0 2.7 %collective-permute-start.14 = (bf16[64,768]{1,0:T(8,128)(2,1)S(1)}, bf16[64,768]{1,0:T(8,128)(2,1)S(1)}, u32[]{:S(2)}, u32[]{:S(2)}) collective-permute-start(bf16[64,768]{1,0:T(8,128)(2,1)S(1)} %get-tuple-element.151), channel_id=1, source_target_pairs={{0,8},{1,9},{2,10},{3,11},{4,12},{5,13},{6,14},{7,15},{8,0},{9,1},... | collective-permute-start | bytes 294920 | tf_op jit(solution)/shard_map/ppermute | solution.py:17
  23.7 2.9 %collective-permute-done.14 = bf16[64,768]{1,0:T(8,128)(2,1)S(1)} collective-permute-done((bf16[64,768]{1,0:T(8,128)(2,1)S(1)}, bf16[64,768]{1,0:T(8,128)(2,1)S(1)}, u32[]{:S(2)}, u32[]{:S(2)}) %collective-permute-start.14) | collective-permute-done | bytes 98336 | tf_op jit(solution)/shard_map/ppermute | solution.py:17
  26.6 1.6 collective-permute-start.15
  28.6 1.8 collective-permute-start.4
  30.4 2.1 collective-permute-done.15
  32.5 2.0 collective-permute-start.3
  34.6 1.3 collective-permute-start.2
  38.2 2.1 collective-permute-done.2
  42.0 2.5 collective-permute-done.11
  44.6 1.8 broadcast_select_fusion.5
  46.3 1.7 fusion.14
  48.1 7.9 %shard_map.212 = (f32[512,256]{1,0:T(8,128)S(1)}, bf16[512,256]{1,0:T(8,128)(2,1)S(1)}, bf16[3,512,256]{2,1,0:T(8,128)(2,1)S(1)}) custom-call(s32[16]{0:T(128)S(1)} %stack.122.group_rows, bf16[512,256]{1,0:T(8,128)(2,1)S(1)} %convolution_convert_fusion.5.query, bf16[512,384]{1,0:T(8,128)(2,1)S(1)} %convolution_convert_fusion.4.kva, ...), custom_call_target="tpu_custom_call" | custom-call | flops 1610612736 | bytes 3211328 | tf_op jit(solution)/shard_map/pallas_call | solution.py:78
  56.9 3.1 %collective-permute-start.10 = (bf16[128,192]{1,0:T(8,128)(2,1)S(1)}, bf16[128,192]{1,0:T(8,128)(2,1)S(1)}, u32[]{:S(2)}, u32[]{:S(2)}) collective-permute-start(bf16[128,192]{1,0:T(8,128)(2,1)S(1)} %get-tuple-element.145), channel_id=1, source_target_pairs={{0,6},{1,7},{2,4},{3,5},{4,2},{5,3},{6,0},{7,1},{8,14},{9,15},{10,... | collective-permute-start | bytes 147464 | tf_op jit(solution)/shard_map/ppermute | solution.py:17
  60.7 1.5 collective-permute-done.10.j3
  62.3 2.0 collective-permute-done.9.j2
  66.3 5.4 %collective-permute-done.12 = bf16[128,768]{1,0:T(8,128)(2,1)S(1)} collective-permute-done((bf16[128,768]{1,0:T(8,128)(2,1)S(1)}, bf16[128,768]{1,0:T(8,128)(2,1)S(1)}, u32[]{:S(2)}, u32[]{:S(2)}) %collective-permute-start.12) | collective-permute-done | bytes 196640 | tf_op jit(solution)/shard_map/ppermute | solution.py:17
  72.2 1.3 collective-permute-done.13
  73.6 4.3 %shard_map.214 = (bf16[512,768]{1,0:T(8,128)(2,1)S(1)}, bf16[512,768]{1,0:T(8,128)(2,1)S(1)}, bf16[512,768]{1,0:T(8,128)(2,1)S(1)}) custom-call(bf16[512,768]{1,0:T(8,128)(2,1)S(1)} %constant_dynamic-update-slice_fusion.rows, bf16[512,768]{1,0:T(8,128)(2,1)S(1)} %pad_maximum_fusion.9.grad, bf16[768,768]{1,0:T(8,128)(2,1)S(1)} %pad_maximum_fusion.4.up, ...), custom_call_target="tpu_custom_call" | custom-call | flops 1811939328 | bytes 7077888 | tf_op jit(solution)/shard_map/pallas_call | solution.py:283
  80.2 1.6 collective-permute-start.51
  83.4 2.1 collective-permute-start.23
  85.5 10.9 %collective-permute-done.51 = bf16[384,768]{1,0:T(8,128)(2,1)S(1)} collective-permute-done((bf16[384,768]{1,0:T(8,128)(2,1)S(1)}, bf16[384,768]{1,0:T(8,128)(2,1)S(1)}, u32[]{:S(2)}, u32[]{:S(2)}) %collective-permute-start.51) | collective-permute-done | bytes 589856 | tf_op jit(solution)/shard_map/ppermute | solution.py:42
  97.6 2.0 dynamic-slice_convert_fusion.9
  99.5 3.6 %collective-permute-start.54 = (bf16[96,768]{1,0:T(8,128)(2,1)}, bf16[96,768]{1,0:T(8,128)(2,1)}, u32[]{:S(2)}, u32[]{:S(2)}) collective-permute-start(bf16[96,768]{1,0:T(8,128)(2,1)} %get-tuple-element.106), channel_id=1, source_target_pairs={{0,12},{1,13},{2,14},{3,15},{4,8},{5,9},{6,10},{7,11},{8,4},{9,5},... | collective-permute-start | bytes 442376 | tf_op jit(solution)/shard_map/ppermute | solution.py:17
  103.1 5.1 %collective-permute-done.58 = bf16[768,384]{1,0:T(8,128)(2,1)S(1)} collective-permute-done((bf16[768,384]{1,0:T(8,128)(2,1)S(1)}, bf16[768,384]{1,0:T(8,128)(2,1)S(1)}, u32[]{:S(2)}, u32[]{:S(2)}) %collective-permute-start.58) | collective-permute-done | bytes 589856 | tf_op jit(solution)/shard_map/ppermute | solution.py:42
  110.3 1.4 collective-permute-start.26
  112.0 1.8 collective-permute-start.24
  114.5 1.4 copy-done.8
  117.5 1.6 collective-permute-start.52
  119.1 2.4 collective-permute-start.61
  124.0 9.3 %shard_map.216 = (bf16[512,256]{1,0:T(8,128)(2,1)S(1)}, f32[512,384]{1,0:T(8,128)S(1)}, bf16[512,384]{1,0:T(8,128)(2,1)S(1)}, f32[256,128]{1,0:T(8,128)S(1)}) custom-call(s32[16]{0:T(128)S(1)} %stack.122.group_rows, bf16[3,512,256]{2,1,0:T(8,128)(2,1)S(1)} %copy-done.5, bf16[512,384]{1,0:T(8,128)(2,1)S(1)} %convolution_convert_fusion.4.kva, ...), custom_call_target="tpu_custom_call" | custom-call | flops 4026531840 | bytes 4522048 | tf_op jit(solution)/shard_map/pallas_call | solution.py:78
  134.9 2.8 %collective-permute-start.60 = (bf16[192,384]{1,0:T(8,128)(2,1)}, bf16[192,384]{1,0:T(8,128)(2,1)S(1)}, u32[]{:S(2)}, u32[]{:S(2)}) collective-permute-start(bf16[192,384]{1,0:T(8,128)(2,1)} %get-tuple-element.104), channel_id=1, source_target_pairs={{0,8},{1,9},{2,10},{3,11},{4,12},{5,13},{6,14},{7,15},{8,0},{9,1},... | collective-permute-start | bytes 442376 | tf_op jit(solution)/shard_map/ppermute | solution.py:17
  142.9 1.7 collective-permute-start.56
  144.7 1.6 collective-permute-start.57
  147.4 3.1 %collective-permute-done.55 = bf16[96,768]{1,0:T(8,128)(2,1)S(1)} collective-permute-done((bf16[96,768]{1,0:T(8,128)(2,1)S(1)}, bf16[96,768]{1,0:T(8,128)(2,1)S(1)}, u32[]{:S(2)}, u32[]{:S(2)}) %collective-permute-start.55) | collective-permute-done | bytes 147488 | tf_op jit(solution)/shard_map/ppermute | solution.py:17
  151.5 10.5 %collective-permute-done.56 = bf16[96,768]{1,0:T(8,128)(2,1)S(1)} collective-permute-done((bf16[96,768]{1,0:T(8,128)(2,1)S(1)}, bf16[96,768]{1,0:T(8,128)(2,1)S(1)}, u32[]{:S(2)}, u32[]{:S(2)}) %collective-permute-start.56) | collective-permute-done | bytes 147488 | tf_op jit(solution)/shard_map/ppermute | solution.py:17
  162.0 1.8 collective-permute-start.64
  164.9 5.6 %collective-permute-done.63 = bf16[192,384]{1,0:T(8,128)(2,1)S(1)} collective-permute-done((bf16[192,384]{1,0:T(8,128)(2,1)S(1)}, bf16[192,384]{1,0:T(8,128)(2,1)S(1)}, u32[]{:S(2)}, u32[]{:S(2)}) %collective-permute-start.63) | collective-permute-done | bytes 147488 | tf_op jit(solution)/shard_map/ppermute | solution.py:17
  173.7 3.2 %collective-permute-start.30 = (bf16[128,768]{1,0:T(8,128)(2,1)S(1)}, bf16[128,768]{1,0:T(8,128)(2,1)S(1)}, u32[]{:S(2)}, u32[]{:S(2)}) collective-permute-start(bf16[128,768]{1,0:T(8,128)(2,1)S(1)} %get-tuple-element.122), channel_id=1, source_target_pairs={{0,6},{1,7},{2,4},{3,5},{4,2},{5,3},{6,0},{7,1},{8,14},{9,15},{10,... | collective-permute-start | bytes 589832 | tf_op jit(solution)/shard_map/ppermute | solution.py:17
  176.9 1.9 fusion.2
  181.5 3.3 %collective-permute-done.30.a3 = bf16[128,768]{1,0:T(8,128)(2,1)S(1)} collective-permute-done((bf16[128,768]{1,0:T(8,128)(2,1)S(1)}, bf16[128,768]{1,0:T(8,128)(2,1)S(1)}, u32[]{:S(2)}, u32[]{:S(2)}) %collective-permute-start.30) | collective-permute-done | bytes 196640 | tf_op jit(solution)/shard_map/ppermute | solution.py:17
  187.1 1.7 collective-permute-start.33
  190.1 7.5 %collective-permute-done.33 = f32[152,128]{1,0:T(8,128)S(1)} collective-permute-done((f32[152,128]{1,0:T(8,128)S(1)}, f32[152,128]{1,0:T(8,128)S(1)}, u32[]{:S(2)}, u32[]{:S(2)}) %collective-permute-start.33) | collective-permute-done | bytes 77856 | tf_op jit(solution)/shard_map/ppermute | solution.py:17
  198.1 1.6 collective-permute-start.46
  199.8 2.2 collective-permute-start.31
  203.4 1.8 collective-permute-start.47
  205.3 2.2 collective-permute-start.38
  207.5 4.6 %collective-permute-done.47 = bf16[384,192]{0,1:T(8,128)(2,1)S(1)} collective-permute-done((bf16[384,192]{0,1:T(8,128)(2,1)S(1)}, bf16[384,192]{0,1:T(8,128)(2,1)S(1)}, u32[]{:S(2)}, u32[]{:S(2)}) %collective-permute-start.47) | collective-permute-done | bytes 147488 | tf_op jit(solution)/shard_map/ppermute | solution.py:17
  212.4 3.0 %collective-permute-start.39 = (bf16[384,288]{0,1:T(8,128)(2,1)S(1)}, bf16[384,288]{0,1:T(8,128)(2,1)S(1)}, u32[]{:S(2)}, u32[]{:S(2)}) collective-permute-start(bf16[384,288]{0,1:T(8,128)(2,1)S(1)} %add_convert_fusion.3), channel_id=1, source_target_pairs={{0,8},{1,9},{2,10},{3,11},{4,12},{5,13},{6,14},{7,15},{8,0},{9,1},... | collective-permute-start | bytes 663560 | tf_op jit(solution)/shard_map/ppermute | solution.py:17
  215.3 8.0 %collective-permute-done.48 = bf16[384,192]{0,1:T(8,128)(2,1)S(1)} collective-permute-done((bf16[384,192]{0,1:T(8,128)(2,1)S(1)}, bf16[384,192]{0,1:T(8,128)(2,1)S(1)}, u32[]{:S(2)}, u32[]{:S(2)}) %collective-permute-start.48) | collective-permute-done | bytes 147488 | tf_op jit(solution)/shard_map/ppermute | solution.py:17
  223.8 2.6 %collective-permute-done.39 = bf16[384,288]{0,1:T(8,128)(2,1)S(1)} collective-permute-done((bf16[384,288]{0,1:T(8,128)(2,1)S(1)}, bf16[384,288]{0,1:T(8,128)(2,1)S(1)}, u32[]{:S(2)}, u32[]{:S(2)}) %collective-permute-start.39) | collective-permute-done | bytes 221216 | tf_op jit(solution)/shard_map/ppermute | solution.py:17
  226.5 1.8 collective-permute-start.41
  228.3 2.6 %collective-permute-done.49 = bf16[384,192]{0,1:T(8,128)(2,1)S(1)} collective-permute-done((bf16[384,192]{0,1:T(8,128)(2,1)S(1)}, bf16[384,192]{0,1:T(8,128)(2,1)S(1)}, u32[]{:S(2)}, u32[]{:S(2)}) %collective-permute-start.49) | collective-permute-done | bytes 147488 | tf_op jit(solution)/shard_map/ppermute | solution.py:17
  231.3 4.3 %collective-permute-done.42 = bf16[384,288]{0,1:T(8,128)(2,1)S(1)} collective-permute-done((bf16[384,288]{0,1:T(8,128)(2,1)S(1)}, bf16[384,288]{0,1:T(8,128)(2,1)S(1)}, u32[]{:S(2)}, u32[]{:S(2)}) %collective-permute-start.42) | collective-permute-done | bytes 221216 | tf_op jit(solution)/shard_map/ppermute | solution.py:17
  239.6 3.2 %collective-permute-start.36 = (f32[152,128]{1,0:T(8,128)S(1)}, f32[152,128]{1,0:T(8,128)S(1)}, u32[]{:S(2)}, u32[]{:S(2)}) collective-permute-start(f32[152,128]{1,0:T(8,128)S(1)} %add.331), channel_id=1, source_target_pairs={{0,16},{16,0},{1,17},{17,1},{2,18},{18,2},{3,19},{19,3},{4,20},{20... | collective-permute-start | bytes 233480 | tf_op jit(solution)/shard_map/ppermute | solution.py:49
  243.5 1.8 collective-permute-done.36
  248.8 1.4 copy.35
  250.2 1.3 broadcast_select_fusion.1
  252.7 2.9 %copy.32 = f32[384,2304]{1,0:T(8,128)} copy(f32[384,2304]{0,1:T(8,128)S(1)} %maximum_convert_fusion) | data formatting | bytes 7077888
  (292 shorter events, 56.3 us)
Async XLA Ops:
  3.7 30.8 %collective-permute-start.5 = (bf16[384,576]{1,0:T(8,128)(2,1)S(1)}, bf16[384,576]{1,0:T(8,128)(2,1)S(1)}, u32[]{:S(2)}, u32[]{:S(2)}) collective-permute-start(bf16[384,576]{1,0:T(8,128)(2,1)S(1)} %concatenate.100), channel_id=1, source_target_pairs={{0,16},{16,0},{1,17},{17,1},{2,18},{18,2},{3,19},{19,3},{4,20},{20... | collective-permute-start | bytes 1327112 | tf_op jit(solution)/shard_map/ppermute | solution.py:23
  6.8 21.6 %collective-permute-start = (f32[64,768]{1,0:T(8,128)S(1)}, f32[64,768]{1,0:T(8,128)S(1)}, u32[]{:S(2)}, u32[]{:S(2)}) collective-permute-start(f32[64,768]{1,0:T(8,128)S(1)} %get-tuple-element.141), channel_id=1, source_target_pairs={{0,8},{1,9},{2,10},{3,11},{4,12},{5,13},{6,14},{7,15},{8,0},{9,1},... | collective-permute-start | bytes 589832 | tf_op jit(solution)/shard_map/ppermute | solution.py:17
  9.5 9.3 %collective-permute-start.1 = (bf16[4,384]{1,0:T(4,128)(2,1)S(1)}, bf16[4,384]{1,0:T(4,128)(2,1)S(1)}, u32[]{:S(2)}, u32[]{:S(2)}) collective-permute-start(bf16[4,384]{1,0:T(4,128)(2,1)S(1)} %pad_maximum_fusion.21), channel_id=1, source_target_pairs={{0,16},{16,0},{1,17},{17,1},{2,18},{18,2},{3,19},{19,3},{4,20},{20... | collective-permute-start | bytes 9224 | tf_op jit(solution)/shard_map/ppermute | solution.py:23
  10.1 10.8 %collective-permute-start.7 = (bf16[2,63,32]{1,2,0:T(8,128)(2,1)S(1)}, bf16[2,63,32]{1,2,0:T(8,128)(2,1)S(1)}, u32[]{:S(2)}, u32[]{:S(2)}) collective-permute-start(bf16[2,63,32]{1,2,0:T(8,128)(2,1)S(1)} %pad_maximum_fusion.20), channel_id=1, source_target_pairs={{0,16},{16,0},{1,17},{17,1},{2,18},{18,2},{3,19},{19,3},{4,20},{20... | collective-permute-start | bytes 24200 | tf_op jit(solution)/shard_map/ppermute | solution.py:23
  11.7 30.3 %collective-permute-start.17 = (bf16[384,768]{1,0:T(8,128)(2,1)}, bf16[384,768]{1,0:T(8,128)(2,1)}, u32[]{:S(2)}, u32[]{:S(2)}) collective-permute-start(bf16[384,768]{1,0:T(8,128)(2,1)} %param.21), channel_id=1, source_target_pairs={{0,16},{16,0},{1,17},{17,1},{2,18},{18,2},{3,19},{19,3},{4,20},{20... | collective-permute-start | bytes 1769480 | tf_op jit(solution)/shard_map/ppermute | solution.py:23
  18.8 25.7 %collective-permute-start.11 = (bf16[384,768]{1,0:T(8,128)(2,1)}, bf16[384,768]{1,0:T(8,128)(2,1)}, u32[]{:S(2)}, u32[]{:S(2)}) collective-permute-start(bf16[384,768]{1,0:T(8,128)(2,1)} %param.18), channel_id=1, source_target_pairs={{0,16},{16,0},{1,17},{17,1},{2,18},{18,2},{3,19},{19,3},{4,20},{20... | collective-permute-start | bytes 1769480 | tf_op jit(solution)/shard_map/ppermute | solution.py:23
  21.0 5.6 %collective-permute-start.14 = (bf16[64,768]{1,0:T(8,128)(2,1)S(1)}, bf16[64,768]{1,0:T(8,128)(2,1)S(1)}, u32[]{:S(2)}, u32[]{:S(2)}) collective-permute-start(bf16[64,768]{1,0:T(8,128)(2,1)S(1)} %get-tuple-element.151), channel_id=1, source_target_pairs={{0,8},{1,9},{2,10},{3,11},{4,12},{5,13},{6,14},{7,15},{8,0},{9,1},... | collective-permute-start | bytes 294920 | tf_op jit(solution)/shard_map/ppermute | solution.py:17
  26.6 5.9 %collective-permute-start.15 = (bf16[128,768]{1,0:T(8,128)(2,1)S(1)}, bf16[128,768]{1,0:T(8,128)(2,1)S(1)}, u32[]{:S(2)}, u32[]{:S(2)}) collective-permute-start(bf16[128,768]{1,0:T(8,128)(2,1)S(1)} %pad_maximum_fusion.18.cot), channel_id=1, source_target_pairs={{0,2},{1,3},{2,0},{3,1},{4,6},{5,7},{6,4},{7,5},{8,10},{9,11},{10,... | collective-permute-start | bytes 589832 | tf_op jit(solution)/shard_map/ppermute | solution.py:17
  28.6 8.1 %collective-permute-start.4 = (bf16[128,768]{1,0:T(8,128)(2,1)S(1)}, bf16[128,768]{1,0:T(8,128)(2,1)S(1)}, u32[]{:S(2)}, u32[]{:S(2)}) collective-permute-start(bf16[128,768]{1,0:T(8,128)(2,1)S(1)} %shard_map.211), channel_id=1, source_target_pairs={{0,6},{1,7},{2,4},{3,5},{4,2},{5,3},{6,0},{7,1},{8,14},{9,15},{10,... | collective-permute-start | bytes 589832 | tf_op jit(solution)/shard_map/ppermute | solution.py:17
  32.5 5.7 %collective-permute-start.3 = (bf16[128,768]{1,0:T(8,128)(2,1)S(1)}, bf16[128,768]{1,0:T(8,128)(2,1)S(1)}, u32[]{:S(2)}, u32[]{:S(2)}) collective-permute-start(bf16[128,768]{1,0:T(8,128)(2,1)S(1)} %shard_map.211), channel_id=1, source_target_pairs={{0,4},{1,5},{2,6},{3,7},{4,0},{5,1},{6,2},{7,3},{8,12},{9,13},{10,... | collective-permute-start | bytes 589832 | tf_op jit(solution)/shard_map/ppermute | solution.py:17
  34.6 5.7 %collective-permute-start.2 = (bf16[128,768]{1,0:T(8,128)(2,1)S(1)}, bf16[128,768]{1,0:T(8,128)(2,1)S(1)}, u32[]{:S(2)}, u32[]{:S(2)}) collective-permute-start(bf16[128,768]{1,0:T(8,128)(2,1)S(1)} %shard_map.211), channel_id=1, source_target_pairs={{0,2},{1,3},{2,0},{3,1},{4,6},{5,7},{6,4},{7,5},{8,10},{9,11},{10,... | collective-permute-start | bytes 589832 | tf_op jit(solution)/shard_map/ppermute | solution.py:17
  36.7 29.3 %collective-permute-start.18 = (bf16[768,384]{1,0:T(8,128)(2,1)S(1)}, bf16[768,384]{1,0:T(8,128)(2,1)S(1)}, u32[]{:S(2)}, u32[]{:S(2)}) collective-permute-start(bf16[768,384]{1,0:T(8,128)(2,1)S(1)} %copy-done.21), channel_id=1, source_target_pairs={{0,16},{16,0},{1,17},{17,1},{2,18},{18,2},{3,19},{19,3},{4,20},{20... | collective-permute-start | bytes 1769480 | tf_op jit(solution)/shard_map/ppermute | solution.py:23
  38.2 33.7 %collective-permute-start.16 = (bf16[256,768]{1,0:T(8,128)(2,1)S(1)}, bf16[256,768]{1,0:T(8,128)(2,1)S(1)}, u32[]{:S(2)}, u32[]{:S(2)}) collective-permute-start(bf16[256,768]{1,0:T(8,128)(2,1)S(1)} %pad_maximum_fusion.16), channel_id=1, source_target_pairs={{0,1},{1,0},{2,3},{3,2},{4,5},{5,4},{6,7},{7,6},{8,9},{9,8},{10,11... | collective-permute-start | bytes 1179656 | tf_op jit(solution)/shard_map/ppermute | solution.py:17
  40.9 7.2 %collective-permute-start.6 = (bf16[512,384]{1,0:T(8,128)(2,1)S(1)}, bf16[512,384]{1,0:T(8,128)(2,1)S(1)}, u32[]{:S(2)}, u32[]{:S(2)}) collective-permute-start(bf16[512,384]{1,0:T(8,128)(2,1)S(1)} %convolution_convert_fusion.4.kva), channel_id=1, source_target_pairs={{0,1},{1,0},{2,3},{3,2},{4,5},{5,4},{6,7},{7,6},{8,9},{9,8},{10,11... | collective-permute-start | bytes 1179656 | tf_op jit(solution)/shard_map/ppermute | solution.py:17
  56.9 5.4 %collective-permute-start.10 = (bf16[128,192]{1,0:T(8,128)(2,1)S(1)}, bf16[128,192]{1,0:T(8,128)(2,1)S(1)}, u32[]{:S(2)}, u32[]{:S(2)}) collective-permute-start(bf16[128,192]{1,0:T(8,128)(2,1)S(1)} %get-tuple-element.145), channel_id=1, source_target_pairs={{0,6},{1,7},{2,4},{3,5},{4,2},{5,3},{6,0},{7,1},{8,14},{9,15},{10,... | collective-permute-start | bytes 147464 | tf_op jit(solution)/shard_map/ppermute | solution.py:17
  60.0 4.3 %collective-permute-start.9 = (bf16[128,192]{1,0:T(8,128)(2,1)S(1)}, bf16[128,192]{1,0:T(8,128)(2,1)S(1)}, u32[]{:S(2)}, u32[]{:S(2)}) collective-permute-start(bf16[128,192]{1,0:T(8,128)(2,1)S(1)} %get-tuple-element.146), channel_id=1, source_target_pairs={{0,4},{1,5},{2,6},{3,7},{4,0},{5,1},{6,2},{7,3},{8,12},{9,13},{10,... | collective-permute-start | bytes 147464 | tf_op jit(solution)/shard_map/ppermute | solution.py:17
  60.5 4.9 %collective-permute-start.8 = (bf16[128,192]{1,0:T(8,128)(2,1)S(1)}, bf16[128,192]{1,0:T(8,128)(2,1)S(1)}, u32[]{:S(2)}, u32[]{:S(2)}) collective-permute-start(bf16[128,192]{1,0:T(8,128)(2,1)S(1)} %get-tuple-element.147), channel_id=1, source_target_pairs={{0,2},{1,3},{2,0},{3,1},{4,6},{5,7},{6,4},{7,5},{8,10},{9,11},{10,... | collective-permute-start | bytes 147464 | tf_op jit(solution)/shard_map/ppermute | solution.py:17
  66.0 5.7 %collective-permute-start.12 = (bf16[128,768]{1,0:T(8,128)(2,1)S(1)}, bf16[128,768]{1,0:T(8,128)(2,1)S(1)}, u32[]{:S(2)}, u32[]{:S(2)}) collective-permute-start(bf16[128,768]{1,0:T(8,128)(2,1)S(1)} %get-tuple-element.37), channel_id=1, source_target_pairs={{0,2},{1,3},{2,0},{3,1},{4,6},{5,7},{6,4},{7,5},{8,10},{9,11},{10,... | collective-permute-start | bytes 589832 | tf_op jit(solution)/shard_map/ppermute | solution.py:17
  71.7 1.8 collective-permute-start.13
  78.7 4.5 %collective-permute-start.19 = (bf16[256,768]{1,0:T(8,128)(2,1)S(1)}, bf16[256,768]{1,0:T(8,128)(2,1)S(1)}, u32[]{:S(2)}, u32[]{:S(2)}) collective-permute-start(bf16[256,768]{1,0:T(8,128)(2,1)S(1)} %slice.233), channel_id=1, source_target_pairs={{0,1},{1,0},{2,3},{3,2},{4,5},{5,4},{6,7},{7,6},{8,9},{9,8},{10,11... | collective-permute-start | bytes 1179656 | tf_op jit(solution)/shard_map/ppermute | solution.py:17
  78.9 4.4 %collective-permute-start.22 = (bf16[256,768]{1,0:T(8,128)(2,1)S(1)}, bf16[256,768]{1,0:T(8,128)(2,1)S(1)}, u32[]{:S(2)}, u32[]{:S(2)}) collective-permute-start(bf16[256,768]{1,0:T(8,128)(2,1)S(1)} %slice.197), channel_id=1, source_target_pairs={{0,1},{1,0},{2,3},{3,2},{4,5},{5,4},{6,7},{7,6},{8,9},{9,8},{10,11... | collective-permute-start | bytes 1179656 | tf_op jit(solution)/shard_map/ppermute | solution.py:17
  80.2 16.2 %collective-permute-start.51 = (bf16[384,768]{1,0:T(8,128)(2,1)S(1)}, bf16[384,768]{1,0:T(8,128)(2,1)S(1)}, u32[]{:S(2)}, u32[]{:S(2)}) collective-permute-start(bf16[384,768]{1,0:T(8,128)(2,1)S(1)} %constant_dynamic-slice_fusion.5), channel_id=1, source_target_pairs={{0,16},{16,0},{1,17},{17,1},{2,18},{18,2},{3,19},{19,3},{4,20},{20... | collective-permute-start | bytes 1769480 | tf_op jit(solution)/shard_map/ppermute | solution.py:42
  82.6 25.6 %collective-permute-start.58 = (bf16[768,384]{1,0:T(8,128)(2,1)S(1)}, bf16[768,384]{1,0:T(8,128)(2,1)S(1)}, u32[]{:S(2)}, u32[]{:S(2)}) collective-permute-start(bf16[768,384]{1,0:T(8,128)(2,1)S(1)} %constant_dynamic-slice_fusion.4), channel_id=1, source_target_pairs={{0,16},{16,0},{1,17},{17,1},{2,18},{18,2},{3,19},{19,3},{4,20},{20... | collective-permute-start | bytes 1769480 | tf_op jit(solution)/shard_map/ppermute | solution.py:42
  83.3 26.0 %collective-permute-start.20 = (bf16[128,768]{1,0:T(8,128)(2,1)S(1)}, bf16[128,768]{1,0:T(8,128)(2,1)S(1)}, u32[]{:S(2)}, u32[]{:S(2)}) collective-permute-start(bf16[128,768]{1,0:T(8,128)(2,1)S(1)} %add_convert_fusion.5), channel_id=1, source_target_pairs={{0,2},{1,3},{2,0},{3,1},{4,6},{5,7},{6,4},{7,5},{8,10},{9,11},{10,... | collective-permute-start | bytes 589832 | tf_op jit(solution)/shard_map/ppermute | solution.py:17
  83.4 26.0 %collective-permute-start.23 = (bf16[128,768]{1,0:T(8,128)(2,1)S(1)}, bf16[128,768]{1,0:T(8,128)(2,1)S(1)}, u32[]{:S(2)}, u32[]{:S(2)}) collective-permute-start(bf16[128,768]{1,0:T(8,128)(2,1)S(1)} %add_convert_fusion.4), channel_id=1, source_target_pairs={{0,2},{1,3},{2,0},{3,1},{4,6},{5,7},{6,4},{7,5},{8,10},{9,11},{10,... | collective-permute-start | bytes 589832 | tf_op jit(solution)/shard_map/ppermute | solution.py:17
  99.5 39.8 %collective-permute-start.54 = (bf16[96,768]{1,0:T(8,128)(2,1)}, bf16[96,768]{1,0:T(8,128)(2,1)}, u32[]{:S(2)}, u32[]{:S(2)}) collective-permute-start(bf16[96,768]{1,0:T(8,128)(2,1)} %get-tuple-element.106), channel_id=1, source_target_pairs={{0,12},{1,13},{2,14},{3,15},{4,8},{5,9},{6,10},{7,11},{8,4},{9,5},... | collective-permute-start | bytes 442376 | tf_op jit(solution)/shard_map/ppermute | solution.py:17
  103.1 36.9 %collective-permute-start.53 = (bf16[96,768]{1,0:T(8,128)(2,1)}, bf16[96,768]{1,0:T(8,128)(2,1)}, u32[]{:S(2)}, u32[]{:S(2)}) collective-permute-start(bf16[96,768]{1,0:T(8,128)(2,1)} %get-tuple-element.107), channel_id=1, source_target_pairs={{0,8},{1,9},{2,10},{3,11},{4,12},{5,13},{6,14},{7,15},{8,0},{9,1},... | collective-permute-start | bytes 442376 | tf_op jit(solution)/shard_map/ppermute | solution.py:17
  110.3 7.2 %collective-permute-start.26 = (bf16[128,192]{1,0:T(8,128)(2,1)S(1)}, bf16[128,192]{1,0:T(8,128)(2,1)S(1)}, u32[]{:S(2)}, u32[]{:S(2)}) collective-permute-start(bf16[128,192]{1,0:T(8,128)(2,1)S(1)} %get-tuple-element.44), channel_id=1, source_target_pairs={{0,6},{1,7},{2,4},{3,5},{4,2},{5,3},{6,0},{7,1},{8,14},{9,15},{10,... | collective-permute-start | bytes 147464 | tf_op jit(solution)/shard_map/ppermute | solution.py:17
  111.7 7.4 %collective-permute-start.25 = (bf16[128,192]{1,0:T(8,128)(2,1)S(1)}, bf16[128,192]{1,0:T(8,128)(2,1)S(1)}, u32[]{:S(2)}, u32[]{:S(2)}) collective-permute-start(bf16[128,192]{1,0:T(8,128)(2,1)S(1)} %get-tuple-element.43), channel_id=1, source_target_pairs={{0,4},{1,5},{2,6},{3,7},{4,0},{5,1},{6,2},{7,3},{8,12},{9,13},{10,... | collective-permute-start | bytes 147464 | tf_op jit(solution)/shard_map/ppermute | solution.py:17
  112.0 9.5 %collective-permute-start.24 = (bf16[128,192]{1,0:T(8,128)(2,1)S(1)}, bf16[128,192]{1,0:T(8,128)(2,1)S(1)}, u32[]{:S(2)}, u32[]{:S(2)}) collective-permute-start(bf16[128,192]{1,0:T(8,128)(2,1)S(1)} %get-tuple-element.42), channel_id=1, source_target_pairs={{0,2},{1,3},{2,0},{3,1},{4,6},{5,7},{6,4},{7,5},{8,10},{9,11},{10,... | collective-permute-start | bytes 147464 | tf_op jit(solution)/shard_map/ppermute | solution.py:17
  117.5 22.6 %collective-permute-start.52 = (bf16[96,768]{1,0:T(8,128)(2,1)}, bf16[96,768]{1,0:T(8,128)(2,1)}, u32[]{:S(2)}, u32[]{:S(2)}) collective-permute-start(bf16[96,768]{1,0:T(8,128)(2,1)} %get-tuple-element.105), channel_id=1, source_target_pairs={{0,4},{1,5},{2,6},{3,7},{4,0},{5,1},{6,2},{7,3},{8,12},{9,13},{10,... | collective-permute-start | bytes 442376 | tf_op jit(solution)/shard_map/ppermute | solution.py:17
  119.1 22.7 %collective-permute-start.61 = (bf16[192,384]{1,0:T(8,128)(2,1)}, bf16[192,384]{1,0:T(8,128)(2,1)}, u32[]{:S(2)}, u32[]{:S(2)}) collective-permute-start(bf16[192,384]{1,0:T(8,128)(2,1)} %get-tuple-element.103), channel_id=1, source_target_pairs={{0,12},{1,13},{2,14},{3,15},{4,8},{5,9},{6,10},{7,11},{8,4},{9,5},... | collective-permute-start | bytes 442376 | tf_op jit(solution)/shard_map/ppermute | solution.py:17
  121.6 13.3 %collective-permute-start.21 = (bf16[64,768]{1,0:T(8,128)(2,1)}, bf16[64,768]{1,0:T(8,128)(2,1)}, u32[]{:S(2)}, u32[]{:S(2)}) collective-permute-start(bf16[64,768]{1,0:T(8,128)(2,1)} %slice.313), channel_id=1, source_target_pairs={{0,8},{1,9},{2,10},{3,11},{4,12},{5,13},{6,14},{7,15},{8,0},{9,1},... | collective-permute-start | bytes 294920 | tf_op jit(solution)/shard_map/ppermute | solution.py:17
  134.9 8.1 %collective-permute-start.60 = (bf16[192,384]{1,0:T(8,128)(2,1)}, bf16[192,384]{1,0:T(8,128)(2,1)S(1)}, u32[]{:S(2)}, u32[]{:S(2)}) collective-permute-start(bf16[192,384]{1,0:T(8,128)(2,1)} %get-tuple-element.104), channel_id=1, source_target_pairs={{0,8},{1,9},{2,10},{3,11},{4,12},{5,13},{6,14},{7,15},{8,0},{9,1},... | collective-permute-start | bytes 442376 | tf_op jit(solution)/shard_map/ppermute | solution.py:17
  139.3 5.4 %collective-permute-start.59 = (bf16[192,384]{1,0:T(8,128)(2,1)}, bf16[192,384]{1,0:T(8,128)(2,1)S(1)}, u32[]{:S(2)}, u32[]{:S(2)}) collective-permute-start(bf16[192,384]{1,0:T(8,128)(2,1)} %get-tuple-element.102), channel_id=1, source_target_pairs={{0,4},{1,5},{2,6},{3,7},{4,0},{5,1},{6,2},{7,3},{8,12},{9,13},{10,... | collective-permute-start | bytes 442376 | tf_op jit(solution)/shard_map/ppermute | solution.py:17
  140.0 38.7 %collective-permute-start.44 = (bf16[768,384]{0,1:T(8,128)(2,1)S(1)}, bf16[768,384]{0,1:T(8,128)(2,1)S(1)}, u32[]{:S(2)}, u32[]{:S(2)}) collective-permute-start(bf16[768,384]{0,1:T(8,128)(2,1)S(1)} %copy-done.22), channel_id=1, source_target_pairs={{0,1},{1,0},{2,3},{3,2},{4,5},{5,4},{6,7},{7,6},{8,9},{9,8},{10,11... | collective-permute-start | bytes 1769480 | tf_op jit(solution)/shard_map/ppermute | solution.py:17
  140.1 31.7 %collective-permute-start.27 = (bf16[512,384]{1,0:T(8,128)(2,1)S(1)}, bf16[512,384]{1,0:T(8,128)(2,1)S(1)}, u32[]{:S(2)}, u32[]{:S(2)}) collective-permute-start(bf16[512,384]{1,0:T(8,128)(2,1)S(1)} %copy-done.1), channel_id=1, source_target_pairs={{0,1},{1,0},{2,3},{3,2},{4,5},{5,4},{6,7},{7,6},{8,9},{9,8},{10,11... | collective-permute-start | bytes 1179656 | tf_op jit(solution)/shard_map/ppermute | solution.py:17
  141.8 8.7 %collective-permute-start.55 = (bf16[96,768]{1,0:T(8,128)(2,1)S(1)}, bf16[96,768]{1,0:T(8,128)(2,1)S(1)}, u32[]{:S(2)}, u32[]{:S(2)}) collective-permute-start(bf16[96,768]{1,0:T(8,128)(2,1)S(1)} %add_convert_fusion.7), channel_id=1, source_target_pairs={{0,12},{1,13},{2,14},{3,15},{4,8},{5,9},{6,10},{7,11},{8,4},{9,5},... | collective-permute-start | bytes 442376 | tf_op jit(solution)/shard_map/ppermute | solution.py:17
  142.9 19.0 %collective-permute-start.56 = (bf16[96,768]{1,0:T(8,128)(2,1)S(1)}, bf16[96,768]{1,0:T(8,128)(2,1)S(1)}, u32[]{:S(2)}, u32[]{:S(2)}) collective-permute-start(bf16[96,768]{1,0:T(8,128)(2,1)S(1)} %add_convert_fusion.7), channel_id=1, source_target_pairs={{0,8},{1,9},{2,10},{3,11},{4,12},{5,13},{6,14},{7,15},{8,0},{9,1},... | collective-permute-start | bytes 442376 | tf_op jit(solution)/shard_map/ppermute | solution.py:17
  144.7 17.3 %collective-permute-start.57 = (bf16[96,768]{1,0:T(8,128)(2,1)S(1)}, bf16[96,768]{1,0:T(8,128)(2,1)S(1)}, u32[]{:S(2)}, u32[]{:S(2)}) collective-permute-start(bf16[96,768]{1,0:T(8,128)(2,1)S(1)} %add_convert_fusion.7), channel_id=1, source_target_pairs={{0,4},{1,5},{2,6},{3,7},{4,0},{5,1},{6,2},{7,3},{8,12},{9,13},{10,... | collective-permute-start | bytes 442376 | tf_op jit(solution)/shard_map/ppermute | solution.py:17
  150.5 14.4 %collective-permute-start.62 = (bf16[192,384]{1,0:T(8,128)(2,1)S(1)}, bf16[192,384]{1,0:T(8,128)(2,1)S(1)}, u32[]{:S(2)}, u32[]{:S(2)}) collective-permute-start(bf16[192,384]{1,0:T(8,128)(2,1)S(1)} %add_convert_fusion.6), channel_id=1, source_target_pairs={{0,12},{1,13},{2,14},{3,15},{4,8},{5,9},{6,10},{7,11},{8,4},{9,5},... | collective-permute-start | bytes 442376 | tf_op jit(solution)/shard_map/ppermute | solution.py:17
  162.0 8.6 %collective-permute-start.63 = (bf16[192,384]{1,0:T(8,128)(2,1)S(1)}, bf16[192,384]{1,0:T(8,128)(2,1)S(1)}, u32[]{:S(2)}, u32[]{:S(2)}) collective-permute-start(bf16[192,384]{1,0:T(8,128)(2,1)S(1)} %add_convert_fusion.6), channel_id=1, source_target_pairs={{0,8},{1,9},{2,10},{3,11},{4,12},{5,13},{6,14},{7,15},{8,0},{9,1},... | collective-permute-start | bytes 442376 | tf_op jit(solution)/shard_map/ppermute | solution.py:17
  162.0 8.6 %collective-permute-start.64 = (bf16[192,384]{1,0:T(8,128)(2,1)S(1)}, bf16[192,384]{1,0:T(8,128)(2,1)S(1)}, u32[]{:S(2)}, u32[]{:S(2)}) collective-permute-start(bf16[192,384]{1,0:T(8,128)(2,1)S(1)} %add_convert_fusion.6), channel_id=1, source_target_pairs={{0,4},{1,5},{2,6},{3,7},{4,0},{5,1},{6,2},{7,3},{8,12},{9,13},{10,... | collective-permute-start | bytes 442376 | tf_op jit(solution)/shard_map/ppermute | solution.py:17
  173.3 7.0 %collective-permute-start.28 = (bf16[128,768]{1,0:T(8,128)(2,1)S(1)}, bf16[128,768]{1,0:T(8,128)(2,1)S(1)}, u32[]{:S(2)}, u32[]{:S(2)}) collective-permute-start(bf16[128,768]{1,0:T(8,128)(2,1)S(1)} %get-tuple-element.124), channel_id=1, source_target_pairs={{0,2},{1,3},{2,0},{3,1},{4,6},{5,7},{6,4},{7,5},{8,10},{9,11},{10,... | collective-permute-start | bytes 589832 | tf_op jit(solution)/shard_map/ppermute | solution.py:17
  173.7 7.8 %collective-permute-start.29 = (bf16[128,768]{1,0:T(8,128)(2,1)S(1)}, bf16[128,768]{1,0:T(8,128)(2,1)S(1)}, u32[]{:S(2)}, u32[]{:S(2)}) collective-permute-start(bf16[128,768]{1,0:T(8,128)(2,1)S(1)} %get-tuple-element.123), channel_id=1, source_target_pairs={{0,4},{1,5},{2,6},{3,7},{4,0},{5,1},{6,2},{7,3},{8,12},{9,13},{10,... | collective-permute-start | bytes 589832 | tf_op jit(solution)/shard_map/ppermute | solution.py:17
  173.7 11.1 %collective-permute-start.30 = (bf16[128,768]{1,0:T(8,128)(2,1)S(1)}, bf16[128,768]{1,0:T(8,128)(2,1)S(1)}, u32[]{:S(2)}, u32[]{:S(2)}) collective-permute-start(bf16[128,768]{1,0:T(8,128)(2,1)S(1)} %get-tuple-element.122), channel_id=1, source_target_pairs={{0,6},{1,7},{2,4},{3,5},{4,2},{5,3},{6,0},{7,1},{8,14},{9,15},{10,... | collective-permute-start | bytes 589832 | tf_op jit(solution)/shard_map/ppermute | solution.py:17
  186.6 11.4 %collective-permute-start.45 = (bf16[768,192]{0,1:T(8,128)(2,1)S(1)}, bf16[768,192]{0,1:T(8,128)(2,1)S(1)}, u32[]{:S(2)}, u32[]{:S(2)}) collective-permute-start(bf16[768,192]{0,1:T(8,128)(2,1)S(1)} %dynamic-slice_convert_fusion.2), channel_id=1, source_target_pairs={{0,2},{1,3},{2,0},{3,1},{4,6},{5,7},{6,4},{7,5},{8,10},{9,11},{10,... | collective-permute-start | bytes 884744 | tf_op jit(solution)/shard_map/ppermute | solution.py:17
  187.1 10.6 %collective-permute-start.33 = (f32[152,128]{1,0:T(8,128)S(1)}, f32[152,128]{1,0:T(8,128)S(1)}, u32[]{:S(2)}, u32[]{:S(2)}) collective-permute-start(f32[152,128]{1,0:T(8,128)S(1)} %bitcast_add_fusion), channel_id=1, source_target_pairs={{0,2},{1,3},{2,0},{3,1},{4,6},{5,7},{6,4},{7,5},{8,10},{9,11},{10,... | collective-permute-start | bytes 233480 | tf_op jit(solution)/shard_map/ppermute | solution.py:17
  190.1 15.1 %collective-permute-start.37 = (bf16[768,288]{0,1:T(8,128)(2,1)S(1)}, bf16[768,288]{0,1:T(8,128)(2,1)S(1)}, u32[]{:S(2)}, u32[]{:S(2)}) collective-permute-start(bf16[768,288]{0,1:T(8,128)(2,1)S(1)} %dynamic-slice_convert_fusion.1), channel_id=1, source_target_pairs={{0,1},{1,0},{2,3},{3,2},{4,5},{5,4},{6,7},{7,6},{8,9},{9,8},{10,11... | collective-permute-start | bytes 1327112 | tf_op jit(solution)/shard_map/ppermute | solution.py:17
  197.7 4.5 %collective-permute-start.34 = (f32[152,128]{1,0:T(8,128)S(1)}, f32[152,128]{1,0:T(8,128)S(1)}, u32[]{:S(2)}, u32[]{:S(2)}) collective-permute-start(f32[152,128]{1,0:T(8,128)S(1)} %fusion.51), channel_id=1, source_target_pairs={{0,4},{1,5},{2,6},{3,7},{4,0},{5,1},{6,2},{7,3},{8,12},{9,13},{10,... | collective-permute-start | bytes 233480 | tf_op jit(solution)/shard_map/ppermute | solution.py:17
  198.1 5.2 %collective-permute-start.46 = (bf16[384,192]{0,1:T(8,128)(2,1)S(1)}, bf16[384,192]{0,1:T(8,128)(2,1)S(1)}, u32[]{:S(2)}, u32[]{:S(2)}) collective-permute-start(bf16[384,192]{0,1:T(8,128)(2,1)S(1)} %dynamic-slice_convert_fusion.10), channel_id=1, source_target_pairs={{0,16},{16,0},{1,17},{17,1},{2,18},{18,2},{3,19},{19,3},{4,20},{20... | collective-permute-start | bytes 442376 | tf_op jit(solution)/shard_map/ppermute | solution.py:42
  199.8 39.7 %collective-permute-start.31 = (bf16[64,768]{1,0:T(8,128)(2,1)S(1)}, bf16[64,768]{1,0:T(8,128)(2,1)S(1)}, u32[]{:S(2)}, u32[]{:S(2)}) collective-permute-start(bf16[64,768]{1,0:T(8,128)(2,1)S(1)} %slice.312), channel_id=1, source_target_pairs={{0,8},{1,9},{2,10},{3,11},{4,12},{5,13},{6,14},{7,15},{8,0},{9,1},... | collective-permute-start | bytes 294920 | tf_op jit(solution)/shard_map/ppermute | solution.py:17
  202.2 37.4 %collective-permute-start.35 = (f32[152,128]{1,0:T(8,128)S(1)}, f32[152,128]{1,0:T(8,128)S(1)}, u32[]{:S(2)}, u32[]{:S(2)}) collective-permute-start(f32[152,128]{1,0:T(8,128)S(1)} %add.330), channel_id=1, source_target_pairs={{0,8},{1,9},{2,10},{3,11},{4,12},{5,13},{6,14},{7,15},{8,0},{9,1},... | collective-permute-start | bytes 233480 | tf_op jit(solution)/shard_map/ppermute | solution.py:17
  203.4 8.8 %collective-permute-start.47 = (bf16[384,192]{0,1:T(8,128)(2,1)S(1)}, bf16[384,192]{0,1:T(8,128)(2,1)S(1)}, u32[]{:S(2)}, u32[]{:S(2)}) collective-permute-start(bf16[384,192]{0,1:T(8,128)(2,1)S(1)} %add_convert_fusion.10), channel_id=1, source_target_pairs={{0,4},{1,5},{2,6},{3,7},{4,0},{5,1},{6,2},{7,3},{8,12},{9,13},{10,... | collective-permute-start | bytes 442376 | tf_op jit(solution)/shard_map/ppermute | solution.py:17
  205.3 7.0 %collective-permute-start.38 = (bf16[384,288]{0,1:T(8,128)(2,1)S(1)}, bf16[384,288]{0,1:T(8,128)(2,1)S(1)}, u32[]{:S(2)}, u32[]{:S(2)}) collective-permute-start(bf16[384,288]{0,1:T(8,128)(2,1)S(1)} %dynamic-slice_convert_fusion.3), channel_id=1, source_target_pairs={{0,16},{16,0},{1,17},{17,1},{2,18},{18,2},{3,19},{19,3},{4,20},{20... | collective-permute-start | bytes 663560 | tf_op jit(solution)/shard_map/ppermute | solution.py:42
  212.2 11.1 %collective-permute-start.48 = (bf16[384,192]{0,1:T(8,128)(2,1)S(1)}, bf16[384,192]{0,1:T(8,128)(2,1)S(1)}, u32[]{:S(2)}, u32[]{:S(2)}) collective-permute-start(bf16[384,192]{0,1:T(8,128)(2,1)S(1)} %add_convert_fusion.9), channel_id=1, source_target_pairs={{0,8},{1,9},{2,10},{3,11},{4,12},{5,13},{6,14},{7,15},{8,0},{9,1},... | collective-permute-start | bytes 442376 | tf_op jit(solution)/shard_map/ppermute | solution.py:17
  212.4 14.0 %collective-permute-start.39 = (bf16[384,288]{0,1:T(8,128)(2,1)S(1)}, bf16[384,288]{0,1:T(8,128)(2,1)S(1)}, u32[]{:S(2)}, u32[]{:S(2)}) collective-permute-start(bf16[384,288]{0,1:T(8,128)(2,1)S(1)} %add_convert_fusion.3), channel_id=1, source_target_pairs={{0,8},{1,9},{2,10},{3,11},{4,12},{5,13},{6,14},{7,15},{8,0},{9,1},... | collective-permute-start | bytes 663560 | tf_op jit(solution)/shard_map/ppermute | solution.py:17
  223.3 7.6 %collective-permute-start.49 = (bf16[384,192]{0,1:T(8,128)(2,1)S(1)}, bf16[384,192]{0,1:T(8,128)(2,1)S(1)}, u32[]{:S(2)}, u32[]{:S(2)}) collective-permute-start(bf16[384,192]{0,1:T(8,128)(2,1)S(1)} %add_convert_fusion.8), channel_id=1, source_target_pairs={{0,2},{1,3},{2,0},{3,1},{4,6},{5,7},{6,4},{7,5},{8,10},{9,11},{10,... | collective-permute-start | bytes 442376 | tf_op jit(solution)/shard_map/ppermute | solution.py:17
  226.4 9.2 %collective-permute-start.42 = (bf16[384,288]{0,1:T(8,128)(2,1)S(1)}, bf16[384,288]{0,1:T(8,128)(2,1)S(1)}, u32[]{:S(2)}, u32[]{:S(2)}) collective-permute-start(bf16[384,288]{0,1:T(8,128)(2,1)S(1)} %add_convert_fusion.2), channel_id=1, source_target_pairs={{0,6},{1,7},{2,4},{3,5},{4,2},{5,3},{6,0},{7,1},{8,14},{9,15},{10,... | collective-permute-start | bytes 663560 | tf_op jit(solution)/shard_map/ppermute | solution.py:17
  226.5 10.3 %collective-permute-start.41 = (bf16[384,288]{0,1:T(8,128)(2,1)S(1)}, bf16[384,288]{0,1:T(8,128)(2,1)S(1)}, u32[]{:S(2)}, u32[]{:S(2)}) collective-permute-start(bf16[384,288]{0,1:T(8,128)(2,1)S(1)} %add_convert_fusion.2), channel_id=1, source_target_pairs={{0,4},{1,5},{2,6},{3,7},{4,0},{5,1},{6,2},{7,3},{8,12},{9,13},{10,... | collective-permute-start | bytes 663560 | tf_op jit(solution)/shard_map/ppermute | solution.py:17
  230.9 7.1 %collective-permute-start.40 = (bf16[384,288]{0,1:T(8,128)(2,1)S(1)}, bf16[384,288]{0,1:T(8,128)(2,1)S(1)}, u32[]{:S(2)}, u32[]{:S(2)}) collective-permute-start(bf16[384,288]{0,1:T(8,128)(2,1)S(1)} %add_convert_fusion.2), channel_id=1, source_target_pairs={{0,2},{1,3},{2,0},{3,1},{4,6},{5,7},{6,4},{7,5},{8,10},{9,11},{10,... | collective-permute-start | bytes 663560 | tf_op jit(solution)/shard_map/ppermute | solution.py:17
  238.2 12.0 %collective-permute-start.43 = (bf16[4,384,288]{1,2,0:T(8,128)(2,1)S(1)}, bf16[4,384,288]{1,2,0:T(8,128)(2,1)S(1)}, u32[]{:S(2)}, u32[]{:S(2)}) collective-permute-start(bf16[4,384,288]{1,2,0:T(8,128)(2,1)S(1)} %pad_maximum_fusion.7), channel_id=1, source_target_pairs={{0,1},{1,0},{2,3},{3,2},{4,5},{5,4},{6,7},{7,6},{8,9},{9,8},{10,11... | collective-permute-start | bytes 2654216 | tf_op jit(solution)/shard_map/ppermute | solution.py:17
  239.0 8.6 %collective-permute-start.50 = (bf16[384,384]{0,1:T(8,128)(2,1)}, bf16[384,384]{0,1:T(8,128)(2,1)}, u32[]{:S(2)}, u32[]{:S(2)}) collective-permute-start(bf16[384,384]{0,1:T(8,128)(2,1)} %pad_maximum_fusion.17), channel_id=1, source_target_pairs={{0,1},{1,0},{2,3},{3,2},{4,5},{5,4},{6,7},{7,6},{8,9},{9,8},{10,11... | collective-permute-start | bytes 884744 | tf_op jit(solution)/shard_map/ppermute | solution.py:17
  239.6 5.7 %collective-permute-start.36 = (f32[152,128]{1,0:T(8,128)S(1)}, f32[152,128]{1,0:T(8,128)S(1)}, u32[]{:S(2)}, u32[]{:S(2)}) collective-permute-start(f32[152,128]{1,0:T(8,128)S(1)} %add.331), channel_id=1, source_target_pairs={{0,16},{16,0},{1,17},{17,1},{2,18},{18,2},{3,19},{19,3},{4,20},{20... | collective-permute-start | bytes 233480 | tf_op jit(solution)/shard_map/ppermute | solution.py:49
  (39 other events, 220.5 us)

commit v2 on v1

v2 whole, which is shorter than its diff:
```python
import math

import jax
import jax.numpy as jnp
from jax import lax
from jax.experimental import pallas as pl
from jax.experimental.pallas import tpu as pltpu
from jax.sharding import PartitionSpec as P

EPS = 1e-06
LOW = jnp.bfloat16
FULL = jnp.float32
LANES = 128
CORE, ROW, NEAR, FAR = 1, 2, 4, 8


def hop(value, bits):
    count = lax.axis_size("seq") * lax.axis_size("tp")
    return lax.ppermute(value, ("seq", "tp"), [(i, i ^ bits) for i in range(count)])


def swap_dp(value):
    return lax.ppermute(value, "dp", [(0, 1), (1, 0)])


def pair_dp(value, axis):
    if lax.axis_size("dp") == 2:
        return value, swap_dp(value), lax.axis_index("dp")
    whole = lax.all_gather(value, "dp", axis=axis, tiled=True)
    low, high = jnp.split(whole, 2, axis=axis)
    return low, high, jnp.int32(0)


def after(value, *events):
    return lax.optimization_barrier((value, *events))[0]


def piece(value, index, size, axis):
    return lax.dynamic_slice_in_dim(value, index * size, size, axis)


def scatter_dp(sent, kept, axis):
    if lax.axis_size("dp") == 2:
        return kept, swap_dp(sent)
    whole = jnp.concatenate([kept, sent], axis=axis)
    return lax.psum_scatter(whole, "dp", scatter_dimension=axis, tiled=True), None


def canon(blocks, index, axis):
    odd = (index & 1) == 1
    upper = (index & 2) == 2
    b = [
        jnp.where(odd, blocks[k ^ 1], blocks[k])
        for k in range(4)
    ]
    return jnp.concatenate([jnp.where(upper, b[k ^ 2], b[k]) for k in range(4)], axis=axis)


def dot_nn(a, b):
    return lax.dot_general(a, b, (((1,), (0,)), ((), ())), preferred_element_type=FULL)


def dot_nt(a, b):
    return lax.dot_general(a, b, (((1,), (1,)), ((), ())), preferred_element_type=FULL)


def dot_tn(a, b):
    return lax.dot_general(a, b, (((0,), (0,)), ((), ())), preferred_element_type=FULL)


def in_order():
    before = []

    def call(kernel, outs, scratch=(), smem=0, extra=2, wait=()):
        def run(*args):
            held = sum(a.size * jnp.dtype(a.dtype).itemsize for a in (*args, *outs))
            held += sum(math.prod(a.shape) * jnp.dtype(a.dtype).itemsize for a in scratch)
            used = len(args)
            events = (*before, *wait)

            def body(*refs):
                kernel(*refs[:used], *refs[used + len(events) :])

            results = pl.pallas_call(
                body,
                name=kernel.__qualname__.split(".")[0],
                out_shape=outs,
                in_specs=[pl.BlockSpec(memory_space=pltpu.SMEM)] * smem
                + [pl.BlockSpec(memory_space=pltpu.VMEM)] * (used - smem)
                + [pl.BlockSpec(memory_space=pl.ANY)] * len(events),
                out_specs=[pl.BlockSpec(memory_space=pltpu.VMEM)] * len(outs),
                scratch_shapes=scratch,
                compiler_params=pltpu.CompilerParams(vmem_limit_bytes=held + extra * 2**20),
                cost_estimate=pl.CostEstimate(flops=0, bytes_accessed=0, transcendentals=0),
            )(*args, *events)
            before[:] = [min(results, key=lambda r: r.size)]
            return results

        return run

    return call


def shape(dims, kind):
    return jax.ShapeDtypeStruct(dims, kind)


def normal(values):
    center = values - jnp.mean(values, axis=-1, keepdims=True)
    scale = lax.rsqrt(jnp.mean(center * center, axis=-1, keepdims=True) + EPS)
    return center * scale, scale


def pick_kernel(ids, array, mine, other):
    mine[...] = array[ids[3]]
    other[...] = array[1 - ids[3]]


def stack_kernel(*refs):
    out, start = refs[-1], 0
    for ref in refs[:-1]:
        out[start : start + ref.shape[0], :] = ref[...]
        start += ref.shape[0]


def pack_kernel(share, heads):
    def kernel(ids, weight, top, bottom):
        width = weight.shape[1] // 3
        head = share // heads
        rows = top.shape[0]
        for g in range(width // share):

            @pl.when(ids[1] == g)
            def _():
                for out, start in ((top, 0), (bottom, rows)):
                    here = slice(start, start + rows)

                    def move(at_col, first):
                        out[:, at_col : at_col + head] = weight[here, first : first + head]

                    for h in range(heads):
                        first = g * share + h * head
                        move(2 * h * head, width + first)
                        move((2 * h + 1) * head, 2 * width + first)
                        move(2 * share + h * head, first)

    return kernel


def rows_kernel(ids, array, out):
    out[...] = array[at(ids[2], out.shape[0]), :]


def fill_rows(ids, out, mine, other, other_two):
    half = mine.shape[0]
    out[at(ids[0], half), :] = mine[...]
    if other.shape[0] == half:
        out[at(1 - ids[0], half), :] = other[...]
        return
    size = half // 2
    out[at((1 - ids[0]) * 2 + ids[2], size), :] = other[...]
    out[at((1 - ids[0]) * 2 + 1 - ids[2], size), :] = other_two[...]


def norm_kernel(ids, mine, other, small, small_other, out, params):
    width = small.shape[1]
    params[:, lanes(ids[0], width)] = small[...].astype(FULL)
    params[:, lanes(1 - ids[0], width)] = small_other[...].astype(FULL)
    half = mine.shape[0]
    for start, part in ((0, mine), (half, other)):
        hat, _ = normal(part[...])
        out[start : start + half, :] = (hat * params[0:1, :] + params[1:2, :]).astype(LOW)


def grid_row(ids, n):
    k, u, i = n // 4, (n // 2) % 2, n % 2
    chunk = ((ids[6] ^ (k >> 1)) ^ (2 * u)) * 4 + ((ids[5] ^ (k & 1)) * 2) + ids[2]
    return chunk * 2 + i


def table_kernel(ids, mine, other, table, spot_one, spot_two):
    part, reach = mine.shape[1:]
    rows = lax.broadcasted_iota(jnp.int32, (reach, LANES), 0)
    cols = lax.broadcasted_iota(jnp.int32, (reach, LANES), 1)
    turn = jnp.where(rows == reach - 1 - cols, 1.0, 0.0).astype(LOW)
    table[...] = jnp.zeros_like(table)
    for k in range(2):
        spot = slice(k * LANES, (k + 1) * LANES)
        table[at(ids[0], part), spot] = dot_nn(mine[k], turn).astype(LOW)
        table[at(1 - ids[0], part), spot] = dot_nn(other[k], turn).astype(LOW)
    side = (reach + 1) // 2
    lane = lane_of(side)
    col = lax.broadcasted_iota(jnp.int32, (side, LANES), 0)
    total = spot_one.shape[0] // side
    for n in range(total):
        row = grid_row(ids, n % (total // 2))
        if n >= total // 2:
            row = row ^ 2
        here = slice(n * side, (n + 1) * side)
        target = jnp.where(lane < 96, row + 64, col + 96)
        one = jnp.where(lane == target, 1.0, 0.0)
        spot_one[here, :] = one.astype(LOW)
        ones = jnp.where((lane >= 64) & (lane < 67), 1.0, 0.0)
        spot_two[here, :] = (pltpu.roll(one, 64, 1) + ones).astype(LOW)


def lane_of(rows):
    return lax.broadcasted_iota(jnp.int32, (rows, LANES), 1)


def pieces_at(lane, first, value, rest):
    high = value.astype(LOW).astype(FULL)
    left = value - high
    mid = left.astype(LOW).astype(FULL)
    tail = left - mid
    out = jnp.where(lane == first, high, rest)
    out = jnp.where(lane == first + 1, mid, out)
    return jnp.where(lane == first + 2, tail, out)


def key_tiles(h, kva, kvb, spot_one, spot_two, keys):
    half = kva.shape[0]
    lane = lane_of(half)
    for start, part in ((0, kva), (half, kvb)):
        tile = part[:, h * LANES : (h + 1) * LANES].astype(FULL)
        spots = spot_one[start : start + half, :].astype(FULL)
        keys[start : start + half, :LANES] = jnp.where(lane < 64, tile, spots).astype(LOW)
        keys[start : start + half, LANES:] = spot_two[start : start + half, :]


def attend_kernel(
    ids, query, kva, kvb, spot_one, spot_two, table, out, a0, a1, a2, a3, left, keys, along
):
    rows = query.shape[0]
    heads = left.shape[0]
    lane32 = lane_of(32)
    block = 128
    lane = lane_of(block)
    for h in range(heads):
        key_tiles(h, kva, kvb, spot_one, spot_two, keys)
        tile = query[:, (h // 2) * LANES : (h // 2 + 1) * LANES].astype(FULL)
        if h % 2:
            tile = pltpu.roll(tile, 64, 1)
        along[...] = dot_nn(tile.astype(LOW), table[...])
        for g in range(rows // 32):
            here = slice(g * 32, (g + 1) * 32)
            term_h = pltpu.roll(along[here, :LANES], 33 + grid_row(ids, g), 1)
            term_w = pltpu.roll(along[here, LANES:], 65, 1, stride=1, stride_axis=0)
            one = jnp.where(
                lane32 < 64, tile[here, :] * 0.125, jnp.where(lane32 < 96, term_h, term_w)
            )
            high = one.astype(LOW)
            rest = pltpu.roll(one - high.astype(FULL), 64, 1)
            left[h, here, :LANES] = high
            left[h, here, LANES:] = rest.astype(LOW)
        for q in range(rows // block):
            here = slice(q * block, (q + 1) * block)
            scores = dot_nt(left[h, here, :], keys[...])
            top = jnp.max(scores, axis=1, keepdims=True)
            expo = jnp.exp(scores - top)
            total = jnp.sum(expo, axis=1, keepdims=True)
            low = expo.astype(LOW)
            half = kva.shape[0]
            cols = slice(h * LANES, (h + 1) * LANES)
            result = dot_nn(low[:, :half], kva[:, cols]) + dot_nn(low[:, half:], kvb[:, cols])
            result = result / total
            if h % 2 == 0:
                result = pltpu.roll(result, 64, 1)
            spot = slice((h // 2) * LANES, (h // 2 + 1) * LANES)
            if h % 2:
                result = jnp.where(lane < 64, out[here, spot], result)
            else:
                result = jnp.where(lane < 64, result, 0.0)
            out[here, spot] = result
            low_out = (a0, a1, a2, a3)[q]
            if h % 2:
                low_out[:, spot] = result.astype(LOW)
            elif h == heads - 1:
                low_out[:, h * 64 :] = result[:, :64].astype(LOW)
            rest = left[h, here, LANES:].astype(FULL)
            left[h, here, LANES:] = pieces_at(lane, 64, -(top + jnp.log(total)), rest).astype(LOW)


def back_kernel(h):
    def kernel(
        ids, left, kva, kvb, spot_one, spot_two, table, g0, g1, g2, g3, value,
        dquery, dkv_mine, dkv_other, dtable,
        keys, vals, gright, qright, along, grad,
    ):
        rows = left.shape[1]
        half = kva.shape[0]
        lane = lane_of(rows)
        lane32 = lane_of(32)
        row = lax.broadcasted_iota(jnp.int32, (rows, LANES), 0)
        chunk = 256
        key_tiles(h, kva, kvb, spot_one, spot_two, keys)
        cols = slice(h * LANES, (h + 1) * LANES)
        spot = slice((h // 2) * LANES, (h // 2 + 1) * LANES)
        for k, part in enumerate((g0, g1, g2, g3)):
            size, width = part.shape
            last = min(width, spot.stop)
            grad[k * size : (k + 1) * size, : last - spot.start] = part[:, spot.start : last].astype(FULL)
        vals[:half, :LANES] = kva[:, cols]
        vals[half:, :LANES] = kvb[:, cols]
        vals[:, LANES:] = spot_two[...]
        gtile = grad[...]
        otile = value[:, spot]
        if h % 2 == 0:
            gtile = pltpu.roll(gtile, 64, 1)
            otile = pltpu.roll(otile, 64, 1)
        gtile = jnp.where(lane >= 64, gtile, 0.0)
        inner = jnp.sum(gtile * otile, axis=1, keepdims=True)
        gright[:, :LANES] = gtile.astype(LOW)
        gright[:, LANES:] = pieces_at(lane, 64, -inner, jnp.zeros_like(gtile)).astype(LOW)
        qright[...] = jnp.where(lane < 64, left[h, :, :LANES].astype(FULL), 0.0).astype(LOW)
        dq_t = jnp.zeros((LANES, rows), FULL)
        for k in range(2 * half // chunk):
            here = slice(k * chunk, (k + 1) * chunk)
            probs = jnp.exp(dot_nt(keys[here, :], left[h]))
            dscores = (probs * dot_nt(vals[here, :], gright[...])).astype(LOW)
            dkv = dot_nn(probs.astype(LOW), gright[:, :LANES]) + dot_nn(dscores, qright[...])
            if k * chunk < half:
                dkv_mine[here, :] = dkv
            else:
                dkv_other[k * chunk - half : (k + 1) * chunk - half, :] = dkv.astype(LOW)
            dq_t = dq_t + dot_tn(keys[here, :LANES], dscores)
        dq = dq_t.T
        for g in range(rows // 32):
            here = slice(g * 32, (g + 1) * 32)
            part_h = jnp.where((lane32 >= 64) & (lane32 < 96), dq[here, :], 0.0)
            along[here, :LANES] = pltpu.roll(part_h, 95 - grid_row(ids, g), 1).astype(LOW)
        part_w = pltpu.roll(jnp.where(lane >= 96, dq, 0.0), 63, 1)
        for bit in range(5):
            moved = pltpu.roll(part_w, LANES - 2**bit, 1)
            part_w = jnp.where((row >> bit) & 1 == 1, moved, part_w)
        along[:, LANES:] = part_w.astype(LOW)
        dq = jnp.where(lane < 64, dq * 0.125 + dot_nt(along[...], table[...]), 0.0)
        if h % 2:
            dq = pltpu.roll(dq, 64, 1)
        dquery[...] = dq.astype(LOW)
        dtable[...] = dot_tn(along[...], qright[...])

    return kernel


def at(index, size):
    return pl.ds(pl.multiple_of(index * size, 16), size)


def lanes(index, size):
    return pl.ds(pl.multiple_of(index * size, LANES), size)


def mix_kernel(ids, n0, n1, n2, n3, w0, w1, o0, o1, kv, query, rows, mix):
    part, last = w0.shape
    kv_cols = kv.shape[1]
    for place, top, bottom in ((ids[0], w0, w1), (1 - ids[0], o0, o1)):
        mix[at(place * 2, part), :last] = top[...]
        mix[at(place * 2 + 1, part), :last] = bottom[...]
    mix[:, last:] = jnp.zeros((mix.shape[0], mix.shape[1] - last), LOW)
    size = n0.shape[0]
    for k, part in enumerate((n0, n1, n2, n3)):
        here = slice(k * size, (k + 1) * size)
        rows[here, :] = part[...]
        both = dot_nn(part[...], mix[...]).astype(LOW)
        kv[here, :] = both[:, :kv_cols]
        query[here, :] = both[:, kv_cols:]


def mid_kernel(
    ids, j0, j1, j2, j3, w_mine, w_other, w_two, own, own_got, params, middle, low, weight, whole
):
    fill_rows(ids, whole, w_mine, w_other, w_two)
    tok = own.shape[0]
    middle[:tok, :] = own[...]
    middle[tok:, :] = own_got[...]
    total = middle[...]
    width = j0.shape[1]
    for k, part in enumerate((j0, j1, j2, j3)):
        block = whole[at(ids[1] ^ k, width), :]
        weight[k * width : (k + 1) * width, :] = block
        total = total + dot_nn(part[...], block)
    middle[...] = total
    hat, _ = normal(total)
    low[...] = (hat * params[2:3, :] + params[3:4, :]).astype(LOW)


def feed_kernel(
    ids, r0, r1, r2, r3, c0, c1, c2, c3, up_mine, up_other, down_mine, down_other,
    d0, d1, d2, d3, active, dhidden, rows, cots, down, up,
):
    half = up_mine.shape[0]
    up[at(ids[0], half), :] = up_mine[...]
    up[at(1 - ids[0], half), :] = up_other[...]
    down[:, lanes(ids[0], half)] = down_mine[...]
    down[:, lanes(1 - ids[0], half)] = down_other[...]
    size = r0.shape[0]
    blocks = ((r0, c0, d0), (r1, c1, d1), (r2, c2, d2), (r3, c3, d3))
    for k, (row, cot, out) in enumerate(blocks):
        here = slice(k * size, (k + 1) * size)
        part, grad = row[...], cot[:size, :]
        rows[here, :] = part
        cots[here, :] = grad
        hidden = dot_nn(part, up[...])
        phi = 0.5 + 0.5 * lax.erf(hidden * 0.7071067811865476)
        active[here, :] = (hidden * phi).astype(LOW)
        slope = phi + hidden * (jnp.exp(hidden * hidden * -0.5) * 0.3989422804014327)
        back = (dot_nt(grad, down[...]) * slope).astype(LOW)
        dhidden[here, :] = back
        out[...] = dot_nt(back, up[...]).astype(LOW)


def fed_kernel(active, down, f0, f1, f2):
    size = f0.shape[0]
    for k, (out, start) in enumerate(((f0, 0), (f1, 0), (f2, 0), (f2, size))):
        part = dot_nn(active[k * size : (k + 1) * size, :], down[...])
        out[start : start + size, :] = part.astype(LOW)


def outer_kernel(which, axis):
    def kernel(ids, a, b, sent, kept):
        half = sent.shape[axis]
        for index, out in ((1 - ids[which], sent), (ids[which], kept)):
            if axis == 0:
                out[...] = dot_tn(a[:, lanes(index, half)], b[...]).astype(LOW)
            else:
                out[...] = dot_tn(a[...], b[:, lanes(index, half)]).astype(LOW)

    return kernel


def proj_grad_kernel(ids, j0, j1, j2, j3, grad, sent, kept, whole):
    width = j0.shape[1]
    for k, part in enumerate((j0, j1, j2, j3)):
        whole[at(ids[1] ^ k, width), :] = dot_tn(part[...], grad[...])
    size = sent.shape[0] // 2
    for k, owner in enumerate((ids[0], 1 - ids[0])):
        here = slice(k * size, (k + 1) * size)
        sent[here, :] = whole[at(owner * 2 + 1 - ids[2], size), :].astype(LOW)
        kept[here, :] = whole[at(owner * 2 + ids[2], size), :].astype(LOW)


def split_kernel(which):
    def kernel(ids, a, b, sent, kept):
        size = sent.shape[0] // 2
        for k in range(2):
            here = slice(k * size, (k + 1) * size)
            for bit, out in ((1 - ids[which], sent), (ids[which], kept)):
                rows = pl.ds(pl.multiple_of(k * 2 * size + bit * size, 16), size)
                out[here, :] = (a[rows, :].astype(FULL) + b[rows, :].astype(FULL)).astype(LOW)

    return kernel


def owner_kernel(a, b, sent, kept):
    size = sent.shape[0]
    kept[...] = (a[:size, :].astype(FULL) + b[:size, :].astype(FULL)).astype(kept.dtype)
    sent[...] = (a[size:, :].astype(FULL) + b[size:, :].astype(FULL)).astype(LOW)


def tail_add_kernel(a, b, out):
    size = a.shape[0]
    out[...] = (a[...].astype(FULL) + b[b.shape[0] - size :, :].astype(FULL)).astype(out.dtype)


def vector_block(out, n0, n1, n2, n3, t0, t1, t2):
    out[...] = jnp.zeros_like(out)
    tables = (t0[...] + t1[...] + t2[...]) * 8.0
    side = 16
    for k in range(8):
        start = k // 4 * LANES + k % 4 * side
        out[:side, k * 64 : (k + 1) * 64] = tables[start : start + side, :64]
    tile = 0
    for row in (n0, n1, n2, n3):
        for k in range(row.shape[1] // LANES):
            spot = slice(tile % 4 * LANES, (tile % 4 + 1) * LANES)
            out[side + tile // 4 : side + tile // 4 + 1, spot] = row[:, k * LANES : (k + 1) * LANES]
            tile += 1


def row_sums(product):
    total = product[:, :LANES]
    for k in range(1, product.shape[1] // LANES):
        total = total + product[:, k * LANES : (k + 1) * LANES]
    return jnp.sum(total.T, axis=0, keepdims=True)


def vector_out_kernel(reach, split):
    def kernel(ids, *refs):
        *parts, params, n0, n1, n2, n3, t0, t1, total, norms = refs
        first = parts[0].shape[0] - total.shape[0]
        total[...] = sum(part[first:, :].astype(FULL) for part in parts)
        side = 16
        for tile in range(norms.shape[0] * norms.shape[1] // LANES):
            each = norms.shape[1] // LANES
            spot = slice(tile % 4 * LANES, (tile % 4 + 1) * LANES)
            norms[tile // each : tile // each + 1, tile % each * LANES : (tile % each + 1) * LANES] = (
                total[side + tile // 4 : side + tile // 4 + 1, spot]
            )
        gain, shift = params[0:1, :], params[1:2, :]
        norms[0:1, :] = (norms[0:1, :] - shift * norms[1:2, :]) / gain
        for k, out in enumerate((n0, n1, n2, n3)):
            width = norms.shape[1] // 2
            if split:
                out[...] = norms[k : k + 1, lanes(ids[7], width)]
            else:
                out[...] = norms[k : k + 1, :]
        rows = lax.broadcasted_iota(jnp.int32, (side, reach), 0)
        cols = lax.broadcasted_iota(jnp.int32, (side, reach), 1)
        for k, out in enumerate((t0, t1)):
            both = jnp.zeros((64, reach), FULL)
            for part in range(4):
                turn = jnp.where(rows + part * side == reach - 1 - cols, 1.0, 0.0)
                start = (k * 4 + part) * 64
                both = both + lax.dot_general(
                    total[:side, start : start + 64],
                    turn,
                    (((0,), (0,)), ((), ())),
                    precision=lax.Precision.HIGHEST,
                    preferred_element_type=FULL,
                )
            if split:
                size = out.shape[0]
                out[...] = jnp.where(ids[7] == 0, both[:size, :], both[size:, :])
            else:
                out[...] = both

    return kernel


def dmix_kernel(dkv, dquery, mix, mine, near, sent):
    size = mine.shape[0]
    cols = dkv.shape[1]
    for k, (out, start) in enumerate(((mine, 0), (sent, 0), (near, 0), (sent, size))):
        here = slice(k * size, (k + 1) * size)
        part = dot_nt(dkv[here, :], mix[:, :cols]) + dot_nt(dquery[here, :], mix[:, cols:])
        out[start : start + size, :] = part.astype(LOW)


def dkv_kernel(m0, m1, m2, o0, o1, o2, q0, q1, q2, dkv, dquery):
    for h, (mine, got) in enumerate(((m0, o0), (m1, o1), (m2, o2))):
        cols = slice(h * LANES, (h + 1) * LANES)
        dkv[:, cols] = (mine[...] + got[...].astype(FULL)).astype(LOW)
    dquery[:, :LANES] = (q0[...].astype(FULL) + q1[...].astype(FULL)).astype(LOW)
    dquery[:, LANES:] = q2[...]


def qkv_grad_kernel(
    ids, rows, m0, m1, m2, o0, o1, o2, q0, q1, q2, mix, v2, v3, t0, t1, t2,
    dkv, dquery, sent, sent_two, kept, whole, vector,
):
    dkv_kernel(m0, m1, m2, o0, o1, o2, q0, q1, q2, dkv, dquery)
    cols = dkv.shape[1]
    whole[:, :cols] = dot_tn(rows[...], dkv[...])
    whole[:, cols:] = dot_tn(rows[...], dquery[...])
    width = kept.shape[1]
    size = (kept.shape[0] - vector.shape[0]) // 2
    extra = vector.shape[0] // 2
    sums_block(whole, dkv, dquery, mix, v2, v3, t0, t1, t2, vector)
    kept[2 * size :, :] = vector[...].astype(LOW)
    for k, (owner, out) in enumerate(((ids[0], sent), (1 - ids[0], sent_two))):
        here = slice(k * size, (k + 1) * size)
        kept[here, :] = whole[at(owner * 2 + ids[2], size), :width].astype(LOW)
        out[:size, :] = whole[at(owner * 2 + 1 - ids[2], size), :width].astype(LOW)
        out[size:, :] = vector[k * extra : (k + 1) * extra, :].astype(LOW)


def sums_block(whole, dkv, dquery, mix, v2, v3, t0, t1, t2, vector):
    weights = mix[...].astype(FULL)
    sums = jnp.concatenate(
        [jnp.sum(part[...].astype(FULL), axis=0, keepdims=True) for part in (dkv, dquery)], axis=1
    )
    both = row_sums(whole[...] * weights)
    shift = row_sums(weights * sums)
    vector_block(vector, both, shift, v2, v3, t0, t1, t2)


def sums_kernel(rows, dkv, dquery, mix, v2, v3, t0, t1, t2, vector, whole):
    cols = dkv.shape[1]
    whole[:, :cols] = dot_tn(rows[...], dkv[...])
    whole[:, cols:] = dot_tn(rows[...], dquery[...])
    sums_block(whole, dkv, dquery, mix, v2, v3, t0, t1, t2, vector)


def qkv_owner_kernel(a, b0, b1, s0, s1, kept):
    size = a.shape[0] - kept.shape[0]
    extra = kept.shape[0] - size
    kept[:size, :] = a[:size, :].astype(FULL) + b0[:size, :].astype(FULL)
    for k, (b, sent) in enumerate(((b0, s0), (b1, s1))):
        step, part = size // 2, extra // 2
        here = slice(size + k * step, size + (k + 1) * step)
        total = a[here, :].astype(FULL) + b1[k * step : (k + 1) * step, :].astype(FULL)
        sent[:step, :] = total.astype(LOW)
        start = 2 * size + k * part
        total = a[start : start + part, :].astype(FULL) + b[size:, :].astype(FULL)
        kept[size + k * part : size + (k + 1) * part, :] = total
        sent[step:, :] = total.astype(LOW)


def qkv_total_kernel(kept, g0, g1, out):
    part = g0.shape[0]
    step = part // 16 * 16 - 16
    size = 2 * step
    for k, got in enumerate((g0, g1)):
        here = slice(k * step, (k + 1) * step)
        out[here, :] = (kept[here, :] + got[:step, :].astype(FULL)).astype(LOW)
        here = slice(size + k * (part - step), size + (k + 1) * (part - step))
        out[here, :] = (kept[here, :] + got[step:, :].astype(FULL)).astype(LOW)


def fc_pack_kernel(ids, k1, g1, k2, g2, out):
    size, width = g1.shape[0], g2.shape[1]
    out[:size, :] = (k1[...] + g1[...].astype(FULL)).astype(LOW)
    for p in range(2):
        here = slice(p * size, (p + 1) * size)
        out[size:, p * width : (p + 1) * width] = (k2[here, :] + g2[here, :].astype(FULL)).astype(LOW)


def fc_join_kernel(ids, mine, got, out):
    size = mine.shape[0] // 2
    width = mine.shape[1] // 2
    for bit, ref in ((ids[3], mine), (1 - ids[3], got)):
        out[at(bit, size), :] = ref[:size, :]
        for p in range(2):
            start = (2 + p) * size
            out[start : start + size, lanes(bit, width)] = ref[size:, p * width : (p + 1) * width]


def fc_out_kernel(ids, mine, got, fc1, fc2):
    size = mine.shape[0] // 4
    width = mine.shape[1] // 2
    for bit, ref in ((ids[4], mine), (1 - ids[4], got)):
        fc1[at(bit, 2 * size), :] = ref[: 2 * size, :].astype(FULL)
        for b in range(2):
            for p in range(2):
                here = pl.ds(pl.multiple_of((bit * 4 + b * 2 + p) * size, 16), size)
                start = (2 + p) * size
                part = ref[start : start + size, b * width : (b + 1) * width]
                fc2[here, :] = part.astype(FULL)


def add_kernel(*refs):
    total = refs[0][...].astype(FULL)
    for ref in refs[1:-1]:
        total = total + ref[...].astype(FULL)
    refs[-1][...] = total.astype(refs[-1].dtype)


def halve_kernel(which):
    def kernel(ids, a, b, sent, kept):
        size = sent.shape[0]
        bit = ids[which]
        for index, out in ((1 - bit, sent), (bit, kept)):
            here = at(index, size)
            out[...] = (a[here, :].astype(FULL) + b[here, :].astype(FULL)).astype(out.dtype)

    return kernel


def join_kernel(which):
    def kernel(ids, mine, other, out):
        size = mine.shape[0]
        out[at(ids[which], size), :] = mine[...].astype(out.dtype)
        out[at(1 - ids[which], size), :] = other[...].astype(out.dtype)

    return kernel


def join_lanes_kernel(which):
    def kernel(ids, mine, other, out):
        size = mine.shape[1]
        out[:, lanes(ids[which], size)] = mine[...].astype(out.dtype)
        out[:, lanes(1 - ids[which], size)] = other[...].astype(out.dtype)

    return kernel


def qkv_out_kernel(heads):
    def kernel(ids, q0, q1, q2, q3, o0, o1, o2, o3, out):
        size = out.shape[0] // 2
        lane = lane_of(size)
        groups = 4
        odd, upper = (ids[1] & 1) == 1, (ids[1] & 2) == 2

        def tile(part, column, g):
            refs = (q0, q1, q2, q3) if part == 0 else (o0, o1, o2, o3)
            cols = slice(column, min(column + LANES, q0.shape[1]))
            v = [r[:size, cols].astype(FULL) for r in refs]
            v = [jnp.where(odd, v[k ^ 1], v[k]) for k in (g, g ^ 2)]
            one = jnp.where(upper, v[1], v[0])
            if one.shape[1] < LANES:
                one = jnp.concatenate([one, jnp.zeros_like(one)], axis=1)
            return one

        share = heads * 64
        for part in range(2):
            place = ids[2] if part == 0 else 1 - ids[2]
            here = pl.ds(pl.multiple_of(place * size, 16), size)
            total = groups * heads
            for pair in range(total // 2):
                ends = []
                for n in (2 * pair, 2 * pair + 1):
                    g, h = n // heads, n % heads
                    kv = tile(part, h * LANES, g)
                    q = tile(part, 2 * share + (h // 2) * LANES, g)
                    if h % 2:
                        q = pltpu.roll(q, 64, 1)
                    ends.append((q, kv))
                (qa, kva), (qb, kvb) = ends
                first = lane < 64
                at_col = pair * LANES
                width = groups * share
                out[here, at_col : at_col + LANES] = jnp.where(first, qa, pltpu.roll(qb, 64, 1))
                out[here, width + at_col : width + at_col + LANES] = jnp.where(
                    first, kva, pltpu.roll(kvb, 64, 1)
                )
                out[here, 2 * width + at_col : 2 * width + at_col + LANES] = jnp.where(
                    first, pltpu.roll(kva, 64, 1), kvb
                )

    return kernel


def change_kernel(middle, own, own_got, f0, f1, f2, mine, sent):
    tok = own.shape[0]
    for part, base, out in ((0, own, mine), (tok, own_got, sent)):
        here = slice(part, part + tok)
        fed = f0[here, :].astype(FULL) + f1[here, :].astype(FULL) + f2[here, :].astype(FULL)
        total = middle[here, :] + fed
        if part:
            total = total - base[...]
        out[...] = total.astype(out.dtype)


def place_kernel(ids, mine, got, base, out):
    out[ids[3]] = mine[...]
    out[1 - ids[3]] = got[...].astype(FULL) + base[...]


def place_two_kernel(ids, mine, got, out):
    out[ids[3]] = mine[...]
    out[1 - ids[3]] = got[...].astype(FULL)


def norm_back(grad, values, gain):
    hat, scale = normal(values)
    scaled = grad * gain
    back = scale * (
        scaled
        - jnp.mean(scaled, axis=-1, keepdims=True)
        - hat * jnp.mean(scaled * hat, axis=-1, keepdims=True)
    )
    return back, jnp.sum(grad * hat, axis=0, keepdims=True), jnp.sum(grad, axis=0, keepdims=True)


def mid_back_kernel(
    a0, a1, a2, middle, params, cot, weight, gmiddle, gbranch, b0, b1, b2, b3, dgain, dshift
):
    size = a0.shape[0]
    grad = a0[...].astype(FULL) + a1[...].astype(FULL) + a2[...].astype(FULL)
    back, dgain[...], dshift[...] = norm_back(grad, middle[...], params[2:3, :])
    total = cot[:size, :].astype(FULL) + back
    gmiddle[...] = total
    low = total.astype(LOW)
    gbranch[...] = low
    width = b0.shape[1]
    for k, out in enumerate((b0, b1, b2, b3)):
        out[...] = dot_nt(low, weight[k * width : (k + 1) * width, :]).astype(LOW)


def first_back_kernel(a0, a1, a2, own, own_got, params, gmiddle, mine, sent, rows):
    tok = own.shape[0]
    rows[:tok, :] = own[...]
    rows[tok:, :] = own_got[...]
    grad = a0[...].astype(FULL) + a1[: 2 * tok, :].astype(FULL) + a2[...].astype(FULL)
    back, _, _ = norm_back(grad, rows[...], params[0:1, :])
    total = gmiddle[...] + back
    mine[...] = total[:tok, :]
    sent[...] = total[tok:, :].astype(LOW)


def on_device(
    tokens,
    ln1_gain,
    ln1_bias,
    qkv_weight,
    rel_h,
    rel_w,
    proj_weight,
    ln2_gain,
    ln2_bias,
    fc1_weight,
    fc2_weight,
    cotangent,
):
    images, tok, width = tokens.shape
    hid = fc1_weight.shape[1]
    dp_count = lax.axis_size("dp")
    head = rel_h.shape[1] * dp_count
    reach = rel_h.shape[0]
    s, t = lax.axis_index("seq"), lax.axis_index("tp")
    d = lax.axis_index("dp")
    y, c = t // 2, t % 2
    image = s // 2
    group = (s % 2) * 2 + y
    groups = 4
    share = width // groups
    heads = share // head
    rows_n = 2 * tok
    half = width // 2
    me = d if dp_count == 2 else jnp.int32(0)
    ids = jnp.stack([me, group, c, image, s % 2, y, s, d]).astype(jnp.int32)
    n = 4 * rows_n
    kv_cols = 2 * share
    pad_share = 2 * LANES
    key_n = 2 * n
    qkv_cols = 3 * share
    low_tok, full_tok = shape((tok, width), LOW), shape((tok, width), FULL)
    low_rows, full_rows = shape((rows_n, width), LOW), shape((rows_n, width), FULL)
    two_rows = shape((2 * rows_n, width), LOW)
    heads_rows = shape((rows_n, share), LOW)
    way = (0, ROW, NEAR, ROW | NEAR)

    def add(kind, *args, wait=()):
        return call(add_kernel, [shape(args[0].shape, kind)], wait=wait)(*args)[0]

    call = in_order()
    quarter, eighth = half // 2, half // 4
    norm_sums = [shape((1, width), FULL)] * 2

    def total_of(kind, *args):
        return call(add_kernel, [shape(args[0].shape, kind)])(*args)[0]

    def halve(which, a, b, kind=FULL):
        dims = (a.shape[0] // 2, a.shape[1])
        return call(halve_kernel(which), [shape(dims, LOW), shape(dims, kind)], smem=1)(ids, a, b)

    def split(which, a, b):
        dims = (a.shape[0] // 2, a.shape[1])
        return call(split_kernel(which), [shape(dims, LOW)] * 2, smem=1)(ids, a, b)

    def join(which, mine, other, kind):
        dims = (2 * mine.shape[0], mine.shape[1])
        return call(join_kernel(which), [shape(dims, kind)], smem=1)(ids, mine, other)[0]

    own, away = call(pick_kernel, [full_tok] * 2, smem=1)(ids, tokens)
    with jax.named_scope("tokens_swap"):
        own_got = hop(away, FAR)
    small = jnp.concatenate([ln1_gain, ln1_bias, ln2_gain, ln2_bias]).reshape(4, -1)
    with jax.named_scope("small_params"):
        small, small_other, _ = pair_dp(after(small, away), 1)
    tables = jnp.stack([rel_h.T, rel_w.T])
    with jax.named_scope("tables_hop"):
        tables, tables_other, _ = pair_dp(after(tables, away), 1)
    cot_mine, cot_away = call(pick_kernel, [low_tok] * 2, smem=1)(ids, cotangent)
    with jax.named_scope("cot_swap"):
        cot_got = hop(cot_away, FAR)
    depth = qkv_weight.shape[0] // 2
    mix_mine = call(pack_kernel(share, heads), [shape((depth, qkv_cols), LOW)] * 2, smem=1)(
        ids, qkv_weight
    )
    with jax.named_scope("qkv_weight_hop"):
        if dp_count == 2:
            mix_other = [swap_dp(after(v, small_other, tables_other)) for v in mix_mine]
        else:
            whole = lax.all_gather(
                jnp.concatenate(mix_mine, axis=0), "dp", axis=0, tiled=True
            )
            *mix_mine, low, high = jnp.split(whole, 4, axis=0)
            mix_other = [low, high]

    normed, params = call(norm_kernel, [low_rows, shape((4, width), FULL)], smem=1)(
        ids, own, own_got, small, small_other
    )
    with jax.named_scope("normed_gather"):
        normed_parts = [normed] + [hop(normed, b) for b in way[1:]]
    cot = call(stack_kernel, [low_rows])(cot_mine, cot_got)[0]
    table, spot_one, spot_two = call(
        table_kernel,
        [shape((LANES, 2 * LANES), LOW)] + [shape((key_n, LANES), LOW)] * 2,
        smem=1,
    )(ids, tables, tables_other)
    if dp_count == 2:
        proj_part = call(rows_kernel, [shape((half // 2, width), LOW)], smem=1)(ids, proj_weight)[0]

    kv, query, normed_all, mix = call(
        mix_kernel,
        [
            shape((n, kv_cols), LOW),
            shape((n, pad_share), LOW),
            shape((n, width), LOW),
            shape((width, kv_cols + pad_share), LOW),
        ],
        smem=1,
        extra=3,
    )(ids, *normed_parts, *mix_mine, *mix_other)
    with jax.named_scope("kv_hop"):
        kv_other = hop(kv, CORE)
    with jax.named_scope("cot_row"):
        cot_row = hop(after(cot, kv), ROW)
    with jax.named_scope("proj_weight_hop"):
        if dp_count == 2:
            proj_mine, proj_other = proj_weight, swap_dp(after(proj_part, kv))
        else:
            proj_mine, proj_other, _ = pair_dp(proj_weight, 0)
    with jax.named_scope("fc1_weight_hop"):
        up_mine, up_other, _ = pair_dp(after(fc1_weight, kv), 0)

    attended, *attended_low, left = call(
        attend_kernel,
        [shape((n, pad_share), FULL)]
        + [heads_rows] * 4
        + [shape((heads, n, 2 * LANES), LOW)],
        [pltpu.VMEM((key_n, 2 * LANES), LOW), pltpu.VMEM((n, 2 * LANES), FULL)],
        smem=1,
        extra=8,
    )(ids, query, kv, kv_other, spot_one, spot_two, table)
    attended_low = lax.optimization_barrier((*attended_low, cot_row))[:4]
    with jax.named_scope("proj_weight_core"):
        proj_two = hop(after(proj_other, attended), CORE)
    with jax.named_scope("attended_hop"):
        joined = [attended_low[0]] + [hop(attended_low[k], way[k]) for k in (1, 2, 3)]
    with jax.named_scope("fc2_weight_hop"):
        down_mine, down_other, _ = pair_dp(after(fc2_weight, *joined), 1)
    middle, normed_two, proj = call(
        mid_kernel,
        [full_rows, low_rows, shape((width, width), LOW)],
        [pltpu.VMEM((width, width), LOW)],
        smem=1,
        wait=(up_other,),
    )(ids, *joined, proj_mine, proj_other, proj_two, own, own_got, params)

    with jax.named_scope("normed_two_row"):
        two_row = hop(normed_two, ROW)
    with jax.named_scope("normed_two_core"):
        two_core = hop(normed_two, CORE)
        two_diag = hop(two_row, CORE)
    with jax.named_scope("cot_core"):
        cot_core = hop(after(cot, two_row), CORE)
        cot_diag = hop(after(cot_row, two_row), CORE)
    d0, d1, d2, d3, active, dhidden, rows_all, cot_all, down = call(
        feed_kernel,
        [low_rows] * 4
        + [shape((n, hid), LOW)] * 2
        + [shape((n, width), LOW)] * 2
        + [shape((hid, width), LOW)],
        [pltpu.VMEM((width, hid), LOW)],
        smem=1,
        extra=6,
    )(
        ids, normed_two, two_row, two_core, two_diag, cot, cot_row, cot_core, cot_diag,
        up_mine, up_other, down_mine, down_other,
    )
    with jax.named_scope("dnorm_core"):
        dnorm_next = hop(d3, CORE)
        dnorm_mine = hop(d2, CORE)
    dnorm_sent = total_of(LOW, d1, dnorm_next)
    with jax.named_scope("dnorm_row"):
        dnorm_row = hop(dnorm_sent, ROW)

    fc1_sent, fc1_kept = call(outer_kernel(0, 0), [shape((half, hid), LOW)] * 2, smem=1, extra=4)(
        ids, rows_all, dhidden
    )
    with jax.named_scope("fc1_dp"):
        fc1_kept, fc1_got = scatter_dp(fc1_sent, fc1_kept, 0)
    fc2_sent, fc2_kept = call(outer_kernel(0, 1), [shape((hid, half), LOW)] * 2, smem=1, extra=4)(
        ids, active, cot_all
    )
    with jax.named_scope("fc2_dp"):
        fc2_kept, fc2_got = scatter_dp(fc2_sent, fc2_kept, 1)
    (gmiddle, gbranch, b0, b1, b2, b3, dgain_two, dshift_two) = call(
        mid_back_kernel, [full_rows, low_rows] + [heads_rows] * 4 + norm_sums
    )(d0, dnorm_mine, dnorm_row, middle, params, cot, proj)
    with jax.named_scope("grad_heads_hop"):
        grad_parts = [b0] + [hop(b, bits) for b, bits in zip((b1, b2, b3), way[1:])]
    proj_sent, proj_kept = call(
        proj_grad_kernel,
        [shape((half, width), LOW)] * 2,
        [pltpu.VMEM((width, width), FULL)],
        smem=1,
    )(ids, *joined, gbranch)
    f0, f1, f2 = call(fed_kernel, [low_rows, low_rows, two_rows])(active, down)
    with jax.named_scope("proj_core"):
        proj_got = hop(after(proj_sent, *grad_parts), CORE)
    with jax.named_scope("fed_core"):
        fed_got = hop(after(f2, *grad_parts), CORE)

    def back(h, wait=()):
        dquery, mine, other, dtable = call(
            back_kernel(h),
            [
                shape((n, LANES), LOW),
                shape((n, LANES), FULL),
                shape((n, LANES), LOW),
                shape((2 * LANES, LANES), FULL),
            ],
            [
                pltpu.VMEM((key_n, 2 * LANES), LOW),
                pltpu.VMEM((key_n, 2 * LANES), LOW),
                pltpu.VMEM((n, 2 * LANES), LOW),
                pltpu.VMEM((n, LANES), LOW),
                pltpu.VMEM((n, 2 * LANES), LOW),
                pltpu.VMEM((n, LANES), FULL),
            ],
            smem=1,
            extra=8,
            wait=wait,
        )(ids, left, kv, kv_other, spot_one, spot_two, table, *grad_parts, attended)
        with jax.named_scope("dkv_hop"):
            return mine, hop(other, CORE), dquery, dtable

    first = back(0)
    fed_sent = call(tail_add_kernel, [low_rows])(f1, fed_got)[0]
    with jax.named_scope("fed_row"):
        fed_row = hop(fed_sent, ROW)
    if dp_count == 2:
        fc1_sent, fc1_kept = halve(4, fc1_kept, fc1_got)
        with jax.named_scope("fc1_near_sum"):
            fc1_got = hop(fc1_sent, NEAR)
    second = back(1, (first[1],))
    if dp_count == 2:
        proj_sent, proj_kept = split(5, proj_kept, proj_got)
        with jax.named_scope("proj_row"):
            proj_got = hop(proj_sent, ROW)
    third = back(2, (second[1],))

    def change():
        return call(change_kernel, [full_tok, low_tok])(
            middle, own, own_got, f0, fed_got, fed_row
        )

    def place_output():
        return call(place_kernel, [shape(tokens.shape, FULL)], smem=1)(
            ids, change_mine, change_got, away
        )[0]

    dkv_mine, dkv_got, dqueries, dtables = zip(first, second, third)
    mixed_shapes = [shape((n, kv_cols), LOW), shape((n, pad_share), LOW)]
    vector_rows = 32
    whole_shape = pltpu.VMEM((width, kv_cols + pad_share), FULL)
    if dp_count == 2:
        fc2_sent, fc2_kept = halve(4, fc2_kept, fc2_got)
        with jax.named_scope("fc2_near_sum"):
            fc2_got = hop(fc2_sent, NEAR)
        fc1_sent, fc1_kept = halve(3, fc1_kept, fc1_got)
        with jax.named_scope("fc1_far_sum"):
            fc1_got = hop(fc1_sent, FAR)
        sent_rows = quarter + vector_rows // 2
        dkv, dquery, *qkv_sent, qkv_kept = call(
            qkv_grad_kernel,
            mixed_shapes
            + [shape((sent_rows, qkv_cols), LOW)] * 2
            + [shape((half + vector_rows, qkv_cols), LOW)],
            [whole_shape, pltpu.VMEM((vector_rows, qkv_cols), FULL)],
            smem=1,
            extra=6,
        )(
            ids, normed_all, *dkv_mine, *dkv_got, *dqueries, mix, dgain_two, dshift_two, *dtables
        )
        with jax.named_scope("qkv_core"):
            qkv_got = [hop(v, CORE) for v in qkv_sent]
    else:
        dkv, dquery = call(dkv_kernel, mixed_shapes)(*dkv_mine, *dkv_got, *dqueries)
    e_mine, e_near, e_row = call(dmix_kernel, [low_rows, low_rows, two_rows])(dkv, dquery, mix)
    with jax.named_scope("dnormed_row"):
        e_got = hop(e_row, ROW)

    def dnormed_near():
        sent = call(tail_add_kernel, [low_rows])(e_near, e_got)[0]
        with jax.named_scope("dnormed_near"):
            return hop(sent, NEAR)

    def first_back():
        return call(
            first_back_kernel, [full_tok, low_tok], [pltpu.VMEM((rows_n, width), FULL)]
        )(e_mine, e_got, dnormed_got, own, own_got, params, gmiddle)

    def place_tokens():
        return call(place_two_kernel, [shape(tokens.shape, FULL)], smem=1)(
            ids, token_mine, token_got
        )[0]

    def vector_out(parts, size, features):
        return call(
            vector_out_kernel(reach, dp_count == 2),
            [shape((1, size), FULL)] * 4 + [shape((features, reach), FULL)] * 2,
            [pltpu.VMEM((vector_rows, qkv_cols), FULL), pltpu.VMEM((4, width), FULL)],
            smem=1,
        )(ids, *parts, params)

    if dp_count == 2:
        qkv_rows = (quarter + vector_rows, qkv_cols)
        part_rows = ((quarter + vector_rows) // 2, qkv_cols)
        *qkv_sent, qkv_kept = call(
            qkv_owner_kernel, [shape(part_rows, LOW)] * 2 + [shape(qkv_rows, FULL)]
        )(qkv_kept, *qkv_got)
        with jax.named_scope("qkv_dp"):
            qkv_got = [swap_dp(v) for v in qkv_sent]
        qkv_part = call(qkv_total_kernel, [shape(qkv_rows, LOW)])(qkv_kept, *qkv_got)[0]
        with jax.named_scope("qkv_far"):
            qkv_got = hop(qkv_part, FAR)
        fc2_sent, fc2_kept = call(
            halve_kernel(3), [shape((quarter, half), LOW), shape((quarter, half), FULL)], smem=1,
            wait=(fc1_got,),
        )(ids, fc2_kept, fc2_got)
        with jax.named_scope("fc2_far_sum"):
            fc2_got = hop(fc2_sent, FAR)
        dnormed_got = dnormed_near()
        proj_low = shape((eighth, width), LOW)
        proj_sent, proj_kept = call(owner_kernel, [proj_low] * 2)(proj_kept, proj_got)
        with jax.named_scope("proj_dp"):
            proj_got = swap_dp(proj_sent)
        qkv_part = total_of(LOW, qkv_part, qkv_got)
        with jax.named_scope("qkv_all"):
            qkv_parts = [qkv_part] + [hop(qkv_part, bits) for bits in way[1:]]
        fc_part = call(fc_pack_kernel, [shape((quarter, width), LOW)], smem=1)(
            ids, fc1_kept, fc1_got, fc2_kept, fc2_got
        )[0]
        with jax.named_scope("fc_far_all"):
            fc_got = hop(fc_part, FAR)
        token_mine, token_sent = first_back()
        with jax.named_scope("tokens_grad_swap"):
            token_got = hop(token_sent, FAR)
        proj_part = total_of(LOW, proj_kept, proj_got)
        with jax.named_scope("proj_near"):
            proj_got = hop(proj_part, NEAR)
        *norms, table_h, table_w = vector_out(qkv_parts, half, head // 2)
        norms = [v.reshape(half) for v in norms]
        dtables = (table_h.T, table_w.T)
        with jax.named_scope("qkv_core_all"):
            qkv_others = [hop(part, CORE) for part in qkv_parts]
        tokens_grad = place_tokens()
        proj_part = total_of(LOW, proj_part, proj_got)
        with jax.named_scope("proj_far"):
            proj_got = hop(proj_part, FAR)
        fc_part = call(fc_join_kernel, [shape((half, width), LOW)], smem=1)(ids, fc_part, fc_got)[0]
        with jax.named_scope("fc_near_all"):
            fc_got = hop(fc_part, NEAR)
        change_mine, change_sent = change()
        with jax.named_scope("output_swap"):
            change_got = hop(change_sent, FAR)
        proj_part = total_of(LOW, proj_part, proj_got)
        with jax.named_scope("proj_all_row"):
            proj_got = hop(proj_part, ROW)
        qkv_grad = call(
            qkv_out_kernel(heads), [shape((half, 3 * width), FULL)], smem=1, extra=4
        )(ids, *qkv_parts, *qkv_others)[0]
        proj_part = join(5, proj_part, proj_got, LOW)
        with jax.named_scope("proj_all_core"):
            proj_got = hop(proj_part, CORE)
        output = place_output()
        proj_grad = join(2, proj_part, proj_got, FULL)
        fc1_grad, fc2_grad = call(
            fc_out_kernel, [shape((half, hid), FULL), shape((hid, half), FULL)], smem=1
        )(ids, fc_part, fc_got)
    else:
        every = ("seq", "tp")
        dnormed_got = dnormed_near()
        token_mine, token_sent = first_back()
        token_got = hop(token_sent, FAR)
        change_mine, change_sent = change()
        change_got = hop(change_sent, FAR)
        output, tokens_grad = place_output(), place_tokens()

        def weight_sum(a, b, axes, axis=0):
            part = lax.psum_scatter(
                dot_tn(a, b).astype(LOW), "dp", scatter_dimension=axis, tiled=True
            )
            return lax.psum(part, axes).astype(FULL)

        fc1_grad = weight_sum(rows_all, dhidden, "seq")
        fc2_grad = weight_sum(active, cot_all, "seq", 1)
        proj_grad = weight_sum(canon(joined, group, 1), gbranch, every)
        dmixed = jnp.concatenate([dkv, dquery], axis=1)[:, :qkv_cols]
        part = dot_tn(normed_all, dmixed).astype(LOW)
        part = lax.psum_scatter(part, "dp", scatter_dimension=0, tiled=True)
        part = part.astype(FULL) + hop(part, FAR).astype(FULL)
        part = part.astype(LOW)
        part = (part.astype(FULL) + hop(part, CORE).astype(FULL)).astype(LOW)
        whole = canon([part[None]] + [hop(part, bits)[None] for bits in way[1:]], group, 0)
        depth = whole.shape[1]
        pairs = whole[:, :, :kv_cols].reshape(groups, depth, heads, 2, head)
        qkv_grad = jnp.concatenate(
            [
                whole[:, :, kv_cols:].transpose(1, 0, 2).reshape(depth, width),
                pairs[:, :, :, 0].transpose(1, 0, 2, 3).reshape(depth, width),
                pairs[:, :, :, 1].transpose(1, 0, 2, 3).reshape(depth, width),
            ],
            axis=1,
        ).astype(FULL)
        vector = call(sums_kernel, [shape((vector_rows, qkv_cols), FULL)], [whole_shape], extra=6)(
            normed_all, dkv, dquery, mix, dgain_two, dshift_two, *dtables
        )[0]
        vector = lax.psum(vector, ("dp", *every))
        *norms, table_h, table_w = vector_out((vector,), width, head)
        norms = [piece(v.reshape(-1), d, width // dp_count, 0) for v in norms]
        dtables = [piece(v.T, d, head // dp_count, 1) for v in (table_h, table_w)]
    return (
        output,
        tokens_grad,
        norms[0],
        norms[1],
        qkv_grad,
        dtables[0],
        dtables[1],
        proj_grad,
        norms[2],
        norms[3],
        fc1_grad,
        fc2_grad,
    )


def solution(mesh):
    split = P("dp", ("seq", "tp"), None)
    params = (
        P("dp"),
        P("dp"),
        P("dp", None),
        P(None, "dp"),
        P(None, "dp"),
        P("dp", None),
        P("dp"),
        P("dp"),
        P("dp", "tp"),
        P("tp", "dp"),
    )
    return jax.shard_map(
        on_device,
        mesh=mesh,
        in_specs=(split, *params, split),
        out_specs=(split, split, *params),
        check_vma=False,
    )
```

time: 256 us -> 213 us (0.83)
  Pallas kernels: 23.4 us -> 57 us
  waiting for transfers between devices: 103 us -> 78.4 us
  local copies, waits for them, and re-layouts: 24.9 us -> 8.79 us
  other arithmetic: 19.9 us -> 3.84 us
  starting transfers between devices: 75.9 us -> 63.3 us
  matrix products: 6.62 us -> 0 us
    pallas_call x7 -> x47, Pallas kernels: 23.4 us -> 57 us  [run(): pl.pallas_call(body, name=kernel.__qualname__.split('.')[0], out_shape=ou...]
    ppermute x11 -> x12, waiting for transfers between devices: 25.9 us -> 13.4 us  [swap_dp(): return lax.ppermute(value, 'dp', [(0, 1), (1, 0)])]
    ppermute x54 -> x53, waiting for transfers between devices: 76.8 us -> 65 us  [hop(): lax.ppermute(value, ('seq', 'tp'), [(i, i ^ bits) for i in range(count)])]
    ppermute x54 -> x53, starting transfers between devices: 58.5 us -> 50.1 us  [hop(): lax.ppermute(value, ('seq', 'tp'), [(i, i ^ bits) for i in range(count)])]
    select_n x16 -> x0, other arithmetic: 6.75 us -> none  [the longest x3 2.41 us: double(): jnp.where(bit == 0, value, got)]
    dot_general x8 -> x0, matrix products: 6.62 us -> none  [the longest x4 4.09 us: dot_tn(): lax.dot_general(a, b, (((0,), (0,)), ((), ())), preferred_element_type=FULL)]
    convert_element_type x7 -> x0, local copies, waits for them, and re-layouts: 6.22 us -> none  [the longest x3 3.3 us: halve(): sent = piece(value, 1 - bit, size, axis).astype(LOW)]
    convert_element_type x16 -> x0, other arithmetic: 5.48 us -> none  [the longest x2 2.36 us: sum_seq(): low = total.astype(LOW)]
  transfers between devices with their start and end apart: 65 -> 65, of which waited for: 32 -> 29; matrix products, arithmetic and copies ran while one was open for 14% -> 2% of each run, Pallas kernels for 7% -> 22%
where the time goes in v2:
time: 213 us; the launch traced here: 212 us
  waiting for transfers between devices  78.4 us (37%)
  starting transfers between devices  63.3 us (30%)
  Pallas kernels  57 us (27%)
  local copies, waits for them, and re-layouts  8.79 us (4%)
  other arithmetic  3.84 us (2%)
    ppermute x53, waiting for transfers between devices, hop(): lax.ppermute(value, ('seq', 'tp'), [(i, i ^ bits) for i in range(count)])  65 us
    pallas_call x47, Pallas kernels, run(): pl.pallas_call(body, name=kernel.__qualname__.split('.')[0], out_shape=ou...  57 us
    ppermute x53, starting transfers between devices, hop(): lax.ppermute(value, ('seq', 'tp'), [(i, i ^ bits) for i in range(count)])  50.1 us
    ppermute x12, waiting for transfers between devices, swap_dp(): return lax.ppermute(value, 'dp', [(0, 1), (1, 0)])  13.4 us
    ppermute x12, starting transfers between devices, swap_dp(): return lax.ppermute(value, 'dp', [(0, 1), (1, 0)])  13.1 us
    unnamed x20, local copies, waits for them, and re-layouts  8.68 us
  transfers between devices with their start and end apart: 65, of which 29 were waited for; matrix products, arithmetic and copies ran while one was open for 2% of the time, Pallas kernels for 22%

profile of v2, /device:TPU:0, one launch (start us, length us, event | category | flops | bytes accessed | tf_op | source)
XLA Modules:
  0.0 212.5 jit_solution(11735832817042101477)
XLA Ops:
  2.3 4.1 %collective-permute-start = (f32[64,768]{1,0:T(8,128)S(1)}, f32[64,768]{1,0:T(8,128)S(1)}, u32[]{:S(2)}, u32[]{:S(2)}) collective-permute-start(f32[64,768]{1,0:T(8,128)S(1)} %get-tuple-element.127.refs_3_), channel_id=1, source_target_pairs={{0,8},{1,9},{2,10},{3,11},{4,12},{5,13},{6,14},{7,15},{8,0},{9,1},... | collective-permute-start | bytes 589832 | tf_op jit(solution)/shard_map/tokens_swap/ppermute | solution.py:19
  7.2 1.5 collective-permute-start.5
  11.6 1.5 copy-done.3
  15.8 1.2 collective-permute-start.7
  17.0 1.5 collective-permute-done.refs_2_.refs_9_.refs_4_
  19.3 1.1 collective-permute-start.4
  20.4 2.2 %collective-permute-start.3 = (bf16[128,768]{1,0:T(8,128)(2,1)S(1)}, bf16[128,768]{1,0:T(8,128)(2,1)S(1)}, u32[]{:S(2)}, u32[]{:S(2)}) collective-permute-start(bf16[128,768]{1,0:T(8,128)(2,1)S(1)} %get-tuple-element.131.refs_1_), channel_id=1, source_target_pairs={{0,4},{1,5},{2,6},{3,7},{4,0},{5,1},{6,2},{7,3},{8,12},{9,13},{10,... | collective-permute-start | bytes 589832 | tf_op jit(solution)/shard_map/normed_gather/ppermute | solution.py:19
  24.2 2.1 %collective-permute-done.7.refs_8_ = bf16[192,576]{1,0:T(8,128)(2,1)S(1)} collective-permute-done((bf16[192,576]{1,0:T(8,128)(2,1)S(1)}, bf16[192,576]{1,0:T(8,128)(2,1)S(1)}, u32[]{:S(2)}, u32[]{:S(2)}) %collective-permute-start.7) | collective-permute-done | bytes 221216 | tf_op jit(solution)/shard_map/qkv_weight_hop/ppermute | solution.py:23
  26.3 1.2 collective-permute-done.4.refs_4_
  27.5 1.4 collective-permute-done.3.refs_3_
  29.5 1.4 mix_kernel.1
  31.0 1.6 collective-permute-start.14
  34.2 7.9 %attend_kernel.1 = (f32[512,256]{1,0:T(8,128)S(1)}, bf16[128,192]{1,0:T(8,128)(2,1)S(1)}, bf16[128,192]{1,0:T(8,128)(2,1)S(1)}, bf16[128,192]{1,0:T(8,128)(2,1)S...) custom-call(s32[8]{0:T(128)S(1)} %stack.41.refs_0_, ...), custom_call_target="tpu_custom_call" | custom-call | tf_op jit(solution)/shard_map/attend_kernel/pallas_call | solution.py:84
  43.2 1.8 collective-permute-start.12
  47.5 2.7 %collective-permute-done.13.refs_4_ = bf16[128,192]{1,0:T(8,128)(2,1)S(1)} collective-permute-done((bf16[128,192]{1,0:T(8,128)(2,1)S(1)}, bf16[128,192]{1,0:T(8,128)(2,1)S(1)}, u32[]{:S(2)}, u32[]{:S(2)}) %collective-permute-start.13) | collective-permute-done | bytes 49184 | tf_op jit(solution)/shard_map/attended_hop/ppermute | solution.py:19
  50.2 1.5 collective-permute-start.22
  51.7 1.8 collective-permute-done.16.refs_12_.refs_10_
  53.5 1.2 mid_kernel.1
  55.9 5.0 %collective-permute-done.17.refs_2_ = bf16[128,768]{1,0:T(8,128)(2,1)S(1)} collective-permute-done((bf16[128,768]{1,0:T(8,128)(2,1)S(1)}, bf16[128,768]{1,0:T(8,128)(2,1)S(1)}, u32[]{:S(2)}, u32[]{:S(2)}) %collective-permute-start.17) | collective-permute-done | bytes 196640 | tf_op jit(solution)/shard_map/normed_two_row/ppermute | solution.py:19
  61.4 4.4 %collective-permute-done.22.refs_12_ = bf16[768,384]{1,0:T(8,128)(2,1)S(1)} collective-permute-done((bf16[768,384]{1,0:T(8,128)(2,1)S(1)}, bf16[768,384]{1,0:T(8,128)(2,1)S(1)}, u32[]{:S(2)}, u32[]{:S(2)}) %collective-permute-start.22) | collective-permute-done | bytes 589856 | tf_op jit(solution)/shard_map/fc2_weight_hop/ppermute | solution.py:23
  65.7 4.5 %feed_kernel.1 = (bf16[128,768]{1,0:T(8,128)(2,1)S(1)}, bf16[128,768]{1,0:T(8,128)(2,1)S(1)}, bf16[128,768]{1,0:T(8,128)(2,1)S(1)}, bf16[128,768]{1,0:T(8,128)(2...) custom-call(s32[8]{0:T(128)S(1)} %stack.41.refs_0_, ...), custom_call_target="tpu_custom_call" | custom-call | tf_op jit(solution)/shard_map/feed_kernel/pallas_call | solution.py:84
  71.8 1.3 collective-permute-start.25
  73.1 1.6 outer_kernel.2
  74.6 1.8 collective-permute-start.31
  76.4 1.6 outer_kernel.3
  79.7 1.3 collective-permute-start.26
  81.0 2.0 collective-permute-start.27
  83.2 1.2 proj_grad_kernel.1
  84.4 1.3 collective-permute-done.27.refs_9_
  85.7 2.4 %collective-permute-done.28.refs_10_ = bf16[128,192]{1,0:T(8,128)(2,1)S(1)} collective-permute-done((bf16[128,192]{1,0:T(8,128)(2,1)S(1)}, bf16[128,192]{1,0:T(8,128)(2,1)S(1)}, u32[]{:S(2)}, u32[]{:S(2)}) %collective-permute-start.28) | collective-permute-done | bytes 49184 | tf_op jit(solution)/shard_map/grad_heads_hop/ppermute | solution.py:19
  89.5 1.5 collective-permute-start.33
  91.0 3.9 %back_kernel.3 = (bf16[512,128]{1,0:T(8,128)(2,1)S(1)}, f32[512,128]{1,0:T(8,128)S(1)}, bf16[512,128]{1,0:T(8,128)(2,1)S(1)}, f32[256,128]{1,0:T(8,128)S(1)}) custom-call(s32[8]{0:T(128)S(1)} %stack.41.refs_0_, bf16[3,512,256]{2,1,0:T(8,128)(2,1)S(1)} %get-tuple-element.184.refs_1_, bf16[512,384]{1,0:T(8,128)(2,1)S(1)} %get-tuple-element.140.refs_2_, ...), custom_call_target="tpu_custom_call" | custom-call | tf_op jit(solution)/shard_map/back_kernel/pallas_call | solution.py:84
  96.3 3.3 %back_kernel.4 = (bf16[512,128]{1,0:T(8,128)(2,1)S(1)}, f32[512,128]{1,0:T(8,128)S(1)}, bf16[512,128]{1,0:T(8,128)(2,1)S(1)}, f32[256,128]{1,0:T(8,128)S(1)}) custom-call(s32[8]{0:T(128)S(1)} %stack.41.refs_0_, bf16[3,512,256]{2,1,0:T(8,128)(2,1)S(1)} %get-tuple-element.184.refs_1_, bf16[512,384]{1,0:T(8,128)(2,1)S(1)} %get-tuple-element.140.refs_2_, ...), custom_call_target="tpu_custom_call" | custom-call | tf_op jit(solution)/shard_map/back_kernel/pallas_call | solution.py:84
  101.0 4.0 %back_kernel.5 = (bf16[512,128]{1,0:T(8,128)(2,1)S(1)}, f32[512,128]{1,0:T(8,128)S(1)}, bf16[512,128]{1,0:T(8,128)(2,1)S(1)}, f32[256,128]{1,0:T(8,128)S(1)}) custom-call(s32[8]{0:T(128)S(1)} %stack.41.refs_0_, bf16[3,512,256]{2,1,0:T(8,128)(2,1)S(1)} %get-tuple-element.184.refs_1_, bf16[512,384]{1,0:T(8,128)(2,1)S(1)} %get-tuple-element.140.refs_2_, ...), custom_call_target="tpu_custom_call" | custom-call | tf_op jit(solution)/shard_map/back_kernel/pallas_call | solution.py:84
  106.7 1.8 qkv_grad_kernel.1
  109.0 1.4 dmix_kernel.1
  112.2 1.4 collective-permute-start.42
  113.5 1.4 collective-permute-start.38
  114.9 1.4 collective-permute-start.46
  116.3 1.8 collective-permute-done.43.refs_2_
  118.1 2.1 collective-permute-done.42.refs_1_
  120.3 3.4 %collective-permute-start.45 = (bf16[224,576]{1,0:T(8,128)(2,1)S(1)}, bf16[224,576]{1,0:T(8,128)(2,1)S(1)}, u32[]{:S(2)}, u32[]{:S(2)}) collective-permute-start(bf16[224,576]{1,0:T(8,128)(2,1)S(1)} %qkv_total_kernel.1.refs_3_.refs_0_), channel_id=1, source_target_pairs={{0,8},{1,9},{2,10},{3,11},{4,12},{5,13},{6,14},{7,15},{8,0},{9,1},... | collective-permute-start | bytes 774152 | tf_op jit(solution)/shard_map/qkv_far/ppermute | solution.py:19
  123.9 18.6 %collective-permute-done.37.refs_4_.refs_2_ = bf16[96,768]{1,0:T(8,128)(2,1)S(1)} collective-permute-done((bf16[96,768]{1,0:T(8,128)(2,1)S(1)}, bf16[96,768]{1,0:T(8,128)(2,1)S(1)}, u32[]{:S(2)}, u32[]{:S(2)}) %collective-permute-start.37) | collective-permute-done | bytes 147488 | tf_op jit(solution)/shard_map/fc1_far_sum/ppermute | solution.py:19
  143.2 4.0 %collective-permute-start.50 = (bf16[128,768]{1,0:T(8,128)(2,1)S(1)}, bf16[128,768]{1,0:T(8,128)(2,1)S(1)}, u32[]{:S(2)}, u32[]{:S(2)}) collective-permute-start(bf16[128,768]{1,0:T(8,128)(2,1)S(1)} %tail_add_kernel.3.refs_2_), channel_id=1, source_target_pairs={{0,4},{1,5},{2,6},{3,7},{4,0},{5,1},{6,2},{7,3},{8,12},{9,13},{10,... | collective-permute-start | bytes 589832 | tf_op jit(solution)/shard_map/dnormed_near/ppermute | solution.py:19
  148.3 2.0 collective-permute-start.54
  150.6 1.6 collective-permute-done.44.refs_4_
  152.2 1.5 collective-permute-start.53
  154.5 1.6 collective-permute-start.48
  156.5 2.1 collective-permute-start.51
  158.6 9.2 %collective-permute-done.55.refs_4_ = bf16[224,576]{1,0:T(8,128)(2,1)S(1)} collective-permute-done((bf16[224,576]{1,0:T(8,128)(2,1)S(1)}, bf16[224,576]{1,0:T(8,128)(2,1)S(1)}, u32[]{:S(2)}, u32[]{:S(2)}) %collective-permute-start.55) | collective-permute-done | bytes 258080 | tf_op jit(solution)/shard_map/qkv_all/ppermute | solution.py:19
  168.1 5.5 %collective-permute-done.54.refs_3_ = bf16[224,576]{1,0:T(8,128)(2,1)S(1)} collective-permute-done((bf16[224,576]{1,0:T(8,128)(2,1)S(1)}, bf16[224,576]{1,0:T(8,128)(2,1)S(1)}, u32[]{:S(2)}, u32[]{:S(2)}) %collective-permute-start.54) | collective-permute-done | bytes 258080 | tf_op jit(solution)/shard_map/qkv_all/ppermute | solution.py:19
  174.8 1.6 vector_out_kernel.1
  176.4 1.3 place_two_kernel.1.refs_2_
  178.8 3.0 %collective-permute-start.57 = (bf16[96,768]{1,0:T(8,128)(2,1)S(1)}, bf16[96,768]{1,0:T(8,128)(2,1)S(1)}, u32[]{:S(2)}, u32[]{:S(2)}) collective-permute-start(bf16[96,768]{1,0:T(8,128)(2,1)S(1)} %add_kernel.8.refs_3_.refs_0_), channel_id=1, source_target_pairs={{0,8},{1,9},{2,10},{3,11},{4,12},{5,13},{6,14},{7,15},{8,0},{9,1},... | collective-permute-start | bytes 442376 | tf_op jit(solution)/shard_map/proj_far/ppermute | solution.py:19
  182.4 2.5 %collective-permute-start.64 = (bf16[384,768]{1,0:T(8,128)(2,1)S(1)}, bf16[384,768]{1,0:T(8,128)(2,1)S(1)}, u32[]{:S(2)}, u32[]{:S(2)}) collective-permute-start(bf16[384,768]{1,0:T(8,128)(2,1)S(1)} %fc_join_kernel.1.refs_6_.refs_1_), channel_id=1, source_target_pairs={{0,4},{1,5},{2,6},{3,7},{4,0},{5,1},{6,2},{7,3},{8,12},{9,13},{10,... | collective-permute-start | bytes 1769480 | tf_op jit(solution)/shard_map/fc_near_all/ppermute | solution.py:19
  185.5 2.3 %collective-permute-done.57.refs_1_ = bf16[96,768]{1,0:T(8,128)(2,1)S(1)} collective-permute-done((bf16[96,768]{1,0:T(8,128)(2,1)S(1)}, bf16[96,768]{1,0:T(8,128)(2,1)S(1)}, u32[]{:S(2)}, u32[]{:S(2)}) %collective-permute-start.57) | collective-permute-done | bytes 147488 | tf_op jit(solution)/shard_map/proj_far/ppermute | solution.py:19
  189.4 3.7 %qkv_out_kernel.1.refs_3_ = f32[384,2304]{1,0:T(8,128)} custom-call(s32[8]{0:T(128)S(1)} %stack.41.refs_0_, bf16[224,576]{1,0:T(8,128)(2,1)S(1)} %add_kernel.6.refs_5_.refs_1_, bf16[224,576]{1,0:T(8,128)(2,1)S(1)} %collective-permute-done.53.refs_2_, bf16[224,576]{1,0:T(8,128)(2,1)S(1)} %collective-permute-done.54.refs_3_, ...), custom_call_target="tpu_custom_call" | custom-call | tf_op jit(solution)/shard_map/qkv_out_kernel/pallas_call | solution.py:84
  193.1 1.2 collective-permute-done.58.refs_2_
  194.3 2.0 copy-done
  199.5 5.7 %collective-permute-done.56.refs_2_ = bf16[64,768]{1,0:T(8,128)(2,1)S(1)} collective-permute-done((bf16[64,768]{1,0:T(8,128)(2,1)S(1)}, bf16[64,768]{1,0:T(8,128)(2,1)S(1)}, u32[]{:S(2)}, u32[]{:S(2)}) %collective-permute-start.56) | collective-permute-done | bytes 98336 | tf_op jit(solution)/shard_map/output_swap/ppermute | solution.py:19
  205.2 1.3 place_kernel.1.refs_3_
  207.5 1.6 join_kernel.3.refs_3_
  209.1 1.3 copy-done.1
  210.4 2.1 fc_out_kernel.1
  (141 shorter events, 42.1 us)
Async XLA Ops:
  2.3 16.2 %collective-permute-start = (f32[64,768]{1,0:T(8,128)S(1)}, f32[64,768]{1,0:T(8,128)S(1)}, u32[]{:S(2)}, u32[]{:S(2)}) collective-permute-start(f32[64,768]{1,0:T(8,128)S(1)} %get-tuple-element.127.refs_3_), channel_id=1, source_target_pairs={{0,8},{1,9},{2,10},{3,11},{4,12},{5,13},{6,14},{7,15},{8,0},{9,1},... | collective-permute-start | bytes 589832 | tf_op jit(solution)/shard_map/tokens_swap/ppermute | solution.py:19
  7.2 7.8 %collective-permute-start.5 = (bf16[2,32,63]{2,1,0:T(8,128)(2,1)S(1)}, bf16[2,32,63]{2,1,0:T(8,128)(2,1)S(1)}, u32[]{:S(2)}, u32[]{:S(2)}) collective-permute-start(bf16[2,32,63]{2,1,0:T(8,128)(2,1)S(1)} %pad_maximum_fusion.refs_1_), channel_id=1, source_target_pairs={{0,16},{16,0},{1,17},{17,1},{2,18},{18,2},{3,19},{19,3},{4,20},{20... | collective-permute-start | bytes 24200 | tf_op jit(solution)/shard_map/tables_hop/ppermute | solution.py:23
  10.2 12.4 %collective-permute-start.8 = (bf16[64,768]{1,0:T(8,128)(2,1)S(1)}, bf16[64,768]{1,0:T(8,128)(2,1)S(1)}, u32[]{:S(2)}, u32[]{:S(2)}) collective-permute-start(bf16[64,768]{1,0:T(8,128)(2,1)S(1)} %get-tuple-element.136), channel_id=1, source_target_pairs={{0,8},{1,9},{2,10},{3,11},{4,12},{5,13},{6,14},{7,15},{8,0},{9,1},... | collective-permute-start | bytes 294920 | tf_op jit(solution)/shard_map/cot_swap/ppermute | solution.py:19
  11.4 3.7 %collective-permute-start.1 = (bf16[4,384]{1,0:T(4,128)(2,1)S(1)}, bf16[4,384]{1,0:T(4,128)(2,1)S(1)}, u32[]{:S(2)}, u32[]{:S(2)}) collective-permute-start(bf16[4,384]{1,0:T(4,128)(2,1)S(1)} %reshape.39.refs_3_), channel_id=1, source_target_pairs={{0,16},{16,0},{1,17},{17,1},{2,18},{18,2},{3,19},{19,3},{4,20},{20... | collective-permute-start | bytes 9224 | tf_op jit(solution)/shard_map/small_params/ppermute | solution.py:23
  15.0 9.1 %collective-permute-start.6 = (bf16[192,576]{1,0:T(8,128)(2,1)S(1)}, bf16[192,576]{1,0:T(8,128)(2,1)S(1)}, u32[]{:S(2)}, u32[]{:S(2)}) collective-permute-start(bf16[192,576]{1,0:T(8,128)(2,1)S(1)} %get-tuple-element.134.refs_5_), channel_id=1, source_target_pairs={{0,16},{16,0},{1,17},{17,1},{2,18},{18,2},{3,19},{19,3},{4,20},{20... | collective-permute-start | bytes 663560 | tf_op jit(solution)/shard_map/qkv_weight_hop/ppermute | solution.py:23
  15.8 10.5 %collective-permute-start.7 = (bf16[192,576]{1,0:T(8,128)(2,1)S(1)}, bf16[192,576]{1,0:T(8,128)(2,1)S(1)}, u32[]{:S(2)}, u32[]{:S(2)}) collective-permute-start(bf16[192,576]{1,0:T(8,128)(2,1)S(1)} %get-tuple-element.135.refs_6_), channel_id=1, source_target_pairs={{0,16},{16,0},{1,17},{17,1},{2,18},{18,2},{3,19},{19,3},{4,20},{20... | collective-permute-start | bytes 663560 | tf_op jit(solution)/shard_map/qkv_weight_hop/ppermute | solution.py:23
  19.3 8.2 %collective-permute-start.4 = (bf16[128,768]{1,0:T(8,128)(2,1)S(1)}, bf16[128,768]{1,0:T(8,128)(2,1)S(1)}, u32[]{:S(2)}, u32[]{:S(2)}) collective-permute-start(bf16[128,768]{1,0:T(8,128)(2,1)S(1)} %get-tuple-element.131.refs_1_), channel_id=1, source_target_pairs={{0,6},{1,7},{2,4},{3,5},{4,2},{5,3},{6,0},{7,1},{8,14},{9,15},{10,... | collective-permute-start | bytes 589832 | tf_op jit(solution)/shard_map/normed_gather/ppermute | solution.py:19
  20.4 8.5 %collective-permute-start.3 = (bf16[128,768]{1,0:T(8,128)(2,1)S(1)}, bf16[128,768]{1,0:T(8,128)(2,1)S(1)}, u32[]{:S(2)}, u32[]{:S(2)}) collective-permute-start(bf16[128,768]{1,0:T(8,128)(2,1)S(1)} %get-tuple-element.131.refs_1_), channel_id=1, source_target_pairs={{0,4},{1,5},{2,6},{3,7},{4,0},{5,1},{6,2},{7,3},{8,12},{9,13},{10,... | collective-permute-start | bytes 589832 | tf_op jit(solution)/shard_map/normed_gather/ppermute | solution.py:19
  22.6 6.9 %collective-permute-start.2 = (bf16[128,768]{1,0:T(8,128)(2,1)S(1)}, bf16[128,768]{1,0:T(8,128)(2,1)S(1)}, u32[]{:S(2)}, u32[]{:S(2)}) collective-permute-start(bf16[128,768]{1,0:T(8,128)(2,1)S(1)} %get-tuple-element.131.refs_1_), channel_id=1, source_target_pairs={{0,2},{1,3},{2,0},{3,1},{4,6},{5,7},{6,4},{7,5},{8,10},{9,11},{10,... | collective-permute-start | bytes 589832 | tf_op jit(solution)/shard_map/normed_gather/ppermute | solution.py:19
  30.9 3.2 %collective-permute-start.9 = (bf16[512,384]{1,0:T(8,128)(2,1)S(1)}, bf16[512,384]{1,0:T(8,128)(2,1)S(1)}, u32[]{:S(2)}, u32[]{:S(2)}) collective-permute-start(bf16[512,384]{1,0:T(8,128)(2,1)S(1)} %get-tuple-element.140.refs_2_), channel_id=1, source_target_pairs={{0,1},{1,0},{2,3},{3,2},{4,5},{5,4},{6,7},{7,6},{8,9},{9,8},{10,11... | collective-permute-start | bytes 1179656 | tf_op jit(solution)/shard_map/kv_hop/ppermute | solution.py:19
  31.0 11.1 %collective-permute-start.14 = (bf16[192,768]{1,0:T(8,128)(2,1)S(1)}, bf16[192,768]{1,0:T(8,128)(2,1)S(1)}, u32[]{:S(2)}, u32[]{:S(2)}) collective-permute-start(bf16[192,768]{1,0:T(8,128)(2,1)S(1)} %rows_kernel.1.refs_9_), channel_id=1, source_target_pairs={{0,16},{16,0},{1,17},{17,1},{2,18},{18,2},{3,19},{19,3},{4,20},{20... | collective-permute-start | bytes 884744 | tf_op jit(solution)/shard_map/proj_weight_hop/ppermute | solution.py:23
  32.7 20.9 %collective-permute-start.16 = (bf16[384,768]{1,0:T(8,128)(2,1)S(1)}, bf16[384,768]{1,0:T(8,128)(2,1)S(1)}, u32[]{:S(2)}, u32[]{:S(2)}) collective-permute-start(bf16[384,768]{1,0:T(8,128)(2,1)S(1)} %copy-done.6), channel_id=1, source_target_pairs={{0,16},{16,0},{1,17},{17,1},{2,18},{18,2},{3,19},{19,3},{4,20},{20... | collective-permute-start | bytes 1769480 | tf_op jit(solution)/shard_map/fc1_weight_hop/ppermute | solution.py:23
  33.1 9.1 %collective-permute-start.10 = (bf16[128,768]{1,0:T(8,128)(2,1)S(1)}, bf16[128,768]{1,0:T(8,128)(2,1)S(1)}, u32[]{:S(2)}, u32[]{:S(2)}) collective-permute-start(bf16[128,768]{1,0:T(8,128)(2,1)S(1)} %stack_kernel.1.refs_3_.refs_5_), channel_id=1, source_target_pairs={{0,2},{1,3},{2,0},{3,1},{4,6},{5,7},{6,4},{7,5},{8,10},{9,11},{10,... | collective-permute-start | bytes 589832 | tf_op jit(solution)/shard_map/cot_row/ppermute | solution.py:19
  42.1 11.4 %collective-permute-start.15 = (bf16[192,768]{1,0:T(8,128)(2,1)S(1)}, bf16[192,768]{1,0:T(8,128)(2,1)S(1)}, u32[]{:S(2)}, u32[]{:S(2)}) collective-permute-start(bf16[192,768]{1,0:T(8,128)(2,1)S(1)} %collective-permute-done.14.refs_6_), channel_id=1, source_target_pairs={{0,1},{1,0},{2,3},{3,2},{4,5},{5,4},{6,7},{7,6},{8,9},{9,8},{10,11... | collective-permute-start | bytes 884744 | tf_op jit(solution)/shard_map/proj_weight_core/ppermute | solution.py:19
  42.2 4.5 %collective-permute-start.11 = (bf16[128,192]{1,0:T(8,128)(2,1)S(1)}, bf16[128,192]{1,0:T(8,128)(2,1)S(1)}, u32[]{:S(2)}, u32[]{:S(2)}) collective-permute-start(bf16[128,192]{1,0:T(8,128)(2,1)S(1)} %get-tuple-element.149), channel_id=1, source_target_pairs={{0,2},{1,3},{2,0},{3,1},{4,6},{5,7},{6,4},{7,5},{8,10},{9,11},{10,... | collective-permute-start | bytes 147464 | tf_op jit(solution)/shard_map/attended_hop/ppermute | solution.py:19
  43.2 4.3 %collective-permute-start.12 = (bf16[128,192]{1,0:T(8,128)(2,1)S(1)}, bf16[128,192]{1,0:T(8,128)(2,1)S(1)}, u32[]{:S(2)}, u32[]{:S(2)}) collective-permute-start(bf16[128,192]{1,0:T(8,128)(2,1)S(1)} %get-tuple-element.150), channel_id=1, source_target_pairs={{0,4},{1,5},{2,6},{3,7},{4,0},{5,1},{6,2},{7,3},{8,12},{9,13},{10,... | collective-permute-start | bytes 147464 | tf_op jit(solution)/shard_map/attended_hop/ppermute | solution.py:19
  45.0 5.2 %collective-permute-start.13 = (bf16[128,192]{1,0:T(8,128)(2,1)S(1)}, bf16[128,192]{1,0:T(8,128)(2,1)S(1)}, u32[]{:S(2)}, u32[]{:S(2)}) collective-permute-start(bf16[128,192]{1,0:T(8,128)(2,1)S(1)} %get-tuple-element.151), channel_id=1, source_target_pairs={{0,6},{1,7},{2,4},{3,5},{4,2},{5,3},{6,0},{7,1},{8,14},{9,15},{10,... | collective-permute-start | bytes 147464 | tf_op jit(solution)/shard_map/attended_hop/ppermute | solution.py:19
  50.2 15.5 %collective-permute-start.22 = (bf16[768,384]{1,0:T(8,128)(2,1)S(1)}, bf16[768,384]{1,0:T(8,128)(2,1)S(1)}, u32[]{:S(2)}, u32[]{:S(2)}) collective-permute-start(bf16[768,384]{1,0:T(8,128)(2,1)S(1)} %copy-done.7), channel_id=1, source_target_pairs={{0,16},{16,0},{1,17},{17,1},{2,18},{18,2},{3,19},{19,3},{4,20},{20... | collective-permute-start | bytes 1769480 | tf_op jit(solution)/shard_map/fc2_weight_hop/ppermute | solution.py:23
  54.8 6.1 %collective-permute-start.17 = (bf16[128,768]{1,0:T(8,128)(2,1)S(1)}, bf16[128,768]{1,0:T(8,128)(2,1)S(1)}, u32[]{:S(2)}, u32[]{:S(2)}) collective-permute-start(bf16[128,768]{1,0:T(8,128)(2,1)S(1)} %get-tuple-element.157.refs_1_), channel_id=1, source_target_pairs={{0,2},{1,3},{2,0},{3,1},{4,6},{5,7},{6,4},{7,5},{8,10},{9,11},{10,... | collective-permute-start | bytes 589832 | tf_op jit(solution)/shard_map/normed_two_row/ppermute | solution.py:19
  55.9 5.5 %collective-permute-start.18 = (bf16[128,768]{1,0:T(8,128)(2,1)S(1)}, bf16[128,768]{1,0:T(8,128)(2,1)S(1)}, u32[]{:S(2)}, u32[]{:S(2)}) collective-permute-start(bf16[128,768]{1,0:T(8,128)(2,1)S(1)} %get-tuple-element.157.refs_1_), channel_id=1, source_target_pairs={{0,1},{1,0},{2,3},{3,2},{4,5},{5,4},{6,7},{7,6},{8,9},{9,8},{10,11... | collective-permute-start | bytes 589832 | tf_op jit(solution)/shard_map/normed_two_core/ppermute | solution.py:19
  60.8 4.9 %collective-permute-start.20 = (bf16[128,768]{1,0:T(8,128)(2,1)S(1)}, bf16[128,768]{1,0:T(8,128)(2,1)S(1)}, u32[]{:S(2)}, u32[]{:S(2)}) collective-permute-start(bf16[128,768]{1,0:T(8,128)(2,1)S(1)} %stack_kernel.1.refs_3_.refs_5_), channel_id=1, source_target_pairs={{0,1},{1,0},{2,3},{3,2},{4,5},{5,4},{6,7},{7,6},{8,9},{9,8},{10,11... | collective-permute-start | bytes 589832 | tf_op jit(solution)/shard_map/cot_core/ppermute | solution.py:19
  60.8 4.9 %collective-permute-start.21 = (bf16[128,768]{1,0:T(8,128)(2,1)S(1)}, bf16[128,768]{1,0:T(8,128)(2,1)S(1)}, u32[]{:S(2)}, u32[]{:S(2)}) collective-permute-start(bf16[128,768]{1,0:T(8,128)(2,1)S(1)} %collective-permute-done.10.refs_6_), channel_id=1, source_target_pairs={{0,1},{1,0},{2,3},{3,2},{4,5},{5,4},{6,7},{7,6},{8,9},{9,8},{10,11... | collective-permute-start | bytes 589832 | tf_op jit(solution)/shard_map/cot_core/ppermute | solution.py:19
  61.4 4.4 %collective-permute-start.19 = (bf16[128,768]{1,0:T(8,128)(2,1)S(1)}, bf16[128,768]{1,0:T(8,128)(2,1)S(1)}, u32[]{:S(2)}, u32[]{:S(2)}) collective-permute-start(bf16[128,768]{1,0:T(8,128)(2,1)S(1)} %collective-permute-done.17.refs_2_), channel_id=1, source_target_pairs={{0,1},{1,0},{2,3},{3,2},{4,5},{5,4},{6,7},{7,6},{8,9},{9,8},{10,11... | collective-permute-start | bytes 589832 | tf_op jit(solution)/shard_map/normed_two_core/ppermute | solution.py:19
  70.2 1.5 collective-permute-start.24
  70.3 7.7 %collective-permute-start.23 = (bf16[128,768]{1,0:T(8,128)(2,1)S(1)}, bf16[128,768]{1,0:T(8,128)(2,1)S(1)}, u32[]{:S(2)}, u32[]{:S(2)}) collective-permute-start(bf16[128,768]{1,0:T(8,128)(2,1)S(1)} %get-tuple-element.164), channel_id=1, source_target_pairs={{0,1},{1,0},{2,3},{3,2},{4,5},{5,4},{6,7},{7,6},{8,9},{9,8},{10,11... | collective-permute-start | bytes 589832 | tf_op jit(solution)/shard_map/dnorm_core/ppermute | solution.py:19
  71.8 7.0 %collective-permute-start.25 = (bf16[128,768]{1,0:T(8,128)(2,1)S(1)}, bf16[128,768]{1,0:T(8,128)(2,1)S(1)}, u32[]{:S(2)}, u32[]{:S(2)}) collective-permute-start(bf16[128,768]{1,0:T(8,128)(2,1)S(1)} %add_kernel.5.refs_3_), channel_id=1, source_target_pairs={{0,2},{1,3},{2,0},{3,1},{4,6},{5,7},{6,4},{7,5},{8,10},{9,11},{10,... | collective-permute-start | bytes 589832 | tf_op jit(solution)/shard_map/dnorm_row/ppermute | solution.py:19
  74.6 20.4 %collective-permute-start.31 = (bf16[384,768]{1,0:T(8,128)(2,1)S(1)}, bf16[384,768]{1,0:T(8,128)(2,1)S(1)}, u32[]{:S(2)}, u32[]{:S(2)}) collective-permute-start(bf16[384,768]{1,0:T(8,128)(2,1)S(1)} %get-tuple-element.171.refs_3_), channel_id=1, source_target_pairs={{0,16},{16,0},{1,17},{17,1},{2,18},{18,2},{3,19},{19,3},{4,20},{20... | collective-permute-start | bytes 1769480 | tf_op jit(solution)/shard_map/fc1_dp/ppermute | solution.py:23
  79.7 4.7 %collective-permute-start.26 = (bf16[128,192]{1,0:T(8,128)(2,1)S(1)}, bf16[128,192]{1,0:T(8,128)(2,1)S(1)}, u32[]{:S(2)}, u32[]{:S(2)}) collective-permute-start(bf16[128,192]{1,0:T(8,128)(2,1)S(1)} %get-tuple-element.179), channel_id=1, source_target_pairs={{0,2},{1,3},{2,0},{3,1},{4,6},{5,7},{6,4},{7,5},{8,10},{9,11},{10,... | collective-permute-start | bytes 147464 | tf_op jit(solution)/shard_map/grad_heads_hop/ppermute | solution.py:19
  81.0 4.8 %collective-permute-start.27 = (bf16[128,192]{1,0:T(8,128)(2,1)S(1)}, bf16[128,192]{1,0:T(8,128)(2,1)S(1)}, u32[]{:S(2)}, u32[]{:S(2)}) collective-permute-start(bf16[128,192]{1,0:T(8,128)(2,1)S(1)} %get-tuple-element.180), channel_id=1, source_target_pairs={{0,4},{1,5},{2,6},{3,7},{4,0},{5,1},{6,2},{7,3},{8,12},{9,13},{10,... | collective-permute-start | bytes 147464 | tf_op jit(solution)/shard_map/grad_heads_hop/ppermute | solution.py:19
  82.9 5.2 %collective-permute-start.28 = (bf16[128,192]{1,0:T(8,128)(2,1)S(1)}, bf16[128,192]{1,0:T(8,128)(2,1)S(1)}, u32[]{:S(2)}, u32[]{:S(2)}) collective-permute-start(bf16[128,192]{1,0:T(8,128)(2,1)S(1)} %get-tuple-element.181), channel_id=1, source_target_pairs={{0,6},{1,7},{2,4},{3,5},{4,2},{5,3},{6,0},{7,1},{8,14},{9,15},{10,... | collective-permute-start | bytes 147464 | tf_op jit(solution)/shard_map/grad_heads_hop/ppermute | solution.py:19
  88.1 11.7 %collective-permute-start.34 = (bf16[384,768]{1,0:T(8,128)(2,1)S(1)}, bf16[384,768]{1,0:T(8,128)(2,1)S(1)}, u32[]{:S(2)}, u32[]{:S(2)}) collective-permute-start(bf16[384,768]{1,0:T(8,128)(2,1)S(1)} %get-tuple-element.191.refs_2_), channel_id=1, source_target_pairs={{0,1},{1,0},{2,3},{3,2},{4,5},{5,4},{6,7},{7,6},{8,9},{9,8},{10,11... | collective-permute-start | bytes 1769480 | tf_op jit(solution)/shard_map/proj_core/ppermute | solution.py:19
  88.9 6.1 %collective-permute-start.29 = (bf16[256,768]{1,0:T(8,128)(2,1)S(1)}, bf16[256,768]{1,0:T(8,128)(2,1)S(1)}, u32[]{:S(2)}, u32[]{:S(2)}) collective-permute-start(bf16[256,768]{1,0:T(8,128)(2,1)S(1)} %get-tuple-element.182), channel_id=1, source_target_pairs={{0,1},{1,0},{2,3},{3,2},{4,5},{5,4},{6,7},{7,6},{8,9},{9,8},{10,11... | collective-permute-start | bytes 1179656 | tf_op jit(solution)/shard_map/fed_core/ppermute | solution.py:19
  89.5 15.9 %collective-permute-start.33 = (bf16[768,384]{1,0:T(8,128)(2,1)S(1)}, bf16[768,384]{1,0:T(8,128)(2,1)S(1)}, u32[]{:S(2)}, u32[]{:S(2)}) collective-permute-start(bf16[768,384]{1,0:T(8,128)(2,1)S(1)} %get-tuple-element.172.refs_7_), channel_id=1, source_target_pairs={{0,16},{16,0},{1,17},{17,1},{2,18},{18,2},{3,19},{19,3},{4,20},{20... | collective-permute-start | bytes 1769480 | tf_op jit(solution)/shard_map/fc2_dp/ppermute | solution.py:23
  95.7 10.4 %collective-permute-start.32 = (bf16[192,768]{1,0:T(8,128)(2,1)S(1)}, bf16[192,768]{1,0:T(8,128)(2,1)S(1)}, u32[]{:S(2)}, u32[]{:S(2)}) collective-permute-start(bf16[192,768]{1,0:T(8,128)(2,1)S(1)} %get-tuple-element.188.refs_12_), channel_id=1, source_target_pairs={{0,4},{1,5},{2,6},{3,7},{4,0},{5,1},{6,2},{7,3},{8,12},{9,13},{10,... | collective-permute-start | bytes 884744 | tf_op jit(solution)/shard_map/fc1_near_sum/ppermute | solution.py:19
  99.6 1.4 collective-permute-start.36
  104.9 1.7 collective-permute-start.39
  108.5 2.9 %collective-permute-start.41 = (bf16[208,576]{1,0:T(8,128)(2,1)S(1)}, bf16[208,576]{1,0:T(8,128)(2,1)S(1)}, u32[]{:S(2)}, u32[]{:S(2)}) collective-permute-start(bf16[208,576]{1,0:T(8,128)(2,1)S(1)} %get-tuple-element.213), channel_id=1, source_target_pairs={{0,1},{1,0},{2,3},{3,2},{4,5},{5,4},{6,7},{7,6},{8,9},{9,8},{10,11... | collective-permute-start | bytes 718856 | tf_op jit(solution)/shard_map/qkv_core/ppermute | solution.py:19
  108.9 2.4 %collective-permute-start.40 = (bf16[208,576]{1,0:T(8,128)(2,1)S(1)}, bf16[208,576]{1,0:T(8,128)(2,1)S(1)}, u32[]{:S(2)}, u32[]{:S(2)}) collective-permute-start(bf16[208,576]{1,0:T(8,128)(2,1)S(1)} %get-tuple-element.212.refs_3_), channel_id=1, source_target_pairs={{0,1},{1,0},{2,3},{3,2},{4,5},{5,4},{6,7},{7,6},{8,9},{9,8},{10,11... | collective-permute-start | bytes 718856 | tf_op jit(solution)/shard_map/qkv_core/ppermute | solution.py:19
  110.4 32.7 %collective-permute-start.47 = (bf16[256,768]{1,0:T(8,128)(2,1)S(1)}, bf16[256,768]{1,0:T(8,128)(2,1)S(1)}, u32[]{:S(2)}, u32[]{:S(2)}) collective-permute-start(bf16[256,768]{1,0:T(8,128)(2,1)S(1)} %get-tuple-element.224), channel_id=1, source_target_pairs={{0,2},{1,3},{2,0},{3,1},{4,6},{5,7},{6,4},{7,5},{8,10},{9,11},{10,... | collective-permute-start | bytes 1179656 | tf_op jit(solution)/shard_map/dnormed_row/ppermute | solution.py:19
  111.4 6.7 %collective-permute-start.43 = (bf16[112,576]{1,0:T(8,128)(2,1)S(1)}, bf16[112,576]{1,0:T(8,128)(2,1)S(1)}, u32[]{:S(2)}, u32[]{:S(2)}) collective-permute-start(bf16[112,576]{1,0:T(8,128)(2,1)S(1)} %get-tuple-element.219), channel_id=1, source_target_pairs={{0,16},{16,0},{1,17},{17,1},{2,18},{18,2},{3,19},{19,3},{4,20},{20... | collective-permute-start | bytes 387080 | tf_op jit(solution)/shard_map/qkv_dp/ppermute | solution.py:23
  112.2 8.1 %collective-permute-start.42 = (bf16[112,576]{1,0:T(8,128)(2,1)S(1)}, bf16[112,576]{1,0:T(8,128)(2,1)S(1)}, u32[]{:S(2)}, u32[]{:S(2)}) collective-permute-start(bf16[112,576]{1,0:T(8,128)(2,1)S(1)} %get-tuple-element.218.refs_3_), channel_id=1, source_target_pairs={{0,16},{16,0},{1,17},{17,1},{2,18},{18,2},{3,19},{19,3},{4,20},{20... | collective-permute-start | bytes 387080 | tf_op jit(solution)/shard_map/qkv_dp/ppermute | solution.py:23
  113.5 28.9 %collective-permute-start.38 = (bf16[384,384]{1,0:T(8,128)(2,1)S(1)}, bf16[384,384]{1,0:T(8,128)(2,1)S(1)}, u32[]{:S(2)}, u32[]{:S(2)}) collective-permute-start(bf16[384,384]{1,0:T(8,128)(2,1)S(1)} %get-tuple-element.197.refs_3_), channel_id=1, source_target_pairs={{0,4},{1,5},{2,6},{3,7},{4,0},{5,1},{6,2},{7,3},{8,12},{9,13},{10,... | collective-permute-start | bytes 884744 | tf_op jit(solution)/shard_map/fc2_near_sum/ppermute | solution.py:19
  114.9 32.3 %collective-permute-start.46 = (bf16[192,768]{1,0:T(8,128)(2,1)S(1)}, bf16[192,768]{1,0:T(8,128)(2,1)S(1)}, u32[]{:S(2)}, u32[]{:S(2)}) collective-permute-start(bf16[192,768]{1,0:T(8,128)(2,1)S(1)} %get-tuple-element.194.refs_12_), channel_id=1, source_target_pairs={{0,2},{1,3},{2,0},{3,1},{4,6},{5,7},{6,4},{7,5},{8,10},{9,11},{10,... | collective-permute-start | bytes 884744 | tf_op jit(solution)/shard_map/proj_row/ppermute | solution.py:19
  120.3 27.0 %collective-permute-start.45 = (bf16[224,576]{1,0:T(8,128)(2,1)S(1)}, bf16[224,576]{1,0:T(8,128)(2,1)S(1)}, u32[]{:S(2)}, u32[]{:S(2)}) collective-permute-start(bf16[224,576]{1,0:T(8,128)(2,1)S(1)} %qkv_total_kernel.1.refs_3_.refs_0_), channel_id=1, source_target_pairs={{0,8},{1,9},{2,10},{3,11},{4,12},{5,13},{6,14},{7,15},{8,0},{9,1},... | collective-permute-start | bytes 774152 | tf_op jit(solution)/shard_map/qkv_far/ppermute | solution.py:19
  123.8 18.6 %collective-permute-start.37 = (bf16[96,768]{1,0:T(8,128)(2,1)S(1)}, bf16[96,768]{1,0:T(8,128)(2,1)S(1)}, u32[]{:S(2)}, u32[]{:S(2)}) collective-permute-start(bf16[96,768]{1,0:T(8,128)(2,1)S(1)} %get-tuple-element.199.refs_17_), channel_id=1, source_target_pairs={{0,8},{1,9},{2,10},{3,11},{4,12},{5,13},{6,14},{7,15},{8,0},{9,1},... | collective-permute-start | bytes 442376 | tf_op jit(solution)/shard_map/fc1_far_sum/ppermute | solution.py:19
  143.0 9.1 %collective-permute-start.44 = (bf16[192,384]{1,0:T(8,128)(2,1)S(1)}, bf16[192,384]{1,0:T(8,128)(2,1)S(1)}, u32[]{:S(2)}, u32[]{:S(2)}) collective-permute-start(bf16[192,384]{1,0:T(8,128)(2,1)S(1)} %get-tuple-element.221.refs_2_), channel_id=1, source_target_pairs={{0,8},{1,9},{2,10},{3,11},{4,12},{5,13},{6,14},{7,15},{8,0},{9,1},... | collective-permute-start | bytes 442376 | tf_op jit(solution)/shard_map/fc2_far_sum/ppermute | solution.py:19
  143.2 11.3 %collective-permute-start.50 = (bf16[128,768]{1,0:T(8,128)(2,1)S(1)}, bf16[128,768]{1,0:T(8,128)(2,1)S(1)}, u32[]{:S(2)}, u32[]{:S(2)}) collective-permute-start(bf16[128,768]{1,0:T(8,128)(2,1)S(1)} %tail_add_kernel.3.refs_2_), channel_id=1, source_target_pairs={{0,4},{1,5},{2,6},{3,7},{4,0},{5,1},{6,2},{7,3},{8,12},{9,13},{10,... | collective-permute-start | bytes 589832 | tf_op jit(solution)/shard_map/dnormed_near/ppermute | solution.py:19
  147.4 20.4 %collective-permute-start.55 = (bf16[224,576]{1,0:T(8,128)(2,1)S(1)}, bf16[224,576]{1,0:T(8,128)(2,1)S(1)}, u32[]{:S(2)}, u32[]{:S(2)}) collective-permute-start(bf16[224,576]{1,0:T(8,128)(2,1)S(1)} %add_kernel.6.refs_5_.refs_1_), channel_id=1, source_target_pairs={{0,6},{1,7},{2,4},{3,5},{4,2},{5,3},{6,0},{7,1},{8,14},{9,15},{10,... | collective-permute-start | bytes 774152 | tf_op jit(solution)/shard_map/qkv_all/ppermute | solution.py:19
  148.3 25.3 %collective-permute-start.54 = (bf16[224,576]{1,0:T(8,128)(2,1)S(1)}, bf16[224,576]{1,0:T(8,128)(2,1)S(1)}, u32[]{:S(2)}, u32[]{:S(2)}) collective-permute-start(bf16[224,576]{1,0:T(8,128)(2,1)S(1)} %add_kernel.6.refs_5_.refs_1_), channel_id=1, source_target_pairs={{0,4},{1,5},{2,6},{3,7},{4,0},{5,1},{6,2},{7,3},{8,12},{9,13},{10,... | collective-permute-start | bytes 774152 | tf_op jit(solution)/shard_map/qkv_all/ppermute | solution.py:19
  150.3 6.1 %collective-permute-start.49 = (bf16[96,768]{1,0:T(8,128)(2,1)S(1)}, bf16[96,768]{1,0:T(8,128)(2,1)S(1)}, u32[]{:S(2)}, u32[]{:S(2)}) collective-permute-start(bf16[96,768]{1,0:T(8,128)(2,1)S(1)} %get-tuple-element.225.refs_2_), channel_id=1, source_target_pairs={{0,16},{16,0},{1,17},{17,1},{2,18},{18,2},{3,19},{19,3},{4,20},{20... | collective-permute-start | bytes 442376 | tf_op jit(solution)/shard_map/proj_dp/ppermute | solution.py:23
  152.2 22.6 %collective-permute-start.53 = (bf16[224,576]{1,0:T(8,128)(2,1)S(1)}, bf16[224,576]{1,0:T(8,128)(2,1)S(1)}, u32[]{:S(2)}, u32[]{:S(2)}) collective-permute-start(bf16[224,576]{1,0:T(8,128)(2,1)S(1)} %add_kernel.6.refs_5_.refs_1_), channel_id=1, source_target_pairs={{0,2},{1,3},{2,0},{3,1},{4,6},{5,7},{6,4},{7,5},{8,10},{9,11},{10,... | collective-permute-start | bytes 774152 | tf_op jit(solution)/shard_map/qkv_all/ppermute | solution.py:19
  154.5 27.4 %collective-permute-start.48 = (bf16[192,768]{1,0:T(8,128)(2,1)S(1)}, bf16[192,768]{1,0:T(8,128)(2,1)S(1)}, u32[]{:S(2)}, u32[]{:S(2)}) collective-permute-start(bf16[192,768]{1,0:T(8,128)(2,1)S(1)} %fc_pack_kernel.1.refs_7_.refs_1_), channel_id=1, source_target_pairs={{0,8},{1,9},{2,10},{3,11},{4,12},{5,13},{6,14},{7,15},{8,0},{9,1},... | collective-permute-start | bytes 884744 | tf_op jit(solution)/shard_map/fc_far_all/ppermute | solution.py:19
  156.5 21.3 %collective-permute-start.51 = (bf16[96,768]{1,0:T(8,128)(2,1)S(1)}, bf16[96,768]{1,0:T(8,128)(2,1)S(1)}, u32[]{:S(2)}, u32[]{:S(2)}) collective-permute-start(bf16[96,768]{1,0:T(8,128)(2,1)S(1)} %add_kernel.7.refs_6_.refs_0_), channel_id=1, source_target_pairs={{0,4},{1,5},{2,6},{3,7},{4,0},{5,1},{6,2},{7,3},{8,12},{9,13},{10,... | collective-permute-start | bytes 442376 | tf_op jit(solution)/shard_map/proj_near/ppermute | solution.py:19
  167.8 8.6 %collective-permute-start.52 = (bf16[64,768]{1,0:T(8,128)(2,1)S(1)}, bf16[64,768]{1,0:T(8,128)(2,1)S(1)}, u32[]{:S(2)}, u32[]{:S(2)}) collective-permute-start(bf16[64,768]{1,0:T(8,128)(2,1)S(1)} %get-tuple-element.229), channel_id=1, source_target_pairs={{0,8},{1,9},{2,10},{3,11},{4,12},{5,13},{6,14},{7,15},{8,0},{9,1},... | collective-permute-start | bytes 294920 | tf_op jit(solution)/shard_map/tokens_grad_swap/ppermute | solution.py:19
  173.6 11.6 %collective-permute-start.30 = (bf16[128,768]{1,0:T(8,128)(2,1)S(1)}, bf16[128,768]{1,0:T(8,128)(2,1)S(1)}, u32[]{:S(2)}, u32[]{:S(2)}) collective-permute-start(bf16[128,768]{1,0:T(8,128)(2,1)S(1)} %tail_add_kernel.2.refs_3_), channel_id=1, source_target_pairs={{0,2},{1,3},{2,0},{3,1},{4,6},{5,7},{6,4},{7,5},{8,10},{9,11},{10,... | collective-permute-start | bytes 589832 | tf_op jit(solution)/shard_map/fed_row/ppermute | solution.py:19
  178.8 9.0 %collective-permute-start.57 = (bf16[96,768]{1,0:T(8,128)(2,1)S(1)}, bf16[96,768]{1,0:T(8,128)(2,1)S(1)}, u32[]{:S(2)}, u32[]{:S(2)}) collective-permute-start(bf16[96,768]{1,0:T(8,128)(2,1)S(1)} %add_kernel.8.refs_3_.refs_0_), channel_id=1, source_target_pairs={{0,8},{1,9},{2,10},{3,11},{4,12},{5,13},{6,14},{7,15},{8,0},{9,1},... | collective-permute-start | bytes 442376 | tf_op jit(solution)/shard_map/proj_far/ppermute | solution.py:19
  181.8 6.2 %collective-permute-start.59 = (bf16[224,576]{1,0:T(8,128)(2,1)S(1)}, bf16[224,576]{1,0:T(8,128)(2,1)S(1)}, u32[]{:S(2)}, u32[]{:S(2)}) collective-permute-start(bf16[224,576]{1,0:T(8,128)(2,1)S(1)} %add_kernel.6.refs_5_.refs_1_), channel_id=1, source_target_pairs={{0,1},{1,0},{2,3},{3,2},{4,5},{5,4},{6,7},{7,6},{8,9},{9,8},{10,11... | collective-permute-start | bytes 774152 | tf_op jit(solution)/shard_map/qkv_core_all/ppermute | solution.py:19
  182.4 26.7 %collective-permute-start.64 = (bf16[384,768]{1,0:T(8,128)(2,1)S(1)}, bf16[384,768]{1,0:T(8,128)(2,1)S(1)}, u32[]{:S(2)}, u32[]{:S(2)}) collective-permute-start(bf16[384,768]{1,0:T(8,128)(2,1)S(1)} %fc_join_kernel.1.refs_6_.refs_1_), channel_id=1, source_target_pairs={{0,4},{1,5},{2,6},{3,7},{4,0},{5,1},{6,2},{7,3},{8,12},{9,13},{10,... | collective-permute-start | bytes 1769480 | tf_op jit(solution)/shard_map/fc_near_all/ppermute | solution.py:19
  185.0 3.7 %collective-permute-start.62 = (bf16[224,576]{1,0:T(8,128)(2,1)S(1)}, bf16[224,576]{1,0:T(8,128)(2,1)S(1)}, u32[]{:S(2)}, u32[]{:S(2)}) collective-permute-start(bf16[224,576]{1,0:T(8,128)(2,1)S(1)} %collective-permute-done.55.refs_4_), channel_id=1, source_target_pairs={{0,1},{1,0},{2,3},{3,2},{4,5},{5,4},{6,7},{7,6},{8,9},{9,8},{10,11... | collective-permute-start | bytes 774152 | tf_op jit(solution)/shard_map/qkv_core_all/ppermute | solution.py:19
  185.2 3.5 %collective-permute-start.61 = (bf16[224,576]{1,0:T(8,128)(2,1)S(1)}, bf16[224,576]{1,0:T(8,128)(2,1)S(1)}, u32[]{:S(2)}, u32[]{:S(2)}) collective-permute-start(bf16[224,576]{1,0:T(8,128)(2,1)S(1)} %collective-permute-done.54.refs_3_), channel_id=1, source_target_pairs={{0,1},{1,0},{2,3},{3,2},{4,5},{5,4},{6,7},{7,6},{8,9},{9,8},{10,11... | collective-permute-start | bytes 774152 | tf_op jit(solution)/shard_map/qkv_core_all/ppermute | solution.py:19
  187.8 1.6 collective-permute-start.60
  188.0 6.3 %collective-permute-start.58 = (bf16[96,768]{1,0:T(8,128)(2,1)S(1)}, bf16[96,768]{1,0:T(8,128)(2,1)S(1)}, u32[]{:S(2)}, u32[]{:S(2)}) collective-permute-start(bf16[96,768]{1,0:T(8,128)(2,1)S(1)} %add_kernel.9.refs_9_.refs_1_), channel_id=1, source_target_pairs={{0,2},{1,3},{2,0},{3,1},{4,6},{5,7},{6,4},{7,5},{8,10},{9,11},{10,... | collective-permute-start | bytes 442376 | tf_op jit(solution)/shard_map/proj_all_row/ppermute | solution.py:19
  196.9 9.6 %collective-permute-start.63 = (bf16[192,768]{1,0:T(8,128)(2,1)S(1)}, bf16[192,768]{1,0:T(8,128)(2,1)S(1)}, u32[]{:S(2)}, u32[]{:S(2)}) collective-permute-start(bf16[192,768]{1,0:T(8,128)(2,1)S(1)} %join_kernel.2.refs_4_.refs_1_), channel_id=1, source_target_pairs={{0,1},{1,0},{2,3},{3,2},{4,5},{5,4},{6,7},{7,6},{8,9},{9,8},{10,11... | collective-permute-start | bytes 884744 | tf_op jit(solution)/shard_map/proj_all_core/ppermute | solution.py:19
  196.9 8.2 %collective-permute-start.56 = (bf16[64,768]{1,0:T(8,128)(2,1)S(1)}, bf16[64,768]{1,0:T(8,128)(2,1)S(1)}, u32[]{:S(2)}, u32[]{:S(2)}) collective-permute-start(bf16[64,768]{1,0:T(8,128)(2,1)S(1)} %get-tuple-element.232), channel_id=1, source_target_pairs={{0,8},{1,9},{2,10},{3,11},{4,12},{5,13},{6,14},{7,15},{8,0},{9,1},... | collective-permute-start | bytes 294920 | tf_op jit(solution)/shard_map/output_swap/ppermute | solution.py:19
  (11 other events, 48.3 us)

commit v3 on v2

v3 whole, which is shorter than its diff:
```python
import math
import types

import jax
import jax.numpy as jnp
from jax import lax
from jax.experimental import pallas as pl
from jax.experimental.pallas import tpu as pltpu
from jax.sharding import PartitionSpec as P

EPS = 1e-06
LOW = jnp.bfloat16
FULL = jnp.float32
LANES = 128
CORE, ROW, NEAR, FAR = 1, 2, 4, 8


def hop(value, bits):
    count = lax.axis_size("seq") * lax.axis_size("tp")
    return lax.ppermute(value, ("seq", "tp"), [(i, i ^ bits) for i in range(count)])


def swap_dp(value):
    return lax.ppermute(value, "dp", [(0, 1), (1, 0)])


def pair_dp(value, axis):
    if lax.axis_size("dp") == 2:
        return value, swap_dp(value), lax.axis_index("dp")
    whole = lax.all_gather(value, "dp", axis=axis, tiled=True)
    low, high = jnp.split(whole, 2, axis=axis)
    return low, high, jnp.int32(0)


def after(value, *events):
    return lax.optimization_barrier((value, *events))[0]


def piece(value, index, size, axis):
    return lax.dynamic_slice_in_dim(value, index * size, size, axis)


def canon(blocks, index, axis):
    odd = (index & 1) == 1
    upper = (index & 2) == 2
    b = [
        jnp.where(odd, blocks[k ^ 1], blocks[k])
        for k in range(4)
    ]
    return jnp.concatenate([jnp.where(upper, b[k ^ 2], b[k]) for k in range(4)], axis=axis)


def dot_nn(a, b):
    return lax.dot_general(a, b, (((1,), (0,)), ((), ())), preferred_element_type=FULL)


def dot_nt(a, b):
    return lax.dot_general(a, b, (((1,), (1,)), ((), ())), preferred_element_type=FULL)


def dot_tn(a, b):
    return lax.dot_general(a, b, (((0,), (0,)), ((), ())), preferred_element_type=FULL)


def in_order():
    before = []

    def call(kernel, outs, scratch=(), smem=0, extra=2, wait=(), written=False):
        def run(*args):
            held = sum(a.size * jnp.dtype(a.dtype).itemsize for a in (*args, *outs))
            held += sum(
                math.prod(a.shape) * jnp.dtype(a.dtype).itemsize
                for a in scratch
                if a.memory_space == pltpu.VMEM
            )
            used = len(args)
            events = (*before, *wait)

            def body(*refs):
                rest = refs[used + len(events) :]
                if written:
                    rest[0][...] = jnp.zeros_like(rest[0])
                    rest = rest[1:]
                kernel(*refs[:used], *rest)

            vmem = pl.BlockSpec(memory_space=pltpu.VMEM)
            out_specs = [vmem] * len(outs)
            out_shape = list(outs)
            if written:
                out_specs = [vmem, pl.BlockSpec(memory_space=pltpu.HBM)]
                out_shape = [shape((8, LANES), FULL), *outs]
            results = pl.pallas_call(
                body,
                name=kernel.__qualname__.split(".")[0],
                out_shape=out_shape,
                in_specs=[pl.BlockSpec(memory_space=pltpu.SMEM)] * smem
                + [vmem] * (used - smem)
                + [pl.BlockSpec(memory_space=pl.ANY)] * len(events),
                out_specs=out_specs,
                scratch_shapes=scratch,
                compiler_params=pltpu.CompilerParams(vmem_limit_bytes=held + extra * 2**20),
                cost_estimate=pl.CostEstimate(flops=0, bytes_accessed=0, transcendentals=0),
            )(*args, *events)
            before[:] = [min(results, key=lambda r: r.size)]
            return results[-1] if written else results

        return run

    return call


def shape(dims, kind):
    return jax.ShapeDtypeStruct(dims, kind)


def normal(values):
    center = values - jnp.mean(values, axis=-1, keepdims=True)
    scale = lax.rsqrt(jnp.mean(center * center, axis=-1, keepdims=True) + EPS)
    return center * scale, scale


def pick_kernel(ids, array, mine, other):
    mine[...] = array[ids[3]]
    other[...] = array[1 - ids[3]]


def stack_kernel(*refs):
    out, start = refs[-1], 0
    for ref in refs[:-1]:
        out[start : start + ref.shape[0], :] = ref[...]
        start += ref.shape[0]


def pack_kernel(share, heads):
    def kernel(ids, weight, out):
        width = weight.shape[1] // 3
        head = share // heads
        for g in range(width // share):

            @pl.when(ids[1] == g)
            def _():
                def move(at_col, first):
                    out[:, at_col : at_col + head] = weight[:, first : first + head]

                for h in range(heads):
                    first = g * share + h * head
                    move(2 * h * head, width + first)
                    move((2 * h + 1) * head, 2 * width + first)
                    move(2 * share + h * head, first)

    return kernel


def rows_kernel(ids, array, out):
    out[...] = array[at(ids[2], out.shape[0]), :]


def fill_rows(ids, out, mine, other, other_two):
    half = mine.shape[0]
    out[at(ids[0], half), :] = mine[...]
    if other.shape[0] == half:
        out[at(1 - ids[0], half), :] = other[...]
        return
    size = half // 2
    out[at((1 - ids[0]) * 2 + ids[2], size), :] = other[...]
    out[at((1 - ids[0]) * 2 + 1 - ids[2], size), :] = other_two[...]


def norm_kernel(ids, mine, other, small, small_other, out, params):
    width = small.shape[1]
    params[:, lanes(ids[0], width)] = small[...].astype(FULL)
    params[:, lanes(1 - ids[0], width)] = small_other[...].astype(FULL)
    half = mine.shape[0]
    for start, part in ((0, mine), (half, other)):
        hat, _ = normal(part[...])
        out[start : start + half, :] = (hat * params[0:1, :] + params[1:2, :]).astype(LOW)


def grid_row(ids, n):
    k, u, i = n // 4, (n // 2) % 2, n % 2
    chunk = ((ids[6] ^ (k >> 1)) ^ (2 * u)) * 4 + ((ids[5] ^ (k & 1)) * 2) + ids[2]
    return chunk * 2 + i


def table_kernel(ids, mine, other, table, spot_one, spot_two):
    part, reach = mine.shape[1:]
    rows = lax.broadcasted_iota(jnp.int32, (reach, LANES), 0)
    cols = lax.broadcasted_iota(jnp.int32, (reach, LANES), 1)
    turn = jnp.where(rows == reach - 1 - cols, 1.0, 0.0).astype(LOW)
    table[...] = jnp.zeros_like(table)
    for k in range(2):
        spot = slice(k * LANES, (k + 1) * LANES)
        table[at(ids[0], part), spot] = dot_nn(mine[k], turn).astype(LOW)
        table[at(1 - ids[0], part), spot] = dot_nn(other[k], turn).astype(LOW)
    side = (reach + 1) // 2
    lane = lane_of(side)
    col = lax.broadcasted_iota(jnp.int32, (side, LANES), 0)
    total = spot_one.shape[0] // side
    for n in range(total):
        row = grid_row(ids, n % (total // 2))
        if n >= total // 2:
            row = row ^ 2
        here = slice(n * side, (n + 1) * side)
        target = jnp.where(lane < 96, row + 64, col + 96)
        one = jnp.where(lane == target, 1.0, 0.0)
        spot_one[here, :] = one.astype(LOW)
        ones = jnp.where((lane >= 64) & (lane < 67), 1.0, 0.0)
        spot_two[here, :] = (pltpu.roll(one, 64, 1) + ones).astype(LOW)


def lane_of(rows):
    return lax.broadcasted_iota(jnp.int32, (rows, LANES), 1)


def pieces_at(lane, first, value, rest):
    high = value.astype(LOW).astype(FULL)
    left = value - high
    mid = left.astype(LOW).astype(FULL)
    tail = left - mid
    out = jnp.where(lane == first, high, rest)
    out = jnp.where(lane == first + 1, mid, out)
    return jnp.where(lane == first + 2, tail, out)


def key_tiles(h, kva, kvb, spot_one, keys):
    half = kva.shape[0]
    lane = lane_of(half)
    for start, part in ((0, kva), (half, kvb)):
        tile = part[:, h * LANES : (h + 1) * LANES].astype(FULL)
        spots = spot_one[start : start + half, :].astype(FULL)
        keys[start : start + half, :LANES] = jnp.where(lane < 64, tile, spots).astype(LOW)


def attend_kernel(
    ids, query, kva, kvb, spot_one, spot_two, table, out, a0, a1, a2, a3, left, keys, turned, along
):
    rows = query.shape[0]
    heads = left.shape[0]
    half = kva.shape[0]
    lane32 = lane_of(32)
    block = 512
    lane = lane_of(block)
    size = a0.shape[0]
    turned[LANES:, :] = spot_two[...].astype(FULL).T.astype(LOW)
    for h in range(heads):
        key_tiles(h, kva, kvb, spot_one, keys)
        turned[:LANES, :] = keys[...].astype(FULL).T.astype(LOW)
        tile = query[:, (h // 2) * LANES : (h // 2 + 1) * LANES].astype(FULL)
        if h % 2:
            tile = pltpu.roll(tile, 64, 1)
        along[...] = dot_nn(tile.astype(LOW), table[...])
        for g in range(rows // 32):
            here = slice(g * 32, (g + 1) * 32)
            term_h = pltpu.roll(along[here, :LANES], 33 + grid_row(ids, g), 1)
            term_w = pltpu.roll(along[here, LANES:], 65, 1, stride=1, stride_axis=0)
            one = jnp.where(
                lane32 < 64, tile[here, :] * 0.125, jnp.where(lane32 < 96, term_h, term_w)
            )
            high = one.astype(LOW)
            rest = pltpu.roll(one - high.astype(FULL), 64, 1)
            left[h, here, :LANES] = high
            left[h, here, LANES:] = rest.astype(LOW)
        cols = slice(h * LANES, (h + 1) * LANES)
        spot = slice((h // 2) * LANES, (h // 2 + 1) * LANES)
        for q in range(rows // block):
            here = slice(q * block, (q + 1) * block)
            scores = dot_nn(left[h, here, :], turned[...])
            top = jnp.max(scores, axis=1, keepdims=True)
            expo = jnp.exp(scores - top)
            total = jnp.sum(expo, axis=1, keepdims=True)
            low = expo.astype(LOW)
            result = dot_nn(low[:, :half], kva[:, cols]) + dot_nn(low[:, half:], kvb[:, cols])
            result = result / total
            if h % 2 == 0:
                result = pltpu.roll(result, 64, 1)
            if h % 2:
                result = jnp.where(lane < 64, out[here, spot], result)
            else:
                result = jnp.where(lane < 64, result, 0.0)
            out[here, spot] = result
            for k in range(block // size):
                low_out = (a0, a1, a2, a3)[q * block // size + k]
                part = result[k * size : (k + 1) * size, :].astype(LOW)
                if h % 2:
                    low_out[:, spot] = part
                elif h == heads - 1:
                    low_out[:, h * 64 :] = part[:, :64]
            rest = left[h, here, LANES:].astype(FULL)
            left[h, here, LANES:] = pieces_at(lane, 64, -(top + jnp.log(total)), rest).astype(LOW)


def back_kernel(h):
    def kernel(
        ids, left, kva, kvb, spot_one, spot_two, table, g0, g1, g2, g3, value,
        dquery, dkv_mine, dkv_other, dtable,
        keys, vals, gright, qright, along, grad, left_t, right_t,
    ):
        rows = left.shape[1]
        half = kva.shape[0]
        lane = lane_of(rows)
        lane32 = lane_of(32)
        row = lax.broadcasted_iota(jnp.int32, (rows, LANES), 0)
        key_tiles(h, kva, kvb, spot_one, keys)
        keys[:, LANES:] = spot_two[...]
        cols = slice(h * LANES, (h + 1) * LANES)
        spot = slice((h // 2) * LANES, (h // 2 + 1) * LANES)
        for k, part in enumerate((g0, g1, g2, g3)):
            size, width = part.shape
            last = min(width, spot.stop)
            grad[k * size : (k + 1) * size, : last - spot.start] = part[:, spot.start : last].astype(FULL)
        vals[:half, :LANES] = kva[:, cols]
        vals[half:, :LANES] = kvb[:, cols]
        vals[:, LANES:] = spot_two[...]
        gtile = grad[...]
        otile = value[:, spot]
        if h % 2 == 0:
            gtile = pltpu.roll(gtile, 64, 1)
            otile = pltpu.roll(otile, 64, 1)
        gtile = jnp.where(lane >= 64, gtile, 0.0)
        inner = jnp.sum(gtile * otile, axis=1, keepdims=True)
        gright[...] = gtile.astype(LOW)
        extra = pieces_at(lane, 64, -inner, jnp.zeros_like(gtile))
        right_t[:LANES, :] = gtile.T.astype(LOW)
        right_t[LANES:, :] = extra.T.astype(LOW)
        for part in (slice(0, LANES), slice(LANES, 2 * LANES)):
            left_t[part, :] = left[h, :, part].astype(FULL).T.astype(LOW)
        qright[...] = jnp.where(lane < 64, left[h, :, :LANES].astype(FULL), 0.0).astype(LOW)
        probs = jnp.exp(dot_nn(keys[...], left_t[...]))
        dscores = (probs * dot_nn(vals[...], right_t[...])).astype(LOW)
        dkv = dot_nn(probs.astype(LOW), gright[...]) + dot_nn(dscores, qright[...])
        dkv_mine[...] = dkv[:half, :]
        dkv_other[...] = dkv[half:, :].astype(LOW)
        dq = dot_tn(keys[:, :LANES], dscores).T
        for g in range(rows // 32):
            here = slice(g * 32, (g + 1) * 32)
            part_h = jnp.where((lane32 >= 64) & (lane32 < 96), dq[here, :], 0.0)
            along[here, :LANES] = pltpu.roll(part_h, 95 - grid_row(ids, g), 1).astype(LOW)
        part_w = pltpu.roll(jnp.where(lane >= 96, dq, 0.0), 63, 1)
        for bit in range(5):
            moved = pltpu.roll(part_w, LANES - 2**bit, 1)
            part_w = jnp.where((row >> bit) & 1 == 1, moved, part_w)
        along[:, LANES:] = part_w.astype(LOW)
        dq = jnp.where(lane < 64, dq * 0.125 + dot_nt(along[...], table[...]), 0.0)
        if h % 2:
            dq = pltpu.roll(dq, 64, 1)
        dquery[...] = dq.astype(LOW)
        dtable[...] = dot_tn(along[...], qright[...])

    return kernel


def at(index, size):
    return pl.ds(pl.multiple_of(index * size, 16), size)


def lanes(index, size):
    return pl.ds(pl.multiple_of(index * size, LANES), size)


def mix_kernel(ids, n0, n1, n2, n3, mine, other, kv, query, rows, mix):
    half, last = mine.shape
    kv_cols = kv.shape[1]
    mix[at(ids[0], half), :last] = mine[...]
    mix[at(1 - ids[0], half), :last] = other[...]
    mix[:, last:] = jnp.zeros((mix.shape[0], mix.shape[1] - last), LOW)
    size = n0.shape[0]
    for k, part in enumerate((n0, n1, n2, n3)):
        here = slice(k * size, (k + 1) * size)
        rows[here, :] = part[...]
    both = dot_nn(rows[...], mix[...]).astype(LOW)
    kv[...] = both[:, :kv_cols]
    query[...] = both[:, kv_cols:]


def mid_kernel(
    ids, j0, j1, j2, j3, w_mine, w_other, w_two, own, own_got, params, middle, low, weight, whole
):
    fill_rows(ids, whole, w_mine, w_other, w_two)
    tok = own.shape[0]
    middle[:tok, :] = own[...]
    middle[tok:, :] = own_got[...]
    total = middle[...]
    width = j0.shape[1]
    for k, part in enumerate((j0, j1, j2, j3)):
        block = whole[at(ids[1] ^ k, width), :]
        weight[k * width : (k + 1) * width, :] = block
        total = total + dot_nn(part[...], block)
    middle[...] = total
    hat, _ = normal(total)
    low[...] = (hat * params[2:3, :] + params[3:4, :]).astype(LOW)


def feed_kernel(
    ids, r0, r1, r2, r3, c0, c1, c2, c3, up_mine, up_other, down_mine, down_other,
    d0, d1, d2, d3, active, dhidden, rows, cots, down, up,
):
    half = up_mine.shape[0]
    up[at(ids[0], half), :] = up_mine[...]
    up[at(1 - ids[0], half), :] = up_other[...]
    down[:, lanes(ids[0], half)] = down_mine[...]
    down[:, lanes(1 - ids[0], half)] = down_other[...]
    size = r0.shape[0]
    blocks = ((r0, c0, d0), (r1, c1, d1), (r2, c2, d2), (r3, c3, d3))
    for k, (row, cot, _) in enumerate(blocks):
        here = slice(k * size, (k + 1) * size)
        rows[here, :] = row[...]
        cots[here, :] = cot[...]
    hidden = dot_nn(rows[...], up[...])
    phi = 0.5 + 0.5 * lax.erf(hidden * 0.7071067811865476)
    active[...] = (hidden * phi).astype(LOW)
    slope = phi + hidden * (jnp.exp(hidden * hidden * -0.5) * 0.3989422804014327)
    dhidden[...] = (dot_nt(cots[...], down[...]) * slope).astype(LOW)
    back = dot_nt(dhidden[...], up[...]).astype(LOW)
    for k, (_, _, out) in enumerate(blocks):
        out[...] = back[k * size : (k + 1) * size, :]


def fed_kernel(active, down, f0, f1, f2):
    size = f0.shape[0]
    total = dot_nn(active[...], down[...]).astype(LOW)
    f0[...] = total[:size, :]
    f1[...] = total[size : 2 * size, :]
    f2[...] = total[2 * size :, :]


def outer_kernel(which, axis):
    def kernel(ids, a, b, sent, kept):
        half = sent.shape[axis]
        for index, out in ((1 - ids[which], sent), (ids[which], kept)):
            if axis == 0:
                out[...] = dot_tn(a[:, lanes(index, half)], b[...]).astype(LOW)
            else:
                out[...] = dot_tn(a[...], b[:, lanes(index, half)]).astype(LOW)

    return kernel


def proj_grad_kernel(ids, j0, j1, j2, j3, grad, sent, kept, whole):
    width = j0.shape[1]
    for k, part in enumerate((j0, j1, j2, j3)):
        whole[at(ids[1] ^ k, width), :] = dot_tn(part[...], grad[...])
    size = sent.shape[0] // 2
    for k, owner in enumerate((ids[0], 1 - ids[0])):
        here = slice(k * size, (k + 1) * size)
        sent[here, :] = whole[at(owner * 2 + 1 - ids[2], size), :].astype(LOW)
        kept[here, :] = whole[at(owner * 2 + ids[2], size), :].astype(LOW)


def split_kernel(which):
    def kernel(ids, a, b, sent, kept):
        size = sent.shape[0] // 2
        for k in range(2):
            here = slice(k * size, (k + 1) * size)
            for bit, out in ((1 - ids[which], sent), (ids[which], kept)):
                rows = pl.ds(pl.multiple_of(k * 2 * size + bit * size, 16), size)
                out[here, :] = (a[rows, :].astype(FULL) + b[rows, :].astype(FULL)).astype(LOW)

    return kernel


def owner_kernel(a, b, sent, kept):
    size = sent.shape[0]
    kept[...] = (a[:size, :].astype(FULL) + b[:size, :].astype(FULL)).astype(kept.dtype)
    sent[...] = (a[size:, :].astype(FULL) + b[size:, :].astype(FULL)).astype(LOW)


def tail_add_kernel(a, b, out):
    size = a.shape[0]
    out[...] = (a[...].astype(FULL) + b[b.shape[0] - size :, :].astype(FULL)).astype(out.dtype)


def vector_block(out, n0, n1, n2, n3, t0, t1, t2):
    out[...] = jnp.zeros_like(out)
    tables = (t0[...] + t1[...] + t2[...]) * 8.0
    side = 16
    for k in range(8):
        start = k // 4 * LANES + k % 4 * side
        out[:side, k * 64 : (k + 1) * 64] = tables[start : start + side, :64]
    tile = 0
    for row in (n0, n1, n2, n3):
        for k in range(row.shape[1] // LANES):
            spot = slice(tile % 4 * LANES, (tile % 4 + 1) * LANES)
            out[side + tile // 4 : side + tile // 4 + 1, spot] = row[:, k * LANES : (k + 1) * LANES]
            tile += 1


def row_sums(product):
    total = product[:, :LANES]
    for k in range(1, product.shape[1] // LANES):
        total = total + product[:, k * LANES : (k + 1) * LANES]
    return jnp.sum(total.T, axis=0, keepdims=True)


def vector_out_kernel(reach, split):
    def kernel(ids, *refs):
        *parts, params, n0, n1, n2, n3, t0, t1, total, norms = refs
        first = parts[0].shape[0] - total.shape[0]
        total[...] = sum(part[first:, :].astype(FULL) for part in parts)
        side = 16
        for tile in range(norms.shape[0] * norms.shape[1] // LANES):
            each = norms.shape[1] // LANES
            spot = slice(tile % 4 * LANES, (tile % 4 + 1) * LANES)
            norms[tile // each : tile // each + 1, tile % each * LANES : (tile % each + 1) * LANES] = (
                total[side + tile // 4 : side + tile // 4 + 1, spot]
            )
        gain, shift = params[0:1, :], params[1:2, :]
        norms[0:1, :] = (norms[0:1, :] - shift * norms[1:2, :]) / gain
        for k, out in enumerate((n0, n1, n2, n3)):
            width = out.shape[0]
            start = ids[7] * width if split else 0
            for tile in range(width // LANES):
                spot = pl.ds(pl.multiple_of(start + tile * LANES, LANES), LANES)
                out[tile * LANES : (tile + 1) * LANES] = norms[k, spot]
        rows = lax.broadcasted_iota(jnp.int32, (side, reach), 0)
        cols = lax.broadcasted_iota(jnp.int32, (side, reach), 1)
        for k, out in enumerate((t0, t1)):
            both = jnp.zeros((64, reach), FULL)
            for part in range(4):
                turn = jnp.where(rows + part * side == reach - 1 - cols, 1.0, 0.0)
                start = (k * 4 + part) * 64
                both = both + lax.dot_general(
                    total[:side, start : start + 64],
                    turn,
                    (((0,), (0,)), ((), ())),
                    precision=lax.Precision.HIGHEST,
                    preferred_element_type=FULL,
                )
            if split:
                size = out.shape[0]
                out[...] = jnp.where(ids[7] == 0, both[:size, :], both[size:, :])
            else:
                out[...] = both

    return kernel


def dmix_kernel(dkv, dquery, mix, mine, near, sent):
    size = mine.shape[0]
    cols = dkv.shape[1]
    total = dot_nt(dkv[...], mix[:, :cols]) + dot_nt(dquery[...], mix[:, cols:])
    for k, (out, start) in enumerate(((mine, 0), (sent, 0), (near, 0), (sent, size))):
        out[start : start + size, :] = total[k * size : (k + 1) * size, :].astype(LOW)


def dkv_kernel(m0, m1, m2, o0, o1, o2, q0, q1, q2, dkv, dquery):
    for h, (mine, got) in enumerate(((m0, o0), (m1, o1), (m2, o2))):
        cols = slice(h * LANES, (h + 1) * LANES)
        dkv[:, cols] = (mine[...] + got[...].astype(FULL)).astype(LOW)
    dquery[:, :LANES] = (q0[...].astype(FULL) + q1[...].astype(FULL)).astype(LOW)
    dquery[:, LANES:] = q2[...]


def qkv_grad_kernel(
    ids, rows, m0, m1, m2, o0, o1, o2, q0, q1, q2, mix, v2, v3, t0, t1, t2,
    dkv, dquery, sent, kept, whole, vector,
):
    dkv_kernel(m0, m1, m2, o0, o1, o2, q0, q1, q2, dkv, dquery)
    cols = dkv.shape[1]
    whole[:, :cols] = dot_tn(rows[...], dkv[...])
    whole[:, cols:] = dot_tn(rows[...], dquery[...])
    width = kept.shape[1]
    size = (kept.shape[0] - vector.shape[0]) // 2
    sums_block(whole, dkv, dquery, mix, v2, v3, t0, t1, t2, vector)
    for out, core in ((sent, 1 - ids[2]), (kept, ids[2])):
        for k, owner in enumerate((ids[0], 1 - ids[0])):
            here = slice(k * size, (k + 1) * size)
            out[here, :] = whole[at(owner * 2 + core, size), :width].astype(LOW)
        out[2 * size :, :] = vector[...].astype(LOW)


def sums_block(whole, dkv, dquery, mix, v2, v3, t0, t1, t2, vector):
    weights = mix[...].astype(FULL)
    sums = jnp.concatenate(
        [jnp.sum(part[...].astype(FULL), axis=0, keepdims=True) for part in (dkv, dquery)], axis=1
    )
    both = row_sums(whole[...] * weights)
    shift = row_sums(weights * sums)
    vector_block(vector, both, shift, v2, v3, t0, t1, t2)


def sums_kernel(rows, dkv, dquery, mix, v2, v3, t0, t1, t2, vector, whole):
    cols = dkv.shape[1]
    whole[:, :cols] = dot_tn(rows[...], dkv[...])
    whole[:, cols:] = dot_tn(rows[...], dquery[...])
    sums_block(whole, dkv, dquery, mix, v2, v3, t0, t1, t2, vector)


def qkv_owner_kernel(a, b, sent, kept):
    size = a.shape[0] - sent.shape[0]
    kept[:size, :] = a[:size, :].astype(FULL) + b[:size, :].astype(FULL)
    total = a[size:, :].astype(FULL) + b[size:, :].astype(FULL)
    kept[size:, :] = total[size:, :]
    sent[...] = total.astype(LOW)


def add_kernel(*refs):
    total = refs[0][...].astype(FULL)
    for ref in refs[1:-1]:
        total = total + ref[...].astype(FULL)
    refs[-1][...] = total.astype(refs[-1].dtype)


def halve_kernel(which):
    def kernel(ids, a, b, sent, kept):
        size = sent.shape[0]
        bit = ids[which]
        for index, out in ((1 - bit, sent), (bit, kept)):
            here = at(index, size)
            out[...] = (a[here, :].astype(FULL) + b[here, :].astype(FULL)).astype(out.dtype)

    return kernel


def join_kernel(which):
    def kernel(ids, mine, other, out):
        size = mine.shape[0]
        out[at(ids[which], size), :] = mine[...].astype(out.dtype)
        out[at(1 - ids[which], size), :] = other[...].astype(out.dtype)

    return kernel


def qkv_out_kernel(heads):
    def kernel(ids, q0, q1, q2, q3, o0, o1, o2, o3, out, whole, sem):
        size = out.shape[0] // 2
        lane = lane_of(size)
        first = lane < 64
        groups = 4
        share = heads * 64
        width = groups * share
        places = [pl.ds(pl.multiple_of(p * size, 16), size) for p in (ids[2], 1 - ids[2])]

        def fill(part, refs):
            here = places[part]

            def tile(g, column):
                stop = min(column + LANES, q0.shape[1])
                one = refs[g][:size, column:stop].astype(FULL)
                if stop - column < LANES:
                    one = jnp.concatenate([one, jnp.zeros_like(one)], axis=1)
                return one

            for pair in range(groups * heads // 2):
                ends = []
                for n in (2 * pair, 2 * pair + 1):
                    g, h = n // heads, n % heads
                    q = tile(g, 2 * share + (h // 2) * LANES)
                    if h % 2:
                        q = pltpu.roll(q, 64, 1)
                    ends.append((q, tile(g, h * LANES)))
                (qa, kva), (qb, kvb) = ends
                at_col = pair * LANES
                for start, a, b in (
                    (0, qa, pltpu.roll(qb, 64, 1)),
                    (width, kva, pltpu.roll(kvb, 64, 1)),
                    (2 * width, pltpu.roll(kva, 64, 1), kvb),
                ):
                    here_cols = slice(start + at_col, start + at_col + LANES)
                    whole[here, here_cols] = jnp.where(first, a, b)

        for part, refs in enumerate(((q0, q1, q2, q3), (o0, o1, o2, o3))):
            for g in range(groups):

                @pl.when(ids[1] == g)
                def _():
                    fill(part, [refs[k ^ g] for k in range(groups)])

            here = places[part]
            pltpu.make_async_copy(whole.at[here], out.at[here], sem.at[part]).start()
        for part, here in enumerate(places):
            pltpu.make_async_copy(whole.at[here], out.at[here], sem.at[part]).wait()

    return kernel


def change_kernel(middle, own, own_got, f0, f1, f2, mine, sent):
    tok = own.shape[0]
    for part, base, out in ((0, own, mine), (tok, own_got, sent)):
        here = slice(part, part + tok)
        fed = f0[here, :].astype(FULL) + f1[here, :].astype(FULL) + f2[here, :].astype(FULL)
        total = middle[here, :] + fed
        if part:
            total = total - base[...]
        out[...] = total.astype(out.dtype)


def place_kernel(ids, mine, got, base, out, low, sem):
    first = pltpu.make_async_copy(mine, out.at[ids[3]], sem.at[0])
    first.start()
    low[...] = got[...].astype(FULL) + base[...]
    second = pltpu.make_async_copy(low, out.at[1 - ids[3]], sem.at[1])
    second.start()
    first.wait()
    second.wait()


def place_two_kernel(ids, mine, got, out, low, sem):
    first = pltpu.make_async_copy(mine, out.at[ids[3]], sem.at[0])
    first.start()
    low[...] = got[...].astype(FULL)
    second = pltpu.make_async_copy(low, out.at[1 - ids[3]], sem.at[1])
    second.start()
    first.wait()
    second.wait()


def join_out_kernel(which):
    def kernel(ids, mine, other, out, whole, sem):
        size = mine.shape[0]
        copies = []
        for k, (place, ref) in enumerate(((ids[which], mine), (1 - ids[which], other))):
            here = at(place, size)
            whole[here, :] = ref[...].astype(FULL)
            copies.append(pltpu.make_async_copy(whole.at[here], out.at[here], sem.at[k]))
            copies[-1].start()
        for copy in copies:
            copy.wait()

    return kernel


def halve_lanes_kernel(which):
    def kernel(ids, a, b, sent, kept):
        size = sent.shape[1]
        for bit, out in ((1 - ids[which], sent), (ids[which], kept)):
            here = lanes(bit, size)
            out[...] = (a[:, here].astype(FULL) + b[:, here].astype(FULL)).astype(out.dtype)

    return kernel


def norm_back(grad, values, gain):
    hat, scale = normal(values)
    scaled = grad * gain
    back = scale * (
        scaled
        - jnp.mean(scaled, axis=-1, keepdims=True)
        - hat * jnp.mean(scaled * hat, axis=-1, keepdims=True)
    )
    return back, jnp.sum(grad * hat, axis=0, keepdims=True), jnp.sum(grad, axis=0, keepdims=True)


def mid_back_kernel(
    a0, a1, a2, middle, params, cot, weight, gmiddle, gbranch, b0, b1, b2, b3, dgain, dshift
):
    size = a0.shape[0]
    grad = a0[...].astype(FULL) + a1[...].astype(FULL) + a2[...].astype(FULL)
    back, dgain[...], dshift[...] = norm_back(grad, middle[...], params[2:3, :])
    total = cot[:size, :].astype(FULL) + back
    gmiddle[...] = total
    low = total.astype(LOW)
    gbranch[...] = low
    width = b0.shape[1]
    for k, out in enumerate((b0, b1, b2, b3)):
        out[...] = dot_nt(low, weight[k * width : (k + 1) * width, :]).astype(LOW)


def first_back_kernel(a0, a1, a2, own, own_got, params, gmiddle, mine, sent, rows):
    tok = own.shape[0]
    rows[:tok, :] = own[...]
    rows[tok:, :] = own_got[...]
    grad = a0[...].astype(FULL) + a1[: 2 * tok, :].astype(FULL) + a2[...].astype(FULL)
    back, _, _ = norm_back(grad, rows[...], params[0:1, :])
    total = gmiddle[...] + back
    mine[...] = total[:tok, :]
    sent[...] = total[tok:, :].astype(LOW)


def on_device(
    tokens,
    ln1_gain,
    ln1_bias,
    qkv_weight,
    rel_h,
    rel_w,
    proj_weight,
    ln2_gain,
    ln2_bias,
    fc1_weight,
    fc2_weight,
    cotangent,
):
    images, tok, width = tokens.shape
    hid = fc1_weight.shape[1]
    dp_count = lax.axis_size("dp")
    head = rel_h.shape[1] * dp_count
    reach = rel_h.shape[0]
    s, t = lax.axis_index("seq"), lax.axis_index("tp")
    d = lax.axis_index("dp")
    y, c = t // 2, t % 2
    image = s // 2
    group = (s % 2) * 2 + y
    groups = 4
    share = width // groups
    heads = share // head
    rows_n = 2 * tok
    half = width // 2
    me = d if dp_count == 2 else jnp.int32(0)
    ids = jnp.stack([me, group, c, image, s % 2, y, s, d]).astype(jnp.int32)
    n = 4 * rows_n
    kv_cols = 2 * share
    pad_share = 2 * LANES
    key_n = 2 * n
    qkv_cols = 3 * share
    low_tok, full_tok = shape((tok, width), LOW), shape((tok, width), FULL)
    low_rows, full_rows = shape((rows_n, width), LOW), shape((rows_n, width), FULL)
    two_rows = shape((2 * rows_n, width), LOW)
    heads_rows = shape((rows_n, share), LOW)
    way = (0, ROW, NEAR, ROW | NEAR)

    def add(kind, *args, wait=()):
        return call(add_kernel, [shape(args[0].shape, kind)], wait=wait)(*args)[0]

    call = in_order()
    quarter, eighth = half // 2, half // 4
    norm_sums = [shape((1, width), FULL)] * 2

    def written(kernel, dims, extra=2):
        return call(
            kernel,
            [shape(dims, FULL)],
            [pltpu.VMEM(dims, FULL), pltpu.SemaphoreType.DMA((2,))],
            smem=1,
            extra=extra,
            written=True,
        )

    def total_of(kind, *args):
        return call(add_kernel, [shape(args[0].shape, kind)])(*args)[0]

    def halve(which, a, b, kind=FULL):
        dims = (a.shape[0] // 2, a.shape[1])
        return call(halve_kernel(which), [shape(dims, LOW), shape(dims, kind)], smem=1)(ids, a, b)

    def split(which, a, b):
        dims = (a.shape[0] // 2, a.shape[1])
        return call(split_kernel(which), [shape(dims, LOW)] * 2, smem=1)(ids, a, b)

    def join(which, mine, other, kind):
        dims = (2 * mine.shape[0], mine.shape[1])
        return call(join_kernel(which), [shape(dims, kind)], smem=1)(ids, mine, other)[0]

    own, away = call(pick_kernel, [full_tok] * 2, smem=1)(ids, tokens)
    own_got = hop(away, FAR)
    small = jnp.concatenate([ln1_gain, ln1_bias, ln2_gain, ln2_bias]).reshape(4, -1)
    small, small_other, _ = pair_dp(after(small, away), 1)
    tables = jnp.stack([rel_h.T, rel_w.T])
    tables, tables_other, _ = pair_dp(after(tables, away), 1)
    cot_mine, cot_away = call(pick_kernel, [low_tok] * 2, smem=1)(ids, cotangent)
    cot_got = hop(cot_away, FAR)
    depth = qkv_weight.shape[0]
    mix_mine = call(
        pack_kernel(share, heads),
        [shape((depth, qkv_cols), LOW)],
        smem=1,
        wait=(small_other, tables_other),
    )(ids, qkv_weight)[0]
    mix_mine, mix_other, _ = pair_dp(after(mix_mine, own_got), 0)

    normed, params = call(norm_kernel, [low_rows, shape((4, width), FULL)], smem=1)(
        ids, own, own_got, small, small_other
    )
    normed_parts = [normed] + [hop(normed, b) for b in way[1:]]
    cot = call(stack_kernel, [low_rows])(cot_mine, cot_got)[0]
    table, spot_one, spot_two = call(
        table_kernel,
        [shape((LANES, 2 * LANES), LOW)] + [shape((key_n, LANES), LOW)] * 2,
        smem=1,
    )(ids, tables, tables_other)
    if dp_count == 2:
        proj_part = call(rows_kernel, [shape((half // 2, width), LOW)], smem=1)(ids, proj_weight)[0]

    kv, query, normed_all, mix = call(
        mix_kernel,
        [
            shape((n, kv_cols), LOW),
            shape((n, pad_share), LOW),
            shape((n, width), LOW),
            shape((width, kv_cols + pad_share), LOW),
        ],
        smem=1,
        extra=3,
    )(ids, *normed_parts, mix_mine, mix_other)
    kv_other = hop(kv, CORE)
    cot_row = hop(after(cot, kv), ROW)
    if dp_count == 2:
        proj_mine, proj_other = proj_weight, swap_dp(after(proj_part, normed))
    else:
        proj_mine, proj_other, _ = pair_dp(proj_weight, 0)
    proj_two = hop(after(proj_other, kv), CORE)
    up_mine, up_other, _ = pair_dp(after(fc1_weight, kv), 0)

    down_mine, down_other, _ = pair_dp(after(fc2_weight, kv), 1)

    attended, *attended_low, left = call(
        attend_kernel,
        [shape((n, pad_share), FULL)]
        + [heads_rows] * 4
        + [shape((heads, n, 2 * LANES), LOW)],
        [
            pltpu.VMEM((key_n, LANES), LOW),
            pltpu.VMEM((2 * LANES, key_n), LOW),
            pltpu.VMEM((n, 2 * LANES), FULL),
        ],
        smem=1,
        extra=16,
    )(ids, query, kv, kv_other, spot_one, spot_two, table)
    attended_low = lax.optimization_barrier((*attended_low, cot_row, proj_two))[:4]
    joined = [attended_low[0]] + [hop(attended_low[k], way[k]) for k in (1, 2, 3)]
    middle, normed_two, proj = call(
        mid_kernel,
        [full_rows, low_rows, shape((width, width), LOW)],
        [pltpu.VMEM((width, width), LOW)],
        smem=1,
    )(ids, *joined, proj_mine, proj_other, proj_two, own, own_got, params)

    two_row = hop(normed_two, ROW)
    two_core = hop(normed_two, CORE)
    two_diag = hop(two_row, CORE)
    cot_core = hop(after(cot, two_row), CORE)
    cot_diag = hop(after(cot_row, two_row), CORE)
    d0, d1, d2, d3, active, dhidden, rows_all, cot_all, down = call(
        feed_kernel,
        [low_rows] * 4
        + [shape((n, hid), LOW)] * 2
        + [shape((n, width), LOW)] * 2
        + [shape((hid, width), LOW)],
        [pltpu.VMEM((width, hid), LOW)],
        smem=1,
        extra=12,
    )(
        ids, normed_two, two_row, two_core, two_diag, cot, cot_row, cot_core, cot_diag,
        up_mine, up_other, down_mine, down_other,
    )
    dnorm_next = hop(d3, CORE)
    dnorm_mine = hop(d2, CORE)

    mixed_shapes = [shape((n, kv_cols), LOW), shape((n, pad_share), LOW)]
    vector_rows = 32
    whole_shape = pltpu.VMEM((width, kv_cols + pad_share), FULL)
    qkv_rows = (quarter + vector_rows, qkv_cols)
    proj_low = shape((eighth, width), LOW)
    v, fc1, fc2 = (types.SimpleNamespace() for _ in range(3))

    def send(value, bits, *events):
        return hop(after(value, *events) if events else value, bits)

    def dnorm_add():
        v.dnorm_row = send(total_of(LOW, d1, dnorm_next), ROW)

    def fc1_outer():
        sent, fc1.kept = call(outer_kernel(0, 0), [shape((half, hid), LOW)] * 2, smem=1, extra=4)(
            ids, rows_all, dhidden
        )
        if dp_count == 2:
            fc1.got = swap_dp(sent)

    def far_sum(part):
        def step():
            sent, part.kept = halve(3, part.kept, part.got)
            part.got = send(sent, FAR)

        return step

    def far_all(part):
        def step():
            part.kept = total_of(LOW, part.kept, part.got)
            part.got = send(part.kept, FAR)

        return step

    def near_all(part):
        def step():
            part.kept = join(3, part.kept, part.got, LOW)
            part.got = send(part.kept, NEAR)

        return step

    def last(part, dims):
        def step():
            part.grad = written(join_out_kernel(4), dims)(ids, part.kept, part.got)

        return step

    def fc2_outer():
        sent, fc2.kept = call(
            outer_kernel(4, 0), [shape((hid // 2, width), LOW)] * 2, smem=1, extra=4
        )(ids, active, cot_all)
        fc2.got = send(sent, NEAR)

    def mid_back():
        v.gmiddle, v.gbranch, *parts, v.dgain_two, v.dshift_two = call(
            mid_back_kernel, [full_rows, low_rows] + [heads_rows] * 4 + norm_sums
        )(d0, dnorm_mine, v.dnorm_row, middle, params, cot, proj)
        v.grads = [parts[0]] + [
            send(b, bits) for b, bits in zip(parts[1:], way[1:])
        ]

    def proj_outer():
        sent, v.proj = call(
            proj_grad_kernel,
            [shape((half, width), LOW)] * 2,
            [pltpu.VMEM((width, width), FULL)],
            smem=1,
        )(ids, *joined, v.gbranch)
        v.proj_got = send(after(sent, *v.grads), CORE)

    def fed():
        v.f0, v.f1, f2 = call(fed_kernel, [low_rows, low_rows, two_rows], extra=4)(
            active, down
        )
        v.fed_got = send(after(f2, *v.grads), CORE)

    def back(h):
        dquery, mine, other, dtable = call(
            back_kernel(h),
            [
                shape((n, LANES), LOW),
                shape((n, LANES), FULL),
                shape((n, LANES), LOW),
                shape((2 * LANES, LANES), FULL),
            ],
            [
                pltpu.VMEM((key_n, 2 * LANES), LOW),
                pltpu.VMEM((key_n, 2 * LANES), LOW),
                pltpu.VMEM((n, LANES), LOW),
                pltpu.VMEM((n, LANES), LOW),
                pltpu.VMEM((n, 2 * LANES), LOW),
                pltpu.VMEM((n, LANES), FULL),
                pltpu.VMEM((2 * LANES, n), LOW),
                pltpu.VMEM((2 * LANES, n), LOW),
            ],
            smem=1,
            extra=20,
            wait=(v.back[-1][1],) if v.back else (),
        )(ids, left, kv, kv_other, spot_one, spot_two, table, *v.grads, attended)
        v.back.append((mine, send(other, CORE), dquery, dtable))

    v.back = []

    def back0():
        back(0)

    def back1():
        back(1)

    def back2():
        back(2)

    def fed_add():
        sent = call(tail_add_kernel, [low_rows])(v.f1, v.fed_got)[0]
        v.fed_row = send(sent, ROW)

    def change():
        v.change, sent = call(change_kernel, [full_tok, low_tok])(
            middle, own, own_got, v.f0, v.fed_got, v.fed_row
        )
        v.change_got = send(sent, FAR)

    def place_output():
        v.output = call(
            place_kernel,
            [shape(tokens.shape, FULL)],
            [pltpu.VMEM((tok, width), FULL), pltpu.SemaphoreType.DMA((2,))],
            smem=1,
            written=True,
        )(ids, v.change, v.change_got, away)

    def qkv_outer():
        mine, got, queries, tables = zip(*v.back)
        v.dkv, v.dquery, sent, v.qkv = call(
            qkv_grad_kernel,
            mixed_shapes + [shape((half + vector_rows, qkv_cols), LOW)] * 2,
            [whole_shape, pltpu.VMEM((vector_rows, qkv_cols), FULL)],
            smem=1,
            extra=6,
        )(
            ids, normed_all, *mine, *got, *queries, mix, v.dgain_two, v.dshift_two, *tables
        )
        v.qkv_got = send(sent, CORE)

    def qkv_owner():
        sent, v.qkv = call(qkv_owner_kernel, [shape(qkv_rows, LOW), shape(qkv_rows, FULL)])(
            v.qkv, v.qkv_got
        )
        v.qkv_got = swap_dp(sent)

    def qkv_images():
        v.qkv = total_of(LOW, v.qkv, v.qkv_got)
        v.qkv_got = send(v.qkv, FAR)

    def qkv_total():
        part = total_of(LOW, v.qkv, v.qkv_got)
        near = send(part, NEAR)
        v.qkv_parts = [part, send(part, ROW), near, send(near, ROW)]

    def vector_last():
        *norms, table_h, table_w = vector_out(v.qkv_parts, half, head // 2)
        v.norms = norms
        v.tables = (table_h.T, table_w.T)
        v.qkv_others = [send(part, CORE) for part in v.qkv_parts]

    def qkv_last():
        v.qkv_grad = written(qkv_out_kernel(heads), (half, 3 * width), 4)(
            ids, *v.qkv_parts, *v.qkv_others
        )

    def mixed_back():
        v.e_mine, v.e_near, e_row = call(
            dmix_kernel, [low_rows, low_rows, two_rows], extra=6
        )(
            v.dkv, v.dquery, mix
        )
        v.e_got = send(e_row, ROW)

    def normed_near():
        sent = call(tail_add_kernel, [low_rows])(v.e_near, v.e_got)[0]
        v.e_last = send(sent, NEAR)

    def first_back():
        v.token, sent = call(
            first_back_kernel, [full_tok, low_tok], [pltpu.VMEM((rows_n, width), FULL)]
        )(v.e_mine, v.e_got, v.e_last, own, own_got, params, v.gmiddle)
        v.token_got = send(sent, FAR)

    def place_tokens():
        v.tokens_grad = call(
            place_two_kernel,
            [shape(tokens.shape, FULL)],
            [pltpu.VMEM((tok, width), FULL), pltpu.SemaphoreType.DMA((2,))],
            smem=1,
            written=True,
        )(ids, v.token, v.token_got)

    def fc1_near_sum():
        sent, fc1.kept = halve(4, fc1.kept, fc1.got)
        fc1.got = send(sent, NEAR)

    def fc2_near_sum():
        dims = (hid // 2, half)
        sent, fc2.kept = call(
            halve_lanes_kernel(0), [shape(dims, LOW), shape(dims, FULL)], smem=1
        )(ids, fc2.kept, fc2.got)
        fc2.got = swap_dp(sent)

    def proj_split():
        sent, v.proj = split(5, v.proj, v.proj_got)
        v.proj_got = send(sent, ROW)

    def proj_owner():
        sent, v.proj = call(owner_kernel, [proj_low] * 2)(v.proj, v.proj_got)
        v.proj_got = swap_dp(sent)

    def proj_sum(bits):
        def step():
            v.proj = total_of(LOW, v.proj, v.proj_got)
            v.proj_got = send(v.proj, bits)

        return step

    def proj_join():
        v.proj = join(5, v.proj, v.proj_got, LOW)
        v.proj_got = send(v.proj, CORE)

    def proj_last():
        v.proj_grad = written(join_out_kernel(2), (half, width))(ids, v.proj, v.proj_got)

    def vector_out(parts, size, features):
        return call(
            vector_out_kernel(reach, dp_count == 2),
            [shape((size,), FULL)] * 4 + [shape((features, reach), FULL)] * 2,
            [pltpu.VMEM((vector_rows, qkv_cols), FULL), pltpu.VMEM((4, width), FULL)],
            smem=1,
        )(ids, *parts, params)

    if dp_count == 2:
        for step in (
            fc2_outer,
            dnorm_add,
            fc1_outer,
            mid_back,
            fc2_near_sum,
            proj_outer,
            back0,
            back1,
            fed,
            back2,
            fc1_near_sum,
            far_sum(fc2),
            qkv_outer,
            qkv_owner,
            fed_add,
            proj_split,
            far_sum(fc1),
            qkv_images,
            mixed_back,
            far_all(fc2),
            proj_owner,
            proj_sum(NEAR),
            qkv_total,
            change,
            near_all(fc2),
            proj_sum(FAR),
            far_all(fc1),
            normed_near,
            proj_sum(ROW),
            place_output,
            first_back,
            proj_join,
            vector_last,
            last(fc2, (hid, half)),
            near_all(fc1),
            place_tokens,
            qkv_last,
            proj_last,
            last(fc1, (half, hid)),
        ):
            step()
        output, tokens_grad, qkv_grad = v.output, v.tokens_grad, v.qkv_grad
        proj_grad, fc1_grad, fc2_grad = v.proj_grad, fc1.grad, fc2.grad
        norms, dtables = v.norms, v.tables
    else:
        every = ("seq", "tp")
        for step in (dnorm_add, mid_back, fed, back0, back1, back2, fed_add, change, place_output):
            step()
        mine, other, queries, tables = zip(*v.back)
        v.dkv, v.dquery = call(dkv_kernel, mixed_shapes)(*mine, *other, *queries)
        for step in (mixed_back, normed_near, first_back, place_tokens):
            step()
        output, tokens_grad = v.output, v.tokens_grad
        dkv, dquery, gbranch = v.dkv, v.dquery, v.gbranch

        def weight_sum(a, b, axes, axis=0):
            part = lax.psum_scatter(
                dot_tn(a, b).astype(LOW), "dp", scatter_dimension=axis, tiled=True
            )
            return lax.psum(part, axes).astype(FULL)

        fc1_grad = weight_sum(rows_all, dhidden, "seq")
        fc2_grad = weight_sum(active, cot_all, "seq", 1)
        proj_grad = weight_sum(canon(joined, group, 1), gbranch, every)
        dmixed = jnp.concatenate([dkv, dquery], axis=1)[:, :qkv_cols]
        part = dot_tn(normed_all, dmixed).astype(LOW)
        part = lax.psum_scatter(part, "dp", scatter_dimension=0, tiled=True)
        part = part.astype(FULL) + hop(part, FAR).astype(FULL)
        part = part.astype(LOW)
        part = (part.astype(FULL) + hop(part, CORE).astype(FULL)).astype(LOW)
        whole = canon([part[None]] + [hop(part, bits)[None] for bits in way[1:]], group, 0)
        depth = whole.shape[1]
        pairs = whole[:, :, :kv_cols].reshape(groups, depth, heads, 2, head)
        qkv_grad = jnp.concatenate(
            [
                whole[:, :, kv_cols:].transpose(1, 0, 2).reshape(depth, width),
                pairs[:, :, :, 0].transpose(1, 0, 2, 3).reshape(depth, width),
                pairs[:, :, :, 1].transpose(1, 0, 2, 3).reshape(depth, width),
            ],
            axis=1,
        ).astype(FULL)
        vector = call(sums_kernel, [shape((vector_rows, qkv_cols), FULL)], [whole_shape], extra=6)(
            normed_all, dkv, dquery, mix, v.dgain_two, v.dshift_two, *tables
        )[0]
        vector = lax.psum(vector, ("dp", *every))
        *norms, table_h, table_w = vector_out((vector,), width, head)
        norms = [piece(row, d, width // dp_count, 0) for row in norms]
        dtables = [piece(t.T, d, head // dp_count, 1) for t in (table_h, table_w)]
    return (
        output,
        tokens_grad,
        norms[0],
        norms[1],
        qkv_grad,
        dtables[0],
        dtables[1],
        proj_grad,
        norms[2],
        norms[3],
        fc1_grad,
        fc2_grad,
    )


def solution(mesh):
    split = P("dp", ("seq", "tp"), None)
    params = (
        P("dp"),
        P("dp"),
        P("dp", None),
        P(None, "dp"),
        P(None, "dp"),
        P("dp", None),
        P("dp"),
        P("dp"),
        P("dp", "tp"),
        P("tp", "dp"),
    )
    return jax.shard_map(
        on_device,
        mesh=mesh,
        in_specs=(split, *params, split),
        out_specs=(split, split, *params),
        check_vma=False,
    )
```

time: 213 us -> 180 us (0.85)
  waiting for transfers between devices: 78.4 us -> 48.2 us
  starting transfers between devices: 63.3 us -> 74.9 us
  Pallas kernels: 57 us -> 49.8 us
  local copies, waits for them, and re-layouts: 8.79 us -> 4.21 us
  other arithmetic: 3.84 us -> 1.46 us
    ppermute x53 -> x54, waiting for transfers between devices: 65 us -> 39.8 us  [hop(): lax.ppermute(value, ('seq', 'tp'), [(i, i ^ bits) for i in range(count)])]
    ppermute x53 -> x54, starting transfers between devices: 50.1 us -> 65.1 us  [hop(): lax.ppermute(value, ('seq', 'tp'), [(i, i ^ bits) for i in range(count)])]
    pallas_call x47 -> x50, Pallas kernels: 57 us -> 49.8 us  [run(): pl.pallas_call(body, name=kernel.__qualname__.split('.')[0], out_shape=ou...]
    ppermute x12 -> x10, waiting for transfers between devices: 13.4 us -> 8.35 us  [swap_dp(): return lax.ppermute(value, 'dp', [(0, 1), (1, 0)])]
    unnamed x20 -> x14, local copies, waits for them, and re-layouts: 8.68 us -> 4.1 us
    ppermute x12 -> x10, starting transfers between devices: 13.1 us -> 9.81 us  [swap_dp(): return lax.ppermute(value, 'dp', [(0, 1), (1, 0)])]
    pallas_call x4 -> x0, other arithmetic: 2.38 us -> none  [run(): pl.pallas_call(body, name=kernel.__qualname__.split('.')[0], out_shape=ou...]
  transfers between devices with their start and end apart: 65 -> 64, of which waited for: 29 -> 27; matrix products, arithmetic and copies ran while one was open for 2% -> 1% of each run, Pallas kernels for 22% -> 24%
where the time goes in v3:
time: 180 us
  starting transfers between devices  74.9 us (42%)
  Pallas kernels  49.8 us (28%)
  waiting for transfers between devices  48.2 us (27%)
  local copies, waits for them, and re-layouts  4.21 us (2%)
    ppermute x54, starting transfers between devices, hop(): lax.ppermute(value, ('seq', 'tp'), [(i, i ^ bits) for i in range(count)])  65.1 us
    pallas_call x50, Pallas kernels, run(): pl.pallas_call(body, name=kernel.__qualname__.split('.')[0], out_shape=ou...  49.8 us
    ppermute x54, waiting for transfers between devices, hop(): lax.ppermute(value, ('seq', 'tp'), [(i, i ^ bits) for i in range(count)])  39.8 us
    ppermute x10, starting transfers between devices, swap_dp(): return lax.ppermute(value, 'dp', [(0, 1), (1, 0)])  9.81 us
    ppermute x10, waiting for transfers between devices, swap_dp(): return lax.ppermute(value, 'dp', [(0, 1), (1, 0)])  8.35 us
    unnamed x14, local copies, waits for them, and re-layouts  4.1 us
  transfers between devices with their start and end apart: 64, of which 27 were waited for; matrix products, arithmetic and copies ran while one was open for 1% of the time, Pallas kernels for 24%

profile of v3, /device:TPU:0, one launch (start us, length us, event | category | flops | bytes accessed | tf_op | source)
XLA Modules:
  0.0 180.0 jit_solution(3604806294925877567)
XLA Ops:
  0.8 1.0 copy-done.4
  2.3 4.1 %collective-permute-start = (f32[64,768]{1,0:T(8,128)S(1)}, f32[64,768]{1,0:T(8,128)S(1)}, u32[]{:S(2)}, u32[]{:S(2)}) collective-permute-start(f32[64,768]{1,0:T(8,128)S(1)} %get-tuple-element.131.refs_3_), channel_id=1, source_target_pairs={{0,8},{1,9},{2,10},{3,11},{4,12},{5,13},{6,14},{7,15},{8,0},{9,1},... | collective-permute-start | bytes 589832 | tf_op jit(solution)/shard_map/ppermute | solution.py:20
  7.2 1.5 collective-permute-start.2
  10.1 0.9 copy-done.5
  11.5 1.6 collective-permute-done.1.refs_3_.refs_4_
  13.1 1.5 copy-done.1
  15.6 1.5 collective-permute-start.6
  17.9 5.1 %collective-permute-start.5 = (bf16[128,768]{1,0:T(8,128)(2,1)S(1)}, bf16[128,768]{1,0:T(8,128)(2,1)S(1)}, u32[]{:S(2)}, u32[]{:S(2)}) collective-permute-start(bf16[128,768]{1,0:T(8,128)(2,1)S(1)} %get-tuple-element.135.refs_1_), channel_id=1, source_target_pairs={{0,6},{1,7},{2,4},{3,5},{4,2},{5,3},{6,0},{7,1},{8,14},{9,15},{10,... | collective-permute-start | bytes 589832 | tf_op jit(solution)/shard_map/ppermute | solution.py:20
  26.0 3.1 %collective-permute-done.5.refs_4_ = bf16[128,768]{1,0:T(8,128)(2,1)S(1)} collective-permute-done((bf16[128,768]{1,0:T(8,128)(2,1)S(1)}, bf16[128,768]{1,0:T(8,128)(2,1)S(1)}, u32[]{:S(2)}, u32[]{:S(2)}) %collective-permute-start.5) | collective-permute-done | bytes 196640 | tf_op jit(solution)/shard_map/ppermute | solution.py:20
  29.2 2.5 %collective-permute-done.4.refs_3_ = bf16[128,768]{1,0:T(8,128)(2,1)S(1)} collective-permute-done((bf16[128,768]{1,0:T(8,128)(2,1)S(1)}, bf16[128,768]{1,0:T(8,128)(2,1)S(1)}, u32[]{:S(2)}, u32[]{:S(2)}) %collective-permute-start.4) | collective-permute-done | bytes 196640 | tf_op jit(solution)/shard_map/ppermute | solution.py:20
  32.3 1.4 mix_kernel.1
  35.6 1.5 collective-permute-start.21
  37.1 4.6 %attend_kernel.1 = (f32[512,256]{1,0:T(8,128)S(1)}, bf16[128,192]{1,0:T(8,128)(2,1)S(1)}, bf16[128,192]{1,0:T(8,128)(2,1)S(1)}, bf16[128,192]{1,0:T(8,128)(2,1)S...) custom-call(s32[8]{0:T(128)S(1)} %stack.41.refs_0_, ...), custom_call_target="tpu_custom_call" | custom-call | tf_op jit(solution)/shard_map/attend_kernel/pallas_call | solution.py:92
  42.9 1.7 collective-permute-start.13
  44.6 1.0 collective-permute-start.14
  46.3 1.1 collective-permute-done.13.refs_3_
  47.5 2.3 %collective-permute-done.14.refs_4_ = bf16[128,192]{1,0:T(8,128)(2,1)S(1)} collective-permute-done((bf16[128,192]{1,0:T(8,128)(2,1)S(1)}, bf16[128,192]{1,0:T(8,128)(2,1)S(1)}, u32[]{:S(2)}, u32[]{:S(2)}) %collective-permute-start.14) | collective-permute-done | bytes 49184 | tf_op jit(solution)/shard_map/ppermute | solution.py:20
  49.8 1.2 mid_kernel.1
  51.0 1.0 collective-permute-start.15
  51.9 4.8 %collective-permute-done.15.refs_2_ = bf16[128,768]{1,0:T(8,128)(2,1)S(1)} collective-permute-done((bf16[128,768]{1,0:T(8,128)(2,1)S(1)}, bf16[128,768]{1,0:T(8,128)(2,1)S(1)}, u32[]{:S(2)}, u32[]{:S(2)}) %collective-permute-start.15) | collective-permute-done | bytes 196640 | tf_op jit(solution)/shard_map/ppermute | solution.py:20
  57.2 5.0 %collective-permute-done.21.refs_12_ = bf16[768,384]{1,0:T(8,128)(2,1)S(1)} collective-permute-done((bf16[768,384]{1,0:T(8,128)(2,1)S(1)}, bf16[768,384]{1,0:T(8,128)(2,1)S(1)}, u32[]{:S(2)}, u32[]{:S(2)}) %collective-permute-start.21) | collective-permute-done | bytes 589856 | tf_op jit(solution)/shard_map/ppermute | solution.py:24
  62.3 2.9 %feed_kernel.1 = (bf16[128,768]{1,0:T(8,128)(2,1)S(1)}, bf16[128,768]{1,0:T(8,128)(2,1)S(1)}, bf16[128,768]{1,0:T(8,128)(2,1)S(1)}, bf16[128,768]{1,0:T(8,128)(2...) custom-call(s32[8]{0:T(128)S(1)} %stack.41.refs_0_, ...), custom_call_target="tpu_custom_call" | custom-call | tf_op jit(solution)/shard_map/feed_kernel/pallas_call | solution.py:92
  65.2 1.4 outer_kernel.2
  66.6 1.2 collective-permute-start.28
  68.3 0.9 collective-permute-done.23.refs_1_
  69.3 1.5 collective-permute-start.24
  70.7 1.4 outer_kernel.3
  72.7 3.6 %collective-permute-done.24.refs_2_ = bf16[128,768]{1,0:T(8,128)(2,1)S(1)} collective-permute-done((bf16[128,768]{1,0:T(8,128)(2,1)S(1)}, bf16[128,768]{1,0:T(8,128)(2,1)S(1)}, u32[]{:S(2)}, u32[]{:S(2)}) %collective-permute-start.24) | collective-permute-done | bytes 196640 | tf_op jit(solution)/shard_map/ppermute | solution.py:20
  77.1 1.5 collective-permute-start.25
  79.0 1.7 collective-permute-start.27
  80.7 2.0 %collective-permute-done.28.refs_2_ = bf16[384,768]{1,0:T(8,128)(2,1)S(1)} collective-permute-done((bf16[384,768]{1,0:T(8,128)(2,1)S(1)}, bf16[384,768]{1,0:T(8,128)(2,1)S(1)}, u32[]{:S(2)}, u32[]{:S(2)}) %collective-permute-start.28) | collective-permute-done | bytes 589856 | tf_op jit(solution)/shard_map/ppermute | solution.py:20
  83.4 1.3 proj_grad_kernel.1
  84.8 3.0 %back_kernel.3 = (bf16[512,128]{1,0:T(8,128)(2,1)S(1)}, f32[512,128]{1,0:T(8,128)S(1)}, bf16[512,128]{1,0:T(8,128)(2,1)S(1)}, f32[256,128]{1,0:T(8,128)S(1)}) custom-call(s32[8]{0:T(128)S(1)} %stack.41.refs_0_, bf16[3,512,256]{2,1,0:T(8,128)(2,1)S(1)} %get-tuple-element.163.refs_1_, bf16[512,384]{1,0:T(8,128)(2,1)S(1)} %get-tuple-element.141.refs_2_, ...), custom_call_target="tpu_custom_call" | custom-call | tf_op jit(solution)/shard_map/back_kernel/pallas_call | solution.py:92
  87.8 1.0 collective-permute-start.33
  89.1 2.9 %back_kernel.4 = (bf16[512,128]{1,0:T(8,128)(2,1)S(1)}, f32[512,128]{1,0:T(8,128)S(1)}, bf16[512,128]{1,0:T(8,128)(2,1)S(1)}, f32[256,128]{1,0:T(8,128)S(1)}) custom-call(s32[8]{0:T(128)S(1)} %stack.41.refs_0_, bf16[3,512,256]{2,1,0:T(8,128)(2,1)S(1)} %get-tuple-element.163.refs_1_, bf16[512,384]{1,0:T(8,128)(2,1)S(1)} %get-tuple-element.141.refs_2_, ...), custom_call_target="tpu_custom_call" | custom-call | tf_op jit(solution)/shard_map/back_kernel/pallas_call | solution.py:92
  93.5 3.0 %back_kernel.5 = (bf16[512,128]{1,0:T(8,128)(2,1)S(1)}, f32[512,128]{1,0:T(8,128)S(1)}, bf16[512,128]{1,0:T(8,128)(2,1)S(1)}, f32[256,128]{1,0:T(8,128)S(1)}) custom-call(s32[8]{0:T(128)S(1)} %stack.41.refs_0_, bf16[3,512,256]{2,1,0:T(8,128)(2,1)S(1)} %get-tuple-element.163.refs_1_, bf16[512,384]{1,0:T(8,128)(2,1)S(1)} %get-tuple-element.141.refs_2_, ...), custom_call_target="tpu_custom_call" | custom-call | tf_op jit(solution)/shard_map/back_kernel/pallas_call | solution.py:92
  98.3 1.8 qkv_grad_kernel.1
  100.7 1.6 collective-permute-start.38
  104.0 1.2 collective-permute-start.41
  105.2 1.8 %collective-permute-start.42 = (bf16[192,384]{1,0:T(8,128)(2,1)S(1)}, bf16[192,384]{1,0:T(8,128)(2,1)S(1)}, u32[]{:S(2)}, u32[]{:S(2)}) collective-permute-start(bf16[192,384]{1,0:T(8,128)(2,1)S(1)} %get-tuple-element.206.refs_17_), channel_id=1, source_target_pairs={{0,8},{1,9},{2,10},{3,11},{4,12},{5,13},{6,14},{7,15},{8,0},{9,1},... | collective-permute-start | bytes 442376 | tf_op jit(solution)/shard_map/ppermute | solution.py:20
  107.0 5.2 %collective-permute-done.38.refs_2_ = bf16[192,768]{1,0:T(8,128)(2,1)S(1)} collective-permute-done((bf16[192,768]{1,0:T(8,128)(2,1)S(1)}, bf16[192,768]{1,0:T(8,128)(2,1)S(1)}, u32[]{:S(2)}, u32[]{:S(2)}) %collective-permute-start.38) | collective-permute-done | bytes 294944 | tf_op jit(solution)/shard_map/ppermute | solution.py:20
  114.1 1.6 collective-permute-start.48
  116.3 1.0 collective-permute-start.43
  117.3 2.5 %collective-permute-start.46 = (bf16[192,384]{1,0:T(8,128)(2,1)S(1)}, bf16[192,384]{1,0:T(8,128)(2,1)S(1)}, u32[]{:S(2)}, u32[]{:S(2)}) collective-permute-start(bf16[192,384]{1,0:T(8,128)(2,1)S(1)} %add_kernel.10.refs_2_.refs_1_), channel_id=1, source_target_pairs={{0,8},{1,9},{2,10},{3,11},{4,12},{5,13},{6,14},{7,15},{8,0},{9,1},... | collective-permute-start | bytes 442376 | tf_op jit(solution)/shard_map/ppermute | solution.py:20
  119.8 1.7 collective-permute-done.43.refs_1_
  121.6 7.0 %collective-permute-start.45 = (bf16[96,768]{1,0:T(8,128)(2,1)S(1)}, bf16[96,768]{1,0:T(8,128)(2,1)S(1)}, u32[]{:S(2)}, u32[]{:S(2)}) collective-permute-start(bf16[96,768]{1,0:T(8,128)(2,1)S(1)} %add_kernel.11.refs_2_.refs_0_), channel_id=1, source_target_pairs={{0,4},{1,5},{2,6},{3,7},{4,0},{5,1},{6,2},{7,3},{8,12},{9,13},{10,... | collective-permute-start | bytes 442376 | tf_op jit(solution)/shard_map/ppermute | solution.py:20
  129.2 3.0 %collective-permute-start.49 = (bf16[96,768]{1,0:T(8,128)(2,1)S(1)}, bf16[96,768]{1,0:T(8,128)(2,1)S(1)}, u32[]{:S(2)}, u32[]{:S(2)}) collective-permute-start(bf16[96,768]{1,0:T(8,128)(2,1)S(1)} %get-tuple-element.216.refs_2_), channel_id=1, source_target_pairs={{0,8},{1,9},{2,10},{3,11},{4,12},{5,13},{6,14},{7,15},{8,0},{9,1},... | collective-permute-start | bytes 442376 | tf_op jit(solution)/shard_map/ppermute | solution.py:20
  132.2 1.5 collective-permute-start.55
  134.4 4.4 %collective-permute-start.54 = (bf16[224,576]{1,0:T(8,128)(2,1)S(1)}, bf16[224,576]{1,0:T(8,128)(2,1)S(1)}, u32[]{:S(2)}, u32[]{:S(2)}) collective-permute-start(bf16[224,576]{1,0:T(8,128)(2,1)S(1)} %add_kernel.12.refs_6_.refs_1_), channel_id=1, source_target_pairs={{0,2},{1,3},{2,0},{3,1},{4,6},{5,7},{6,4},{7,5},{8,10},{9,11},{10,... | collective-permute-start | bytes 774152 | tf_op jit(solution)/shard_map/ppermute | solution.py:20
  138.8 3.1 %collective-permute-start.44 = (bf16[64,768]{1,0:T(8,128)(2,1)S(1)}, bf16[64,768]{1,0:T(8,128)(2,1)S(1)}, u32[]{:S(2)}, u32[]{:S(2)}) collective-permute-start(bf16[64,768]{1,0:T(8,128)(2,1)S(1)} %get-tuple-element.224), channel_id=1, source_target_pairs={{0,8},{1,9},{2,10},{3,11},{4,12},{5,13},{6,14},{7,15},{8,0},{9,1},... | collective-permute-start | bytes 294920 | tf_op jit(solution)/shard_map/ppermute | solution.py:20
  142.8 2.7 %collective-permute-start.50 = (bf16[128,768]{1,0:T(8,128)(2,1)S(1)}, bf16[128,768]{1,0:T(8,128)(2,1)S(1)}, u32[]{:S(2)}, u32[]{:S(2)}) collective-permute-start(bf16[128,768]{1,0:T(8,128)(2,1)S(1)} %tail_add_kernel.3.refs_2_), channel_id=1, source_target_pairs={{0,4},{1,5},{2,6},{3,7},{4,0},{5,1},{6,2},{7,3},{8,12},{9,13},{10,... | collective-permute-start | bytes 589832 | tf_op jit(solution)/shard_map/ppermute | solution.py:20
  145.5 3.5 %collective-permute-done.44.refs_2_ = bf16[64,768]{1,0:T(8,128)(2,1)S(1)} collective-permute-done((bf16[64,768]{1,0:T(8,128)(2,1)S(1)}, bf16[64,768]{1,0:T(8,128)(2,1)S(1)}, u32[]{:S(2)}, u32[]{:S(2)}) %collective-permute-start.44) | collective-permute-done | bytes 98336 | tf_op jit(solution)/shard_map/ppermute | solution.py:20
  149.7 2.9 %collective-permute-done.47.refs_1_ = bf16[96,768]{1,0:T(8,128)(2,1)S(1)} collective-permute-done((bf16[96,768]{1,0:T(8,128)(2,1)S(1)}, bf16[96,768]{1,0:T(8,128)(2,1)S(1)}, u32[]{:S(2)}, u32[]{:S(2)}) %collective-permute-start.47) | collective-permute-done | bytes 147488 | tf_op jit(solution)/shard_map/ppermute | solution.py:20
  153.0 1.5 collective-permute-done.50.refs_2_
  154.5 2.7 %collective-permute-start.52 = (bf16[96,768]{1,0:T(8,128)(2,1)S(1)}, bf16[96,768]{1,0:T(8,128)(2,1)S(1)}, u32[]{:S(2)}, u32[]{:S(2)}) collective-permute-start(bf16[96,768]{1,0:T(8,128)(2,1)S(1)} %add_kernel.14.refs_2_.refs_1_), channel_id=1, source_target_pairs={{0,8},{1,9},{2,10},{3,11},{4,12},{5,13},{6,14},{7,15},{8,0},{9,1},... | collective-permute-start | bytes 442376 | tf_op jit(solution)/shard_map/ppermute | solution.py:20
  157.2 1.3 place_kernel.1
  159.3 3.5 %collective-permute-start.51 = (bf16[64,768]{1,0:T(8,128)(2,1)S(1)}, bf16[64,768]{1,0:T(8,128)(2,1)S(1)}, u32[]{:S(2)}, u32[]{:S(2)}) collective-permute-start(bf16[64,768]{1,0:T(8,128)(2,1)S(1)} %get-tuple-element.232), channel_id=1, source_target_pairs={{0,8},{1,9},{2,10},{3,11},{4,12},{5,13},{6,14},{7,15},{8,0},{9,1},... | collective-permute-start | bytes 294920 | tf_op jit(solution)/shard_map/ppermute | solution.py:20
  163.4 1.6 vector_out_kernel.1
  165.8 1.6 join_out_kernel.3
  168.0 1.9 %collective-permute-start.63 = (bf16[192,768]{1,0:T(8,128)(2,1)S(1)}, bf16[192,768]{1,0:T(8,128)(2,1)S(1)}, u32[]{:S(2)}, u32[]{:S(2)}) collective-permute-start(bf16[192,768]{1,0:T(8,128)(2,1)S(1)} %join_kernel.5.refs_3_.refs_1_), channel_id=1, source_target_pairs={{0,4},{1,5},{2,6},{3,7},{4,0},{5,1},{6,2},{7,3},{8,12},{9,13},{10,... | collective-permute-start | bytes 884744 | tf_op jit(solution)/shard_map/ppermute | solution.py:20
  170.7 1.3 place_two_kernel.1
  172.3 2.8 %qkv_out_kernel.1 = (f32[8,128]{1,0:T(8,128)S(1)}, f32[384,2304]{1,0:T(8,128)}) custom-call(s32[8]{0:T(128)S(1)} %stack.41.refs_0_, bf16[224,576]{1,0:T(8,128)(2,1)S(1)} %add_kernel.12.refs_6_.refs_1_, bf16[224,576]{1,0:T(8,128)(2,1)S(1)} %collective-permute-done.54.refs_2_, bf16[224,576]{1,0:T(8,128)(2,1)S(1)} %collective-permute-done.55.refs_3_, ...), custom_call_target="tpu_custom_call" | custom-call | tf_op jit(solution)/shard_map/qkv_out_kernel/pallas_call | solution.py:92
  175.1 1.6 join_out_kernel.4
  177.6 2.2 %join_out_kernel.5 = (f32[8,128]{1,0:T(8,128)}, f32[384,768]{1,0:T(8,128)}) custom-call(s32[8]{0:T(128)S(1)} %stack.41.refs_0_, bf16[192,768]{1,0:T(8,128)(2,1)S(1)} %join_kernel.5.refs_3_.refs_1_, bf16[192,768]{1,0:T(8,128)(2,1)S(1)} %collective-permute-done.63.refs_2_, f32[8,128]{1,0:T(8,128)S(1)} %get-tuple-element.245.refs_3_), custom_call_target="tpu_custom_call" | custom-call | tf_op jit(solution)/shard_map/join_out_kernel/pallas_call | solution.py:92
  (132 shorter events, 32.5 us)
Async XLA Ops:
  2.3 13.2 %collective-permute-start = (f32[64,768]{1,0:T(8,128)S(1)}, f32[64,768]{1,0:T(8,128)S(1)}, u32[]{:S(2)}, u32[]{:S(2)}) collective-permute-start(f32[64,768]{1,0:T(8,128)S(1)} %get-tuple-element.131.refs_3_), channel_id=1, source_target_pairs={{0,8},{1,9},{2,10},{3,11},{4,12},{5,13},{6,14},{7,15},{8,0},{9,1},... | collective-permute-start | bytes 589832 | tf_op jit(solution)/shard_map/ppermute | solution.py:20
  7.2 6.0 %collective-permute-start.2 = (bf16[2,32,63]{2,1,0:T(8,128)(2,1)S(1)}, bf16[2,32,63]{2,1,0:T(8,128)(2,1)S(1)}, u32[]{:S(2)}, u32[]{:S(2)}) collective-permute-start(bf16[2,32,63]{2,1,0:T(8,128)(2,1)S(1)} %pad_maximum_fusion.refs_1_), channel_id=1, source_target_pairs={{0,16},{16,0},{1,17},{17,1},{2,18},{18,2},{3,19},{19,3},{4,20},{20... | collective-permute-start | bytes 24200 | tf_op jit(solution)/shard_map/ppermute | solution.py:24
  9.5 3.7 %collective-permute-start.1 = (bf16[4,384]{1,0:T(4,128)(2,1)S(1)}, bf16[4,384]{1,0:T(4,128)(2,1)S(1)}, u32[]{:S(2)}, u32[]{:S(2)}) collective-permute-start(bf16[4,384]{1,0:T(4,128)(2,1)S(1)} %reshape.27.refs_3_), channel_id=1, source_target_pairs={{0,16},{16,0},{1,17},{17,1},{2,18},{18,2},{3,19},{19,3},{4,20},{20... | collective-permute-start | bytes 9224 | tf_op jit(solution)/shard_map/ppermute | solution.py:24
  15.6 16.8 %collective-permute-start.6 = (bf16[384,576]{1,0:T(8,128)(2,1)S(1)}, bf16[384,576]{1,0:T(8,128)(2,1)S(1)}, u32[]{:S(2)}, u32[]{:S(2)}) collective-permute-start(bf16[384,576]{1,0:T(8,128)(2,1)S(1)} %pack_kernel.1.refs_5_), channel_id=1, source_target_pairs={{0,16},{16,0},{1,17},{17,1},{2,18},{18,2},{3,19},{19,3},{4,20},{20... | collective-permute-start | bytes 1327112 | tf_op jit(solution)/shard_map/ppermute | solution.py:24
  17.1 7.3 %collective-permute-start.7 = (bf16[64,768]{1,0:T(8,128)(2,1)S(1)}, bf16[64,768]{1,0:T(8,128)(2,1)S(1)}, u32[]{:S(2)}, u32[]{:S(2)}) collective-permute-start(bf16[64,768]{1,0:T(8,128)(2,1)S(1)} %get-tuple-element.137), channel_id=1, source_target_pairs={{0,8},{1,9},{2,10},{3,11},{4,12},{5,13},{6,14},{7,15},{8,0},{9,1},... | collective-permute-start | bytes 294920 | tf_op jit(solution)/shard_map/ppermute | solution.py:20
  17.9 11.3 %collective-permute-start.5 = (bf16[128,768]{1,0:T(8,128)(2,1)S(1)}, bf16[128,768]{1,0:T(8,128)(2,1)S(1)}, u32[]{:S(2)}, u32[]{:S(2)}) collective-permute-start(bf16[128,768]{1,0:T(8,128)(2,1)S(1)} %get-tuple-element.135.refs_1_), channel_id=1, source_target_pairs={{0,6},{1,7},{2,4},{3,5},{4,2},{5,3},{6,0},{7,1},{8,14},{9,15},{10,... | collective-permute-start | bytes 589832 | tf_op jit(solution)/shard_map/ppermute | solution.py:20
  22.9 8.8 %collective-permute-start.4 = (bf16[128,768]{1,0:T(8,128)(2,1)S(1)}, bf16[128,768]{1,0:T(8,128)(2,1)S(1)}, u32[]{:S(2)}, u32[]{:S(2)}) collective-permute-start(bf16[128,768]{1,0:T(8,128)(2,1)S(1)} %get-tuple-element.135.refs_1_), channel_id=1, source_target_pairs={{0,4},{1,5},{2,6},{3,7},{4,0},{5,1},{6,2},{7,3},{8,12},{9,13},{10,... | collective-permute-start | bytes 589832 | tf_op jit(solution)/shard_map/ppermute | solution.py:20
  23.0 9.4 %collective-permute-start.3 = (bf16[128,768]{1,0:T(8,128)(2,1)S(1)}, bf16[128,768]{1,0:T(8,128)(2,1)S(1)}, u32[]{:S(2)}, u32[]{:S(2)}) collective-permute-start(bf16[128,768]{1,0:T(8,128)(2,1)S(1)} %get-tuple-element.135.refs_1_), channel_id=1, source_target_pairs={{0,2},{1,3},{2,0},{3,1},{4,6},{5,7},{6,4},{7,5},{8,10},{9,11},{10,... | collective-permute-start | bytes 589832 | tf_op jit(solution)/shard_map/ppermute | solution.py:20
  25.8 9.0 %collective-permute-start.10 = (bf16[192,768]{1,0:T(8,128)(2,1)S(1)}, bf16[192,768]{1,0:T(8,128)(2,1)S(1)}, u32[]{:S(2)}, u32[]{:S(2)}) collective-permute-start(bf16[192,768]{1,0:T(8,128)(2,1)S(1)} %rows_kernel.1.refs_7_), channel_id=1, source_target_pairs={{0,16},{16,0},{1,17},{17,1},{2,18},{18,2},{3,19},{19,3},{4,20},{20... | collective-permute-start | bytes 884744 | tf_op jit(solution)/shard_map/ppermute | solution.py:24
  33.8 3.3 %collective-permute-start.8 = (bf16[512,384]{1,0:T(8,128)(2,1)S(1)}, bf16[512,384]{1,0:T(8,128)(2,1)S(1)}, u32[]{:S(2)}, u32[]{:S(2)}) collective-permute-start(bf16[512,384]{1,0:T(8,128)(2,1)S(1)} %get-tuple-element.141.refs_2_), channel_id=1, source_target_pairs={{0,1},{1,0},{2,3},{3,2},{4,5},{5,4},{6,7},{7,6},{8,9},{9,8},{10,11... | collective-permute-start | bytes 1179656 | tf_op jit(solution)/shard_map/ppermute | solution.py:20
  33.9 23.4 %collective-permute-start.20 = (bf16[384,768]{1,0:T(8,128)(2,1)S(1)}, bf16[384,768]{1,0:T(8,128)(2,1)S(1)}, u32[]{:S(2)}, u32[]{:S(2)}) collective-permute-start(bf16[384,768]{1,0:T(8,128)(2,1)S(1)} %copy-done.2), channel_id=1, source_target_pairs={{0,16},{16,0},{1,17},{17,1},{2,18},{18,2},{3,19},{19,3},{4,20},{20... | collective-permute-start | bytes 1769480 | tf_op jit(solution)/shard_map/ppermute | solution.py:24
  34.7 7.3 %collective-permute-start.11 = (bf16[192,768]{1,0:T(8,128)(2,1)S(1)}, bf16[192,768]{1,0:T(8,128)(2,1)S(1)}, u32[]{:S(2)}, u32[]{:S(2)}) collective-permute-start(bf16[192,768]{1,0:T(8,128)(2,1)S(1)} %collective-permute-done.10.refs_6_), channel_id=1, source_target_pairs={{0,1},{1,0},{2,3},{3,2},{4,5},{5,4},{6,7},{7,6},{8,9},{9,8},{10,11... | collective-permute-start | bytes 884744 | tf_op jit(solution)/shard_map/ppermute | solution.py:20
  34.9 7.2 %collective-permute-start.9 = (bf16[128,768]{1,0:T(8,128)(2,1)S(1)}, bf16[128,768]{1,0:T(8,128)(2,1)S(1)}, u32[]{:S(2)}, u32[]{:S(2)}) collective-permute-start(bf16[128,768]{1,0:T(8,128)(2,1)S(1)} %stack_kernel.1.refs_3_.refs_5_), channel_id=1, source_target_pairs={{0,2},{1,3},{2,0},{3,1},{4,6},{5,7},{6,4},{7,5},{8,10},{9,11},{10,... | collective-permute-start | bytes 589832 | tf_op jit(solution)/shard_map/ppermute | solution.py:20
  35.6 26.7 %collective-permute-start.21 = (bf16[768,384]{1,0:T(8,128)(2,1)S(1)}, bf16[768,384]{1,0:T(8,128)(2,1)S(1)}, u32[]{:S(2)}, u32[]{:S(2)}) collective-permute-start(bf16[768,384]{1,0:T(8,128)(2,1)S(1)} %copy-done.3), channel_id=1, source_target_pairs={{0,16},{16,0},{1,17},{17,1},{2,18},{18,2},{3,19},{19,3},{4,20},{20... | collective-permute-start | bytes 1769480 | tf_op jit(solution)/shard_map/ppermute | solution.py:24
  42.1 4.3 %collective-permute-start.12 = (bf16[128,192]{1,0:T(8,128)(2,1)S(1)}, bf16[128,192]{1,0:T(8,128)(2,1)S(1)}, u32[]{:S(2)}, u32[]{:S(2)}) collective-permute-start(bf16[128,192]{1,0:T(8,128)(2,1)S(1)} %get-tuple-element.152), channel_id=1, source_target_pairs={{0,2},{1,3},{2,0},{3,1},{4,6},{5,7},{6,4},{7,5},{8,10},{9,11},{10,... | collective-permute-start | bytes 147464 | tf_op jit(solution)/shard_map/ppermute | solution.py:20
  42.9 4.6 %collective-permute-start.13 = (bf16[128,192]{1,0:T(8,128)(2,1)S(1)}, bf16[128,192]{1,0:T(8,128)(2,1)S(1)}, u32[]{:S(2)}, u32[]{:S(2)}) collective-permute-start(bf16[128,192]{1,0:T(8,128)(2,1)S(1)} %get-tuple-element.153), channel_id=1, source_target_pairs={{0,4},{1,5},{2,6},{3,7},{4,0},{5,1},{6,2},{7,3},{8,12},{9,13},{10,... | collective-permute-start | bytes 147464 | tf_op jit(solution)/shard_map/ppermute | solution.py:20
  44.6 5.2 %collective-permute-start.14 = (bf16[128,192]{1,0:T(8,128)(2,1)S(1)}, bf16[128,192]{1,0:T(8,128)(2,1)S(1)}, u32[]{:S(2)}, u32[]{:S(2)}) collective-permute-start(bf16[128,192]{1,0:T(8,128)(2,1)S(1)} %get-tuple-element.154), channel_id=1, source_target_pairs={{0,6},{1,7},{2,4},{3,5},{4,2},{5,3},{6,0},{7,1},{8,14},{9,15},{10,... | collective-permute-start | bytes 147464 | tf_op jit(solution)/shard_map/ppermute | solution.py:20
  51.0 5.7 %collective-permute-start.15 = (bf16[128,768]{1,0:T(8,128)(2,1)S(1)}, bf16[128,768]{1,0:T(8,128)(2,1)S(1)}, u32[]{:S(2)}, u32[]{:S(2)}) collective-permute-start(bf16[128,768]{1,0:T(8,128)(2,1)S(1)} %get-tuple-element.156.refs_1_), channel_id=1, source_target_pairs={{0,2},{1,3},{2,0},{3,1},{4,6},{5,7},{6,4},{7,5},{8,10},{9,11},{10,... | collective-permute-start | bytes 589832 | tf_op jit(solution)/shard_map/ppermute | solution.py:20
  51.9 10.3 %collective-permute-start.16 = (bf16[128,768]{1,0:T(8,128)(2,1)S(1)}, bf16[128,768]{1,0:T(8,128)(2,1)S(1)}, u32[]{:S(2)}, u32[]{:S(2)}) collective-permute-start(bf16[128,768]{1,0:T(8,128)(2,1)S(1)} %get-tuple-element.156.refs_1_), channel_id=1, source_target_pairs={{0,1},{1,0},{2,3},{3,2},{4,5},{5,4},{6,7},{7,6},{8,9},{9,8},{10,11... | collective-permute-start | bytes 589832 | tf_op jit(solution)/shard_map/ppermute | solution.py:20
  56.7 5.5 %collective-permute-start.18 = (bf16[128,768]{1,0:T(8,128)(2,1)S(1)}, bf16[128,768]{1,0:T(8,128)(2,1)S(1)}, u32[]{:S(2)}, u32[]{:S(2)}) collective-permute-start(bf16[128,768]{1,0:T(8,128)(2,1)S(1)} %stack_kernel.1.refs_3_.refs_5_), channel_id=1, source_target_pairs={{0,1},{1,0},{2,3},{3,2},{4,5},{5,4},{6,7},{7,6},{8,9},{9,8},{10,11... | collective-permute-start | bytes 589832 | tf_op jit(solution)/shard_map/ppermute | solution.py:20
  56.7 5.5 %collective-permute-start.19 = (bf16[128,768]{1,0:T(8,128)(2,1)S(1)}, bf16[128,768]{1,0:T(8,128)(2,1)S(1)}, u32[]{:S(2)}, u32[]{:S(2)}) collective-permute-start(bf16[128,768]{1,0:T(8,128)(2,1)S(1)} %collective-permute-done.9.refs_6_), channel_id=1, source_target_pairs={{0,1},{1,0},{2,3},{3,2},{4,5},{5,4},{6,7},{7,6},{8,9},{9,8},{10,11... | collective-permute-start | bytes 589832 | tf_op jit(solution)/shard_map/ppermute | solution.py:20
  57.2 5.0 %collective-permute-start.17 = (bf16[128,768]{1,0:T(8,128)(2,1)S(1)}, bf16[128,768]{1,0:T(8,128)(2,1)S(1)}, u32[]{:S(2)}, u32[]{:S(2)}) collective-permute-start(bf16[128,768]{1,0:T(8,128)(2,1)S(1)} %collective-permute-done.15.refs_2_), channel_id=1, source_target_pairs={{0,1},{1,0},{2,3},{3,2},{4,5},{5,4},{6,7},{7,6},{8,9},{9,8},{10,11... | collective-permute-start | bytes 589832 | tf_op jit(solution)/shard_map/ppermute | solution.py:20
  66.6 16.1 %collective-permute-start.28 = (bf16[384,768]{1,0:T(8,128)(2,1)S(1)}, bf16[384,768]{1,0:T(8,128)(2,1)S(1)}, u32[]{:S(2)}, u32[]{:S(2)}) collective-permute-start(bf16[384,768]{1,0:T(8,128)(2,1)S(1)} %get-tuple-element.169.refs_2_), channel_id=1, source_target_pairs={{0,4},{1,5},{2,6},{3,7},{4,0},{5,1},{6,2},{7,3},{8,12},{9,13},{10,... | collective-permute-start | bytes 1769480 | tf_op jit(solution)/shard_map/ppermute | solution.py:20
  67.8 1.4 collective-permute-start.23
  67.8 4.9 %collective-permute-start.22 = (bf16[128,768]{1,0:T(8,128)(2,1)S(1)}, bf16[128,768]{1,0:T(8,128)(2,1)S(1)}, u32[]{:S(2)}, u32[]{:S(2)}) collective-permute-start(bf16[128,768]{1,0:T(8,128)(2,1)S(1)} %get-tuple-element.165), channel_id=1, source_target_pairs={{0,1},{1,0},{2,3},{3,2},{4,5},{5,4},{6,7},{7,6},{8,9},{9,8},{10,11... | collective-permute-start | bytes 589832 | tf_op jit(solution)/shard_map/ppermute | solution.py:20
  69.3 7.0 %collective-permute-start.24 = (bf16[128,768]{1,0:T(8,128)(2,1)S(1)}, bf16[128,768]{1,0:T(8,128)(2,1)S(1)}, u32[]{:S(2)}, u32[]{:S(2)}) collective-permute-start(bf16[128,768]{1,0:T(8,128)(2,1)S(1)} %add_kernel.8.refs_3_), channel_id=1, source_target_pairs={{0,2},{1,3},{2,0},{3,1},{4,6},{5,7},{6,4},{7,5},{8,10},{9,11},{10,... | collective-permute-start | bytes 589832 | tf_op jit(solution)/shard_map/ppermute | solution.py:20
  72.1 24.9 %collective-permute-start.34 = (bf16[384,768]{1,0:T(8,128)(2,1)S(1)}, bf16[384,768]{1,0:T(8,128)(2,1)S(1)}, u32[]{:S(2)}, u32[]{:S(2)}) collective-permute-start(bf16[384,768]{1,0:T(8,128)(2,1)S(1)} %get-tuple-element.173.refs_7_), channel_id=1, source_target_pairs={{0,16},{16,0},{1,17},{17,1},{2,18},{18,2},{3,19},{19,3},{4,20},{20... | collective-permute-start | bytes 1769480 | tf_op jit(solution)/shard_map/ppermute | solution.py:24
  77.1 7.6 %collective-permute-start.25 = (bf16[128,192]{1,0:T(8,128)(2,1)S(1)}, bf16[128,192]{1,0:T(8,128)(2,1)S(1)}, u32[]{:S(2)}, u32[]{:S(2)}) collective-permute-start(bf16[128,192]{1,0:T(8,128)(2,1)S(1)} %get-tuple-element.175), channel_id=1, source_target_pairs={{0,2},{1,3},{2,0},{3,1},{4,6},{5,7},{6,4},{7,5},{8,10},{9,11},{10,... | collective-permute-start | bytes 147464 | tf_op jit(solution)/shard_map/ppermute | solution.py:20
  78.6 6.1 %collective-permute-start.26 = (bf16[128,192]{1,0:T(8,128)(2,1)S(1)}, bf16[128,192]{1,0:T(8,128)(2,1)S(1)}, u32[]{:S(2)}, u32[]{:S(2)}) collective-permute-start(bf16[128,192]{1,0:T(8,128)(2,1)S(1)} %get-tuple-element.176), channel_id=1, source_target_pairs={{0,4},{1,5},{2,6},{3,7},{4,0},{5,1},{6,2},{7,3},{8,12},{9,13},{10,... | collective-permute-start | bytes 147464 | tf_op jit(solution)/shard_map/ppermute | solution.py:20
  79.0 5.7 %collective-permute-start.27 = (bf16[128,192]{1,0:T(8,128)(2,1)S(1)}, bf16[128,192]{1,0:T(8,128)(2,1)S(1)}, u32[]{:S(2)}, u32[]{:S(2)}) collective-permute-start(bf16[128,192]{1,0:T(8,128)(2,1)S(1)} %get-tuple-element.177), channel_id=1, source_target_pairs={{0,6},{1,7},{2,4},{3,5},{4,2},{5,3},{6,0},{7,1},{8,14},{9,15},{10,... | collective-permute-start | bytes 147464 | tf_op jit(solution)/shard_map/ppermute | solution.py:20
  87.7 1.4 collective-permute-start.29
  87.8 9.9 %collective-permute-start.33 = (bf16[384,384]{1,0:T(8,128)(2,1)S(1)}, bf16[384,384]{1,0:T(8,128)(2,1)S(1)}, u32[]{:S(2)}, u32[]{:S(2)}) collective-permute-start(bf16[384,384]{1,0:T(8,128)(2,1)S(1)} %get-tuple-element.182.refs_6_), channel_id=1, source_target_pairs={{0,16},{16,0},{1,17},{17,1},{2,18},{18,2},{3,19},{19,3},{4,20},{20... | collective-permute-start | bytes 884744 | tf_op jit(solution)/shard_map/ppermute | solution.py:24
  92.0 1.4 collective-permute-start.31
  96.4 1.9 %collective-permute-start.32 = (bf16[512,128]{1,0:T(8,128)(2,1)S(1)}, bf16[512,128]{1,0:T(8,128)(2,1)S(1)}, u32[]{:S(2)}, u32[]{:S(2)}) collective-permute-start(bf16[512,128]{1,0:T(8,128)(2,1)S(1)} %get-tuple-element.196), channel_id=1, source_target_pairs={{0,1},{1,0},{2,3},{3,2},{4,5},{5,4},{6,7},{7,6},{8,9},{9,8},{10,11... | collective-permute-start | bytes 393224 | tf_op jit(solution)/shard_map/ppermute | solution.py:20
  96.7 6.7 %collective-permute-start.39 = (bf16[384,768]{1,0:T(8,128)(2,1)S(1)}, bf16[384,768]{1,0:T(8,128)(2,1)S(1)}, u32[]{:S(2)}, u32[]{:S(2)}) collective-permute-start(bf16[384,768]{1,0:T(8,128)(2,1)S(1)} %get-tuple-element.214.refs_12_), channel_id=1, source_target_pairs={{0,1},{1,0},{2,3},{3,2},{4,5},{5,4},{6,7},{7,6},{8,9},{9,8},{10,11... | collective-permute-start | bytes 1769480 | tf_op jit(solution)/shard_map/ppermute | solution.py:20
  100.1 2.1 %collective-permute-start.35 = (bf16[416,576]{1,0:T(8,128)(2,1)S(1)}, bf16[416,576]{1,0:T(8,128)(2,1)S(1)}, u32[]{:S(2)}, u32[]{:S(2)}) collective-permute-start(bf16[416,576]{1,0:T(8,128)(2,1)S(1)} %get-tuple-element.208), channel_id=1, source_target_pairs={{0,1},{1,0},{2,3},{3,2},{4,5},{5,4},{6,7},{7,6},{8,9},{9,8},{10,11... | collective-permute-start | bytes 1437704 | tf_op jit(solution)/shard_map/ppermute | solution.py:20
  100.3 3.0 %collective-permute-start.30 = (bf16[256,768]{1,0:T(8,128)(2,1)S(1)}, bf16[256,768]{1,0:T(8,128)(2,1)S(1)}, u32[]{:S(2)}, u32[]{:S(2)}) collective-permute-start(bf16[256,768]{1,0:T(8,128)(2,1)S(1)} %get-tuple-element.189), channel_id=1, source_target_pairs={{0,1},{1,0},{2,3},{3,2},{4,5},{5,4},{6,7},{7,6},{8,9},{9,8},{10,11... | collective-permute-start | bytes 1179656 | tf_op jit(solution)/shard_map/ppermute | solution.py:20
  100.7 11.5 %collective-permute-start.38 = (bf16[192,768]{1,0:T(8,128)(2,1)S(1)}, bf16[192,768]{1,0:T(8,128)(2,1)S(1)}, u32[]{:S(2)}, u32[]{:S(2)}) collective-permute-start(bf16[192,768]{1,0:T(8,128)(2,1)S(1)} %get-tuple-element.205.refs_3_), channel_id=1, source_target_pairs={{0,4},{1,5},{2,6},{3,7},{4,0},{5,1},{6,2},{7,3},{8,12},{9,13},{10,... | collective-permute-start | bytes 884744 | tf_op jit(solution)/shard_map/ppermute | solution.py:20
  102.4 10.4 %collective-permute-start.37 = (bf16[224,576]{1,0:T(8,128)(2,1)S(1)}, bf16[224,576]{1,0:T(8,128)(2,1)S(1)}, u32[]{:S(2)}, u32[]{:S(2)}) collective-permute-start(bf16[224,576]{1,0:T(8,128)(2,1)S(1)} %get-tuple-element.210.refs_2_), channel_id=1, source_target_pairs={{0,16},{16,0},{1,17},{17,1},{2,18},{18,2},{3,19},{19,3},{4,20},{20... | collective-permute-start | bytes 774152 | tf_op jit(solution)/shard_map/ppermute | solution.py:24
  104.0 12.2 %collective-permute-start.41 = (bf16[192,768]{1,0:T(8,128)(2,1)S(1)}, bf16[192,768]{1,0:T(8,128)(2,1)S(1)}, u32[]{:S(2)}, u32[]{:S(2)}) collective-permute-start(bf16[192,768]{1,0:T(8,128)(2,1)S(1)} %get-tuple-element.215.refs_3_), channel_id=1, source_target_pairs={{0,2},{1,3},{2,0},{3,1},{4,6},{5,7},{6,4},{7,5},{8,10},{9,11},{10,... | collective-permute-start | bytes 884744 | tf_op jit(solution)/shard_map/ppermute | solution.py:20
  105.2 11.0 %collective-permute-start.42 = (bf16[192,384]{1,0:T(8,128)(2,1)S(1)}, bf16[192,384]{1,0:T(8,128)(2,1)S(1)}, u32[]{:S(2)}, u32[]{:S(2)}) collective-permute-start(bf16[192,384]{1,0:T(8,128)(2,1)S(1)} %get-tuple-element.206.refs_17_), channel_id=1, source_target_pairs={{0,8},{1,9},{2,10},{3,11},{4,12},{5,13},{6,14},{7,15},{8,0},{9,1},... | collective-permute-start | bytes 442376 | tf_op jit(solution)/shard_map/ppermute | solution.py:20
  112.9 16.3 %collective-permute-start.40 = (bf16[224,576]{1,0:T(8,128)(2,1)S(1)}, bf16[224,576]{1,0:T(8,128)(2,1)S(1)}, u32[]{:S(2)}, u32[]{:S(2)}) collective-permute-start(bf16[224,576]{1,0:T(8,128)(2,1)S(1)} %add_kernel.9.refs_3_.refs_0_), channel_id=1, source_target_pairs={{0,8},{1,9},{2,10},{3,11},{4,12},{5,13},{6,14},{7,15},{8,0},{9,1},... | collective-permute-start | bytes 774152 | tf_op jit(solution)/shard_map/ppermute | solution.py:20
  114.1 28.6 %collective-permute-start.48 = (bf16[256,768]{1,0:T(8,128)(2,1)S(1)}, bf16[256,768]{1,0:T(8,128)(2,1)S(1)}, u32[]{:S(2)}, u32[]{:S(2)}) collective-permute-start(bf16[256,768]{1,0:T(8,128)(2,1)S(1)} %get-tuple-element.226), channel_id=1, source_target_pairs={{0,2},{1,3},{2,0},{3,1},{4,6},{5,7},{6,4},{7,5},{8,10},{9,11},{10,... | collective-permute-start | bytes 1179656 | tf_op jit(solution)/shard_map/ppermute | solution.py:20
  115.7 16.6 %collective-permute-start.36 = (bf16[128,768]{1,0:T(8,128)(2,1)S(1)}, bf16[128,768]{1,0:T(8,128)(2,1)S(1)}, u32[]{:S(2)}, u32[]{:S(2)}) collective-permute-start(bf16[128,768]{1,0:T(8,128)(2,1)S(1)} %tail_add_kernel.2.refs_3_), channel_id=1, source_target_pairs={{0,2},{1,3},{2,0},{3,1},{4,6},{5,7},{6,4},{7,5},{8,10},{9,11},{10,... | collective-permute-start | bytes 589832 | tf_op jit(solution)/shard_map/ppermute | solution.py:20
  116.3 5.2 %collective-permute-start.43 = (bf16[96,768]{1,0:T(8,128)(2,1)S(1)}, bf16[96,768]{1,0:T(8,128)(2,1)S(1)}, u32[]{:S(2)}, u32[]{:S(2)}) collective-permute-start(bf16[96,768]{1,0:T(8,128)(2,1)S(1)} %get-tuple-element.222.refs_2_), channel_id=1, source_target_pairs={{0,16},{16,0},{1,17},{17,1},{2,18},{18,2},{3,19},{19,3},{4,20},{20... | collective-permute-start | bytes 442376 | tf_op jit(solution)/shard_map/ppermute | solution.py:24
  117.3 17.1 %collective-permute-start.46 = (bf16[192,384]{1,0:T(8,128)(2,1)S(1)}, bf16[192,384]{1,0:T(8,128)(2,1)S(1)}, u32[]{:S(2)}, u32[]{:S(2)}) collective-permute-start(bf16[192,384]{1,0:T(8,128)(2,1)S(1)} %add_kernel.10.refs_2_.refs_1_), channel_id=1, source_target_pairs={{0,8},{1,9},{2,10},{3,11},{4,12},{5,13},{6,14},{7,15},{8,0},{9,1},... | collective-permute-start | bytes 442376 | tf_op jit(solution)/shard_map/ppermute | solution.py:20
  121.6 17.3 %collective-permute-start.45 = (bf16[96,768]{1,0:T(8,128)(2,1)S(1)}, bf16[96,768]{1,0:T(8,128)(2,1)S(1)}, u32[]{:S(2)}, u32[]{:S(2)}) collective-permute-start(bf16[96,768]{1,0:T(8,128)(2,1)S(1)} %add_kernel.11.refs_2_.refs_0_), channel_id=1, source_target_pairs={{0,4},{1,5},{2,6},{3,7},{4,0},{5,1},{6,2},{7,3},{8,12},{9,13},{10,... | collective-permute-start | bytes 442376 | tf_op jit(solution)/shard_map/ppermute | solution.py:20
  129.2 13.4 %collective-permute-start.49 = (bf16[96,768]{1,0:T(8,128)(2,1)S(1)}, bf16[96,768]{1,0:T(8,128)(2,1)S(1)}, u32[]{:S(2)}, u32[]{:S(2)}) collective-permute-start(bf16[96,768]{1,0:T(8,128)(2,1)S(1)} %get-tuple-element.216.refs_2_), channel_id=1, source_target_pairs={{0,8},{1,9},{2,10},{3,11},{4,12},{5,13},{6,14},{7,15},{8,0},{9,1},... | collective-permute-start | bytes 442376 | tf_op jit(solution)/shard_map/ppermute | solution.py:20
  132.2 17.3 %collective-permute-start.55 = (bf16[224,576]{1,0:T(8,128)(2,1)S(1)}, bf16[224,576]{1,0:T(8,128)(2,1)S(1)}, u32[]{:S(2)}, u32[]{:S(2)}) collective-permute-start(bf16[224,576]{1,0:T(8,128)(2,1)S(1)} %add_kernel.12.refs_6_.refs_1_), channel_id=1, source_target_pairs={{0,4},{1,5},{2,6},{3,7},{4,0},{5,1},{6,2},{7,3},{8,12},{9,13},{10,... | collective-permute-start | bytes 774152 | tf_op jit(solution)/shard_map/ppermute | solution.py:20
  134.4 18.3 %collective-permute-start.54 = (bf16[224,576]{1,0:T(8,128)(2,1)S(1)}, bf16[224,576]{1,0:T(8,128)(2,1)S(1)}, u32[]{:S(2)}, u32[]{:S(2)}) collective-permute-start(bf16[224,576]{1,0:T(8,128)(2,1)S(1)} %add_kernel.12.refs_6_.refs_1_), channel_id=1, source_target_pairs={{0,2},{1,3},{2,0},{3,1},{4,6},{5,7},{6,4},{7,5},{8,10},{9,11},{10,... | collective-permute-start | bytes 774152 | tf_op jit(solution)/shard_map/ppermute | solution.py:20
  138.8 10.1 %collective-permute-start.44 = (bf16[64,768]{1,0:T(8,128)(2,1)S(1)}, bf16[64,768]{1,0:T(8,128)(2,1)S(1)}, u32[]{:S(2)}, u32[]{:S(2)}) collective-permute-start(bf16[64,768]{1,0:T(8,128)(2,1)S(1)} %get-tuple-element.224), channel_id=1, source_target_pairs={{0,8},{1,9},{2,10},{3,11},{4,12},{5,13},{6,14},{7,15},{8,0},{9,1},... | collective-permute-start | bytes 294920 | tf_op jit(solution)/shard_map/ppermute | solution.py:20
  142.6 10.1 %collective-permute-start.47 = (bf16[96,768]{1,0:T(8,128)(2,1)S(1)}, bf16[96,768]{1,0:T(8,128)(2,1)S(1)}, u32[]{:S(2)}, u32[]{:S(2)}) collective-permute-start(bf16[96,768]{1,0:T(8,128)(2,1)S(1)} %add_kernel.13.refs_2_.refs_0_), channel_id=1, source_target_pairs={{0,8},{1,9},{2,10},{3,11},{4,12},{5,13},{6,14},{7,15},{8,0},{9,1},... | collective-permute-start | bytes 442376 | tf_op jit(solution)/shard_map/ppermute | solution.py:20
  142.8 11.7 %collective-permute-start.50 = (bf16[128,768]{1,0:T(8,128)(2,1)S(1)}, bf16[128,768]{1,0:T(8,128)(2,1)S(1)}, u32[]{:S(2)}, u32[]{:S(2)}) collective-permute-start(bf16[128,768]{1,0:T(8,128)(2,1)S(1)} %tail_add_kernel.3.refs_2_), channel_id=1, source_target_pairs={{0,4},{1,5},{2,6},{3,7},{4,0},{5,1},{6,2},{7,3},{8,12},{9,13},{10,... | collective-permute-start | bytes 589832 | tf_op jit(solution)/shard_map/ppermute | solution.py:20
  148.9 16.2 %collective-permute-start.53 = (bf16[384,384]{1,0:T(8,128)(2,1)S(1)}, bf16[384,384]{1,0:T(8,128)(2,1)S(1)}, u32[]{:S(2)}, u32[]{:S(2)}) collective-permute-start(bf16[384,384]{1,0:T(8,128)(2,1)S(1)} %join_kernel.3.refs_2_.refs_1_), channel_id=1, source_target_pairs={{0,4},{1,5},{2,6},{3,7},{4,0},{5,1},{6,2},{7,3},{8,12},{9,13},{10,... | collective-permute-start | bytes 884744 | tf_op jit(solution)/shard_map/ppermute | solution.py:20
  149.5 13.8 %collective-permute-start.56 = (bf16[224,576]{1,0:T(8,128)(2,1)S(1)}, bf16[224,576]{1,0:T(8,128)(2,1)S(1)}, u32[]{:S(2)}, u32[]{:S(2)}) collective-permute-start(bf16[224,576]{1,0:T(8,128)(2,1)S(1)} %collective-permute-done.55.refs_3_), channel_id=1, source_target_pairs={{0,2},{1,3},{2,0},{3,1},{4,6},{5,7},{6,4},{7,5},{8,10},{9,11},{10,... | collective-permute-start | bytes 774152 | tf_op jit(solution)/shard_map/ppermute | solution.py:20
  152.7 17.5 %collective-permute-start.58 = (bf16[224,576]{1,0:T(8,128)(2,1)S(1)}, bf16[224,576]{1,0:T(8,128)(2,1)S(1)}, u32[]{:S(2)}, u32[]{:S(2)}) collective-permute-start(bf16[224,576]{1,0:T(8,128)(2,1)S(1)} %add_kernel.12.refs_6_.refs_1_), channel_id=1, source_target_pairs={{0,1},{1,0},{2,3},{3,2},{4,5},{5,4},{6,7},{7,6},{8,9},{9,8},{10,11... | collective-permute-start | bytes 774152 | tf_op jit(solution)/shard_map/ppermute | solution.py:20
  152.7 6.6 %collective-permute-start.57 = (bf16[96,768]{1,0:T(8,128)(2,1)S(1)}, bf16[96,768]{1,0:T(8,128)(2,1)S(1)}, u32[]{:S(2)}, u32[]{:S(2)}) collective-permute-start(bf16[96,768]{1,0:T(8,128)(2,1)S(1)} %add_kernel.15.refs_4_.refs_1_), channel_id=1, source_target_pairs={{0,2},{1,3},{2,0},{3,1},{4,6},{5,7},{6,4},{7,5},{8,10},{9,11},{10,... | collective-permute-start | bytes 442376 | tf_op jit(solution)/shard_map/ppermute | solution.py:20
  154.5 12.9 %collective-permute-start.52 = (bf16[96,768]{1,0:T(8,128)(2,1)S(1)}, bf16[96,768]{1,0:T(8,128)(2,1)S(1)}, u32[]{:S(2)}, u32[]{:S(2)}) collective-permute-start(bf16[96,768]{1,0:T(8,128)(2,1)S(1)} %add_kernel.14.refs_2_.refs_1_), channel_id=1, source_target_pairs={{0,8},{1,9},{2,10},{3,11},{4,12},{5,13},{6,14},{7,15},{8,0},{9,1},... | collective-permute-start | bytes 442376 | tf_op jit(solution)/shard_map/ppermute | solution.py:20
  159.3 11.1 %collective-permute-start.51 = (bf16[64,768]{1,0:T(8,128)(2,1)S(1)}, bf16[64,768]{1,0:T(8,128)(2,1)S(1)}, u32[]{:S(2)}, u32[]{:S(2)}) collective-permute-start(bf16[64,768]{1,0:T(8,128)(2,1)S(1)} %get-tuple-element.232), channel_id=1, source_target_pairs={{0,8},{1,9},{2,10},{3,11},{4,12},{5,13},{6,14},{7,15},{8,0},{9,1},... | collective-permute-start | bytes 294920 | tf_op jit(solution)/shard_map/ppermute | solution.py:20
  163.4 11.8 %collective-permute-start.62 = (bf16[192,768]{1,0:T(8,128)(2,1)S(1)}, bf16[192,768]{1,0:T(8,128)(2,1)S(1)}, u32[]{:S(2)}, u32[]{:S(2)}) collective-permute-start(bf16[192,768]{1,0:T(8,128)(2,1)S(1)} %join_kernel.4.refs_6_.refs_1_), channel_id=1, source_target_pairs={{0,1},{1,0},{2,3},{3,2},{4,5},{5,4},{6,7},{7,6},{8,9},{9,8},{10,11... | collective-permute-start | bytes 884744 | tf_op jit(solution)/shard_map/ppermute | solution.py:20
  168.0 9.6 %collective-permute-start.63 = (bf16[192,768]{1,0:T(8,128)(2,1)S(1)}, bf16[192,768]{1,0:T(8,128)(2,1)S(1)}, u32[]{:S(2)}, u32[]{:S(2)}) collective-permute-start(bf16[192,768]{1,0:T(8,128)(2,1)S(1)} %join_kernel.5.refs_3_.refs_1_), channel_id=1, source_target_pairs={{0,4},{1,5},{2,6},{3,7},{4,0},{5,1},{6,2},{7,3},{8,12},{9,13},{10,... | collective-permute-start | bytes 884744 | tf_op jit(solution)/shard_map/ppermute | solution.py:20
  169.9 2.0 %collective-permute-start.60 = (bf16[224,576]{1,0:T(8,128)(2,1)S(1)}, bf16[224,576]{1,0:T(8,128)(2,1)S(1)}, u32[]{:S(2)}, u32[]{:S(2)}) collective-permute-start(bf16[224,576]{1,0:T(8,128)(2,1)S(1)} %collective-permute-done.55.refs_3_), channel_id=1, source_target_pairs={{0,1},{1,0},{2,3},{3,2},{4,5},{5,4},{6,7},{7,6},{8,9},{9,8},{10,11... | collective-permute-start | bytes 774152 | tf_op jit(solution)/shard_map/ppermute | solution.py:20
  170.1 1.8 %collective-permute-start.59 = (bf16[224,576]{1,0:T(8,128)(2,1)S(1)}, bf16[224,576]{1,0:T(8,128)(2,1)S(1)}, u32[]{:S(2)}, u32[]{:S(2)}) collective-permute-start(bf16[224,576]{1,0:T(8,128)(2,1)S(1)} %collective-permute-done.54.refs_2_), channel_id=1, source_target_pairs={{0,1},{1,0},{2,3},{3,2},{4,5},{5,4},{6,7},{7,6},{8,9},{9,8},{10,11... | collective-permute-start | bytes 774152 | tf_op jit(solution)/shard_map/ppermute | solution.py:20
  170.4 1.9 %collective-permute-start.61 = (bf16[224,576]{1,0:T(8,128)(2,1)S(1)}, bf16[224,576]{1,0:T(8,128)(2,1)S(1)}, u32[]{:S(2)}, u32[]{:S(2)}) collective-permute-start(bf16[224,576]{1,0:T(8,128)(2,1)S(1)} %collective-permute-done.56.refs_4_), channel_id=1, source_target_pairs={{0,1},{1,0},{2,3},{3,2},{4,5},{5,4},{6,7},{7,6},{8,9},{9,8},{10,11... | collective-permute-start | bytes 774152 | tf_op jit(solution)/shard_map/ppermute | solution.py:20
  (7 other events, 31.8 us)

commit v4 on v3

--- a/solution.py
+++ b/solution.py
@@ -65,7 +65,7 @@
 def in_order():
     before = []
 
-    def call(kernel, outs, scratch=(), smem=0, extra=2, wait=(), written=False):
+    def call(kernel, outs, scratch=(), smem=0, extra=2, wait=(), written=0, mark=False):
         def run(*args):
             held = sum(a.size * jnp.dtype(a.dtype).itemsize for a in (*args, *outs))
             held += sum(
@@ -78,7 +78,7 @@
 
             def body(*refs):
                 rest = refs[used + len(events) :]
-                if written:
+                if written or mark:
                     rest[0][...] = jnp.zeros_like(rest[0])
                     rest = rest[1:]
                 kernel(*refs[:used], *rest)
@@ -86,8 +86,9 @@
             vmem = pl.BlockSpec(memory_space=pltpu.VMEM)
             out_specs = [vmem] * len(outs)
             out_shape = list(outs)
-            if written:
-                out_specs = [vmem, pl.BlockSpec(memory_space=pltpu.HBM)]
+            if written or mark:
+                hbm = pl.BlockSpec(memory_space=pltpu.HBM)
+                out_specs = [vmem] + [hbm if written else vmem] * len(outs)
                 out_shape = [shape((8, LANES), FULL), *outs]
             results = pl.pallas_call(
                 body,
@@ -102,7 +103,7 @@
                 cost_estimate=pl.CostEstimate(flops=0, bytes_accessed=0, transcendentals=0),
             )(*args, *events)
             before[:] = [min(results, key=lambda r: r.size)]
-            return results[-1] if written else results
+            return results[1:] if written or mark else results
 
         return run
 
@@ -620,103 +621,49 @@
     return kernel
 
 
-def qkv_out_kernel(heads):
-    def kernel(ids, q0, q1, q2, q3, o0, o1, o2, o3, out, whole, sem):
-        size = out.shape[0] // 2
-        lane = lane_of(size)
-        first = lane < 64
-        groups = 4
-        share = heads * 64
-        width = groups * share
-        places = [pl.ds(pl.multiple_of(p * size, 16), size) for p in (ids[2], 1 - ids[2])]
-
-        def fill(part, refs):
-            here = places[part]
-
-            def tile(g, column):
-                stop = min(column + LANES, q0.shape[1])
-                one = refs[g][:size, column:stop].astype(FULL)
-                if stop - column < LANES:
-                    one = jnp.concatenate([one, jnp.zeros_like(one)], axis=1)
-                return one
-
-            for pair in range(groups * heads // 2):
-                ends = []
-                for n in (2 * pair, 2 * pair + 1):
-                    g, h = n // heads, n % heads
-                    q = tile(g, 2 * share + (h // 2) * LANES)
-                    if h % 2:
-                        q = pltpu.roll(q, 64, 1)
-                    ends.append((q, tile(g, h * LANES)))
-                (qa, kva), (qb, kvb) = ends
-                at_col = pair * LANES
-                for start, a, b in (
-                    (0, qa, pltpu.roll(qb, 64, 1)),
-                    (width, kva, pltpu.roll(kvb, 64, 1)),
-                    (2 * width, pltpu.roll(kva, 64, 1), kvb),
-                ):
-                    here_cols = slice(start + at_col, start + at_col + LANES)
-                    whole[here, here_cols] = jnp.where(first, a, b)
-
-        for part, refs in enumerate(((q0, q1, q2, q3), (o0, o1, o2, o3))):
-            for g in range(groups):
-
-                @pl.when(ids[1] == g)
-                def _():
-                    fill(part, [refs[k ^ g] for k in range(groups)])
-
-            here = places[part]
-            pltpu.make_async_copy(whole.at[here], out.at[here], sem.at[part]).start()
-        for part, here in enumerate(places):
-            pltpu.make_async_copy(whole.at[here], out.at[here], sem.at[part]).wait()
-
-    return kernel
-
-
-def change_kernel(middle, own, own_got, f0, f1, f2, mine, sent):
-    tok = own.shape[0]
-    for part, base, out in ((0, own, mine), (tok, own_got, sent)):
-        here = slice(part, part + tok)
-        fed = f0[here, :].astype(FULL) + f1[here, :].astype(FULL) + f2[here, :].astype(FULL)
-        total = middle[here, :] + fed
-        if part:
-            total = total - base[...]
-        out[...] = total.astype(out.dtype)
-
-
-def place_kernel(ids, mine, got, base, out, low, sem):
-    first = pltpu.make_async_copy(mine, out.at[ids[3]], sem.at[0])
-    first.start()
-    low[...] = got[...].astype(FULL) + base[...]
-    second = pltpu.make_async_copy(low, out.at[1 - ids[3]], sem.at[1])
-    second.start()
-    first.wait()
-    second.wait()
-
-
-def place_two_kernel(ids, mine, got, out, low, sem):
-    first = pltpu.make_async_copy(mine, out.at[ids[3]], sem.at[0])
-    first.start()
-    low[...] = got[...].astype(FULL)
-    second = pltpu.make_async_copy(low, out.at[1 - ids[3]], sem.at[1])
-    second.start()
-    first.wait()
-    second.wait()
-
-
-def join_out_kernel(which):
-    def kernel(ids, mine, other, out, whole, sem):
-        size = mine.shape[0]
-        copies = []
-        for k, (place, ref) in enumerate(((ids[which], mine), (1 - ids[which], other))):
-            here = at(place, size)
-            whole[here, :] = ref[...].astype(FULL)
-            copies.append(pltpu.make_async_copy(whole.at[here], out.at[here], sem.at[k]))
-            copies[-1].start()
-        for copy in copies:
-            copy.wait()
-
-    return kernel
+def qkv_out(heads, ids, mine, others, out, whole, sem, copies):
+    size = out.shape[0] // 2
+    lane = lane_of(size)
+    first = lane < 64
+    groups = 4
+    share = heads * 64
+    width = groups * share
+
+    def fill(here, refs):
+        def tile(g, column):
+            stop = min(column + LANES, refs[g].shape[1])
+            one = refs[g][:size, column:stop].astype(FULL)
+            if stop - column < LANES:
+                one = jnp.concatenate([one, jnp.zeros_like(one)], axis=1)
+            return one
+
+        for pair in range(groups * heads // 2):
+            ends = []
+            for n in (2 * pair, 2 * pair + 1):
+                g, h = n // heads, n % heads
+                q = tile(g, 2 * share + (h // 2) * LANES)
+                if h % 2:
+                    q = pltpu.roll(q, 64, 1)
+                ends.append((q, tile(g, h * LANES)))
+            (qa, kva), (qb, kvb) = ends
+            at_col = pair * LANES
+            for begin, a, b in (
+                (0, qa, pltpu.roll(qb, 64, 1)),
+                (width, kva, pltpu.roll(kvb, 64, 1)),
+                (2 * width, pltpu.roll(kva, 64, 1), kvb),
+            ):
+                cols = slice(begin + at_col, begin + at_col + LANES)
+                whole[here, cols] = jnp.where(first, a, b)
+
+    for place, refs in ((ids[2], mine), (1 - ids[2], others)):
+        here = pl.ds(pl.multiple_of(place * size, 16), size)
+        for g in range(groups):
+
+            @pl.when(ids[1] == g)
+            def _():
+                fill(here, [refs[k ^ g] for k in range(groups)])
+
+        start(whole.at[here], out.at[here], sem, copies)
 
 
 def halve_lanes_kernel(which):
@@ -725,6 +672,58 @@
         for bit, out in ((1 - ids[which], sent), (ids[which], kept)):
             here = lanes(bit, size)
             out[...] = (a[:, here].astype(FULL) + b[:, here].astype(FULL)).astype(out.dtype)
+
+    return kernel
+
+
+def start(source, target, sem, copies):
+    copies.append(pltpu.make_async_copy(source, target, sem.at[len(copies)]))
+    copies[-1].start()
+
+
+def place_out(ids, mine, other, out, sem, copies):
+    start(mine, out.at[ids[3]], sem, copies)
+    start(other, out.at[1 - ids[3]], sem, copies)
+
+
+def join_out(ids, which, mine, other, out, whole, sem, copies):
+    size = mine.shape[0]
+    for place, ref in ((ids[which], mine), (1 - ids[which], other)):
+        here = at(place, size)
+        whole[here, :] = ref[...].astype(FULL)
+        start(whole.at[here], out.at[here], sem, copies)
+
+
+def place_kernel(ids, token, change, got, away, output, tokens_grad, low, sem):
+    copies = []
+    tok = token.shape[0]
+    low[:tok, :] = got[:tok, :].astype(FULL)
+    place_out(ids, token, low.at[:tok], tokens_grad, sem, copies)
+    low[tok:, :] = got[tok:, :].astype(FULL) + away[...]
+    place_out(ids, change, low.at[tok:], output, sem, copies)
+    for copy in copies:
+        copy.wait()
+
+
+def last_kernel(heads):
+    def kernel(
+        ids, q0, q1, q2, q3, o0, o1, o2, o3, token, change, got, away,
+        proj, proj_got, first, first_got, second, second_got,
+        output, tokens_grad, qkv_grad, proj_grad, fc1_grad, fc2_grad,
+        low, qkv, wide, one, two, sem,
+    ):
+        copies = []
+        tok = token.shape[0]
+        low[:tok, :] = got[:tok, :].astype(FULL)
+        place_out(ids, token, low.at[:tok], tokens_grad, sem, copies)
+        low[tok:, :] = got[tok:, :].astype(FULL) + away[...]
+        place_out(ids, change, low.at[tok:], output, sem, copies)
+        join_out(ids, 2, proj, proj_got, proj_grad, wide, sem, copies)
+        join_out(ids, 4, first, first_got, fc1_grad, one, sem, copies)
+        join_out(ids, 4, second, second_got, fc2_grad, two, sem, copies)
+        qkv_out(heads, ids, (q0, q1, q2, q3), (o0, o1, o2, o3), qkv_grad, qkv, sem, copies)
+        for copy in copies:
+            copy.wait()
 
     return kernel
 
@@ -755,15 +754,21 @@
         out[...] = dot_nt(low, weight[k * width : (k + 1) * width, :]).astype(LOW)
 
 
-def first_back_kernel(a0, a1, a2, own, own_got, params, gmiddle, mine, sent, rows):
+def first_back_kernel(
+    a0, a1, a2, own, own_got, params, gmiddle, middle, f0, f1, f2, mine, change, sent, rows
+):
     tok = own.shape[0]
+    fed = f0[...].astype(FULL) + f1[: 2 * tok, :].astype(FULL) + f2[...].astype(FULL)
+    total = middle[...] + fed
+    change[...] = total[:tok, :]
+    sent[tok:, :] = (total[tok:, :] - own_got[...]).astype(LOW)
     rows[:tok, :] = own[...]
     rows[tok:, :] = own_got[...]
     grad = a0[...].astype(FULL) + a1[: 2 * tok, :].astype(FULL) + a2[...].astype(FULL)
     back, _, _ = norm_back(grad, rows[...], params[0:1, :])
     total = gmiddle[...] + back
     mine[...] = total[:tok, :]
-    sent[...] = total[tok:, :].astype(LOW)
+    sent[:tok, :] = total[tok:, :].astype(LOW)
 
 
 def on_device(
@@ -815,16 +820,6 @@
     quarter, eighth = half // 2, half // 4
     norm_sums = [shape((1, width), FULL)] * 2
 
-    def written(kernel, dims, extra=2):
-        return call(
-            kernel,
-            [shape(dims, FULL)],
-            [pltpu.VMEM(dims, FULL), pltpu.SemaphoreType.DMA((2,))],
-            smem=1,
-            extra=extra,
-            written=True,
-        )
-
     def total_of(kind, *args):
         return call(add_kernel, [shape(args[0].shape, kind)])(*args)[0]
 
@@ -862,13 +857,14 @@
     )
     normed_parts = [normed] + [hop(normed, b) for b in way[1:]]
     cot = call(stack_kernel, [low_rows])(cot_mine, cot_got)[0]
+    if dp_count == 2:
+        proj_part = call(rows_kernel, [shape((half // 2, width), LOW)], smem=1)(ids, proj_weight)[0]
     table, spot_one, spot_two = call(
         table_kernel,
         [shape((LANES, 2 * LANES), LOW)] + [shape((key_n, LANES), LOW)] * 2,
         smem=1,
+        wait=(mix_other,),
     )(ids, tables, tables_other)
-    if dp_count == 2:
-        proj_part = call(rows_kernel, [shape((half // 2, width), LOW)], smem=1)(ids, proj_weight)[0]
 
     kv, query, normed_all, mix = call(
         mix_kernel,
@@ -888,7 +884,7 @@
     else:
         proj_mine, proj_other, _ = pair_dp(proj_weight, 0)
     proj_two = hop(after(proj_other, kv), CORE)
-    up_mine, up_other, _ = pair_dp(after(fc1_weight, kv), 0)
+    up_mine, up_other, _ = pair_dp(after(fc1_weight, normed), 0)
 
     down_mine, down_other, _ = pair_dp(after(fc2_weight, kv), 1)
 
@@ -912,6 +908,7 @@
         [full_rows, low_rows, shape((width, width), LOW)],
         [pltpu.VMEM((width, width), LOW)],
         smem=1,
+        wait=(up_other,),
     )(ids, *joined, proj_mine, proj_other, proj_two, own, own_got, params)
 
     two_row = hop(normed_two, ROW)
@@ -973,12 +970,6 @@
         def step():
             part.kept = join(3, part.kept, part.got, LOW)
             part.got = send(part.kept, NEAR)
-
-        return step
-
-    def last(part, dims):
-        def step():
-            part.grad = written(join_out_kernel(4), dims)(ids, part.kept, part.got)
 
         return step
 
@@ -1051,20 +1042,23 @@
         sent = call(tail_add_kernel, [low_rows])(v.f1, v.fed_got)[0]
         v.fed_row = send(sent, ROW)
 
-    def change():
-        v.change, sent = call(change_kernel, [full_tok, low_tok])(
-            middle, own, own_got, v.f0, v.fed_got, v.fed_row
+    def last():
+        dims = [tokens.shape] * 2 + [(half, 3 * width), (half, width), (half, hid), (hid, half)]
+        (
+            v.output, v.tokens_grad, v.qkv_grad, v.proj_grad, fc1.grad, fc2.grad,
+        ) = call(
+            last_kernel(heads),
+            [shape(d, FULL) for d in dims],
+            [pltpu.VMEM((rows_n, width), FULL)]
+            + [pltpu.VMEM(d, FULL) for d in dims[2:]]
+            + [pltpu.SemaphoreType.DMA((12,))],
+            smem=1,
+            extra=8,
+            written=6,
+        )(
+            ids, *v.qkv_parts, *v.qkv_others, v.token, v.change, v.token_got, away,
+            v.proj, v.proj_got, fc1.kept, fc1.got, fc2.kept, fc2.got,
         )
-        v.change_got = send(sent, FAR)
-
-    def place_output():
-        v.output = call(
-            place_kernel,
-            [shape(tokens.shape, FULL)],
-            [pltpu.VMEM((tok, width), FULL), pltpu.SemaphoreType.DMA((2,))],
-            smem=1,
-            written=True,
-        )(ids, v.change, v.change_got, away)
 
     def qkv_outer():
         mine, got, queries, tables = zip(*v.back)
@@ -1100,11 +1094,6 @@
         v.tables = (table_h.T, table_w.T)
         v.qkv_others = [send(part, CORE) for part in v.qkv_parts]
 
-    def qkv_last():
-        v.qkv_grad = written(qkv_out_kernel(heads), (half, 3 * width), 4)(
-            ids, *v.qkv_parts, *v.qkv_others
-        )
-
     def mixed_back():
         v.e_mine, v.e_near, e_row = call(
             dmix_kernel, [low_rows, low_rows, two_rows], extra=6
@@ -1118,19 +1107,13 @@
         v.e_last = send(sent, NEAR)
 
     def first_back():
-        v.token, sent = call(
-            first_back_kernel, [full_tok, low_tok], [pltpu.VMEM((rows_n, width), FULL)]
-        )(v.e_mine, v.e_got, v.e_last, own, own_got, params, v.gmiddle)
+        v.token, v.change, sent = call(
+            first_back_kernel, [full_tok, full_tok, low_rows], [pltpu.VMEM((rows_n, width), FULL)]
+        )(
+            v.e_mine, v.e_got, v.e_last, own, own_got, params, v.gmiddle,
+            middle, v.f0, v.fed_got, v.fed_row,
+        )
         v.token_got = send(sent, FAR)
-
-    def place_tokens():
-        v.tokens_grad = call(
-            place_two_kernel,
-            [shape(tokens.shape, FULL)],
-            [pltpu.VMEM((tok, width), FULL), pltpu.SemaphoreType.DMA((2,))],
-            smem=1,
-            written=True,
-        )(ids, v.token, v.token_got)
 
     def fc1_near_sum():
         sent, fc1.kept = halve(4, fc1.kept, fc1.got)
@@ -1162,15 +1145,13 @@
         v.proj = join(5, v.proj, v.proj_got, LOW)
         v.proj_got = send(v.proj, CORE)
 
-    def proj_last():
-        v.proj_grad = written(join_out_kernel(2), (half, width))(ids, v.proj, v.proj_got)
-
     def vector_out(parts, size, features):
         return call(
             vector_out_kernel(reach, dp_count == 2),
             [shape((size,), FULL)] * 4 + [shape((features, reach), FULL)] * 2,
             [pltpu.VMEM((vector_rows, qkv_cols), FULL), pltpu.VMEM((4, width), FULL)],
             smem=1,
+            mark=True,
         )(ids, *parts, params)
 
     if dp_count == 2:
@@ -1182,38 +1163,32 @@
             fc2_near_sum,
             proj_outer,
             back0,
+            fc1_near_sum,
             back1,
+            proj_split,
+            back2,
+            far_sum(fc1),
+            qkv_outer,
             fed,
-            back2,
-            fc1_near_sum,
+            qkv_owner,
+            mixed_back,
+            proj_owner,
+            qkv_images,
+            far_all(fc1),
             far_sum(fc2),
-            qkv_outer,
-            qkv_owner,
             fed_add,
-            proj_split,
-            far_sum(fc1),
-            qkv_images,
-            mixed_back,
-            far_all(fc2),
-            proj_owner,
             proj_sum(NEAR),
             qkv_total,
-            change,
+            far_all(fc2),
+            normed_near,
+            near_all(fc1),
+            proj_sum(FAR),
             near_all(fc2),
-            proj_sum(FAR),
-            far_all(fc1),
-            normed_near,
+            first_back,
             proj_sum(ROW),
-            place_output,
-            first_back,
+            vector_last,
             proj_join,
-            vector_last,
-            last(fc2, (hid, half)),
-            near_all(fc1),
-            place_tokens,
-            qkv_last,
-            proj_last,
-            last(fc1, (half, hid)),
+            last,
         ):
             step()
         output, tokens_grad, qkv_grad = v.output, v.tokens_grad, v.qkv_grad
@@ -1221,13 +1196,19 @@
         norms, dtables = v.norms, v.tables
     else:
         every = ("seq", "tp")
-        for step in (dnorm_add, mid_back, fed, back0, back1, back2, fed_add, change, place_output):
+        for step in (dnorm_add, mid_back, fed, back0, back1, back2, fed_add):
             step()
         mine, other, queries, tables = zip(*v.back)
         v.dkv, v.dquery = call(dkv_kernel, mixed_shapes)(*mine, *other, *queries)
-        for step in (mixed_back, normed_near, first_back, place_tokens):
+        for step in (mixed_back, normed_near, first_back):
             step()
-        output, tokens_grad = v.output, v.tokens_grad
+        output, tokens_grad = call(
+            place_kernel,
+            [shape(tokens.shape, FULL)] * 2,
+            [pltpu.VMEM((rows_n, width), FULL), pltpu.SemaphoreType.DMA((4,))],
+            smem=1,
+            written=2,
+        )(ids, v.token, v.change, v.token_got, away)
         dkv, dquery, gbranch = v.dkv, v.dquery, v.gbranch
 
         def weight_sum(a, b, axes, axis=0):

time: 180 us -> 177 us (0.983)
  waiting for transfers between devices: 48.2 us -> 58.2 us
  starting transfers between devices: 74.9 us -> 68 us
  Pallas kernels: 49.8 us -> 43.6 us
    ppermute x54 -> x53, starting transfers between devices: 65.1 us -> 49.8 us  [hop(): lax.ppermute(value, ('seq', 'tp'), [(i, i ^ bits) for i in range(count)])]
    ppermute x10, starting transfers between devices: 9.81 us -> 18.2 us  [swap_dp(): return lax.ppermute(value, 'dp', [(0, 1), (1, 0)])]
    pallas_call x50 -> x44, Pallas kernels: 49.8 us -> 43.6 us  [run(): pl.pallas_call(body, name=kernel.__qualname__.split('.')[0], out_shape=ou...]
    ppermute x10, waiting for transfers between devices: 8.35 us -> 13.5 us  [swap_dp(): return lax.ppermute(value, 'dp', [(0, 1), (1, 0)])]
    ppermute x54 -> x53, waiting for transfers between devices: 39.8 us -> 44.7 us  [hop(): lax.ppermute(value, ('seq', 'tp'), [(i, i ^ bits) for i in range(count)])]
  transfers between devices with their start and end apart: 64 -> 63, of which waited for: 27 -> 30; matrix products, arithmetic and copies ran while one was open for 1% -> 1% of each run, Pallas kernels for 24% -> 18%
where the time goes in v4:
time: 177 us
  starting transfers between devices  68 us (38%)
  waiting for transfers between devices  58.2 us (33%)
  Pallas kernels  43.6 us (25%)
  local copies, waits for them, and re-layouts  4.2 us (2%)
    ppermute x53, starting transfers between devices, hop(): lax.ppermute(value, ('seq', 'tp'), [(i, i ^ bits) for i in range(count)])  49.8 us
    ppermute x53, waiting for transfers between devices, hop(): lax.ppermute(value, ('seq', 'tp'), [(i, i ^ bits) for i in range(count)])  44.7 us
    pallas_call x44, Pallas kernels, run(): pl.pallas_call(body, name=kernel.__qualname__.split('.')[0], out_shape=ou...  43.6 us
    ppermute x10, starting transfers between devices, swap_dp(): return lax.ppermute(value, 'dp', [(0, 1), (1, 0)])  18.2 us
    ppermute x10, waiting for transfers between devices, swap_dp(): return lax.ppermute(value, 'dp', [(0, 1), (1, 0)])  13.5 us
    unnamed x14, local copies, waits for them, and re-layouts  4.1 us
  transfers between devices with their start and end apart: 63, of which 30 were waited for; matrix products, arithmetic and copies ran while one was open for 1% of the time, Pallas kernels for 18%

profile of v4, /device:TPU:0, one launch (start us, length us, event | category | flops | bytes accessed | tf_op | source)
XLA Modules:
  0.0 176.9 jit_solution(9357924149369857449)
XLA Ops:
  0.8 1.0 copy-done.4
  2.3 4.1 %collective-permute-start = (f32[64,768]{1,0:T(8,128)S(1)}, f32[64,768]{1,0:T(8,128)S(1)}, u32[]{:S(2)}, u32[]{:S(2)}) collective-permute-start(f32[64,768]{1,0:T(8,128)S(1)} %get-tuple-element.125.refs_12_), channel_id=1, source_target_pairs={{0,8},{1,9},{2,10},{3,11},{4,12},{5,13},{6,14},{7,15},{8,0},{9,1},... | collective-permute-start | bytes 589832 | tf_op jit(solution)/shard_map/ppermute | solution.py:20
  7.2 1.5 collective-permute-start.2
  10.1 0.9 copy-done.5
  11.5 1.6 collective-permute-done.1.refs_3_.refs_4_
  13.1 1.5 copy-done.1
  15.6 1.5 collective-permute-start.6
  17.9 5.1 %collective-permute-start.5 = (bf16[128,768]{1,0:T(8,128)(2,1)S(1)}, bf16[128,768]{1,0:T(8,128)(2,1)S(1)}, u32[]{:S(2)}, u32[]{:S(2)}) collective-permute-start(bf16[128,768]{1,0:T(8,128)(2,1)S(1)} %get-tuple-element.129.refs_1_), channel_id=1, source_target_pairs={{0,6},{1,7},{2,4},{3,5},{4,2},{5,3},{6,0},{7,1},{8,14},{9,15},{10,... | collective-permute-start | bytes 589832 | tf_op jit(solution)/shard_map/ppermute | solution.py:20
  25.3 4.4 %collective-permute-done.6.refs_4_.refs_6_ = bf16[384,576]{1,0:T(8,128)(2,1)S(1)} collective-permute-done((bf16[384,576]{1,0:T(8,128)(2,1)S(1)}, bf16[384,576]{1,0:T(8,128)(2,1)S(1)}, u32[]{:S(2)}, u32[]{:S(2)}) %collective-permute-start.6) | collective-permute-done | bytes 442400 | tf_op jit(solution)/shard_map/ppermute | solution.py:24
  29.7 1.5 collective-permute-start.15
  32.3 1.4 mix_kernel.1
  33.9 2.2 %collective-permute-done.10.refs_6_ = bf16[192,768]{1,0:T(8,128)(2,1)S(1)} collective-permute-done((bf16[192,768]{1,0:T(8,128)(2,1)S(1)}, bf16[192,768]{1,0:T(8,128)(2,1)S(1)}, u32[]{:S(2)}, u32[]{:S(2)}) %collective-permute-start.10) | collective-permute-done | bytes 294944 | tf_op jit(solution)/shard_map/ppermute | solution.py:24
  36.0 1.6 collective-permute-start.9
  37.6 1.5 collective-permute-start.21
  39.1 4.6 %attend_kernel.1 = (f32[512,256]{1,0:T(8,128)S(1)}, bf16[128,192]{1,0:T(8,128)(2,1)S(1)}, bf16[128,192]{1,0:T(8,128)(2,1)S(1)}, bf16[128,192]{1,0:T(8,128)(2,1)S...) custom-call(s32[8]{0:T(128)S(1)} %stack.41.refs_0_, ...), custom_call_target="tpu_custom_call" | custom-call | tf_op jit(solution)/shard_map/attend_kernel/pallas_call | solution.py:93
  43.7 1.2 collective-permute-start.12
  44.9 1.6 collective-permute-start.13
  47.3 1.4 collective-permute-done.15.refs_12_.refs_10_
  49.5 2.2 %collective-permute-done.14.refs_4_ = bf16[128,192]{1,0:T(8,128)(2,1)S(1)} collective-permute-done((bf16[128,192]{1,0:T(8,128)(2,1)S(1)}, bf16[128,192]{1,0:T(8,128)(2,1)S(1)}, u32[]{:S(2)}, u32[]{:S(2)}) %collective-permute-start.14) | collective-permute-done | bytes 49184 | tf_op jit(solution)/shard_map/ppermute | solution.py:20
  51.7 1.2 mid_kernel.1
  53.3 5.3 %collective-permute-done.16.refs_2_ = bf16[128,768]{1,0:T(8,128)(2,1)S(1)} collective-permute-done((bf16[128,768]{1,0:T(8,128)(2,1)S(1)}, bf16[128,768]{1,0:T(8,128)(2,1)S(1)}, u32[]{:S(2)}, u32[]{:S(2)}) %collective-permute-start.16) | collective-permute-done | bytes 196640 | tf_op jit(solution)/shard_map/ppermute | solution.py:20
  60.7 2.9 %feed_kernel.1 = (bf16[128,768]{1,0:T(8,128)(2,1)S(1)}, bf16[128,768]{1,0:T(8,128)(2,1)S(1)}, bf16[128,768]{1,0:T(8,128)(2,1)S(1)}, bf16[128,768]{1,0:T(8,128)(2...) custom-call(s32[8]{0:T(128)S(1)} %stack.41.refs_0_, ...), custom_call_target="tpu_custom_call" | custom-call | tf_op jit(solution)/shard_map/feed_kernel/pallas_call | solution.py:93
  63.6 1.4 outer_kernel.2
  65.9 0.9 collective-permute-done.23.refs_1_
  66.9 1.5 collective-permute-start.24
  68.5 1.4 outer_kernel.3
  69.8 1.6 collective-permute-start.29
  71.4 2.6 %collective-permute-done.24.refs_2_ = bf16[128,768]{1,0:T(8,128)(2,1)S(1)} collective-permute-done((bf16[128,768]{1,0:T(8,128)(2,1)S(1)}, bf16[128,768]{1,0:T(8,128)(2,1)S(1)}, u32[]{:S(2)}, u32[]{:S(2)}) %collective-permute-start.24) | collective-permute-done | bytes 196640 | tf_op jit(solution)/shard_map/ppermute | solution.py:20
  73.9 0.9 mid_back_kernel.1
  74.8 1.5 collective-permute-start.25
  76.8 1.5 collective-permute-start.27
  78.4 2.8 %collective-permute-done.28.refs_2_ = bf16[384,768]{1,0:T(8,128)(2,1)S(1)} collective-permute-done((bf16[384,768]{1,0:T(8,128)(2,1)S(1)}, bf16[384,768]{1,0:T(8,128)(2,1)S(1)}, u32[]{:S(2)}, u32[]{:S(2)}) %collective-permute-start.28) | collective-permute-done | bytes 589856 | tf_op jit(solution)/shard_map/ppermute | solution.py:20
  81.8 1.3 proj_grad_kernel.1
  83.3 3.0 %back_kernel.3 = (bf16[512,128]{1,0:T(8,128)(2,1)S(1)}, f32[512,128]{1,0:T(8,128)S(1)}, bf16[512,128]{1,0:T(8,128)(2,1)S(1)}, f32[256,128]{1,0:T(8,128)S(1)}) custom-call(s32[8]{0:T(128)S(1)} %stack.41.refs_0_, bf16[3,512,256]{2,1,0:T(8,128)(2,1)S(1)} %get-tuple-element.139.refs_1_, bf16[512,384]{1,0:T(8,128)(2,1)S(1)} %get-tuple-element.136.refs_2_, ...), custom_call_target="tpu_custom_call" | custom-call | tf_op jit(solution)/shard_map/back_kernel/pallas_call | solution.py:93
  88.3 2.9 %back_kernel.4 = (bf16[512,128]{1,0:T(8,128)(2,1)S(1)}, f32[512,128]{1,0:T(8,128)S(1)}, bf16[512,128]{1,0:T(8,128)(2,1)S(1)}, f32[256,128]{1,0:T(8,128)S(1)}) custom-call(s32[8]{0:T(128)S(1)} %stack.41.refs_0_, bf16[3,512,256]{2,1,0:T(8,128)(2,1)S(1)} %get-tuple-element.139.refs_1_, bf16[512,384]{1,0:T(8,128)(2,1)S(1)} %get-tuple-element.136.refs_2_, ...), custom_call_target="tpu_custom_call" | custom-call | tf_op jit(solution)/shard_map/back_kernel/pallas_call | solution.py:93
  92.6 3.0 %back_kernel.5 = (bf16[512,128]{1,0:T(8,128)(2,1)S(1)}, f32[512,128]{1,0:T(8,128)S(1)}, bf16[512,128]{1,0:T(8,128)(2,1)S(1)}, f32[256,128]{1,0:T(8,128)S(1)}) custom-call(s32[8]{0:T(128)S(1)} %stack.41.refs_0_, bf16[3,512,256]{2,1,0:T(8,128)(2,1)S(1)} %get-tuple-element.139.refs_1_, bf16[512,384]{1,0:T(8,128)(2,1)S(1)} %get-tuple-element.136.refs_2_, ...), custom_call_target="tpu_custom_call" | custom-call | tf_op jit(solution)/shard_map/back_kernel/pallas_call | solution.py:93
  97.1 1.8 qkv_grad_kernel.1
  99.0 1.5 collective-permute-start.37
  101.4 1.2 collective-permute-start.36
  103.5 2.7 %collective-permute-start.42 = (bf16[96,768]{1,0:T(8,128)(2,1)S(1)}, bf16[96,768]{1,0:T(8,128)(2,1)S(1)}, u32[]{:S(2)}, u32[]{:S(2)}) collective-permute-start(bf16[96,768]{1,0:T(8,128)(2,1)S(1)} %get-tuple-element.198.refs_17_), channel_id=1, source_target_pairs={{0,8},{1,9},{2,10},{3,11},{4,12},{5,13},{6,14},{7,15},{8,0},{9,1},... | collective-permute-start | bytes 442376 | tf_op jit(solution)/shard_map/ppermute | solution.py:20
  107.1 1.3 collective-permute-done.37.refs_1_
  108.4 1.5 collective-permute-start.50
  109.9 1.2 collective-permute-done.36.refs_1_
  111.2 2.8 %collective-permute-start.38 = (bf16[224,576]{1,0:T(8,128)(2,1)S(1)}, bf16[224,576]{1,0:T(8,128)(2,1)S(1)}, u32[]{:S(2)}, u32[]{:S(2)}) collective-permute-start(bf16[224,576]{1,0:T(8,128)(2,1)S(1)} %add_kernel.9.refs_2_.refs_0_), channel_id=1, source_target_pairs={{0,8},{1,9},{2,10},{3,11},{4,12},{5,13},{6,14},{7,15},{8,0},{9,1},... | collective-permute-start | bytes 774152 | tf_op jit(solution)/shard_map/ppermute | solution.py:20
  114.0 7.6 %collective-permute-start.39 = (bf16[96,768]{1,0:T(8,128)(2,1)S(1)}, bf16[96,768]{1,0:T(8,128)(2,1)S(1)}, u32[]{:S(2)}, u32[]{:S(2)}) collective-permute-start(bf16[96,768]{1,0:T(8,128)(2,1)S(1)} %get-tuple-element.209.refs_2_), channel_id=1, source_target_pairs={{0,16},{16,0},{1,17},{17,1},{2,18},{18,2},{3,19},{19,3},{4,20},{20... | collective-permute-start | bytes 442376 | tf_op jit(solution)/shard_map/ppermute | solution.py:24
  122.5 2.3 %collective-permute-done.39.refs_1_ = bf16[96,768]{1,0:T(8,128)(2,1)S(1)} collective-permute-done((bf16[96,768]{1,0:T(8,128)(2,1)S(1)}, bf16[96,768]{1,0:T(8,128)(2,1)S(1)}, u32[]{:S(2)}, u32[]{:S(2)}) %collective-permute-start.39) | collective-permute-done | bytes 147488 | tf_op jit(solution)/shard_map/ppermute | solution.py:24
  124.8 1.3 collective-permute-start.55
  126.1 2.8 %collective-permute-start.56 = (bf16[96,768]{1,0:T(8,128)(2,1)S(1)}, bf16[96,768]{1,0:T(8,128)(2,1)S(1)}, u32[]{:S(2)}, u32[]{:S(2)}) collective-permute-start(bf16[96,768]{1,0:T(8,128)(2,1)S(1)} %add_kernel.10.refs_3_.refs_1_), channel_id=1, source_target_pairs={{0,8},{1,9},{2,10},{3,11},{4,12},{5,13},{6,14},{7,15},{8,0},{9,1},... | collective-permute-start | bytes 442376 | tf_op jit(solution)/shard_map/ppermute | solution.py:20
  128.9 2.2 %collective-permute-done.38.refs_1_ = bf16[224,576]{1,0:T(8,128)(2,1)S(1)} collective-permute-done((bf16[224,576]{1,0:T(8,128)(2,1)S(1)}, bf16[224,576]{1,0:T(8,128)(2,1)S(1)}, u32[]{:S(2)}, u32[]{:S(2)}) %collective-permute-start.38) | collective-permute-done | bytes 258080 | tf_op jit(solution)/shard_map/ppermute | solution.py:20
  131.4 4.5 %collective-permute-done.51.refs_1_ = bf16[192,384]{1,0:T(8,128)(2,1)S(1)} collective-permute-done((bf16[192,384]{1,0:T(8,128)(2,1)S(1)}, bf16[192,384]{1,0:T(8,128)(2,1)S(1)}, u32[]{:S(2)}, u32[]{:S(2)}) %collective-permute-start.51) | collective-permute-done | bytes 147488 | tf_op jit(solution)/shard_map/ppermute | solution.py:20
  135.9 1.2 collective-permute-start.53
  137.2 3.4 %collective-permute-start.54 = (bf16[192,384]{1,0:T(8,128)(2,1)S(1)}, bf16[192,384]{1,0:T(8,128)(2,1)S(1)}, u32[]{:S(2)}, u32[]{:S(2)}) collective-permute-start(bf16[192,384]{1,0:T(8,128)(2,1)S(1)} %add_kernel.13.refs_2_.refs_1_), channel_id=1, source_target_pairs={{0,8},{1,9},{2,10},{3,11},{4,12},{5,13},{6,14},{7,15},{8,0},{9,1},... | collective-permute-start | bytes 442376 | tf_op jit(solution)/shard_map/ppermute | solution.py:20
  140.7 1.0 collective-permute-start.43
  142.8 6.2 %collective-permute-done.44.refs_3_ = bf16[224,576]{1,0:T(8,128)(2,1)S(1)} collective-permute-done((bf16[224,576]{1,0:T(8,128)(2,1)S(1)}, bf16[224,576]{1,0:T(8,128)(2,1)S(1)}, u32[]{:S(2)}, u32[]{:S(2)}) %collective-permute-start.44) | collective-permute-done | bytes 258080 | tf_op jit(solution)/shard_map/ppermute | solution.py:20
  149.0 2.1 %collective-permute-start.45 = (bf16[224,576]{1,0:T(8,128)(2,1)S(1)}, bf16[224,576]{1,0:T(8,128)(2,1)S(1)}, u32[]{:S(2)}, u32[]{:S(2)}) collective-permute-start(bf16[224,576]{1,0:T(8,128)(2,1)S(1)} %collective-permute-done.44.refs_3_), channel_id=1, source_target_pairs={{0,2},{1,3},{2,0},{3,1},{4,6},{5,7},{6,4},{7,5},{8,10},{9,11},{10,... | collective-permute-start | bytes 774152 | tf_op jit(solution)/shard_map/ppermute | solution.py:20
  151.1 4.3 %collective-permute-done.52.refs_2_ = bf16[128,768]{1,0:T(8,128)(2,1)S(1)} collective-permute-done((bf16[128,768]{1,0:T(8,128)(2,1)S(1)}, bf16[128,768]{1,0:T(8,128)(2,1)S(1)}, u32[]{:S(2)}, u32[]{:S(2)}) %collective-permute-start.52) | collective-permute-done | bytes 196640 | tf_op jit(solution)/shard_map/ppermute | solution.py:20
  156.8 1.1 collective-permute-start.57
  158.0 0.9 collective-permute-start.59
  158.9 2.5 %collective-permute-start.62 = (bf16[384,384]{1,0:T(8,128)(2,1)S(1)}, bf16[384,384]{1,0:T(8,128)(2,1)S(1)}, u32[]{:S(2)}, u32[]{:S(2)}) collective-permute-start(bf16[384,384]{1,0:T(8,128)(2,1)S(1)} %join_kernel.4.refs_11_.refs_17_), channel_id=1, source_target_pairs={{0,4},{1,5},{2,6},{3,7},{4,0},{5,1},{6,2},{7,3},{8,12},{9,13},{10,... | collective-permute-start | bytes 884744 | tf_op jit(solution)/shard_map/ppermute | solution.py:20
  161.4 1.6 vector_out_kernel.1
  163.0 1.0 collective-permute-done.59.refs_2_
  165.9 3.4 %collective-permute-done.57.refs_11_ = bf16[128,768]{1,0:T(8,128)(2,1)S(1)} collective-permute-done((bf16[128,768]{1,0:T(8,128)(2,1)S(1)}, bf16[128,768]{1,0:T(8,128)(2,1)S(1)}, u32[]{:S(2)}, u32[]{:S(2)}) %collective-permute-start.57) | collective-permute-done | bytes 196640 | tf_op jit(solution)/shard_map/ppermute | solution.py:20
  169.4 2.9 %collective-permute-done.62.refs_18_ = bf16[384,384]{1,0:T(8,128)(2,1)S(1)} collective-permute-done((bf16[384,384]{1,0:T(8,128)(2,1)S(1)}, bf16[384,384]{1,0:T(8,128)(2,1)S(1)}, u32[]{:S(2)}, u32[]{:S(2)}) %collective-permute-start.62) | collective-permute-done | bytes 294944 | tf_op jit(solution)/shard_map/ppermute | solution.py:20
  172.3 4.4 %last_kernel.1 = (f32[8,128]{1,0:T(8,128)}, f32[2,64,768]{2,1,0:T(8,128)}, f32[2,64,768]{2,1,0:T(8,128)}, f32[384,2304]{1,0:T(8,128)}, f32[384,768]{1,0:T(8,128)...) custom-call(s32[8]{0:T(128)S(1)} %stack.41.refs_0_, bf16[224,576]{1,0:T(8,128)(2,1)S(1)} %add_kernel.12.refs_2_.refs_1_, ...), custom_call_target="tpu_custom_call" | custom-call | tf_op jit(solution)/shard_map/last_kernel/pallas_call | solution.py:93
  (124 shorter events, 28.2 us)
Async XLA Ops:
  2.3 13.2 %collective-permute-start = (f32[64,768]{1,0:T(8,128)S(1)}, f32[64,768]{1,0:T(8,128)S(1)}, u32[]{:S(2)}, u32[]{:S(2)}) collective-permute-start(f32[64,768]{1,0:T(8,128)S(1)} %get-tuple-element.125.refs_12_), channel_id=1, source_target_pairs={{0,8},{1,9},{2,10},{3,11},{4,12},{5,13},{6,14},{7,15},{8,0},{9,1},... | collective-permute-start | bytes 589832 | tf_op jit(solution)/shard_map/ppermute | solution.py:20
  7.2 6.0 %collective-permute-start.2 = (bf16[2,32,63]{2,1,0:T(8,128)(2,1)S(1)}, bf16[2,32,63]{2,1,0:T(8,128)(2,1)S(1)}, u32[]{:S(2)}, u32[]{:S(2)}) collective-permute-start(bf16[2,32,63]{2,1,0:T(8,128)(2,1)S(1)} %pad_maximum_fusion.refs_1_), channel_id=1, source_target_pairs={{0,16},{16,0},{1,17},{17,1},{2,18},{18,2},{3,19},{19,3},{4,20},{20... | collective-permute-start | bytes 24200 | tf_op jit(solution)/shard_map/ppermute | solution.py:24
  9.5 3.7 %collective-permute-start.1 = (bf16[4,384]{1,0:T(4,128)(2,1)S(1)}, bf16[4,384]{1,0:T(4,128)(2,1)S(1)}, u32[]{:S(2)}, u32[]{:S(2)}) collective-permute-start(bf16[4,384]{1,0:T(4,128)(2,1)S(1)} %reshape.27.refs_3_), channel_id=1, source_target_pairs={{0,16},{16,0},{1,17},{17,1},{2,18},{18,2},{3,19},{19,3},{4,20},{20... | collective-permute-start | bytes 9224 | tf_op jit(solution)/shard_map/ppermute | solution.py:24
  15.6 14.2 %collective-permute-start.6 = (bf16[384,576]{1,0:T(8,128)(2,1)S(1)}, bf16[384,576]{1,0:T(8,128)(2,1)S(1)}, u32[]{:S(2)}, u32[]{:S(2)}) collective-permute-start(bf16[384,576]{1,0:T(8,128)(2,1)S(1)} %pack_kernel.1.refs_5_), channel_id=1, source_target_pairs={{0,16},{16,0},{1,17},{17,1},{2,18},{18,2},{3,19},{19,3},{4,20},{20... | collective-permute-start | bytes 1327112 | tf_op jit(solution)/shard_map/ppermute | solution.py:24
  17.1 12.6 %copy-start.2 = (bf16[384,768]{1,0:T(8,128)(2,1)S(1)}, bf16[384,768]{1,0:T(8,128)(2,1)}, u32[]{:S(2)}) copy-start(bf16[384,768]{1,0:T(8,128)(2,1)} %refs_9_) | copy-start | bytes 1769476
  17.1 7.3 %collective-permute-start.7 = (bf16[64,768]{1,0:T(8,128)(2,1)S(1)}, bf16[64,768]{1,0:T(8,128)(2,1)S(1)}, u32[]{:S(2)}, u32[]{:S(2)}) collective-permute-start(bf16[64,768]{1,0:T(8,128)(2,1)S(1)} %get-tuple-element.131), channel_id=1, source_target_pairs={{0,8},{1,9},{2,10},{3,11},{4,12},{5,13},{6,14},{7,15},{8,0},{9,1},... | collective-permute-start | bytes 294920 | tf_op jit(solution)/shard_map/ppermute | solution.py:20
  17.9 14.1 %collective-permute-start.5 = (bf16[128,768]{1,0:T(8,128)(2,1)S(1)}, bf16[128,768]{1,0:T(8,128)(2,1)S(1)}, u32[]{:S(2)}, u32[]{:S(2)}) collective-permute-start(bf16[128,768]{1,0:T(8,128)(2,1)S(1)} %get-tuple-element.129.refs_1_), channel_id=1, source_target_pairs={{0,6},{1,7},{2,4},{3,5},{4,2},{5,3},{6,0},{7,1},{8,14},{9,15},{10,... | collective-permute-start | bytes 589832 | tf_op jit(solution)/shard_map/ppermute | solution.py:20
  22.9 9.0 %collective-permute-start.4 = (bf16[128,768]{1,0:T(8,128)(2,1)S(1)}, bf16[128,768]{1,0:T(8,128)(2,1)S(1)}, u32[]{:S(2)}, u32[]{:S(2)}) collective-permute-start(bf16[128,768]{1,0:T(8,128)(2,1)S(1)} %get-tuple-element.129.refs_1_), channel_id=1, source_target_pairs={{0,4},{1,5},{2,6},{3,7},{4,0},{5,1},{6,2},{7,3},{8,12},{9,13},{10,... | collective-permute-start | bytes 589832 | tf_op jit(solution)/shard_map/ppermute | solution.py:20
  23.0 9.4 %collective-permute-start.3 = (bf16[128,768]{1,0:T(8,128)(2,1)S(1)}, bf16[128,768]{1,0:T(8,128)(2,1)S(1)}, u32[]{:S(2)}, u32[]{:S(2)}) collective-permute-start(bf16[128,768]{1,0:T(8,128)(2,1)S(1)} %get-tuple-element.129.refs_1_), channel_id=1, source_target_pairs={{0,2},{1,3},{2,0},{3,1},{4,6},{5,7},{6,4},{7,5},{8,10},{9,11},{10,... | collective-permute-start | bytes 589832 | tf_op jit(solution)/shard_map/ppermute | solution.py:20
  25.1 11.0 %collective-permute-start.10 = (bf16[192,768]{1,0:T(8,128)(2,1)S(1)}, bf16[192,768]{1,0:T(8,128)(2,1)S(1)}, u32[]{:S(2)}, u32[]{:S(2)}) collective-permute-start(bf16[192,768]{1,0:T(8,128)(2,1)S(1)} %rows_kernel.1.refs_3_), channel_id=1, source_target_pairs={{0,16},{16,0},{1,17},{17,1},{2,18},{18,2},{3,19},{19,3},{4,20},{20... | collective-permute-start | bytes 884744 | tf_op jit(solution)/shard_map/ppermute | solution.py:24
  29.7 19.0 %collective-permute-start.15 = (bf16[384,768]{1,0:T(8,128)(2,1)S(1)}, bf16[384,768]{1,0:T(8,128)(2,1)S(1)}, u32[]{:S(2)}, u32[]{:S(2)}) collective-permute-start(bf16[384,768]{1,0:T(8,128)(2,1)S(1)} %copy-done.2), channel_id=1, source_target_pairs={{0,16},{16,0},{1,17},{17,1},{2,18},{18,2},{3,19},{19,3},{4,20},{20... | collective-permute-start | bytes 1769480 | tf_op jit(solution)/shard_map/ppermute | solution.py:24
  33.8 5.3 %collective-permute-start.8 = (bf16[512,384]{1,0:T(8,128)(2,1)S(1)}, bf16[512,384]{1,0:T(8,128)(2,1)S(1)}, u32[]{:S(2)}, u32[]{:S(2)}) collective-permute-start(bf16[512,384]{1,0:T(8,128)(2,1)S(1)} %get-tuple-element.136.refs_2_), channel_id=1, source_target_pairs={{0,1},{1,0},{2,3},{3,2},{4,5},{5,4},{6,7},{7,6},{8,9},{9,8},{10,11... | collective-permute-start | bytes 1179656 | tf_op jit(solution)/shard_map/ppermute | solution.py:20
  36.0 7.7 %collective-permute-start.11 = (bf16[192,768]{1,0:T(8,128)(2,1)S(1)}, bf16[192,768]{1,0:T(8,128)(2,1)S(1)}, u32[]{:S(2)}, u32[]{:S(2)}) collective-permute-start(bf16[192,768]{1,0:T(8,128)(2,1)S(1)} %collective-permute-done.10.refs_6_), channel_id=1, source_target_pairs={{0,1},{1,0},{2,3},{3,2},{4,5},{5,4},{6,7},{7,6},{8,9},{9,8},{10,11... | collective-permute-start | bytes 884744 | tf_op jit(solution)/shard_map/ppermute | solution.py:20
  36.0 7.7 %collective-permute-start.9 = (bf16[128,768]{1,0:T(8,128)(2,1)S(1)}, bf16[128,768]{1,0:T(8,128)(2,1)S(1)}, u32[]{:S(2)}, u32[]{:S(2)}) collective-permute-start(bf16[128,768]{1,0:T(8,128)(2,1)S(1)} %stack_kernel.1.refs_2_.refs_5_), channel_id=1, source_target_pairs={{0,2},{1,3},{2,0},{3,1},{4,6},{5,7},{6,4},{7,5},{8,10},{9,11},{10,... | collective-permute-start | bytes 589832 | tf_op jit(solution)/shard_map/ppermute | solution.py:20
  37.6 21.9 %collective-permute-start.21 = (bf16[768,384]{1,0:T(8,128)(2,1)S(1)}, bf16[768,384]{1,0:T(8,128)(2,1)S(1)}, u32[]{:S(2)}, u32[]{:S(2)}) collective-permute-start(bf16[768,384]{1,0:T(8,128)(2,1)S(1)} %copy-done.3), channel_id=1, source_target_pairs={{0,16},{16,0},{1,17},{17,1},{2,18},{18,2},{3,19},{19,3},{4,20},{20... | collective-permute-start | bytes 1769480 | tf_op jit(solution)/shard_map/ppermute | solution.py:24
  43.7 5.0 %collective-permute-start.12 = (bf16[128,192]{1,0:T(8,128)(2,1)S(1)}, bf16[128,192]{1,0:T(8,128)(2,1)S(1)}, u32[]{:S(2)}, u32[]{:S(2)}) collective-permute-start(bf16[128,192]{1,0:T(8,128)(2,1)S(1)} %get-tuple-element.148), channel_id=1, source_target_pairs={{0,2},{1,3},{2,0},{3,1},{4,6},{5,7},{6,4},{7,5},{8,10},{9,11},{10,... | collective-permute-start | bytes 147464 | tf_op jit(solution)/shard_map/ppermute | solution.py:20
  44.9 4.5 %collective-permute-start.13 = (bf16[128,192]{1,0:T(8,128)(2,1)S(1)}, bf16[128,192]{1,0:T(8,128)(2,1)S(1)}, u32[]{:S(2)}, u32[]{:S(2)}) collective-permute-start(bf16[128,192]{1,0:T(8,128)(2,1)S(1)} %get-tuple-element.149), channel_id=1, source_target_pairs={{0,4},{1,5},{2,6},{3,7},{4,0},{5,1},{6,2},{7,3},{8,12},{9,13},{10,... | collective-permute-start | bytes 147464 | tf_op jit(solution)/shard_map/ppermute | solution.py:20
  46.5 5.2 %collective-permute-start.14 = (bf16[128,192]{1,0:T(8,128)(2,1)S(1)}, bf16[128,192]{1,0:T(8,128)(2,1)S(1)}, u32[]{:S(2)}, u32[]{:S(2)}) collective-permute-start(bf16[128,192]{1,0:T(8,128)(2,1)S(1)} %get-tuple-element.150), channel_id=1, source_target_pairs={{0,6},{1,7},{2,4},{3,5},{4,2},{5,3},{6,0},{7,1},{8,14},{9,15},{10,... | collective-permute-start | bytes 147464 | tf_op jit(solution)/shard_map/ppermute | solution.py:20
  52.9 5.7 %collective-permute-start.16 = (bf16[128,768]{1,0:T(8,128)(2,1)S(1)}, bf16[128,768]{1,0:T(8,128)(2,1)S(1)}, u32[]{:S(2)}, u32[]{:S(2)}) collective-permute-start(bf16[128,768]{1,0:T(8,128)(2,1)S(1)} %get-tuple-element.152.refs_1_), channel_id=1, source_target_pairs={{0,2},{1,3},{2,0},{3,1},{4,6},{5,7},{6,4},{7,5},{8,10},{9,11},{10,... | collective-permute-start | bytes 589832 | tf_op jit(solution)/shard_map/ppermute | solution.py:20
  53.3 6.2 %collective-permute-start.17 = (bf16[128,768]{1,0:T(8,128)(2,1)S(1)}, bf16[128,768]{1,0:T(8,128)(2,1)S(1)}, u32[]{:S(2)}, u32[]{:S(2)}) collective-permute-start(bf16[128,768]{1,0:T(8,128)(2,1)S(1)} %get-tuple-element.152.refs_1_), channel_id=1, source_target_pairs={{0,1},{1,0},{2,3},{3,2},{4,5},{5,4},{6,7},{7,6},{8,9},{9,8},{10,11... | collective-permute-start | bytes 589832 | tf_op jit(solution)/shard_map/ppermute | solution.py:20
  58.6 1.4 collective-permute-start.19
  58.7 1.7 collective-permute-start.20
  59.2 1.5 collective-permute-start.18
  64.9 16.2 %collective-permute-start.28 = (bf16[384,768]{1,0:T(8,128)(2,1)S(1)}, bf16[384,768]{1,0:T(8,128)(2,1)S(1)}, u32[]{:S(2)}, u32[]{:S(2)}) collective-permute-start(bf16[384,768]{1,0:T(8,128)(2,1)S(1)} %get-tuple-element.163.refs_2_), channel_id=1, source_target_pairs={{0,4},{1,5},{2,6},{3,7},{4,0},{5,1},{6,2},{7,3},{8,12},{9,13},{10,... | collective-permute-start | bytes 1769480 | tf_op jit(solution)/shard_map/ppermute | solution.py:20
  65.4 1.4 collective-permute-start.23
  65.4 5.9 %collective-permute-start.22 = (bf16[128,768]{1,0:T(8,128)(2,1)S(1)}, bf16[128,768]{1,0:T(8,128)(2,1)S(1)}, u32[]{:S(2)}, u32[]{:S(2)}) collective-permute-start(bf16[128,768]{1,0:T(8,128)(2,1)S(1)} %get-tuple-element.158), channel_id=1, source_target_pairs={{0,1},{1,0},{2,3},{3,2},{4,5},{5,4},{6,7},{7,6},{8,9},{9,8},{10,11... | collective-permute-start | bytes 589832 | tf_op jit(solution)/shard_map/ppermute | solution.py:20
  66.9 7.0 %collective-permute-start.24 = (bf16[128,768]{1,0:T(8,128)(2,1)S(1)}, bf16[128,768]{1,0:T(8,128)(2,1)S(1)}, u32[]{:S(2)}, u32[]{:S(2)}) collective-permute-start(bf16[128,768]{1,0:T(8,128)(2,1)S(1)} %add_kernel.8.refs_3_), channel_id=1, source_target_pairs={{0,2},{1,3},{2,0},{3,1},{4,6},{5,7},{6,4},{7,5},{8,10},{9,11},{10,... | collective-permute-start | bytes 589832 | tf_op jit(solution)/shard_map/ppermute | solution.py:20
  69.8 17.0 %collective-permute-start.29 = (bf16[384,768]{1,0:T(8,128)(2,1)S(1)}, bf16[384,768]{1,0:T(8,128)(2,1)S(1)}, u32[]{:S(2)}, u32[]{:S(2)}) collective-permute-start(bf16[384,768]{1,0:T(8,128)(2,1)S(1)} %get-tuple-element.167.refs_7_), channel_id=1, source_target_pairs={{0,16},{16,0},{1,17},{17,1},{2,18},{18,2},{3,19},{19,3},{4,20},{20... | collective-permute-start | bytes 1769480 | tf_op jit(solution)/shard_map/ppermute | solution.py:24
  74.8 8.4 %collective-permute-start.25 = (bf16[128,192]{1,0:T(8,128)(2,1)S(1)}, bf16[128,192]{1,0:T(8,128)(2,1)S(1)}, u32[]{:S(2)}, u32[]{:S(2)}) collective-permute-start(bf16[128,192]{1,0:T(8,128)(2,1)S(1)} %get-tuple-element.169), channel_id=1, source_target_pairs={{0,2},{1,3},{2,0},{3,1},{4,6},{5,7},{6,4},{7,5},{8,10},{9,11},{10,... | collective-permute-start | bytes 147464 | tf_op jit(solution)/shard_map/ppermute | solution.py:20
  76.3 6.8 %collective-permute-start.26 = (bf16[128,192]{1,0:T(8,128)(2,1)S(1)}, bf16[128,192]{1,0:T(8,128)(2,1)S(1)}, u32[]{:S(2)}, u32[]{:S(2)}) collective-permute-start(bf16[128,192]{1,0:T(8,128)(2,1)S(1)} %get-tuple-element.170), channel_id=1, source_target_pairs={{0,4},{1,5},{2,6},{3,7},{4,0},{5,1},{6,2},{7,3},{8,12},{9,13},{10,... | collective-permute-start | bytes 147464 | tf_op jit(solution)/shard_map/ppermute | solution.py:20
  76.8 6.4 %collective-permute-start.27 = (bf16[128,192]{1,0:T(8,128)(2,1)S(1)}, bf16[128,192]{1,0:T(8,128)(2,1)S(1)}, u32[]{:S(2)}, u32[]{:S(2)}) collective-permute-start(bf16[128,192]{1,0:T(8,128)(2,1)S(1)} %get-tuple-element.171), channel_id=1, source_target_pairs={{0,6},{1,7},{2,4},{3,5},{4,2},{5,3},{6,0},{7,1},{8,14},{9,15},{10,... | collective-permute-start | bytes 147464 | tf_op jit(solution)/shard_map/ppermute | solution.py:20
  83.2 8.1 %collective-permute-start.31 = (bf16[384,768]{1,0:T(8,128)(2,1)S(1)}, bf16[384,768]{1,0:T(8,128)(2,1)S(1)}, u32[]{:S(2)}, u32[]{:S(2)}) collective-permute-start(bf16[384,768]{1,0:T(8,128)(2,1)S(1)} %get-tuple-element.185.refs_12_), channel_id=1, source_target_pairs={{0,1},{1,0},{2,3},{3,2},{4,5},{5,4},{6,7},{7,6},{8,9},{9,8},{10,11... | collective-permute-start | bytes 1769480 | tf_op jit(solution)/shard_map/ppermute | solution.py:20
  86.3 2.0 %collective-permute-start.30 = (bf16[512,128]{1,0:T(8,128)(2,1)S(1)}, bf16[512,128]{1,0:T(8,128)(2,1)S(1)}, u32[]{:S(2)}, u32[]{:S(2)}) collective-permute-start(bf16[512,128]{1,0:T(8,128)(2,1)S(1)} %get-tuple-element.182), channel_id=1, source_target_pairs={{0,1},{1,0},{2,3},{3,2},{4,5},{5,4},{6,7},{7,6},{8,9},{9,8},{10,11... | collective-permute-start | bytes 393224 | tf_op jit(solution)/shard_map/ppermute | solution.py:20
  87.5 9.0 %collective-permute-start.34 = (bf16[192,768]{1,0:T(8,128)(2,1)S(1)}, bf16[192,768]{1,0:T(8,128)(2,1)S(1)}, u32[]{:S(2)}, u32[]{:S(2)}) collective-permute-start(bf16[192,768]{1,0:T(8,128)(2,1)S(1)} %get-tuple-element.181.refs_12_), channel_id=1, source_target_pairs={{0,4},{1,5},{2,6},{3,7},{4,0},{5,1},{6,2},{7,3},{8,12},{9,13},{10,... | collective-permute-start | bytes 884744 | tf_op jit(solution)/shard_map/ppermute | solution.py:20
  91.2 1.4 collective-permute-start.32
  95.6 1.5 collective-permute-start.33
  98.9 2.4 %collective-permute-start.35 = (bf16[416,576]{1,0:T(8,128)(2,1)S(1)}, bf16[416,576]{1,0:T(8,128)(2,1)S(1)}, u32[]{:S(2)}, u32[]{:S(2)}) collective-permute-start(bf16[416,576]{1,0:T(8,128)(2,1)S(1)} %get-tuple-element.200), channel_id=1, source_target_pairs={{0,1},{1,0},{2,3},{3,2},{4,5},{5,4},{6,7},{7,6},{8,9},{9,8},{10,11... | collective-permute-start | bytes 1437704 | tf_op jit(solution)/shard_map/ppermute | solution.py:20
  99.0 9.4 %collective-permute-start.37 = (bf16[192,768]{1,0:T(8,128)(2,1)S(1)}, bf16[192,768]{1,0:T(8,128)(2,1)S(1)}, u32[]{:S(2)}, u32[]{:S(2)}) collective-permute-start(bf16[192,768]{1,0:T(8,128)(2,1)S(1)} %get-tuple-element.187.refs_12_), channel_id=1, source_target_pairs={{0,2},{1,3},{2,0},{3,1},{4,6},{5,7},{6,4},{7,5},{8,10},{9,11},{10,... | collective-permute-start | bytes 884744 | tf_op jit(solution)/shard_map/ppermute | solution.py:20
  101.4 9.7 %collective-permute-start.36 = (bf16[224,576]{1,0:T(8,128)(2,1)S(1)}, bf16[224,576]{1,0:T(8,128)(2,1)S(1)}, u32[]{:S(2)}, u32[]{:S(2)}) collective-permute-start(bf16[224,576]{1,0:T(8,128)(2,1)S(1)} %get-tuple-element.205.refs_3_), channel_id=1, source_target_pairs={{0,16},{16,0},{1,17},{17,1},{2,18},{18,2},{3,19},{19,3},{4,20},{20... | collective-permute-start | bytes 774152 | tf_op jit(solution)/shard_map/ppermute | solution.py:24
  102.6 19.8 %collective-permute-start.40 = (bf16[256,768]{1,0:T(8,128)(2,1)S(1)}, bf16[256,768]{1,0:T(8,128)(2,1)S(1)}, u32[]{:S(2)}, u32[]{:S(2)}) collective-permute-start(bf16[256,768]{1,0:T(8,128)(2,1)S(1)} %get-tuple-element.213), channel_id=1, source_target_pairs={{0,1},{1,0},{2,3},{3,2},{4,5},{5,4},{6,7},{7,6},{8,9},{9,8},{10,11... | collective-permute-start | bytes 1179656 | tf_op jit(solution)/shard_map/ppermute | solution.py:20
  102.6 19.1 %collective-permute-start.41 = (bf16[384,384]{1,0:T(8,128)(2,1)S(1)}, bf16[384,384]{1,0:T(8,128)(2,1)S(1)}, u32[]{:S(2)}, u32[]{:S(2)}) collective-permute-start(bf16[384,384]{1,0:T(8,128)(2,1)S(1)} %get-tuple-element.176.refs_6_), channel_id=1, source_target_pairs={{0,16},{16,0},{1,17},{17,1},{2,18},{18,2},{3,19},{19,3},{4,20},{20... | collective-permute-start | bytes 884744 | tf_op jit(solution)/shard_map/ppermute | solution.py:24
  103.5 10.5 %collective-permute-start.42 = (bf16[96,768]{1,0:T(8,128)(2,1)S(1)}, bf16[96,768]{1,0:T(8,128)(2,1)S(1)}, u32[]{:S(2)}, u32[]{:S(2)}) collective-permute-start(bf16[96,768]{1,0:T(8,128)(2,1)S(1)} %get-tuple-element.198.refs_17_), channel_id=1, source_target_pairs={{0,8},{1,9},{2,10},{3,11},{4,12},{5,13},{6,14},{7,15},{8,0},{9,1},... | collective-permute-start | bytes 442376 | tf_op jit(solution)/shard_map/ppermute | solution.py:20
  108.4 28.7 %collective-permute-start.50 = (bf16[256,768]{1,0:T(8,128)(2,1)S(1)}, bf16[256,768]{1,0:T(8,128)(2,1)S(1)}, u32[]{:S(2)}, u32[]{:S(2)}) collective-permute-start(bf16[256,768]{1,0:T(8,128)(2,1)S(1)} %get-tuple-element.217), channel_id=1, source_target_pairs={{0,2},{1,3},{2,0},{3,1},{4,6},{5,7},{6,4},{7,5},{8,10},{9,11},{10,... | collective-permute-start | bytes 1179656 | tf_op jit(solution)/shard_map/ppermute | solution.py:20
  111.2 19.9 %collective-permute-start.38 = (bf16[224,576]{1,0:T(8,128)(2,1)S(1)}, bf16[224,576]{1,0:T(8,128)(2,1)S(1)}, u32[]{:S(2)}, u32[]{:S(2)}) collective-permute-start(bf16[224,576]{1,0:T(8,128)(2,1)S(1)} %add_kernel.9.refs_2_.refs_0_), channel_id=1, source_target_pairs={{0,8},{1,9},{2,10},{3,11},{4,12},{5,13},{6,14},{7,15},{8,0},{9,1},... | collective-permute-start | bytes 774152 | tf_op jit(solution)/shard_map/ppermute | solution.py:20
  114.0 10.7 %collective-permute-start.39 = (bf16[96,768]{1,0:T(8,128)(2,1)S(1)}, bf16[96,768]{1,0:T(8,128)(2,1)S(1)}, u32[]{:S(2)}, u32[]{:S(2)}) collective-permute-start(bf16[96,768]{1,0:T(8,128)(2,1)S(1)} %get-tuple-element.209.refs_2_), channel_id=1, source_target_pairs={{0,16},{16,0},{1,17},{17,1},{2,18},{18,2},{3,19},{19,3},{4,20},{20... | collective-permute-start | bytes 442376 | tf_op jit(solution)/shard_map/ppermute | solution.py:24
  122.3 13.6 %collective-permute-start.51 = (bf16[192,384]{1,0:T(8,128)(2,1)S(1)}, bf16[192,384]{1,0:T(8,128)(2,1)S(1)}, u32[]{:S(2)}, u32[]{:S(2)}) collective-permute-start(bf16[192,384]{1,0:T(8,128)(2,1)S(1)} %get-tuple-element.216.refs_2_), channel_id=1, source_target_pairs={{0,8},{1,9},{2,10},{3,11},{4,12},{5,13},{6,14},{7,15},{8,0},{9,1},... | collective-permute-start | bytes 442376 | tf_op jit(solution)/shard_map/ppermute | solution.py:20
  124.8 12.4 %collective-permute-start.55 = (bf16[96,768]{1,0:T(8,128)(2,1)S(1)}, bf16[96,768]{1,0:T(8,128)(2,1)S(1)}, u32[]{:S(2)}, u32[]{:S(2)}) collective-permute-start(bf16[96,768]{1,0:T(8,128)(2,1)S(1)} %add_kernel.11.refs_2_.refs_0_), channel_id=1, source_target_pairs={{0,4},{1,5},{2,6},{3,7},{4,0},{5,1},{6,2},{7,3},{8,12},{9,13},{10,... | collective-permute-start | bytes 442376 | tf_op jit(solution)/shard_map/ppermute | solution.py:20
  126.1 14.6 %collective-permute-start.56 = (bf16[96,768]{1,0:T(8,128)(2,1)S(1)}, bf16[96,768]{1,0:T(8,128)(2,1)S(1)}, u32[]{:S(2)}, u32[]{:S(2)}) collective-permute-start(bf16[96,768]{1,0:T(8,128)(2,1)S(1)} %add_kernel.10.refs_3_.refs_1_), channel_id=1, source_target_pairs={{0,8},{1,9},{2,10},{3,11},{4,12},{5,13},{6,14},{7,15},{8,0},{9,1},... | collective-permute-start | bytes 442376 | tf_op jit(solution)/shard_map/ppermute | solution.py:20
  131.2 17.8 %collective-permute-start.44 = (bf16[224,576]{1,0:T(8,128)(2,1)S(1)}, bf16[224,576]{1,0:T(8,128)(2,1)S(1)}, u32[]{:S(2)}, u32[]{:S(2)}) collective-permute-start(bf16[224,576]{1,0:T(8,128)(2,1)S(1)} %add_kernel.12.refs_2_.refs_1_), channel_id=1, source_target_pairs={{0,4},{1,5},{2,6},{3,7},{4,0},{5,1},{6,2},{7,3},{8,12},{9,13},{10,... | collective-permute-start | bytes 774152 | tf_op jit(solution)/shard_map/ppermute | solution.py:20
  135.9 6.9 %collective-permute-start.53 = (bf16[128,768]{1,0:T(8,128)(2,1)S(1)}, bf16[128,768]{1,0:T(8,128)(2,1)S(1)}, u32[]{:S(2)}, u32[]{:S(2)}) collective-permute-start(bf16[128,768]{1,0:T(8,128)(2,1)S(1)} %tail_add_kernel.2.refs_2_), channel_id=1, source_target_pairs={{0,2},{1,3},{2,0},{3,1},{4,6},{5,7},{6,4},{7,5},{8,10},{9,11},{10,... | collective-permute-start | bytes 589832 | tf_op jit(solution)/shard_map/ppermute | solution.py:20
  137.2 18.3 %collective-permute-start.52 = (bf16[128,768]{1,0:T(8,128)(2,1)S(1)}, bf16[128,768]{1,0:T(8,128)(2,1)S(1)}, u32[]{:S(2)}, u32[]{:S(2)}) collective-permute-start(bf16[128,768]{1,0:T(8,128)(2,1)S(1)} %tail_add_kernel.3.refs_3_), channel_id=1, source_target_pairs={{0,4},{1,5},{2,6},{3,7},{4,0},{5,1},{6,2},{7,3},{8,12},{9,13},{10,... | collective-permute-start | bytes 589832 | tf_op jit(solution)/shard_map/ppermute | solution.py:20
  137.2 13.9 %collective-permute-start.54 = (bf16[192,384]{1,0:T(8,128)(2,1)S(1)}, bf16[192,384]{1,0:T(8,128)(2,1)S(1)}, u32[]{:S(2)}, u32[]{:S(2)}) collective-permute-start(bf16[192,384]{1,0:T(8,128)(2,1)S(1)} %add_kernel.13.refs_2_.refs_1_), channel_id=1, source_target_pairs={{0,8},{1,9},{2,10},{3,11},{4,12},{5,13},{6,14},{7,15},{8,0},{9,1},... | collective-permute-start | bytes 442376 | tf_op jit(solution)/shard_map/ppermute | solution.py:20
  140.7 17.3 %collective-permute-start.43 = (bf16[224,576]{1,0:T(8,128)(2,1)S(1)}, bf16[224,576]{1,0:T(8,128)(2,1)S(1)}, u32[]{:S(2)}, u32[]{:S(2)}) collective-permute-start(bf16[224,576]{1,0:T(8,128)(2,1)S(1)} %add_kernel.12.refs_2_.refs_1_), channel_id=1, source_target_pairs={{0,2},{1,3},{2,0},{3,1},{4,6},{5,7},{6,4},{7,5},{8,10},{9,11},{10,... | collective-permute-start | bytes 774152 | tf_op jit(solution)/shard_map/ppermute | solution.py:20
  142.8 14.0 %collective-permute-start.58 = (bf16[96,768]{1,0:T(8,128)(2,1)S(1)}, bf16[96,768]{1,0:T(8,128)(2,1)S(1)}, u32[]{:S(2)}, u32[]{:S(2)}) collective-permute-start(bf16[96,768]{1,0:T(8,128)(2,1)S(1)} %add_kernel.14.refs_3_.refs_0_), channel_id=1, source_target_pairs={{0,8},{1,9},{2,10},{3,11},{4,12},{5,13},{6,14},{7,15},{8,0},{9,1},... | collective-permute-start | bytes 442376 | tf_op jit(solution)/shard_map/ppermute | solution.py:20
  149.0 9.9 %collective-permute-start.45 = (bf16[224,576]{1,0:T(8,128)(2,1)S(1)}, bf16[224,576]{1,0:T(8,128)(2,1)S(1)}, u32[]{:S(2)}, u32[]{:S(2)}) collective-permute-start(bf16[224,576]{1,0:T(8,128)(2,1)S(1)} %collective-permute-done.44.refs_3_), channel_id=1, source_target_pairs={{0,2},{1,3},{2,0},{3,1},{4,6},{5,7},{6,4},{7,5},{8,10},{9,11},{10,... | collective-permute-start | bytes 774152 | tf_op jit(solution)/shard_map/ppermute | solution.py:20
  151.1 14.7 %collective-permute-start.61 = (bf16[192,768]{1,0:T(8,128)(2,1)S(1)}, bf16[192,768]{1,0:T(8,128)(2,1)S(1)}, u32[]{:S(2)}, u32[]{:S(2)}) collective-permute-start(bf16[192,768]{1,0:T(8,128)(2,1)S(1)} %join_kernel.3.refs_2_.refs_15_), channel_id=1, source_target_pairs={{0,4},{1,5},{2,6},{3,7},{4,0},{5,1},{6,2},{7,3},{8,12},{9,13},{10,... | collective-permute-start | bytes 884744 | tf_op jit(solution)/shard_map/ppermute | solution.py:20
  155.4 9.9 %collective-permute-start.46 = (bf16[224,576]{1,0:T(8,128)(2,1)S(1)}, bf16[224,576]{1,0:T(8,128)(2,1)S(1)}, u32[]{:S(2)}, u32[]{:S(2)}) collective-permute-start(bf16[224,576]{1,0:T(8,128)(2,1)S(1)} %add_kernel.12.refs_2_.refs_1_), channel_id=1, source_target_pairs={{0,1},{1,0},{2,3},{3,2},{4,5},{5,4},{6,7},{7,6},{8,9},{9,8},{10,11... | collective-permute-start | bytes 774152 | tf_op jit(solution)/shard_map/ppermute | solution.py:20
  156.8 12.6 %collective-permute-start.57 = (bf16[128,768]{1,0:T(8,128)(2,1)S(1)}, bf16[128,768]{1,0:T(8,128)(2,1)S(1)}, u32[]{:S(2)}, u32[]{:S(2)}) collective-permute-start(bf16[128,768]{1,0:T(8,128)(2,1)S(1)} %get-tuple-element.223), channel_id=1, source_target_pairs={{0,8},{1,9},{2,10},{3,11},{4,12},{5,13},{6,14},{7,15},{8,0},{9,1},... | collective-permute-start | bytes 589832 | tf_op jit(solution)/shard_map/ppermute | solution.py:20
  158.0 6.0 %collective-permute-start.59 = (bf16[96,768]{1,0:T(8,128)(2,1)S(1)}, bf16[96,768]{1,0:T(8,128)(2,1)S(1)}, u32[]{:S(2)}, u32[]{:S(2)}) collective-permute-start(bf16[96,768]{1,0:T(8,128)(2,1)S(1)} %add_kernel.15.refs_6_.refs_1_), channel_id=1, source_target_pairs={{0,2},{1,3},{2,0},{3,1},{4,6},{5,7},{6,4},{7,5},{8,10},{9,11},{10,... | collective-permute-start | bytes 442376 | tf_op jit(solution)/shard_map/ppermute | solution.py:20
  158.9 13.4 %collective-permute-start.62 = (bf16[384,384]{1,0:T(8,128)(2,1)S(1)}, bf16[384,384]{1,0:T(8,128)(2,1)S(1)}, u32[]{:S(2)}, u32[]{:S(2)}) collective-permute-start(bf16[384,384]{1,0:T(8,128)(2,1)S(1)} %join_kernel.4.refs_11_.refs_17_), channel_id=1, source_target_pairs={{0,4},{1,5},{2,6},{3,7},{4,0},{5,1},{6,2},{7,3},{8,12},{9,13},{10,... | collective-permute-start | bytes 884744 | tf_op jit(solution)/shard_map/ppermute | solution.py:20
  165.3 7.0 %collective-permute-start.60 = (bf16[192,768]{1,0:T(8,128)(2,1)S(1)}, bf16[192,768]{1,0:T(8,128)(2,1)S(1)}, u32[]{:S(2)}, u32[]{:S(2)}) collective-permute-start(bf16[192,768]{1,0:T(8,128)(2,1)S(1)} %join_kernel.5.refs_13_.refs_19_), channel_id=1, source_target_pairs={{0,1},{1,0},{2,3},{3,2},{4,5},{5,4},{6,7},{7,6},{8,9},{9,8},{10,11... | collective-permute-start | bytes 884744 | tf_op jit(solution)/shard_map/ppermute | solution.py:20
  165.3 6.9 %collective-permute-start.48 = (bf16[224,576]{1,0:T(8,128)(2,1)S(1)}, bf16[224,576]{1,0:T(8,128)(2,1)S(1)}, u32[]{:S(2)}, u32[]{:S(2)}) collective-permute-start(bf16[224,576]{1,0:T(8,128)(2,1)S(1)} %collective-permute-done.44.refs_3_), channel_id=1, source_target_pairs={{0,1},{1,0},{2,3},{3,2},{4,5},{5,4},{6,7},{7,6},{8,9},{9,8},{10,11... | collective-permute-start | bytes 774152 | tf_op jit(solution)/shard_map/ppermute | solution.py:20
  165.8 6.4 %collective-permute-start.47 = (bf16[224,576]{1,0:T(8,128)(2,1)S(1)}, bf16[224,576]{1,0:T(8,128)(2,1)S(1)}, u32[]{:S(2)}, u32[]{:S(2)}) collective-permute-start(bf16[224,576]{1,0:T(8,128)(2,1)S(1)} %collective-permute-done.43.refs_2_), channel_id=1, source_target_pairs={{0,1},{1,0},{2,3},{3,2},{4,5},{5,4},{6,7},{7,6},{8,9},{9,8},{10,11... | collective-permute-start | bytes 774152 | tf_op jit(solution)/shard_map/ppermute | solution.py:20
  169.4 2.9 %collective-permute-start.49 = (bf16[224,576]{1,0:T(8,128)(2,1)S(1)}, bf16[224,576]{1,0:T(8,128)(2,1)S(1)}, u32[]{:S(2)}, u32[]{:S(2)}) collective-permute-start(bf16[224,576]{1,0:T(8,128)(2,1)S(1)} %collective-permute-done.45.refs_4_), channel_id=1, source_target_pairs={{0,1},{1,0},{2,3},{3,2},{4,5},{5,4},{6,7},{7,6},{8,9},{9,8},{10,11... | collective-permute-start | bytes 774152 | tf_op jit(solution)/shard_map/ppermute | solution.py:20
  (6 other events, 25.7 us)

commit v5 on v4

--- a/solution.py
+++ b/solution.py
@@ -705,12 +705,19 @@
         copy.wait()
 
 
+def early_kernel(ids, first, first_got, out, whole, sem):
+    copies = []
+    join_out(ids, 4, first, first_got, out, whole, sem, copies)
+    for copy in copies:
+        copy.wait()
+
+
 def last_kernel(heads):
     def kernel(
         ids, q0, q1, q2, q3, o0, o1, o2, o3, token, change, got, away,
-        proj, proj_got, first, first_got, second, second_got,
-        output, tokens_grad, qkv_grad, proj_grad, fc1_grad, fc2_grad,
-        low, qkv, wide, one, two, sem,
+        proj, proj_got, second, second_got,
+        output, tokens_grad, qkv_grad, proj_grad, fc2_grad,
+        low, qkv, wide, two, sem,
     ):
         copies = []
         tok = token.shape[0]
@@ -719,7 +726,6 @@
         low[tok:, :] = got[tok:, :].astype(FULL) + away[...]
         place_out(ids, change, low.at[tok:], output, sem, copies)
         join_out(ids, 2, proj, proj_got, proj_grad, wide, sem, copies)
-        join_out(ids, 4, first, first_got, fc1_grad, one, sem, copies)
         join_out(ids, 4, second, second_got, fc2_grad, two, sem, copies)
         qkv_out(heads, ids, (q0, q1, q2, q3), (o0, o1, o2, o3), qkv_grad, qkv, sem, copies)
         for copy in copies:
@@ -1042,22 +1048,32 @@
         sent = call(tail_add_kernel, [low_rows])(v.f1, v.fed_got)[0]
         v.fed_row = send(sent, ROW)
 
+    def early():
+        dims = (half, hid)
+        (fc1.grad,) = call(
+            early_kernel,
+            [shape(dims, FULL)],
+            [pltpu.VMEM(dims, FULL), pltpu.SemaphoreType.DMA((2,))],
+            smem=1,
+            written=1,
+        )(ids, fc1.kept, fc1.got)
+
     def last():
-        dims = [tokens.shape] * 2 + [(half, 3 * width), (half, width), (half, hid), (hid, half)]
+        dims = [tokens.shape] * 2 + [(half, 3 * width), (half, width), (hid, half)]
         (
-            v.output, v.tokens_grad, v.qkv_grad, v.proj_grad, fc1.grad, fc2.grad,
+            v.output, v.tokens_grad, v.qkv_grad, v.proj_grad, fc2.grad,
         ) = call(
             last_kernel(heads),
             [shape(d, FULL) for d in dims],
             [pltpu.VMEM((rows_n, width), FULL)]
             + [pltpu.VMEM(d, FULL) for d in dims[2:]]
-            + [pltpu.SemaphoreType.DMA((12,))],
+            + [pltpu.SemaphoreType.DMA((10,))],
             smem=1,
             extra=8,
-            written=6,
+            written=5,
         )(
             ids, *v.qkv_parts, *v.qkv_others, v.token, v.change, v.token_got, away,
-            v.proj, v.proj_got, fc1.kept, fc1.got, fc2.kept, fc2.got,
+            v.proj, v.proj_got, fc2.kept, fc2.got,
         )
 
     def qkv_outer():
@@ -1181,12 +1197,13 @@
             qkv_total,
             far_all(fc2),
             normed_near,
-            near_all(fc1),
             proj_sum(FAR),
             near_all(fc2),
+            near_all(fc1),
             first_back,
             proj_sum(ROW),
             vector_last,
+            early,
             proj_join,
             last,
         ):

time: 177 us -> 177 us (level)
  waiting for transfers between devices: 58.2 us -> 54.4 us
  starting transfers between devices: 68 us -> 70.2 us
    ppermute x53, waiting for transfers between devices: 44.7 us -> 40.9 us  [hop(): lax.ppermute(value, ('seq', 'tp'), [(i, i ^ bits) for i in range(count)])]
    ppermute x53, starting transfers between devices: 49.8 us -> 51.9 us  [hop(): lax.ppermute(value, ('seq', 'tp'), [(i, i ^ bits) for i in range(count)])]
    pallas_call x44 -> x45, Pallas kernels: 43.6 us -> 44.9 us  [run(): pl.pallas_call(body, name=kernel.__qualname__.split('.')[0], out_shape=ou...]
  transfers between devices with their start and end apart: 63 -> 63, of which waited for: 30 -> 28; matrix products, arithmetic and copies ran while one was open for 1% -> 1% of each run, Pallas kernels for 18% -> 19%
where the time goes in v5:
time: 177 us; the launch traced here: 176 us
  starting transfers between devices  70.2 us (40%)
  waiting for transfers between devices  54.4 us (31%)
  Pallas kernels  44.9 us (25%)
  local copies, waits for them, and re-layouts  4.21 us (2%)
    ppermute x53, starting transfers between devices, hop(): lax.ppermute(value, ('seq', 'tp'), [(i, i ^ bits) for i in range(count)])  51.9 us
    pallas_call x45, Pallas kernels, run(): pl.pallas_call(body, name=kernel.__qualname__.split('.')[0], out_shape=ou...  44.9 us
    ppermute x53, waiting for transfers between devices, hop(): lax.ppermute(value, ('seq', 'tp'), [(i, i ^ bits) for i in range(count)])  40.9 us
    ppermute x10, starting transfers between devices, swap_dp(): return lax.ppermute(value, 'dp', [(0, 1), (1, 0)])  18.2 us
    ppermute x10, waiting for transfers between devices, swap_dp(): return lax.ppermute(value, 'dp', [(0, 1), (1, 0)])  13.5 us
    unnamed x14, local copies, waits for them, and re-layouts  4.1 us
  transfers between devices with their start and end apart: 63, of which 28 were waited for; matrix products, arithmetic and copies ran while one was open for 1% of the time, Pallas kernels for 19%

profile of v5, /device:TPU:0, one launch (start us, length us, event | category | flops | bytes accessed | tf_op | source)
XLA Modules:
  0.0 176.5 jit_solution(535145221147445508)
XLA Ops:
  0.8 1.0 copy-done.4
  2.3 4.1 %collective-permute-start = (f32[64,768]{1,0:T(8,128)S(1)}, f32[64,768]{1,0:T(8,128)S(1)}, u32[]{:S(2)}, u32[]{:S(2)}) collective-permute-start(f32[64,768]{1,0:T(8,128)S(1)} %get-tuple-element.126.refs_12_), channel_id=1, source_target_pairs={{0,8},{1,9},{2,10},{3,11},{4,12},{5,13},{6,14},{7,15},{8,0},{9,1},... | collective-permute-start | bytes 589832 | tf_op jit(solution)/shard_map/ppermute | solution.py:20
  7.2 1.5 collective-permute-start.2
  10.1 0.9 copy-done.5
  11.5 1.6 collective-permute-done.1.refs_3_.refs_4_
  13.1 1.5 copy-done.1
  15.6 1.5 collective-permute-start.6
  17.9 5.1 %collective-permute-start.5 = (bf16[128,768]{1,0:T(8,128)(2,1)S(1)}, bf16[128,768]{1,0:T(8,128)(2,1)S(1)}, u32[]{:S(2)}, u32[]{:S(2)}) collective-permute-start(bf16[128,768]{1,0:T(8,128)(2,1)S(1)} %get-tuple-element.130.refs_1_), channel_id=1, source_target_pairs={{0,6},{1,7},{2,4},{3,5},{4,2},{5,3},{6,0},{7,1},{8,14},{9,15},{10,... | collective-permute-start | bytes 589832 | tf_op jit(solution)/shard_map/ppermute | solution.py:20
  25.3 4.4 %collective-permute-done.6.refs_4_.refs_6_ = bf16[384,576]{1,0:T(8,128)(2,1)S(1)} collective-permute-done((bf16[384,576]{1,0:T(8,128)(2,1)S(1)}, bf16[384,576]{1,0:T(8,128)(2,1)S(1)}, u32[]{:S(2)}, u32[]{:S(2)}) %collective-permute-start.6) | collective-permute-done | bytes 442400 | tf_op jit(solution)/shard_map/ppermute | solution.py:24
  29.7 1.5 collective-permute-start.15
  32.3 1.4 mix_kernel.1
  33.9 2.2 %collective-permute-done.10.refs_6_ = bf16[192,768]{1,0:T(8,128)(2,1)S(1)} collective-permute-done((bf16[192,768]{1,0:T(8,128)(2,1)S(1)}, bf16[192,768]{1,0:T(8,128)(2,1)S(1)}, u32[]{:S(2)}, u32[]{:S(2)}) %collective-permute-start.10) | collective-permute-done | bytes 294944 | tf_op jit(solution)/shard_map/ppermute | solution.py:24
  36.0 1.6 collective-permute-start.9
  37.6 1.5 collective-permute-start.21
  39.1 4.6 %attend_kernel.1 = (f32[512,256]{1,0:T(8,128)S(1)}, bf16[128,192]{1,0:T(8,128)(2,1)S(1)}, bf16[128,192]{1,0:T(8,128)(2,1)S(1)}, bf16[128,192]{1,0:T(8,128)(2,1)S...) custom-call(s32[8]{0:T(128)S(1)} %stack.41.refs_0_, ...), custom_call_target="tpu_custom_call" | custom-call | tf_op jit(solution)/shard_map/attend_kernel/pallas_call | solution.py:93
  43.7 1.2 collective-permute-start.12
  44.9 1.6 collective-permute-start.13
  47.3 1.4 collective-permute-done.15.refs_12_.refs_10_
  49.5 2.2 %collective-permute-done.14.refs_4_ = bf16[128,192]{1,0:T(8,128)(2,1)S(1)} collective-permute-done((bf16[128,192]{1,0:T(8,128)(2,1)S(1)}, bf16[128,192]{1,0:T(8,128)(2,1)S(1)}, u32[]{:S(2)}, u32[]{:S(2)}) %collective-permute-start.14) | collective-permute-done | bytes 49184 | tf_op jit(solution)/shard_map/ppermute | solution.py:20
  51.7 1.2 mid_kernel.1
  53.4 5.3 %collective-permute-done.16.refs_2_ = bf16[128,768]{1,0:T(8,128)(2,1)S(1)} collective-permute-done((bf16[128,768]{1,0:T(8,128)(2,1)S(1)}, bf16[128,768]{1,0:T(8,128)(2,1)S(1)}, u32[]{:S(2)}, u32[]{:S(2)}) %collective-permute-start.16) | collective-permute-done | bytes 196640 | tf_op jit(solution)/shard_map/ppermute | solution.py:20
  60.7 2.9 %feed_kernel.1 = (bf16[128,768]{1,0:T(8,128)(2,1)S(1)}, bf16[128,768]{1,0:T(8,128)(2,1)S(1)}, bf16[128,768]{1,0:T(8,128)(2,1)S(1)}, bf16[128,768]{1,0:T(8,128)(2...) custom-call(s32[8]{0:T(128)S(1)} %stack.41.refs_0_, ...), custom_call_target="tpu_custom_call" | custom-call | tf_op jit(solution)/shard_map/feed_kernel/pallas_call | solution.py:93
  63.6 1.4 outer_kernel.2
  65.9 0.9 collective-permute-done.23.refs_1_
  66.9 1.5 collective-permute-start.24
  68.5 1.4 outer_kernel.3
  69.8 1.5 collective-permute-start.29
  71.4 2.6 %collective-permute-done.24.refs_2_ = bf16[128,768]{1,0:T(8,128)(2,1)S(1)} collective-permute-done((bf16[128,768]{1,0:T(8,128)(2,1)S(1)}, bf16[128,768]{1,0:T(8,128)(2,1)S(1)}, u32[]{:S(2)}, u32[]{:S(2)}) %collective-permute-start.24) | collective-permute-done | bytes 196640 | tf_op jit(solution)/shard_map/ppermute | solution.py:20
  74.8 1.5 collective-permute-start.25
  76.8 1.5 collective-permute-start.27
  78.4 2.8 %collective-permute-done.28.refs_2_ = bf16[384,768]{1,0:T(8,128)(2,1)S(1)} collective-permute-done((bf16[384,768]{1,0:T(8,128)(2,1)S(1)}, bf16[384,768]{1,0:T(8,128)(2,1)S(1)}, u32[]{:S(2)}, u32[]{:S(2)}) %collective-permute-start.28) | collective-permute-done | bytes 589856 | tf_op jit(solution)/shard_map/ppermute | solution.py:20
  81.8 1.3 proj_grad_kernel.1
  83.3 3.0 %back_kernel.3 = (bf16[512,128]{1,0:T(8,128)(2,1)S(1)}, f32[512,128]{1,0:T(8,128)S(1)}, bf16[512,128]{1,0:T(8,128)(2,1)S(1)}, f32[256,128]{1,0:T(8,128)S(1)}) custom-call(s32[8]{0:T(128)S(1)} %stack.41.refs_0_, bf16[3,512,256]{2,1,0:T(8,128)(2,1)S(1)} %get-tuple-element.140.refs_1_, bf16[512,384]{1,0:T(8,128)(2,1)S(1)} %get-tuple-element.137.refs_2_, ...), custom_call_target="tpu_custom_call" | custom-call | tf_op jit(solution)/shard_map/back_kernel/pallas_call | solution.py:93
  88.3 2.9 %back_kernel.4 = (bf16[512,128]{1,0:T(8,128)(2,1)S(1)}, f32[512,128]{1,0:T(8,128)S(1)}, bf16[512,128]{1,0:T(8,128)(2,1)S(1)}, f32[256,128]{1,0:T(8,128)S(1)}) custom-call(s32[8]{0:T(128)S(1)} %stack.41.refs_0_, bf16[3,512,256]{2,1,0:T(8,128)(2,1)S(1)} %get-tuple-element.140.refs_1_, bf16[512,384]{1,0:T(8,128)(2,1)S(1)} %get-tuple-element.137.refs_2_, ...), custom_call_target="tpu_custom_call" | custom-call | tf_op jit(solution)/shard_map/back_kernel/pallas_call | solution.py:93
  92.6 3.0 %back_kernel.5 = (bf16[512,128]{1,0:T(8,128)(2,1)S(1)}, f32[512,128]{1,0:T(8,128)S(1)}, bf16[512,128]{1,0:T(8,128)(2,1)S(1)}, f32[256,128]{1,0:T(8,128)S(1)}) custom-call(s32[8]{0:T(128)S(1)} %stack.41.refs_0_, bf16[3,512,256]{2,1,0:T(8,128)(2,1)S(1)} %get-tuple-element.140.refs_1_, bf16[512,384]{1,0:T(8,128)(2,1)S(1)} %get-tuple-element.137.refs_2_, ...), custom_call_target="tpu_custom_call" | custom-call | tf_op jit(solution)/shard_map/back_kernel/pallas_call | solution.py:93
  97.1 1.8 %qkv_grad_kernel.1 = (bf16[512,384]{1,0:T(8,128)(2,1)S(1)}, bf16[512,256]{1,0:T(8,128)(2,1)S(1)}, bf16[416,576]{1,0:T(8,128)(2,1)S(1)}, bf16[416,576]{1,0:T(8,128)(2,1)S(1)}) custom-call(s32[8]{0:T(128)S(1)} %stack.41.refs_0_, bf16[512,768]{1,0:T(8,128)(2,1)S(1)} %get-tuple-element.135.refs_1_, f32[512,128]{1,0:T(8,128)S(1)} %get-tuple-element.179.refs_2_, ...), custom_call_target="tpu_custom_call" | custom-call | tf_op jit(solution)/shard_map/qkv_grad_kernel/pallas_call | solution.py:93
  99.0 1.5 collective-permute-start.37
  101.4 1.2 collective-permute-start.36
  103.5 2.7 %collective-permute-start.42 = (bf16[96,768]{1,0:T(8,128)(2,1)S(1)}, bf16[96,768]{1,0:T(8,128)(2,1)S(1)}, u32[]{:S(2)}, u32[]{:S(2)}) collective-permute-start(bf16[96,768]{1,0:T(8,128)(2,1)S(1)} %get-tuple-element.199.refs_17_), channel_id=1, source_target_pairs={{0,8},{1,9},{2,10},{3,11},{4,12},{5,13},{6,14},{7,15},{8,0},{9,1},... | collective-permute-start | bytes 442376 | tf_op jit(solution)/shard_map/ppermute | solution.py:20
  107.1 1.3 collective-permute-done.37.refs_1_
  108.4 1.4 collective-permute-start.50
  109.9 1.2 collective-permute-done.36.refs_1_
  111.2 2.8 %collective-permute-start.38 = (bf16[224,576]{1,0:T(8,128)(2,1)S(1)}, bf16[224,576]{1,0:T(8,128)(2,1)S(1)}, u32[]{:S(2)}, u32[]{:S(2)}) collective-permute-start(bf16[224,576]{1,0:T(8,128)(2,1)S(1)} %add_kernel.9.refs_2_.refs_0_), channel_id=1, source_target_pairs={{0,8},{1,9},{2,10},{3,11},{4,12},{5,13},{6,14},{7,15},{8,0},{9,1},... | collective-permute-start | bytes 774152 | tf_op jit(solution)/shard_map/ppermute | solution.py:20
  114.0 7.6 %collective-permute-start.39 = (bf16[96,768]{1,0:T(8,128)(2,1)S(1)}, bf16[96,768]{1,0:T(8,128)(2,1)S(1)}, u32[]{:S(2)}, u32[]{:S(2)}) collective-permute-start(bf16[96,768]{1,0:T(8,128)(2,1)S(1)} %get-tuple-element.210.refs_2_), channel_id=1, source_target_pairs={{0,16},{16,0},{1,17},{17,1},{2,18},{18,2},{3,19},{19,3},{4,20},{20... | collective-permute-start | bytes 442376 | tf_op jit(solution)/shard_map/ppermute | solution.py:24
  122.5 2.3 %collective-permute-done.39.refs_1_ = bf16[96,768]{1,0:T(8,128)(2,1)S(1)} collective-permute-done((bf16[96,768]{1,0:T(8,128)(2,1)S(1)}, bf16[96,768]{1,0:T(8,128)(2,1)S(1)}, u32[]{:S(2)}, u32[]{:S(2)}) %collective-permute-start.39) | collective-permute-done | bytes 147488 | tf_op jit(solution)/shard_map/ppermute | solution.py:24
  124.8 1.3 collective-permute-start.56
  126.1 2.8 %collective-permute-start.54 = (bf16[96,768]{1,0:T(8,128)(2,1)S(1)}, bf16[96,768]{1,0:T(8,128)(2,1)S(1)}, u32[]{:S(2)}, u32[]{:S(2)}) collective-permute-start(bf16[96,768]{1,0:T(8,128)(2,1)S(1)} %add_kernel.10.refs_3_.refs_1_), channel_id=1, source_target_pairs={{0,8},{1,9},{2,10},{3,11},{4,12},{5,13},{6,14},{7,15},{8,0},{9,1},... | collective-permute-start | bytes 442376 | tf_op jit(solution)/shard_map/ppermute | solution.py:20
  128.9 2.2 %collective-permute-done.38.refs_1_ = bf16[224,576]{1,0:T(8,128)(2,1)S(1)} collective-permute-done((bf16[224,576]{1,0:T(8,128)(2,1)S(1)}, bf16[224,576]{1,0:T(8,128)(2,1)S(1)}, u32[]{:S(2)}, u32[]{:S(2)}) %collective-permute-start.38) | collective-permute-done | bytes 258080 | tf_op jit(solution)/shard_map/ppermute | solution.py:20
  131.4 4.5 %collective-permute-done.51.refs_1_ = bf16[192,384]{1,0:T(8,128)(2,1)S(1)} collective-permute-done((bf16[192,384]{1,0:T(8,128)(2,1)S(1)}, bf16[192,384]{1,0:T(8,128)(2,1)S(1)}, u32[]{:S(2)}, u32[]{:S(2)}) %collective-permute-start.51) | collective-permute-done | bytes 147488 | tf_op jit(solution)/shard_map/ppermute | solution.py:20
  135.9 1.2 collective-permute-start.53
  137.5 3.2 %collective-permute-start.52 = (bf16[128,768]{1,0:T(8,128)(2,1)S(1)}, bf16[128,768]{1,0:T(8,128)(2,1)S(1)}, u32[]{:S(2)}, u32[]{:S(2)}) collective-permute-start(bf16[128,768]{1,0:T(8,128)(2,1)S(1)} %tail_add_kernel.3.refs_2_), channel_id=1, source_target_pairs={{0,4},{1,5},{2,6},{3,7},{4,0},{5,1},{6,2},{7,3},{8,12},{9,13},{10,... | collective-permute-start | bytes 589832 | tf_op jit(solution)/shard_map/ppermute | solution.py:20
  140.7 1.0 collective-permute-start.43
  141.8 3.9 %collective-permute-done.55.refs_2_ = bf16[192,384]{1,0:T(8,128)(2,1)S(1)} collective-permute-done((bf16[192,384]{1,0:T(8,128)(2,1)S(1)}, bf16[192,384]{1,0:T(8,128)(2,1)S(1)}, u32[]{:S(2)}, u32[]{:S(2)}) %collective-permute-start.55) | collective-permute-done | bytes 147488 | tf_op jit(solution)/shard_map/ppermute | solution.py:20
  146.9 3.0 %collective-permute-start.60 = (bf16[192,768]{1,0:T(8,128)(2,1)S(1)}, bf16[192,768]{1,0:T(8,128)(2,1)S(1)}, u32[]{:S(2)}, u32[]{:S(2)}) collective-permute-start(bf16[192,768]{1,0:T(8,128)(2,1)S(1)} %join_kernel.4.refs_11_.refs_1_), channel_id=1, source_target_pairs={{0,4},{1,5},{2,6},{3,7},{4,0},{5,1},{6,2},{7,3},{8,12},{9,13},{10,... | collective-permute-start | bytes 884744 | tf_op jit(solution)/shard_map/ppermute | solution.py:20
  150.0 1.0 collective-permute-start.45
  151.0 4.4 %collective-permute-done.52.refs_2_ = bf16[128,768]{1,0:T(8,128)(2,1)S(1)} collective-permute-done((bf16[128,768]{1,0:T(8,128)(2,1)S(1)}, bf16[128,768]{1,0:T(8,128)(2,1)S(1)}, u32[]{:S(2)}, u32[]{:S(2)}) %collective-permute-start.52) | collective-permute-done | bytes 196640 | tf_op jit(solution)/shard_map/ppermute | solution.py:20
  156.2 1.1 collective-permute-start.57
  157.4 0.9 collective-permute-start.59
  158.3 2.5 %collective-permute-start.62 = (bf16[384,384]{1,0:T(8,128)(2,1)S(1)}, bf16[384,384]{1,0:T(8,128)(2,1)S(1)}, u32[]{:S(2)}, u32[]{:S(2)}) collective-permute-start(bf16[384,384]{1,0:T(8,128)(2,1)S(1)} %join_kernel.3.refs_3_.refs_15_), channel_id=1, source_target_pairs={{0,4},{1,5},{2,6},{3,7},{4,0},{5,1},{6,2},{7,3},{8,12},{9,13},{10,... | collective-permute-start | bytes 884744 | tf_op jit(solution)/shard_map/ppermute | solution.py:20
  160.8 1.6 vector_out_kernel.1
  163.1 1.6 early_kernel.1
  166.0 2.8 %collective-permute-done.57.refs_11_ = bf16[128,768]{1,0:T(8,128)(2,1)S(1)} collective-permute-done((bf16[128,768]{1,0:T(8,128)(2,1)S(1)}, bf16[128,768]{1,0:T(8,128)(2,1)S(1)}, u32[]{:S(2)}, u32[]{:S(2)}) %collective-permute-start.57) | collective-permute-done | bytes 196640 | tf_op jit(solution)/shard_map/ppermute | solution.py:20
  168.8 3.4 %collective-permute-done.62.refs_16_ = bf16[384,384]{1,0:T(8,128)(2,1)S(1)} collective-permute-done((bf16[384,384]{1,0:T(8,128)(2,1)S(1)}, bf16[384,384]{1,0:T(8,128)(2,1)S(1)}, u32[]{:S(2)}, u32[]{:S(2)}) %collective-permute-start.62) | collective-permute-done | bytes 294944 | tf_op jit(solution)/shard_map/ppermute | solution.py:20
  172.2 4.1 %last_kernel.1 = (f32[8,128]{1,0:T(8,128)}, f32[2,64,768]{2,1,0:T(8,128)}, f32[2,64,768]{2,1,0:T(8,128)}, f32[384,2304]{1,0:T(8,128)}, f32[384,768]{1,0:T(8,128)}, /*index=5*/f32[768,384]{1,0:T(8,128)}) custom-call(s32[8]{0:T(128)S(1)} %stack.41.refs_0_, bf16[224,576]{1,0:T(8,128)(2,1)S(1)} %add_kernel.12.refs_2_.refs_1_, ...), custom_call_target="tpu_custom_call" | custom-call | tf_op jit(solution)/shard_map/last_kernel/pallas_call | solution.py:93
  (125 shorter events, 28.9 us)
Async XLA Ops:
  2.3 13.2 %collective-permute-start = (f32[64,768]{1,0:T(8,128)S(1)}, f32[64,768]{1,0:T(8,128)S(1)}, u32[]{:S(2)}, u32[]{:S(2)}) collective-permute-start(f32[64,768]{1,0:T(8,128)S(1)} %get-tuple-element.126.refs_12_), channel_id=1, source_target_pairs={{0,8},{1,9},{2,10},{3,11},{4,12},{5,13},{6,14},{7,15},{8,0},{9,1},... | collective-permute-start | bytes 589832 | tf_op jit(solution)/shard_map/ppermute | solution.py:20
  7.2 6.0 %collective-permute-start.2 = (bf16[2,32,63]{2,1,0:T(8,128)(2,1)S(1)}, bf16[2,32,63]{2,1,0:T(8,128)(2,1)S(1)}, u32[]{:S(2)}, u32[]{:S(2)}) collective-permute-start(bf16[2,32,63]{2,1,0:T(8,128)(2,1)S(1)} %pad_maximum_fusion.refs_1_), channel_id=1, source_target_pairs={{0,16},{16,0},{1,17},{17,1},{2,18},{18,2},{3,19},{19,3},{4,20},{20... | collective-permute-start | bytes 24200 | tf_op jit(solution)/shard_map/ppermute | solution.py:24
  9.5 3.7 %collective-permute-start.1 = (bf16[4,384]{1,0:T(4,128)(2,1)S(1)}, bf16[4,384]{1,0:T(4,128)(2,1)S(1)}, u32[]{:S(2)}, u32[]{:S(2)}) collective-permute-start(bf16[4,384]{1,0:T(4,128)(2,1)S(1)} %reshape.27.refs_3_), channel_id=1, source_target_pairs={{0,16},{16,0},{1,17},{17,1},{2,18},{18,2},{3,19},{19,3},{4,20},{20... | collective-permute-start | bytes 9224 | tf_op jit(solution)/shard_map/ppermute | solution.py:24
  15.6 14.2 %collective-permute-start.6 = (bf16[384,576]{1,0:T(8,128)(2,1)S(1)}, bf16[384,576]{1,0:T(8,128)(2,1)S(1)}, u32[]{:S(2)}, u32[]{:S(2)}) collective-permute-start(bf16[384,576]{1,0:T(8,128)(2,1)S(1)} %pack_kernel.1.refs_5_), channel_id=1, source_target_pairs={{0,16},{16,0},{1,17},{17,1},{2,18},{18,2},{3,19},{19,3},{4,20},{20... | collective-permute-start | bytes 1327112 | tf_op jit(solution)/shard_map/ppermute | solution.py:24
  17.1 12.6 %copy-start.2 = (bf16[384,768]{1,0:T(8,128)(2,1)S(1)}, bf16[384,768]{1,0:T(8,128)(2,1)}, u32[]{:S(2)}) copy-start(bf16[384,768]{1,0:T(8,128)(2,1)} %refs_9_) | copy-start | bytes 1769476
  17.1 7.3 %collective-permute-start.7 = (bf16[64,768]{1,0:T(8,128)(2,1)S(1)}, bf16[64,768]{1,0:T(8,128)(2,1)S(1)}, u32[]{:S(2)}, u32[]{:S(2)}) collective-permute-start(bf16[64,768]{1,0:T(8,128)(2,1)S(1)} %get-tuple-element.132), channel_id=1, source_target_pairs={{0,8},{1,9},{2,10},{3,11},{4,12},{5,13},{6,14},{7,15},{8,0},{9,1},... | collective-permute-start | bytes 294920 | tf_op jit(solution)/shard_map/ppermute | solution.py:20
  17.9 14.1 %collective-permute-start.5 = (bf16[128,768]{1,0:T(8,128)(2,1)S(1)}, bf16[128,768]{1,0:T(8,128)(2,1)S(1)}, u32[]{:S(2)}, u32[]{:S(2)}) collective-permute-start(bf16[128,768]{1,0:T(8,128)(2,1)S(1)} %get-tuple-element.130.refs_1_), channel_id=1, source_target_pairs={{0,6},{1,7},{2,4},{3,5},{4,2},{5,3},{6,0},{7,1},{8,14},{9,15},{10,... | collective-permute-start | bytes 589832 | tf_op jit(solution)/shard_map/ppermute | solution.py:20
  23.0 9.0 %collective-permute-start.4 = (bf16[128,768]{1,0:T(8,128)(2,1)S(1)}, bf16[128,768]{1,0:T(8,128)(2,1)S(1)}, u32[]{:S(2)}, u32[]{:S(2)}) collective-permute-start(bf16[128,768]{1,0:T(8,128)(2,1)S(1)} %get-tuple-element.130.refs_1_), channel_id=1, source_target_pairs={{0,4},{1,5},{2,6},{3,7},{4,0},{5,1},{6,2},{7,3},{8,12},{9,13},{10,... | collective-permute-start | bytes 589832 | tf_op jit(solution)/shard_map/ppermute | solution.py:20
  23.0 9.4 %collective-permute-start.3 = (bf16[128,768]{1,0:T(8,128)(2,1)S(1)}, bf16[128,768]{1,0:T(8,128)(2,1)S(1)}, u32[]{:S(2)}, u32[]{:S(2)}) collective-permute-start(bf16[128,768]{1,0:T(8,128)(2,1)S(1)} %get-tuple-element.130.refs_1_), channel_id=1, source_target_pairs={{0,2},{1,3},{2,0},{3,1},{4,6},{5,7},{6,4},{7,5},{8,10},{9,11},{10,... | collective-permute-start | bytes 589832 | tf_op jit(solution)/shard_map/ppermute | solution.py:20
  25.1 11.0 %collective-permute-start.10 = (bf16[192,768]{1,0:T(8,128)(2,1)S(1)}, bf16[192,768]{1,0:T(8,128)(2,1)S(1)}, u32[]{:S(2)}, u32[]{:S(2)}) collective-permute-start(bf16[192,768]{1,0:T(8,128)(2,1)S(1)} %rows_kernel.1.refs_3_), channel_id=1, source_target_pairs={{0,16},{16,0},{1,17},{17,1},{2,18},{18,2},{3,19},{19,3},{4,20},{20... | collective-permute-start | bytes 884744 | tf_op jit(solution)/shard_map/ppermute | solution.py:24
  29.7 19.0 %collective-permute-start.15 = (bf16[384,768]{1,0:T(8,128)(2,1)S(1)}, bf16[384,768]{1,0:T(8,128)(2,1)S(1)}, u32[]{:S(2)}, u32[]{:S(2)}) collective-permute-start(bf16[384,768]{1,0:T(8,128)(2,1)S(1)} %copy-done.2), channel_id=1, source_target_pairs={{0,16},{16,0},{1,17},{17,1},{2,18},{18,2},{3,19},{19,3},{4,20},{20... | collective-permute-start | bytes 1769480 | tf_op jit(solution)/shard_map/ppermute | solution.py:24
  33.8 5.3 %collective-permute-start.8 = (bf16[512,384]{1,0:T(8,128)(2,1)S(1)}, bf16[512,384]{1,0:T(8,128)(2,1)S(1)}, u32[]{:S(2)}, u32[]{:S(2)}) collective-permute-start(bf16[512,384]{1,0:T(8,128)(2,1)S(1)} %get-tuple-element.137.refs_2_), channel_id=1, source_target_pairs={{0,1},{1,0},{2,3},{3,2},{4,5},{5,4},{6,7},{7,6},{8,9},{9,8},{10,11... | collective-permute-start | bytes 1179656 | tf_op jit(solution)/shard_map/ppermute | solution.py:20
  36.0 7.7 %collective-permute-start.11 = (bf16[192,768]{1,0:T(8,128)(2,1)S(1)}, bf16[192,768]{1,0:T(8,128)(2,1)S(1)}, u32[]{:S(2)}, u32[]{:S(2)}) collective-permute-start(bf16[192,768]{1,0:T(8,128)(2,1)S(1)} %collective-permute-done.10.refs_6_), channel_id=1, source_target_pairs={{0,1},{1,0},{2,3},{3,2},{4,5},{5,4},{6,7},{7,6},{8,9},{9,8},{10,11... | collective-permute-start | bytes 884744 | tf_op jit(solution)/shard_map/ppermute | solution.py:20
  36.0 7.7 %collective-permute-start.9 = (bf16[128,768]{1,0:T(8,128)(2,1)S(1)}, bf16[128,768]{1,0:T(8,128)(2,1)S(1)}, u32[]{:S(2)}, u32[]{:S(2)}) collective-permute-start(bf16[128,768]{1,0:T(8,128)(2,1)S(1)} %stack_kernel.1.refs_2_.refs_5_), channel_id=1, source_target_pairs={{0,2},{1,3},{2,0},{3,1},{4,6},{5,7},{6,4},{7,5},{8,10},{9,11},{10,... | collective-permute-start | bytes 589832 | tf_op jit(solution)/shard_map/ppermute | solution.py:20
  37.6 21.9 %collective-permute-start.21 = (bf16[768,384]{1,0:T(8,128)(2,1)S(1)}, bf16[768,384]{1,0:T(8,128)(2,1)S(1)}, u32[]{:S(2)}, u32[]{:S(2)}) collective-permute-start(bf16[768,384]{1,0:T(8,128)(2,1)S(1)} %copy-done.3), channel_id=1, source_target_pairs={{0,16},{16,0},{1,17},{17,1},{2,18},{18,2},{3,19},{19,3},{4,20},{20... | collective-permute-start | bytes 1769480 | tf_op jit(solution)/shard_map/ppermute | solution.py:24
  43.7 5.0 %collective-permute-start.12 = (bf16[128,192]{1,0:T(8,128)(2,1)S(1)}, bf16[128,192]{1,0:T(8,128)(2,1)S(1)}, u32[]{:S(2)}, u32[]{:S(2)}) collective-permute-start(bf16[128,192]{1,0:T(8,128)(2,1)S(1)} %get-tuple-element.149), channel_id=1, source_target_pairs={{0,2},{1,3},{2,0},{3,1},{4,6},{5,7},{6,4},{7,5},{8,10},{9,11},{10,... | collective-permute-start | bytes 147464 | tf_op jit(solution)/shard_map/ppermute | solution.py:20
  44.9 4.5 %collective-permute-start.13 = (bf16[128,192]{1,0:T(8,128)(2,1)S(1)}, bf16[128,192]{1,0:T(8,128)(2,1)S(1)}, u32[]{:S(2)}, u32[]{:S(2)}) collective-permute-start(bf16[128,192]{1,0:T(8,128)(2,1)S(1)} %get-tuple-element.150), channel_id=1, source_target_pairs={{0,4},{1,5},{2,6},{3,7},{4,0},{5,1},{6,2},{7,3},{8,12},{9,13},{10,... | collective-permute-start | bytes 147464 | tf_op jit(solution)/shard_map/ppermute | solution.py:20
  46.5 5.2 %collective-permute-start.14 = (bf16[128,192]{1,0:T(8,128)(2,1)S(1)}, bf16[128,192]{1,0:T(8,128)(2,1)S(1)}, u32[]{:S(2)}, u32[]{:S(2)}) collective-permute-start(bf16[128,192]{1,0:T(8,128)(2,1)S(1)} %get-tuple-element.151), channel_id=1, source_target_pairs={{0,6},{1,7},{2,4},{3,5},{4,2},{5,3},{6,0},{7,1},{8,14},{9,15},{10,... | collective-permute-start | bytes 147464 | tf_op jit(solution)/shard_map/ppermute | solution.py:20
  52.9 5.7 %collective-permute-start.16 = (bf16[128,768]{1,0:T(8,128)(2,1)S(1)}, bf16[128,768]{1,0:T(8,128)(2,1)S(1)}, u32[]{:S(2)}, u32[]{:S(2)}) collective-permute-start(bf16[128,768]{1,0:T(8,128)(2,1)S(1)} %get-tuple-element.153.refs_1_), channel_id=1, source_target_pairs={{0,2},{1,3},{2,0},{3,1},{4,6},{5,7},{6,4},{7,5},{8,10},{9,11},{10,... | collective-permute-start | bytes 589832 | tf_op jit(solution)/shard_map/ppermute | solution.py:20
  53.3 6.2 %collective-permute-start.17 = (bf16[128,768]{1,0:T(8,128)(2,1)S(1)}, bf16[128,768]{1,0:T(8,128)(2,1)S(1)}, u32[]{:S(2)}, u32[]{:S(2)}) collective-permute-start(bf16[128,768]{1,0:T(8,128)(2,1)S(1)} %get-tuple-element.153.refs_1_), channel_id=1, source_target_pairs={{0,1},{1,0},{2,3},{3,2},{4,5},{5,4},{6,7},{7,6},{8,9},{9,8},{10,11... | collective-permute-start | bytes 589832 | tf_op jit(solution)/shard_map/ppermute | solution.py:20
  58.6 1.4 collective-permute-start.19
  58.7 1.7 collective-permute-start.20
  59.2 1.5 collective-permute-start.18
  64.9 16.2 %collective-permute-start.28 = (bf16[384,768]{1,0:T(8,128)(2,1)S(1)}, bf16[384,768]{1,0:T(8,128)(2,1)S(1)}, u32[]{:S(2)}, u32[]{:S(2)}) collective-permute-start(bf16[384,768]{1,0:T(8,128)(2,1)S(1)} %get-tuple-element.164.refs_2_), channel_id=1, source_target_pairs={{0,4},{1,5},{2,6},{3,7},{4,0},{5,1},{6,2},{7,3},{8,12},{9,13},{10,... | collective-permute-start | bytes 1769480 | tf_op jit(solution)/shard_map/ppermute | solution.py:20
  65.4 1.4 collective-permute-start.23
  65.4 5.9 %collective-permute-start.22 = (bf16[128,768]{1,0:T(8,128)(2,1)S(1)}, bf16[128,768]{1,0:T(8,128)(2,1)S(1)}, u32[]{:S(2)}, u32[]{:S(2)}) collective-permute-start(bf16[128,768]{1,0:T(8,128)(2,1)S(1)} %get-tuple-element.159), channel_id=1, source_target_pairs={{0,1},{1,0},{2,3},{3,2},{4,5},{5,4},{6,7},{7,6},{8,9},{9,8},{10,11... | collective-permute-start | bytes 589832 | tf_op jit(solution)/shard_map/ppermute | solution.py:20
  66.9 7.0 %collective-permute-start.24 = (bf16[128,768]{1,0:T(8,128)(2,1)S(1)}, bf16[128,768]{1,0:T(8,128)(2,1)S(1)}, u32[]{:S(2)}, u32[]{:S(2)}) collective-permute-start(bf16[128,768]{1,0:T(8,128)(2,1)S(1)} %add_kernel.8.refs_3_), channel_id=1, source_target_pairs={{0,2},{1,3},{2,0},{3,1},{4,6},{5,7},{6,4},{7,5},{8,10},{9,11},{10,... | collective-permute-start | bytes 589832 | tf_op jit(solution)/shard_map/ppermute | solution.py:20
  69.8 17.0 %collective-permute-start.29 = (bf16[384,768]{1,0:T(8,128)(2,1)S(1)}, bf16[384,768]{1,0:T(8,128)(2,1)S(1)}, u32[]{:S(2)}, u32[]{:S(2)}) collective-permute-start(bf16[384,768]{1,0:T(8,128)(2,1)S(1)} %get-tuple-element.168.refs_7_), channel_id=1, source_target_pairs={{0,16},{16,0},{1,17},{17,1},{2,18},{18,2},{3,19},{19,3},{4,20},{20... | collective-permute-start | bytes 1769480 | tf_op jit(solution)/shard_map/ppermute | solution.py:24
  74.8 8.4 %collective-permute-start.25 = (bf16[128,192]{1,0:T(8,128)(2,1)S(1)}, bf16[128,192]{1,0:T(8,128)(2,1)S(1)}, u32[]{:S(2)}, u32[]{:S(2)}) collective-permute-start(bf16[128,192]{1,0:T(8,128)(2,1)S(1)} %get-tuple-element.170), channel_id=1, source_target_pairs={{0,2},{1,3},{2,0},{3,1},{4,6},{5,7},{6,4},{7,5},{8,10},{9,11},{10,... | collective-permute-start | bytes 147464 | tf_op jit(solution)/shard_map/ppermute | solution.py:20
  76.4 6.8 %collective-permute-start.26 = (bf16[128,192]{1,0:T(8,128)(2,1)S(1)}, bf16[128,192]{1,0:T(8,128)(2,1)S(1)}, u32[]{:S(2)}, u32[]{:S(2)}) collective-permute-start(bf16[128,192]{1,0:T(8,128)(2,1)S(1)} %get-tuple-element.171), channel_id=1, source_target_pairs={{0,4},{1,5},{2,6},{3,7},{4,0},{5,1},{6,2},{7,3},{8,12},{9,13},{10,... | collective-permute-start | bytes 147464 | tf_op jit(solution)/shard_map/ppermute | solution.py:20
  76.8 6.4 %collective-permute-start.27 = (bf16[128,192]{1,0:T(8,128)(2,1)S(1)}, bf16[128,192]{1,0:T(8,128)(2,1)S(1)}, u32[]{:S(2)}, u32[]{:S(2)}) collective-permute-start(bf16[128,192]{1,0:T(8,128)(2,1)S(1)} %get-tuple-element.172), channel_id=1, source_target_pairs={{0,6},{1,7},{2,4},{3,5},{4,2},{5,3},{6,0},{7,1},{8,14},{9,15},{10,... | collective-permute-start | bytes 147464 | tf_op jit(solution)/shard_map/ppermute | solution.py:20
  83.2 8.1 %collective-permute-start.31 = (bf16[384,768]{1,0:T(8,128)(2,1)S(1)}, bf16[384,768]{1,0:T(8,128)(2,1)S(1)}, u32[]{:S(2)}, u32[]{:S(2)}) collective-permute-start(bf16[384,768]{1,0:T(8,128)(2,1)S(1)} %get-tuple-element.186.refs_12_), channel_id=1, source_target_pairs={{0,1},{1,0},{2,3},{3,2},{4,5},{5,4},{6,7},{7,6},{8,9},{9,8},{10,11... | collective-permute-start | bytes 1769480 | tf_op jit(solution)/shard_map/ppermute | solution.py:20
  86.3 2.1 %collective-permute-start.30 = (bf16[512,128]{1,0:T(8,128)(2,1)S(1)}, bf16[512,128]{1,0:T(8,128)(2,1)S(1)}, u32[]{:S(2)}, u32[]{:S(2)}) collective-permute-start(bf16[512,128]{1,0:T(8,128)(2,1)S(1)} %get-tuple-element.183), channel_id=1, source_target_pairs={{0,1},{1,0},{2,3},{3,2},{4,5},{5,4},{6,7},{7,6},{8,9},{9,8},{10,11... | collective-permute-start | bytes 393224 | tf_op jit(solution)/shard_map/ppermute | solution.py:20
  87.5 9.0 %collective-permute-start.34 = (bf16[192,768]{1,0:T(8,128)(2,1)S(1)}, bf16[192,768]{1,0:T(8,128)(2,1)S(1)}, u32[]{:S(2)}, u32[]{:S(2)}) collective-permute-start(bf16[192,768]{1,0:T(8,128)(2,1)S(1)} %get-tuple-element.182.refs_12_), channel_id=1, source_target_pairs={{0,4},{1,5},{2,6},{3,7},{4,0},{5,1},{6,2},{7,3},{8,12},{9,13},{10,... | collective-permute-start | bytes 884744 | tf_op jit(solution)/shard_map/ppermute | solution.py:20
  91.2 1.4 collective-permute-start.32
  95.6 1.5 collective-permute-start.33
  98.9 2.4 %collective-permute-start.35 = (bf16[416,576]{1,0:T(8,128)(2,1)S(1)}, bf16[416,576]{1,0:T(8,128)(2,1)S(1)}, u32[]{:S(2)}, u32[]{:S(2)}) collective-permute-start(bf16[416,576]{1,0:T(8,128)(2,1)S(1)} %get-tuple-element.201), channel_id=1, source_target_pairs={{0,1},{1,0},{2,3},{3,2},{4,5},{5,4},{6,7},{7,6},{8,9},{9,8},{10,11... | collective-permute-start | bytes 1437704 | tf_op jit(solution)/shard_map/ppermute | solution.py:20
  99.0 9.4 %collective-permute-start.37 = (bf16[192,768]{1,0:T(8,128)(2,1)S(1)}, bf16[192,768]{1,0:T(8,128)(2,1)S(1)}, u32[]{:S(2)}, u32[]{:S(2)}) collective-permute-start(bf16[192,768]{1,0:T(8,128)(2,1)S(1)} %get-tuple-element.188.refs_12_), channel_id=1, source_target_pairs={{0,2},{1,3},{2,0},{3,1},{4,6},{5,7},{6,4},{7,5},{8,10},{9,11},{10,... | collective-permute-start | bytes 884744 | tf_op jit(solution)/shard_map/ppermute | solution.py:20
  101.4 9.7 %collective-permute-start.36 = (bf16[224,576]{1,0:T(8,128)(2,1)S(1)}, bf16[224,576]{1,0:T(8,128)(2,1)S(1)}, u32[]{:S(2)}, u32[]{:S(2)}) collective-permute-start(bf16[224,576]{1,0:T(8,128)(2,1)S(1)} %get-tuple-element.206.refs_3_), channel_id=1, source_target_pairs={{0,16},{16,0},{1,17},{17,1},{2,18},{18,2},{3,19},{19,3},{4,20},{20... | collective-permute-start | bytes 774152 | tf_op jit(solution)/shard_map/ppermute | solution.py:24
  102.6 19.7 %collective-permute-start.40 = (bf16[256,768]{1,0:T(8,128)(2,1)S(1)}, bf16[256,768]{1,0:T(8,128)(2,1)S(1)}, u32[]{:S(2)}, u32[]{:S(2)}) collective-permute-start(bf16[256,768]{1,0:T(8,128)(2,1)S(1)} %get-tuple-element.214), channel_id=1, source_target_pairs={{0,1},{1,0},{2,3},{3,2},{4,5},{5,4},{6,7},{7,6},{8,9},{9,8},{10,11... | collective-permute-start | bytes 1179656 | tf_op jit(solution)/shard_map/ppermute | solution.py:20
  102.6 19.0 %collective-permute-start.41 = (bf16[384,384]{1,0:T(8,128)(2,1)S(1)}, bf16[384,384]{1,0:T(8,128)(2,1)S(1)}, u32[]{:S(2)}, u32[]{:S(2)}) collective-permute-start(bf16[384,384]{1,0:T(8,128)(2,1)S(1)} %get-tuple-element.177.refs_6_), channel_id=1, source_target_pairs={{0,16},{16,0},{1,17},{17,1},{2,18},{18,2},{3,19},{19,3},{4,20},{20... | collective-permute-start | bytes 884744 | tf_op jit(solution)/shard_map/ppermute | solution.py:24
  103.5 10.5 %collective-permute-start.42 = (bf16[96,768]{1,0:T(8,128)(2,1)S(1)}, bf16[96,768]{1,0:T(8,128)(2,1)S(1)}, u32[]{:S(2)}, u32[]{:S(2)}) collective-permute-start(bf16[96,768]{1,0:T(8,128)(2,1)S(1)} %get-tuple-element.199.refs_17_), channel_id=1, source_target_pairs={{0,8},{1,9},{2,10},{3,11},{4,12},{5,13},{6,14},{7,15},{8,0},{9,1},... | collective-permute-start | bytes 442376 | tf_op jit(solution)/shard_map/ppermute | solution.py:20
  108.4 28.7 %collective-permute-start.50 = (bf16[256,768]{1,0:T(8,128)(2,1)S(1)}, bf16[256,768]{1,0:T(8,128)(2,1)S(1)}, u32[]{:S(2)}, u32[]{:S(2)}) collective-permute-start(bf16[256,768]{1,0:T(8,128)(2,1)S(1)} %get-tuple-element.218), channel_id=1, source_target_pairs={{0,2},{1,3},{2,0},{3,1},{4,6},{5,7},{6,4},{7,5},{8,10},{9,11},{10,... | collective-permute-start | bytes 1179656 | tf_op jit(solution)/shard_map/ppermute | solution.py:20
  111.2 19.9 %collective-permute-start.38 = (bf16[224,576]{1,0:T(8,128)(2,1)S(1)}, bf16[224,576]{1,0:T(8,128)(2,1)S(1)}, u32[]{:S(2)}, u32[]{:S(2)}) collective-permute-start(bf16[224,576]{1,0:T(8,128)(2,1)S(1)} %add_kernel.9.refs_2_.refs_0_), channel_id=1, source_target_pairs={{0,8},{1,9},{2,10},{3,11},{4,12},{5,13},{6,14},{7,15},{8,0},{9,1},... | collective-permute-start | bytes 774152 | tf_op jit(solution)/shard_map/ppermute | solution.py:20
  114.0 10.7 %collective-permute-start.39 = (bf16[96,768]{1,0:T(8,128)(2,1)S(1)}, bf16[96,768]{1,0:T(8,128)(2,1)S(1)}, u32[]{:S(2)}, u32[]{:S(2)}) collective-permute-start(bf16[96,768]{1,0:T(8,128)(2,1)S(1)} %get-tuple-element.210.refs_2_), channel_id=1, source_target_pairs={{0,16},{16,0},{1,17},{17,1},{2,18},{18,2},{3,19},{19,3},{4,20},{20... | collective-permute-start | bytes 442376 | tf_op jit(solution)/shard_map/ppermute | solution.py:24
  122.3 13.6 %collective-permute-start.51 = (bf16[192,384]{1,0:T(8,128)(2,1)S(1)}, bf16[192,384]{1,0:T(8,128)(2,1)S(1)}, u32[]{:S(2)}, u32[]{:S(2)}) collective-permute-start(bf16[192,384]{1,0:T(8,128)(2,1)S(1)} %get-tuple-element.217.refs_2_), channel_id=1, source_target_pairs={{0,8},{1,9},{2,10},{3,11},{4,12},{5,13},{6,14},{7,15},{8,0},{9,1},... | collective-permute-start | bytes 442376 | tf_op jit(solution)/shard_map/ppermute | solution.py:20
  124.8 12.7 %collective-permute-start.56 = (bf16[96,768]{1,0:T(8,128)(2,1)S(1)}, bf16[96,768]{1,0:T(8,128)(2,1)S(1)}, u32[]{:S(2)}, u32[]{:S(2)}) collective-permute-start(bf16[96,768]{1,0:T(8,128)(2,1)S(1)} %add_kernel.11.refs_2_.refs_0_), channel_id=1, source_target_pairs={{0,4},{1,5},{2,6},{3,7},{4,0},{5,1},{6,2},{7,3},{8,12},{9,13},{10,... | collective-permute-start | bytes 442376 | tf_op jit(solution)/shard_map/ppermute | solution.py:20
  126.1 14.6 %collective-permute-start.54 = (bf16[96,768]{1,0:T(8,128)(2,1)S(1)}, bf16[96,768]{1,0:T(8,128)(2,1)S(1)}, u32[]{:S(2)}, u32[]{:S(2)}) collective-permute-start(bf16[96,768]{1,0:T(8,128)(2,1)S(1)} %add_kernel.10.refs_3_.refs_1_), channel_id=1, source_target_pairs={{0,8},{1,9},{2,10},{3,11},{4,12},{5,13},{6,14},{7,15},{8,0},{9,1},... | collective-permute-start | bytes 442376 | tf_op jit(solution)/shard_map/ppermute | solution.py:20
  131.2 18.8 %collective-permute-start.44 = (bf16[224,576]{1,0:T(8,128)(2,1)S(1)}, bf16[224,576]{1,0:T(8,128)(2,1)S(1)}, u32[]{:S(2)}, u32[]{:S(2)}) collective-permute-start(bf16[224,576]{1,0:T(8,128)(2,1)S(1)} %add_kernel.12.refs_2_.refs_1_), channel_id=1, source_target_pairs={{0,4},{1,5},{2,6},{3,7},{4,0},{5,1},{6,2},{7,3},{8,12},{9,13},{10,... | collective-permute-start | bytes 774152 | tf_op jit(solution)/shard_map/ppermute | solution.py:20
  135.9 11.0 %collective-permute-start.53 = (bf16[128,768]{1,0:T(8,128)(2,1)S(1)}, bf16[128,768]{1,0:T(8,128)(2,1)S(1)}, u32[]{:S(2)}, u32[]{:S(2)}) collective-permute-start(bf16[128,768]{1,0:T(8,128)(2,1)S(1)} %tail_add_kernel.2.refs_2_), channel_id=1, source_target_pairs={{0,2},{1,3},{2,0},{3,1},{4,6},{5,7},{6,4},{7,5},{8,10},{9,11},{10,... | collective-permute-start | bytes 589832 | tf_op jit(solution)/shard_map/ppermute | solution.py:20
  137.1 8.7 %collective-permute-start.55 = (bf16[192,384]{1,0:T(8,128)(2,1)S(1)}, bf16[192,384]{1,0:T(8,128)(2,1)S(1)}, u32[]{:S(2)}, u32[]{:S(2)}) collective-permute-start(bf16[192,384]{1,0:T(8,128)(2,1)S(1)} %add_kernel.13.refs_2_.refs_1_), channel_id=1, source_target_pairs={{0,8},{1,9},{2,10},{3,11},{4,12},{5,13},{6,14},{7,15},{8,0},{9,1},... | collective-permute-start | bytes 442376 | tf_op jit(solution)/shard_map/ppermute | solution.py:20
  137.5 17.9 %collective-permute-start.52 = (bf16[128,768]{1,0:T(8,128)(2,1)S(1)}, bf16[128,768]{1,0:T(8,128)(2,1)S(1)}, u32[]{:S(2)}, u32[]{:S(2)}) collective-permute-start(bf16[128,768]{1,0:T(8,128)(2,1)S(1)} %tail_add_kernel.3.refs_2_), channel_id=1, source_target_pairs={{0,4},{1,5},{2,6},{3,7},{4,0},{5,1},{6,2},{7,3},{8,12},{9,13},{10,... | collective-permute-start | bytes 589832 | tf_op jit(solution)/shard_map/ppermute | solution.py:20
  140.7 16.6 %collective-permute-start.43 = (bf16[224,576]{1,0:T(8,128)(2,1)S(1)}, bf16[224,576]{1,0:T(8,128)(2,1)S(1)}, u32[]{:S(2)}, u32[]{:S(2)}) collective-permute-start(bf16[224,576]{1,0:T(8,128)(2,1)S(1)} %add_kernel.12.refs_2_.refs_1_), channel_id=1, source_target_pairs={{0,2},{1,3},{2,0},{3,1},{4,6},{5,7},{6,4},{7,5},{8,10},{9,11},{10,... | collective-permute-start | bytes 774152 | tf_op jit(solution)/shard_map/ppermute | solution.py:20
  145.8 10.4 %collective-permute-start.58 = (bf16[96,768]{1,0:T(8,128)(2,1)S(1)}, bf16[96,768]{1,0:T(8,128)(2,1)S(1)}, u32[]{:S(2)}, u32[]{:S(2)}) collective-permute-start(bf16[96,768]{1,0:T(8,128)(2,1)S(1)} %add_kernel.14.refs_3_.refs_0_), channel_id=1, source_target_pairs={{0,8},{1,9},{2,10},{3,11},{4,12},{5,13},{6,14},{7,15},{8,0},{9,1},... | collective-permute-start | bytes 442376 | tf_op jit(solution)/shard_map/ppermute | solution.py:20
  146.9 15.5 %collective-permute-start.60 = (bf16[192,768]{1,0:T(8,128)(2,1)S(1)}, bf16[192,768]{1,0:T(8,128)(2,1)S(1)}, u32[]{:S(2)}, u32[]{:S(2)}) collective-permute-start(bf16[192,768]{1,0:T(8,128)(2,1)S(1)} %join_kernel.4.refs_11_.refs_1_), channel_id=1, source_target_pairs={{0,4},{1,5},{2,6},{3,7},{4,0},{5,1},{6,2},{7,3},{8,12},{9,13},{10,... | collective-permute-start | bytes 884744 | tf_op jit(solution)/shard_map/ppermute | solution.py:20
  150.0 8.4 %collective-permute-start.45 = (bf16[224,576]{1,0:T(8,128)(2,1)S(1)}, bf16[224,576]{1,0:T(8,128)(2,1)S(1)}, u32[]{:S(2)}, u32[]{:S(2)}) collective-permute-start(bf16[224,576]{1,0:T(8,128)(2,1)S(1)} %collective-permute-done.44.refs_3_), channel_id=1, source_target_pairs={{0,2},{1,3},{2,0},{3,1},{4,6},{5,7},{6,4},{7,5},{8,10},{9,11},{10,... | collective-permute-start | bytes 774152 | tf_op jit(solution)/shard_map/ppermute | solution.py:20
  155.4 10.5 %collective-permute-start.46 = (bf16[224,576]{1,0:T(8,128)(2,1)S(1)}, bf16[224,576]{1,0:T(8,128)(2,1)S(1)}, u32[]{:S(2)}, u32[]{:S(2)}) collective-permute-start(bf16[224,576]{1,0:T(8,128)(2,1)S(1)} %add_kernel.12.refs_2_.refs_1_), channel_id=1, source_target_pairs={{0,1},{1,0},{2,3},{3,2},{4,5},{5,4},{6,7},{7,6},{8,9},{9,8},{10,11... | collective-permute-start | bytes 774152 | tf_op jit(solution)/shard_map/ppermute | solution.py:20
  156.2 12.6 %collective-permute-start.57 = (bf16[128,768]{1,0:T(8,128)(2,1)S(1)}, bf16[128,768]{1,0:T(8,128)(2,1)S(1)}, u32[]{:S(2)}, u32[]{:S(2)}) collective-permute-start(bf16[128,768]{1,0:T(8,128)(2,1)S(1)} %get-tuple-element.224), channel_id=1, source_target_pairs={{0,8},{1,9},{2,10},{3,11},{4,12},{5,13},{6,14},{7,15},{8,0},{9,1},... | collective-permute-start | bytes 589832 | tf_op jit(solution)/shard_map/ppermute | solution.py:20
  157.4 7.4 %collective-permute-start.59 = (bf16[96,768]{1,0:T(8,128)(2,1)S(1)}, bf16[96,768]{1,0:T(8,128)(2,1)S(1)}, u32[]{:S(2)}, u32[]{:S(2)}) collective-permute-start(bf16[96,768]{1,0:T(8,128)(2,1)S(1)} %add_kernel.15.refs_6_.refs_1_), channel_id=1, source_target_pairs={{0,2},{1,3},{2,0},{3,1},{4,6},{5,7},{6,4},{7,5},{8,10},{9,11},{10,... | collective-permute-start | bytes 442376 | tf_op jit(solution)/shard_map/ppermute | solution.py:20
  158.3 13.9 %collective-permute-start.62 = (bf16[384,384]{1,0:T(8,128)(2,1)S(1)}, bf16[384,384]{1,0:T(8,128)(2,1)S(1)}, u32[]{:S(2)}, u32[]{:S(2)}) collective-permute-start(bf16[384,384]{1,0:T(8,128)(2,1)S(1)} %join_kernel.3.refs_3_.refs_15_), channel_id=1, source_target_pairs={{0,4},{1,5},{2,6},{3,7},{4,0},{5,1},{6,2},{7,3},{8,12},{9,13},{10,... | collective-permute-start | bytes 884744 | tf_op jit(solution)/shard_map/ppermute | solution.py:20
  165.3 6.9 %collective-permute-start.61 = (bf16[192,768]{1,0:T(8,128)(2,1)S(1)}, bf16[192,768]{1,0:T(8,128)(2,1)S(1)}, u32[]{:S(2)}, u32[]{:S(2)}) collective-permute-start(bf16[192,768]{1,0:T(8,128)(2,1)S(1)} %join_kernel.5.refs_13_.refs_17_), channel_id=1, source_target_pairs={{0,1},{1,0},{2,3},{3,2},{4,5},{5,4},{6,7},{7,6},{8,9},{9,8},{10,11... | collective-permute-start | bytes 884744 | tf_op jit(solution)/shard_map/ppermute | solution.py:20
  165.4 6.8 %collective-permute-start.48 = (bf16[224,576]{1,0:T(8,128)(2,1)S(1)}, bf16[224,576]{1,0:T(8,128)(2,1)S(1)}, u32[]{:S(2)}, u32[]{:S(2)}) collective-permute-start(bf16[224,576]{1,0:T(8,128)(2,1)S(1)} %collective-permute-done.44.refs_3_), channel_id=1, source_target_pairs={{0,1},{1,0},{2,3},{3,2},{4,5},{5,4},{6,7},{7,6},{8,9},{9,8},{10,11... | collective-permute-start | bytes 774152 | tf_op jit(solution)/shard_map/ppermute | solution.py:20
  165.9 6.3 %collective-permute-start.47 = (bf16[224,576]{1,0:T(8,128)(2,1)S(1)}, bf16[224,576]{1,0:T(8,128)(2,1)S(1)}, u32[]{:S(2)}, u32[]{:S(2)}) collective-permute-start(bf16[224,576]{1,0:T(8,128)(2,1)S(1)} %collective-permute-done.43.refs_2_), channel_id=1, source_target_pairs={{0,1},{1,0},{2,3},{3,2},{4,5},{5,4},{6,7},{7,6},{8,9},{9,8},{10,11... | collective-permute-start | bytes 774152 | tf_op jit(solution)/shard_map/ppermute | solution.py:20
  168.8 3.4 %collective-permute-start.49 = (bf16[224,576]{1,0:T(8,128)(2,1)S(1)}, bf16[224,576]{1,0:T(8,128)(2,1)S(1)}, u32[]{:S(2)}, u32[]{:S(2)}) collective-permute-start(bf16[224,576]{1,0:T(8,128)(2,1)S(1)} %collective-permute-done.45.refs_4_), channel_id=1, source_target_pairs={{0,1},{1,0},{2,3},{3,2},{4,5},{5,4},{6,7},{7,6},{8,9},{9,8},{10,11... | collective-permute-start | bytes 774152 | tf_op jit(solution)/shard_map/ppermute | solution.py:20
  (6 other events, 25.7 us)
